TPU v7x, 32 devices: a whole 2x2x4 slice. The times are simulated.
32 devices in a mesh: wide: 8 (over y, x, core), narrow: 4 (over z).
Axes of the slice: x: 2, y: 2, z: 4, core: 2. Of those that a mesh axis runs over, the one named last changes fastest.
Arguments:
- tokens: bfloat16 [8192, 768], P('wide'), may hold values from -6 to 6
- segments: int32 [8, 1024], P('wide'), may hold values from 0 to 21, never falling along the last dimension, each value on 1 to 256 neighbouring positions
- first_gain: float32 [768], replicated, may hold values from 0.1 to 1.9
- qkv_weight: bfloat16 [3, 768, 768], P(None, None, 'narrow'), may hold values from -0.21875 to 0.21875
- output_weight: bfloat16 [768, 768], P('narrow'), may hold values from -0.875 to 0.875
- second_gain: float32 [768], replicated, may hold values from 0.1 to 1.9
- geglu_weight: bfloat16 [2, 768, 1152], P(None, None, 'narrow'), may hold values from -0.21875 to 0.21875
- down_weight: bfloat16 [1152, 768], P('narrow'), may hold values from -0.25 to 0.25
- cotangent: bfloat16 [8192, 768], P('wide'), may hold values from -6 to 6
Outputs:
- layer_out: bfloat16 [8192, 768], P(('wide', 'narrow'))
- tokens_grad: float32 [8192, 768], P(('wide', 'narrow'))
- first_gain_grad: float32 [768], replicated
- qkv_grad: float32 [3, 768, 768], P(None, 'wide', 'narrow')
- output_grad: float32 [768, 768], P('narrow', 'wide')
- second_gain_grad: float32 [768], replicated
- geglu_grad: float32 [2, 768, 1152], P(None, 'wide', 'narrow')
- down_grad: float32 [1152, 768], P('narrow', 'wide')
Inputs may be any that keep to these rules, and one draw needn't show every extreme that they name: `segments`: segment numbers never fall along a row; each number names one document of 1 to 256 consecutive tokens, and every number from 0 up to the largest is used in each row.
All inputs are finite; a program needn't handle non-finite values.
Results may differ from a plain program's by a relative error of at most 0.014.
The roundings to bfloat16 on the way count: a program that leaves them out, or rounds other values in their place, can miss the bound.
Values may be sent and summed in bfloat16 or wider, within the bound.
No kernel may reach another device: no remote copies, remote signals or barrier semaphores. Data moves between devices by JAX's collectives and lax.ppermute only.
A program may use at most 128 MiB of HBM per device.

v0:
```python
import math

import jax
import jax.numpy as jnp
from jax import lax
from jax.sharding import PartitionSpec as P

HEAD = 64
LEN = 1024


EPSILON = 1e-05
ROPE_BASE = 160000.0


def normalize(values):
    centre = values - jnp.mean(values, axis=-1, keepdims=True)
    spread = jnp.mean(centre * centre, axis=-1, keepdims=True)
    inverse = lax.rsqrt(spread + EPSILON)
    return (centre * inverse, inverse)


def norm_back(upstream, unit_rows, inverse, gain):
    scaled = upstream * gain
    first_mean = jnp.mean(scaled, axis=-1, keepdims=True)
    second_mean = jnp.mean(scaled * unit_rows, axis=-1, keepdims=True)
    return (
        inverse * (scaled - first_mean - unit_rows * second_mean),
        jnp.sum(upstream * unit_rows, axis=0),
    )


def rotary_tables(segments):
    earlier = jnp.sum((segments[:, None, :] < segments[:, :, None]).astype(jnp.int32), axis=2)
    places = (
        (jnp.arange(segments.shape[1], dtype=jnp.int32)[None, :] - earlier)
        .reshape(-1)
        .astype(jnp.float32)
    )
    frequency = jnp.power(ROPE_BASE, -2.0 * jnp.arange(HEAD // 2, dtype=jnp.float32) / HEAD)
    angles = places[:, None] * frequency[None, :]
    return (jnp.cos(angles)[:, None, :], jnp.sin(angles)[:, None, :])


def rotate(values, cosine, sine_table):
    half_size = values.shape[-1] // 2
    first_half = values[..., :half_size]
    second = values[..., half_size:]
    return jnp.concatenate(
        [first_half * cosine - second * sine_table, second * cosine + first_half * sine_table],
        axis=-1,
    )


def rotate_back(upstream, cosine, sine_table):
    half_size = upstream.shape[-1] // 2
    first_half = upstream[..., :half_size]
    second = upstream[..., half_size:]
    return jnp.concatenate(
        [first_half * cosine + second * sine_table, second * cosine - first_half * sine_table],
        axis=-1,
    )


def own_rows(whole_rows):
    share_rows = whole_rows.shape[0] // lax.axis_size("narrow")
    return lax.dynamic_slice_in_dim(
        whole_rows, lax.axis_index("narrow") * share_rows, share_rows, 0
    )


def to_items(block_in, rows_count):
    heads_here = block_in.shape[1]
    return (
        block_in.reshape(rows_count, LEN, heads_here, HEAD)
        .transpose(0, 2, 1, 3)
        .reshape(rows_count * heads_here, LEN, HEAD)
    )


def from_items(item_rows, rows_count):
    heads_here = item_rows.shape[0] // rows_count
    return (
        item_rows.reshape(rows_count, heads_here, LEN, HEAD)
        .transpose(0, 2, 1, 3)
        .reshape(rows_count * LEN, heads_here * HEAD)
    )


def score_block(queries, key_rows, segment_row):
    scores = jnp.einsum(
        "qd,kd->qk", queries, key_rows, preferred_element_type=jnp.float32
    ) / math.sqrt(HEAD)
    same_doc = segment_row[:, None] == segment_row[None, :]
    return jnp.where(same_doc, scores, -1e30)


def attend_forward(pieces):
    queries, key_rows, values, segment_row = pieces
    scores = score_block(queries, key_rows, segment_row)
    highest = jnp.max(scores, axis=-1, keepdims=True)
    weights = jnp.exp(scores - highest)
    row_total = jnp.sum(weights, axis=-1, keepdims=True)
    probability = (weights / row_total).astype(jnp.bfloat16)
    context = jnp.dot(probability, values, preferred_element_type=jnp.float32)
    return (context, (highest + jnp.log(row_total))[:, 0])


def attend_backward(pieces):
    queries, key_rows, values, segment_row, log_total, context_back = pieces
    scores = score_block(queries, key_rows, segment_row)
    probability = jnp.exp(scores - log_total[:, None])
    prob_back = jnp.einsum("qd,kd->qk", context_back, values, preferred_element_type=jnp.float32)
    values_back = jnp.einsum(
        "qk,qd->kd",
        probability.astype(jnp.bfloat16),
        context_back,
        preferred_element_type=jnp.float32,
    )
    inner_sum = jnp.sum(probability * prob_back, axis=-1, keepdims=True)
    scores_back = (probability * (prob_back - inner_sum)).astype(jnp.bfloat16)
    queries_back = jnp.dot(scores_back, key_rows, preferred_element_type=jnp.float32) / math.sqrt(
        HEAD
    )
    keys_back = jnp.einsum(
        "qk,qd->kd", scores_back, queries, preferred_element_type=jnp.float32
    ) / math.sqrt(HEAD)
    return (queries_back, keys_back, values_back)


def geglu_act(gated_part, linear):
    return jax.nn.gelu(gated_part, approximate=False) * linear


def per_device(
    tokens,
    segments,
    first_gain,
    qkv_weight,
    output_weight,
    second_gain,
    geglu_weight,
    down_weight,
    cotangent,
):
    rows_count = segments.shape[0]
    inputs = tokens.astype(jnp.float32)
    tokens_count = inputs.shape[0]
    unit_one, inverse_one = normalize(inputs)
    normed_one = (unit_one * first_gain).astype(jnp.bfloat16)
    projected = jnp.einsum(
        "td,sde->ste", normed_one, qkv_weight, preferred_element_type=jnp.float32
    )
    heads_here = projected.shape[2] // HEAD
    cosine, sine_table = rotary_tables(segments)

    def heads_of(block_in):
        return block_in.reshape(tokens_count, heads_here, HEAD)

    queries = rotate(heads_of(projected[0]), cosine, sine_table).astype(jnp.bfloat16)
    key_rows = rotate(heads_of(projected[1]), cosine, sine_table).astype(jnp.bfloat16)
    values = heads_of(projected[2]).astype(jnp.bfloat16)
    item_segments = jnp.repeat(segments, heads_here, axis=0)
    query_items = to_items(queries, rows_count)
    key_items = to_items(key_rows, rows_count)
    value_items = to_items(values, rows_count)
    context_items, log_totals = lax.map(
        attend_forward, (query_items, key_items, value_items, item_segments)
    )
    context = from_items(context_items, rows_count).astype(jnp.bfloat16)
    attended = jnp.dot(context, output_weight, preferred_element_type=jnp.float32)
    residual = inputs + lax.psum(attended, "narrow")
    unit_two, inverse_two = normalize(residual)
    normed_two = (unit_two * second_gain).astype(jnp.bfloat16)
    geglu_out = jnp.einsum(
        "td,sdf->stf", normed_two, geglu_weight, preferred_element_type=jnp.float32
    )
    act_value, act_pull = jax.vjp(geglu_act, geglu_out[0], geglu_out[1])
    activated = act_value.astype(jnp.bfloat16)
    branch = jnp.dot(activated, down_weight, preferred_element_type=jnp.float32)
    layer_out = own_rows(residual + lax.psum(branch, "narrow")).astype(jnp.bfloat16)
    down_part = jnp.einsum("tf,td->fd", activated, cotangent, preferred_element_type=jnp.float32)
    act_back = jnp.einsum("td,fd->tf", cotangent, down_weight, preferred_element_type=jnp.float32)
    gated_back, linear_back = act_pull(act_back)
    geglu_back = jnp.stack([gated_back, linear_back]).astype(jnp.bfloat16)
    geglu_part = jnp.einsum(
        "td,stf->sdf", normed_two, geglu_back, preferred_element_type=jnp.float32
    )
    normed_two_back = jnp.einsum(
        "stf,sdf->td", geglu_back, geglu_weight, preferred_element_type=jnp.float32
    )
    cotangent_full = cotangent.astype(jnp.float32)
    residual_part, gain_two_grad = norm_back(normed_two_back, unit_two, inverse_two, second_gain)
    residual_back = cotangent_full + lax.psum(residual_part, "narrow")
    residual_low = residual_back.astype(jnp.bfloat16)
    output_part = jnp.einsum("tc,td->cd", context, residual_low, preferred_element_type=jnp.float32)
    context_back = jnp.einsum(
        "td,cd->tc", residual_low, output_weight, preferred_element_type=jnp.float32
    ).astype(jnp.bfloat16)
    back_items = to_items(heads_of(context_back), rows_count)
    query_grads, key_grads, value_grads = lax.map(
        attend_backward,
        (query_items, key_items, value_items, item_segments, log_totals, back_items),
    )
    query_rows = rotate_back(
        heads_of(from_items(query_grads, rows_count)), cosine, sine_table
    ).reshape(tokens_count, -1)
    key_grad_rows = rotate_back(
        heads_of(from_items(key_grads, rows_count)), cosine, sine_table
    ).reshape(tokens_count, -1)
    qkv_back = jnp.stack([query_rows, key_grad_rows, from_items(value_grads, rows_count)]).astype(
        jnp.bfloat16
    )
    qkv_part = jnp.einsum("td,ste->sde", normed_one, qkv_back, preferred_element_type=jnp.float32)
    normed_one_back = jnp.einsum(
        "ste,sde->td", qkv_back, qkv_weight, preferred_element_type=jnp.float32
    )
    input_part, gain_one_grad = norm_back(normed_one_back, unit_one, inverse_one, first_gain)
    tokens_grad = own_rows(residual_back + lax.psum(input_part, "narrow"))
    qkv_share, output_share, geglu_share, down_share = (
        lax.psum_scatter(qkv_part, "wide", scatter_dimension=1, tiled=True),
        lax.psum_scatter(output_part, "wide", scatter_dimension=1, tiled=True),
        lax.psum_scatter(geglu_part, "wide", scatter_dimension=1, tiled=True),
        lax.psum_scatter(down_part, "wide", scatter_dimension=1, tiled=True),
    )
    gain_one_sum, gain_two_sum = lax.psum((gain_one_grad, gain_two_grad), ("wide", "narrow"))
    return (
        layer_out,
        tokens_grad,
        gain_one_sum,
        qkv_share,
        output_share,
        gain_two_sum,
        geglu_share,
        down_share,
    )


def solution(mesh):
    return jax.shard_map(
        per_device,
        mesh=mesh,
        in_specs=(
            P("wide", None),
            P("wide", None),
            P(),
            P(None, None, "narrow"),
            P("narrow", None),
            P(),
            P(None, None, "narrow"),
            P("narrow", None),
            P("wide", None),
        ),
        out_specs=(
            P(("wide", "narrow"), None),
            P(("wide", "narrow"), None),
            P(),
            P(None, "wide", "narrow"),
            P("narrow", "wide"),
            P(),
            P(None, "wide", "narrow"),
            P("narrow", "wide"),
        ),
        check_vma=False,
    )
```

profile of v0, /device:TPU:0, one launch (start us, length us, event | category | flops | bytes accessed | tf_op | source)
XLA Modules:
  0.0 709.8 jit_solution(10616122116033907553)
XLA Ops:
  27.2 17.7 %while.28 = (s32[]{:T(128)}, bf16[3,1024,64]{1,2,0:T(8,128)(2,1)}, f32[3,1024]{1,0:T(4,128)S(1)}, s32[3,1024]{1,0:T(4,128)S(1)}, bf16[3,1024,64]{2,1,0:T(8,128)(...) while((s32[]{:T(128)}, bf16[3,1024,64]{1,2,0:T(8,128)(2,1)}, ...), condition=%wide.region_6.7_spmd.clone, body=%wide.region_3.6_spmd.sunk.clone | while | flops 284163072 | bytes 16849044 | solution.py:167
  30.0 2.3 fusion.168
  35.9 2.3 fusion.168
  41.8 2.3 fusion.168
  44.9 3.4 fusion.114
  48.6 3.2 fusion.116
  51.7 120.5 %all-reduce.6.cloned.1.call-done = f32[1024,768]{1,0:T(8,128)} async-done(((f32[1024,768]{1,0:T(8,128)}), f32[1024,768]{1,0:T(8,128)}) %all-reduce.6.cloned.1.call-update) | async-done | bytes 3145744 | tf_op jit(solution)/shard_map/psum | solution.py:172
  172.3 2.3 fusion.110
  177.7 2.8 fusion.94
  182.0 2.8 fusion.60
  184.7 2.3 subtract_multiply_fusion
  187.1 3.7 convolution_bitcast_fusion.2
  190.9 5.3 convolution_bitcast_fusion.1
  196.2 5.1 copy.79
  201.3 3.9 reshape.346
  205.5 101.8 %all-reduce.8.cloned.1.call-done = f32[1024,768]{1,0:T(8,128)} async-done(((f32[1024,768]{1,0:T(8,128)}), f32[1024,768]{1,0:T(8,128)}) %all-reduce.8.cloned.1.call-update) | async-done | bytes 3145744 | tf_op jit(solution)/shard_map/psum | solution.py:194
  307.3 2.7 convert_add_fusion.1
  313.1 2.2 copy.60
  315.3 27.2 %while.29 = (s32[]{:T(128)}, f32[3,1024,64]{1,2,0:T(8,128)}, f32[3,1024,64]{1,2,0:T(8,128)}, bf16[3,1024,64]{1,2,0:T(8,128)(2,1)}, s32[3,1024]{1,0:T(4,128)S(1)}...) while((s32[]{:T(128)}, f32[3,1024,64]{1,2,0:T(8,128)}, ...), condition=%wide.region_16.17_spmd.clone, body=%wide.region_14.16_spmd.sunk.clone | while | flops 681704448 | bytes 45131008 | solution.py:201
  342.5 3.6 convolution_bitcast_fusion.3
  348.8 2.5 fusion.66
  351.3 4.3 copy.75
  355.6 4.7 reshape.342
  361.4 3.8 fusion.115
  365.2 2.2 fusion.58
  367.4 2.3 fusion.57
  371.4 18.9 %reduce-scatter.17.cloned.1.call-done = f32[96,576]{1,0:T(8,128)} async-done(((f32[768,576]{1,0:T(8,128)}), f32[96,576]{1,0:T(8,128)}) %reduce-scatter.17.cloned.1.call-update) | async-done | bytes 221200
  392.3 39.4 %all-reduce = (f32[768]{0:T(1024)}, f32[768]{0:T(1024)}) all-reduce(f32[768]{0:T(1024)S(1)} %get-tuple-element.207, f32[768]{0:T(1024)S(1)} %copy-done.27), channel_id=1, replica_groups=mesh['wide'=8,'narrow'=4] {'wide','narrow'}, use_global_device_ids=true, to_apply=%region_21.22 | all-reduce | flops 1536 | bytes 12288 | tf_op jit(solution)/shard_map/psum | solution.py:226
  433.3 39.4 %reduce-scatter.13.cloned.1.call-done = f32[96,576]{1,0:T(8,128)} async-done(((f32[768,576]{1,0:T(8,128)}), f32[96,576]{1,0:T(8,128)}) %reduce-scatter.13.cloned.1.call-update) | async-done | bytes 221200
  474.6 223.9 %all-reduce.10.cloned.1.call-done = (f32[1024,768]{1,0:T(8,128)}, f32[1024,768]{1,0:T(8,128)}) async-done(((f32[1024,768]{1,0:T(8,128)}, f32[1024,768]{1,0:T(8,128)}), (f32[1024,768]{1,0:T(8,128)}, f32[1024,768]{1,0:T(8,128)})) %all-reduce.10.cloned.1.call-update) | async-done | bytes 6291472 | tf_op jit(solution)/shard_map/psum | solution.py:181
  698.4 2.3 dynamic-slice_add_fusion
  700.8 2.2 fusion.89
  (184 shorter events, 76.6 us)
Async XLA Ops:
  7.2 3.2 copy-start
  7.2 2.6 copy-start.3
  7.2 3.2 copy-start.24
  7.2 165.1 %all-reduce.6.cloned.1.call-start = ((), (), s32[]{:S(2)}) async-start(), calls=%async_computation.4 | async-start | bytes 6291456 | tf_op jit(solution)/shard_map/psum | solution.py:172
  13.9 4.7 copy-start.8
  48.3 259.0 %all-reduce.8.cloned.1.call-start = ((), (), s32[]{:S(2)}) async-start(), calls=%async_computation.5 | async-start | bytes 6291456 | tf_op jit(solution)/shard_map/psum | solution.py:194
  174.5 10.2 %copy-start.1 = (f32[1024,768]{1,0:T(8,128)}, f32[1024,768]{1,0:T(8,128)S(1)}, u32[]{:S(2)}) copy-start(f32[1024,768]{1,0:T(8,128)S(1)} %get-tuple-element.252) | copy-start | bytes 9437188
  174.6 1.9 copy-start.28
  180.5 1.4 copy-start.18
  182.0 2.8 copy-start.17
  187.0 182.7 %reduce-scatter.19.cloned.1.call-start = ((), (), s32[]{:S(2)}) async-start(), calls=%async_computation.9 | async-start | bytes 1327104
  190.8 199.5 %reduce-scatter.17.cloned.1.call-start = ((), (), s32[]{:S(2)}) async-start(), calls=%async_computation.8 | async-start | bytes 2211840
  205.2 226.4 %reduce-scatter.15.cloned.1.call-start = ((), (), s32[]{:S(2)}) async-start(), calls=%async_computation.7 | async-start | bytes 884736
  307.3 4.4 copy-start.14
  310.0 1.7 copy-start.2
  315.3 1.8 copy-start.4
  321.4 2.0 copy-start.11
  321.4 1.5 copy-start.15
  324.4 1.8 copy-start.4
  330.5 2.0 copy-start.11
  330.5 1.5 copy-start.15
  333.4 1.8 copy-start.4
  339.5 2.0 copy-start.11
  339.5 1.5 copy-start.15
  346.1 126.5 %reduce-scatter.13.cloned.1.call-start = ((), (), s32[]{:S(2)}) async-start(), calls=%async_computation.6 | async-start | bytes 2211840
  346.2 2.6 copy-start.12
  346.2 2.6 copy-start.25
  360.3 338.1 %all-reduce.10.cloned.1.call-start = ((), (), s32[]{:S(2)}) async-start(), calls=%async_computation.10 | async-start | bytes 12582912 | tf_op jit(solution)/shard_map/psum | solution.py:181
  361.4 3.8 copy-start.13
  361.4 3.8 copy-start.20
  361.4 3.8 copy-start.22
  369.7 22.6 %copy-start.27 = (f32[768]{0:T(1024)S(1)}, f32[768]{0:T(1024)}, u32[]{:S(2)}) copy-start(f32[768]{0:T(1024)} %get-tuple-element.205) | copy-start | bytes 9220
  (18 other events, 17.4 us)
Sparse Core Ops, SparseCore 0:
  48.5 123.7 all-reduce.5
  187.2 120.0 all-reduce.7
  310.5 35.7 reduce-scatter.18
  350.0 40.2 reduce-scatter.16
  393.9 35.0 reduce-scatter.14
  432.2 40.4 reduce-scatter.12
  475.2 223.1 all-reduce.9
where the time goes:
time: 711 us; the launch traced here: 710 us
  waiting for transfers between devices  505 us (71%)
  matrix products  67 us (9%)
  local copies, waits for them, and re-layouts  47.5 us (7%)
  blocking collectives  39.4 us (6%)
  other arithmetic  35.4 us (5%)
  between operations  14.5 us (2%)
    psum x1, waiting for transfers between devices, per_device(): lax.psum(branch, 'narrow')  224 us
    psum x1, waiting for transfers between devices, per_device(): residual = inputs + lax.psum(attended, 'narrow')  121 us
    psum x1, waiting for transfers between devices, per_device(): residual_back = cotangent_full + lax.psum(residual_part, 'narrow')  102 us
    unnamed x11, waiting for transfers between devices  58.4 us
    psum x1, blocking collectives, per_device(): lax.psum((gain_one_grad, gain_two_grad), ('wide', 'narrow'))  39.4 us
    unnamed x55, local copies, waits for them, and re-layouts  31.6 us
  transfers between devices with their start and end apart: 7, of which 5 were waited for; matrix products, arithmetic and copies ran while one was open for 12% of the time, Pallas kernels for 0%

commit v1 on v0

v1 whole, which is shorter than its diff:
```python
import functools
import math

import jax
import jax.numpy as jnp
import numpy as np
from jax import lax
from jax.experimental import pallas as pl
from jax.experimental.pallas import tpu as pltpu
from jax.sharding import PartitionSpec as P

HEAD = 64
LEN = 1024
D = 768
HEADS_HERE = 3
COLS = HEADS_HERE * HEAD
LANES = 256
DOC = 256
QB = 128
EPSILON = 1e-05
ROPE_BASE = 160000.0
NARROW = 4
BLOCK = LEN // NARROW
F32 = jnp.float32
BF16 = jnp.bfloat16
NEGATIVE = -1e30
VMEM_LIMIT = 48 * 1024 * 1024

NN = (((1,), (0,)), ((), ()))
NT = (((1,), (1,)), ((), ()))
TN = (((0,), (0,)), ((), ()))


def dot(a, b, dims=NN):
    return lax.dot_general(a, b, dims, preferred_element_type=F32)


def call(body, ins, outs, scratch=(), flops=0, scalars=1):
    specs = [pl.BlockSpec(memory_space=pltpu.SMEM)] * scalars
    specs += [pl.BlockSpec(memory_space=pltpu.VMEM)] * (len(ins) - scalars)
    size = sum(math.prod(x.shape) * x.dtype.itemsize for x in (*ins, *outs))
    return pl.pallas_call(
        body,
        out_shape=tuple(jax.ShapeDtypeStruct(o.shape, o.dtype) for o in outs),
        in_specs=specs,
        out_specs=tuple(pl.BlockSpec(memory_space=pltpu.VMEM) for _ in outs),
        scratch_shapes=list(scratch),
        compiler_params=pltpu.CompilerParams(vmem_limit_bytes=VMEM_LIMIT),
        cost_estimate=pl.CostEstimate(flops=flops, bytes_accessed=size, transcendentals=0),
    )(*ins)


def sds(shape, dtype):
    return jax.ShapeDtypeStruct(shape, dtype)


def rotary_table():
    position = np.arange(DOC, dtype=np.float64)
    frequency = ROPE_BASE ** (-2.0 * np.arange(HEAD // 2, dtype=np.float64) / HEAD)
    angle = position[:, None] * frequency[None, :]
    cosine, sine = np.cos(angle), np.sin(angle)
    table = np.zeros((DOC, 2 * LANES), np.float32)
    for h in range(HEADS_HERE):
        base = h * HEAD
        table[:, base : base + 32] = cosine
        table[:, base + 32 : base + 64] = cosine
        table[:, LANES + base : LANES + base + 32] = -sine
        table[:, LANES + base + 32 : LANES + base + 64] = sine
    high = table.astype(jnp.bfloat16)
    low = (table - high.astype(np.float32)).astype(jnp.bfloat16)
    return np.stack([high, low])


def normalize(values):
    centre = values - jnp.mean(values, axis=-1, keepdims=True)
    spread = jnp.mean(centre * centre, axis=-1, keepdims=True)
    inverse = lax.rsqrt(spread + EPSILON)
    return centre * inverse, inverse


def norm_back(upstream, unit_rows, inverse, gain):
    scaled = upstream * gain
    first_mean = jnp.mean(scaled, axis=-1, keepdims=True)
    second_mean = jnp.mean(scaled * unit_rows, axis=-1, keepdims=True)
    return inverse * (scaled - first_mean - unit_rows * second_mean)


def lane_head(rows):
    return lax.broadcasted_iota(jnp.int32, (rows, LANES), 1) // HEAD


def swap_halves(x):
    lane = lax.broadcasted_iota(jnp.int32, x.shape, 1)
    return jnp.where(
        lane % HEAD < HEAD // 2,
        pltpu.roll(x, LANES - HEAD // 2, 1),
        pltpu.roll(x, HEAD // 2, 1),
    )


def by_head(block, head):
    return jnp.concatenate(
        [jnp.where(head == h, block, jnp.zeros_like(block)) for h in range(HEADS_HERE)], axis=0
    )


def merge_heads(stacked, head):
    parts = jnp.split(stacked, HEADS_HERE, axis=0)
    return jnp.where(head == 0, parts[0], jnp.where(head == 1, parts[1], parts[2]))


def window(i):
    reach = DOC // QB
    return max(0, i - reach) * QB, min(LEN // QB, i + reach + 1) * QB


def forward_kernel(
    z_ref, tok_ref, seg_ref, gain_ref, w_ref, table_ref,
    c0_ref, c1_ref, c2_ref, c3_ref, q_ref, k_ref, v_ref, normed_ref, lse_ref, trig_ref, segc_ref,
    proj_ref, ctx_ref,
):
    z = z_ref[0]
    seg = jnp.broadcast_to(seg_ref[...].astype(F32), (8, LEN))
    index = lax.broadcasted_iota(jnp.int32, (8, LEN), 1)
    first = jnp.where(seg != pltpu.roll(seg, 1, 1), index, 0)
    first = jnp.where(index == 0, 0, first).astype(F32)
    shift = 1
    while shift < DOC:
        first = jnp.maximum(first, jnp.where(index >= shift, pltpu.roll(first, shift, 1), 0.0))
        shift *= 2
    place = index.astype(F32) - first
    segc_ref[...] = jnp.transpose(jnp.broadcast_to(seg[:1], (128, LEN)))
    placec = jnp.transpose(jnp.broadcast_to(place[:1], (128, LEN)))
    lane = lax.broadcasted_iota(jnp.int32, (LEN, 128), 1).astype(F32)
    hot = jnp.concatenate(
        [jnp.where(placec == lane + 128.0 * j, 1.0, 0.0) for j in range(DOC // 128)], axis=1
    ).astype(BF16)
    trig_ref[...] = dot(hot, table_ref[0]) + dot(hot, table_ref[1])

    def norm_rows(i, carry):
        rows = pl.ds(pl.multiple_of(i * 128, 128), 128)
        unit, _ = normalize(tok_ref[rows, :].astype(F32))
        normed_ref[rows, :] = (unit * gain_ref[...]).astype(BF16)
        return carry

    lax.fori_loop(0, LEN // 128, norm_rows, 0)
    proj_ref[:, COLS:] = jnp.zeros((LEN, LANES - COLS), F32)
    for s, out in enumerate((q_ref, k_ref)):
        proj_ref[:, :COLS] = dot(normed_ref[...], w_ref[s])
        x = proj_ref[...]
        out[...] = (x * trig_ref[:, :LANES] + swap_halves(x) * trig_ref[:, LANES:]).astype(BF16)
    proj_ref[:, :COLS] = dot(normed_ref[...], w_ref[2])
    v_ref[...] = proj_ref[...].astype(BF16)

    head = lane_head(QB)
    column = lax.broadcasted_iota(jnp.int32, (QB, 128), 1)
    for i in range(LEN // QB):
        low, high = window(i)
        rows = slice(i * QB, (i + 1) * QB)
        stacked = by_head(q_ref[rows, :] * jnp.asarray(1.0 / math.sqrt(HEAD), BF16), head)
        scores = dot(stacked, k_ref[low:high, :], NT)
        same = segc_ref[rows, 0:1] == seg_ref[0:1, low:high].astype(F32)
        parts, logs = [], []
        for h in range(HEADS_HERE):
            mine = jnp.where(same, scores[h * QB : (h + 1) * QB], NEGATIVE)
            top = jnp.max(mine, axis=-1, keepdims=True)
            weights = jnp.exp(mine - top)
            total = jnp.sum(weights, axis=-1, keepdims=True)
            parts.append((weights * (1.0 / total)).astype(BF16))
            logs.append(top + jnp.log(total))
        lse_ref[rows, :] = jnp.where(column == 0, logs[0], jnp.where(column == 1, logs[1], logs[2]))
        mixed = dot(jnp.concatenate(parts, axis=0), v_ref[low:high, :])
        context = merge_heads(mixed, head)[:, :COLS].astype(BF16)
        block, r = i * QB // BLOCK, i * QB % BLOCK
        ctx_ref[block, r : r + QB, :COLS] = context
        ctx_ref[block ^ 1, r : r + QB, COLS:] = context
    for k, out in enumerate((c0_ref, c1_ref, c2_ref, c3_ref)):
        out[...] = ctx_ref[z ^ k]


def middle_kernel(
    tok_own, tok_par, cot_own, cot_par, c0, c1, c2, c3, wo_ref, gain_ref, gw_ref, dw_ref, other_ref,
    res_ref, normed_ref, act_ref, gb_ref, keep_ref, send_ref, out_keep_ref, out_send_ref,
    cot_ref,
):
    for half, tok in enumerate((tok_own, tok_par)):
        rows = slice(half * BLOCK, (half + 1) * BLOCK)
        attended = jnp.zeros((BLOCK, D), F32)
        for k, c in enumerate((c0, c1, c2, c3)):
            attended += dot(c[:, half * COLS : (half + 1) * COLS], wo_ref[k])
        residual = tok[...].astype(F32) + attended
        res_ref[rows, :] = residual
        unit, _ = normalize(residual)
        normed_ref[rows, :] = (unit * gain_ref[...]).astype(BF16)
    cot_ref[:BLOCK, :] = cot_own[...]
    cot_ref[BLOCK:, :] = cot_par[...]
    branch, back = None, None
    for j in range(2):
        w0 = gw_ref[0] if j == 0 else other_ref[0]
        w1 = gw_ref[1] if j == 0 else other_ref[1]
        gate = dot(normed_ref[...], w0)
        linear = dot(normed_ref[...], w1)
        act_back = dot(cot_ref[...], dw_ref[...], NT) if j == 0 else dot(cot_ref[...], other_ref[2])
        cdf = 0.5 * (1.0 + lax.erf(gate * math.sqrt(0.5)))
        slope = cdf + gate * (jnp.exp(-0.5 * gate * gate) * (1.0 / math.sqrt(2.0 * math.pi)))
        gelu = gate * cdf
        act = (gelu * linear).astype(BF16)
        gb0 = (act_back * linear * slope).astype(BF16)
        gb1 = (act_back * gelu).astype(BF16)
        act_ref[j] = act
        gb_ref[j, 0] = gb0
        gb_ref[j, 1] = gb1
        branch_part = dot(act, dw_ref[...]) if j == 0 else dot(act, other_ref[2], NT)
        back_part = dot(gb0, w0, NT) + dot(gb1, w1, NT)
        branch = branch_part if branch is None else branch + branch_part
        back = back_part if back is None else back + back_part
    keep_ref[...] = back[:BLOCK]
    send_ref[...] = back[BLOCK:].astype(BF16)
    out_keep_ref[...] = branch[:BLOCK] + res_ref[:BLOCK, :]
    out_send_ref[...] = branch[BLOCK:].astype(BF16)


def ff_grad_kernel(normed_ref, act_ref, gb_ref, cot_own, cot_par, out_ref):
    width = act_ref.shape[2]
    for j in range(2):
        base = j * 3 * width
        for s in range(2):
            at = base + s * width
            out_ref[:, at : at + width] = dot(normed_ref[...], gb_ref[j, s], TN).astype(BF16)
        at = base + 2 * width
        part = dot(cot_own[...], act_ref[j, :BLOCK], TN) + dot(cot_par[...], act_ref[j, BLOCK:], TN)
        out_ref[:, at : at + width] = part.astype(BF16)


def residual_kernel(
    keep_ref, recv_ref, res_ref, gain_ref, cot_ref, wo_ref,
    back_ref, low_ref, gain_out, b0, b1, b2, b3,
):
    unit, inverse = normalize(res_ref[:BLOCK, :])
    upstream = keep_ref[...] + recv_ref[...].astype(F32)
    back = cot_ref[...].astype(F32) + norm_back(upstream, unit, inverse, gain_ref[...])
    back_ref[...] = back
    gain_out[...] = jnp.sum(upstream * unit, axis=0, keepdims=True)
    low = back.astype(BF16)
    low_ref[...] = low
    for k, out in enumerate((b0, b1, b2, b3)):
        part = dot(low, wo_ref[k], NT).astype(BF16)
        out[:, :COLS] = part[: BLOCK // 2]
        out[:, COLS:] = part[BLOCK // 2 :]


def output_grad_kernel(low_ref, c0, c1, c2, c3, out_ref):
    for k, c in enumerate((c0, c1, c2, c3)):
        out_ref[:, k * COLS : (k + 1) * COLS] = dot(low_ref[...], c[:, :COLS], TN).astype(BF16)


def backward_kernel(
    z_ref, seg_ref, segc_ref, q_ref, k_ref, v_ref, lse_ref, trig_ref, b0, b1, b2, b3, w_ref,
    qkv_ref, n0, n1, n2, n3,
    back_ref, dq_ref, dk_ref, dv_ref,
):
    z = z_ref[0]
    half = BLOCK // 2
    back_ref[:, COLS:] = jnp.zeros((LEN, LANES - COLS), BF16)
    for k, b in enumerate((b0, b1, b2, b3)):
        base = pl.multiple_of((z ^ k) * BLOCK, BLOCK)
        back_ref[pl.ds(base, half), :COLS] = b[:, :COLS]
        back_ref[pl.ds(pl.multiple_of(base + half, half), half), :COLS] = b[:, COLS:]
    dk_ref[...] = jnp.zeros_like(dk_ref)
    dv_ref[...] = jnp.zeros_like(dv_ref)
    head = lane_head(QB)
    scale = jnp.asarray(1.0 / math.sqrt(HEAD), BF16)
    for i in range(LEN // QB):
        low, high = window(i)
        rows = slice(i * QB, (i + 1) * QB)
        stacked = by_head(q_ref[rows, :] * scale, head)
        upstream = by_head(back_ref[rows, :], head)
        scores = dot(stacked, k_ref[low:high, :], NT)
        prob_back = dot(upstream, v_ref[low:high, :], NT)
        same = segc_ref[rows, 0:1] == seg_ref[0:1, low:high].astype(F32)
        probs, grads = [], []
        for h in range(HEADS_HERE):
            at = slice(h * QB, (h + 1) * QB)
            prob = jnp.exp(jnp.where(same, scores[at], NEGATIVE) - lse_ref[rows, h : h + 1])
            inner = jnp.sum(prob * prob_back[at], axis=-1, keepdims=True)
            probs.append(prob.astype(BF16))
            grads.append((prob * (prob_back[at] - inner)).astype(BF16))
        prob = jnp.concatenate(probs, axis=0)
        grad = jnp.concatenate(grads, axis=0)
        dv_ref[low:high, :] += dot(prob, upstream, TN)
        dk_ref[low:high, :] += dot(grad, stacked, TN)
        dq_ref[rows, :] = merge_heads(dot(grad, k_ref[low:high, :]), head) * (1.0 / math.sqrt(HEAD))
    cosine, signed = trig_ref[:, :LANES], trig_ref[:, LANES:]
    for s, grad_ref in enumerate((dq_ref, dk_ref)):
        g = grad_ref[...]
        turned = g * cosine - swap_halves(g) * signed
        qkv_ref[:, s * COLS : (s + 1) * COLS] = turned[:, :COLS].astype(BF16)
    qkv_ref[:, 2 * COLS :] = dv_ref[:, :COLS].astype(BF16)
    for k, out in enumerate((n0, n1, n2, n3)):
        base = pl.multiple_of((z ^ k) * BLOCK, BLOCK)
        part = None
        for s in range(3):
            piece = dot(qkv_ref[pl.ds(base, BLOCK), s * COLS : (s + 1) * COLS], w_ref[s], NT)
            part = piece if part is None else part + piece
        out[...] = part.astype(out.dtype)


def qkv_grad_kernel(normed_ref, qkv_ref, w_ref, out_ref, gain_out):
    total = None
    for s in range(3):
        part = dot(normed_ref[...], qkv_ref[:, s * COLS : (s + 1) * COLS], TN)
        out_ref[:, s * COLS : (s + 1) * COLS] = part.astype(BF16)
        weighted = jnp.sum(part * w_ref[s].astype(F32), axis=1, keepdims=True)
        total = weighted if total is None else total + weighted
    gain_out[...] = jnp.broadcast_to(total, gain_out.shape)


def final_kernel(tok_ref, gain_ref, back_ref, n0, n1, n2, n3, out_ref):
    upstream = n0[...] + n1[...].astype(F32) + n2[...].astype(F32) + n3[...].astype(F32)
    unit, inverse = normalize(tok_ref[...].astype(F32))
    out_ref[...] = back_ref[...] + norm_back(upstream, unit, inverse, gain_ref[...])


def along_narrow(x, k):
    return lax.ppermute(x, "narrow", [(i, i ^ k) for i in range(NARROW)])


def in_plane(x):
    size = lax.axis_size("wide")
    copies = jnp.broadcast_to(x[None], (size, *x.shape))
    return lax.all_to_all(copies, "wide", 0, 0)


def per_device(
    tokens, segments, first_gain, qkv_weight, output_weight, second_gain, geglu_weight, down_weight,
    cotangent,
):
    size = lax.axis_size("wide")
    mine = lax.axis_index("wide")
    z = lax.axis_index("narrow")
    z_array = z.astype(jnp.int32).reshape(1)
    hidden = geglu_weight.shape[2]
    rows_d = D // size
    gain_one = first_gain.reshape(1, D)
    gain_two = second_gain.reshape(1, D)

    geglu_slice = lax.dynamic_slice_in_dim(geglu_weight, mine * rows_d, rows_d, 1)
    down_slice = lax.dynamic_slice_in_dim(down_weight, mine * rows_d, rows_d, 1).T
    ff_slice = jnp.concatenate([geglu_slice, down_slice[None]], axis=0)
    out_rows = COLS // size
    out_slice = lax.dynamic_slice_in_dim(output_weight, mine * out_rows, out_rows, 0)
    ff_there = in_plane(along_narrow(ff_slice, 2))
    out_there = in_plane(jnp.stack([along_narrow(out_slice, k) for k in (1, 2, 3)]))
    other = ff_there.transpose(1, 0, 2, 3).reshape(3, D, hidden)
    whole_out = jnp.concatenate(
        [output_weight[None], out_there.transpose(1, 0, 2, 3).reshape(3, COLS, D)], axis=0
    )

    def block_of(x, k):
        return lax.dynamic_slice_in_dim(x, (z ^ k) * BLOCK, BLOCK, 0)

    tok_own, tok_par = block_of(tokens, 0), block_of(tokens, 1)
    cot_own, cot_par = block_of(cotangent, 0), block_of(cotangent, 1)

    piece = sds((BLOCK, 2 * COLS), BF16)
    wide_rows = sds((LEN, LANES), BF16)
    c0, c1, c2, c3, q, k, v, normed_one, lse, trig, segc = call(
        forward_kernel,
        (z_array, tokens, segments, gain_one, qkv_weight, jnp.asarray(rotary_table())),
        (piece, piece, piece, piece, wide_rows, wide_rows, wide_rows, sds((LEN, D), BF16),
         sds((LEN, 128), F32), sds((LEN, 2 * LANES), F32), sds((LEN, 128), F32)),
        [pltpu.VMEM((LEN, LANES), F32), pltpu.VMEM((NARROW, BLOCK, 2 * COLS), BF16)],
        flops=5_000_000_000,
    )
    context = (c0, *(along_narrow(c, k) for k, c in ((1, c1), (2, c2), (3, c3))))

    own = sds((BLOCK, D), F32)
    own_low = sds((BLOCK, D), BF16)
    res, normed_two, act, gb, keep, send, out_keep, out_send = call(
        middle_kernel,
        (tok_own, tok_par, cot_own, cot_par, *context, whole_out, gain_two, geglu_weight,
         down_weight, other),
        (sds((2 * BLOCK, D), F32), sds((2 * BLOCK, D), BF16), sds((2, 2 * BLOCK, hidden), BF16),
         sds((2, 2, 2 * BLOCK, hidden), BF16), own, own_low, own, own_low),
        [pltpu.VMEM((2 * BLOCK, D), BF16)],
        flops=8_000_000_000,
        scalars=0,
    )
    recv = along_narrow(send, 1)
    layer_out = (out_keep + along_narrow(out_send, 1).astype(F32)).astype(BF16)
    (ff_part,) = call(
        ff_grad_kernel,
        (normed_two, act, gb, cot_own, cot_par),
        (sds((D, 6 * hidden), BF16),),
        flops=4_000_000_000,
        scalars=0,
    )
    ff_blocks = lax.all_to_all(ff_part.reshape(size, rows_d, 6 * hidden), "wide", 0, 0)

    low_piece = sds((BLOCK // 2, 2 * COLS), BF16)
    back, low, gain_two_part, b0, b1, b2, b3 = call(
        residual_kernel,
        (keep, recv, res, gain_two, cot_own, whole_out),
        (own, own_low, sds((1, D), F32), low_piece, low_piece, low_piece, low_piece),
        flops=1_000_000_000,
        scalars=0,
    )
    upstream = (b0, *(along_narrow(b, k) for k, b in ((1, b1), (2, b2), (3, b3))))
    (out_part,) = call(
        output_grad_kernel,
        (low, *context),
        (sds((D, NARROW * COLS), BF16),),
        flops=500_000_000,
        scalars=0,
    )
    out_blocks = lax.all_to_all(out_part.reshape(size, rows_d, NARROW * COLS), "wide", 0, 0)

    qkv_back, n0, n1, n2, n3 = call(
        backward_kernel,
        (z_array, segments, segc, q, k, v, lse, trig, *upstream, qkv_weight),
        (sds((LEN, 3 * COLS), BF16), own, own_low, own_low, own_low),
        [pltpu.VMEM((LEN, LANES), BF16)] + [pltpu.VMEM((LEN, LANES), F32)] * 3,
        flops=6_000_000_000,
    )
    others = [along_narrow(n, k) for k, n in ((1, n1), (2, n2), (3, n3))]
    qkv_part, gain_one_part = call(
        qkv_grad_kernel,
        (normed_one, qkv_back, qkv_weight),
        (sds((D, 3 * COLS), BF16), sds((D, 128), F32)),
        flops=1_000_000_000,
        scalars=0,
    )
    qkv_blocks = lax.all_to_all(qkv_part.reshape(size, rows_d, 3 * COLS), "wide", 0, 0)
    gains = jnp.stack([gain_one_part[:, 0] / first_gain, gain_two_part[0]])
    bit = 1
    while bit < size:
        gains = gains + lax.ppermute(gains, "wide", [(i, i ^ bit) for i in range(size)])
        bit *= 2
    for bit in (1, 2):
        gains = gains + along_narrow(gains, bit)

    (tokens_grad,) = call(
        final_kernel, (tok_own, gain_one, back, n0, *others), (own,), scalars=0
    )

    ff_sum = jnp.sum(ff_blocks.astype(F32), axis=0)
    half = 3 * hidden
    ff_own = ff_sum[:, :half] + along_narrow(ff_sum[:, half:].astype(BF16), 2).astype(F32)
    geglu_grad = ff_own[:, : 2 * hidden].reshape(rows_d, 2, hidden).transpose(1, 0, 2)
    down_grad = ff_own[:, 2 * hidden :].T
    out_sum = jnp.sum(out_blocks.astype(F32), axis=0)
    out_own = out_sum[:, :COLS]
    for k in (1, 2, 3):
        there = out_sum[:, k * COLS : (k + 1) * COLS].astype(BF16)
        out_own = out_own + along_narrow(there, k).astype(F32)
    qkv_sum = jnp.sum(qkv_blocks.astype(F32), axis=0)
    qkv_grad = qkv_sum.reshape(rows_d, 3, COLS).transpose(1, 0, 2)
    return (
        layer_out, tokens_grad, gains[0], qkv_grad, out_own.T, gains[1], geglu_grad, down_grad,
    )


def solution(mesh):
    return jax.shard_map(
        per_device,
        mesh=mesh,
        in_specs=(
            P("wide", None),
            P("wide", None),
            P(),
            P(None, None, "narrow"),
            P("narrow", None),
            P(),
            P(None, None, "narrow"),
            P("narrow", None),
            P("wide", None),
        ),
        out_specs=(
            P(("wide", "narrow"), None),
            P(("wide", "narrow"), None),
            P(),
            P(None, "wide", "narrow"),
            P("narrow", "wide"),
            P(),
            P(None, "wide", "narrow"),
            P("narrow", "wide"),
        ),
        check_vma=False,
    )
```

time: 711 us -> 246 us (0.35)
  waiting for transfers between devices: 505 us -> 90.9 us
  matrix products: 67 us -> 0 us
  starting transfers between devices: 0.95 us -> 62.3 us
  Pallas kernels: 0 us -> 48.4 us
  blocking collectives: 39.4 us -> 0 us
  other arithmetic: 35.4 us -> 8.33 us
  local copies, waits for them, and re-layouts: 47.5 us -> 33.6 us
  between operations: 14.5 us -> 1.19 us
    psum x3 -> x0, waiting for transfers between devices: 446 us -> none  [the longest x1 224 us: per_device(): lax.psum(branch, 'narrow')]
    ppermute x0 -> x24, waiting for transfers between devices: none -> 68 us  [the longest x21 41.6 us: along_narrow(): return lax.ppermute(x, 'narrow', [(i, i ^ k) for i in range(NARROW)])]
    unnamed x11 -> x0, waiting for transfers between devices: 58.4 us -> none
    dot_general x30 -> x0, matrix products: 58.4 us -> none  [the longest x6 9.06 us: score_block(): jnp.einsum('qd,kd->qk', queries, key_rows, preferred_element_type=jnp.flo...]
    pallas_call x0 -> x8, Pallas kernels: none -> 48.4 us  [call(): pl.pallas_call(body, out_shape=tuple((jax.ShapeDtypeStruct(o.shape, o.dty...]
    ppermute x0 -> x24, starting transfers between devices: none -> 40.7 us  [the longest x21 37.2 us: along_narrow(): return lax.ppermute(x, 'narrow', [(i, i ^ k) for i in range(NARROW)])]
    psum x1 -> x0, blocking collectives: 39.4 us -> none  [per_device(): lax.psum((gain_one_grad, gain_two_grad), ('wide', 'narrow'))]
    all_to_all x0 -> x5, waiting for transfers between devices: none -> 22.9 us  [the longest x1 12.9 us: per_device(): lax.all_to_all(qkv_part.reshape(size, rows_d, 3 * COLS), 'wide', 0, 0)]
  transfers between devices with their start and end apart: 7 -> 29, of which waited for: 5 -> 15; matrix products, arithmetic and copies ran while one was open for 12% -> 9% of each run, Pallas kernels for 0% -> 8%
where the time goes in v1:
time: 246 us; the launch traced here: 245 us
  waiting for transfers between devices  90.9 us (37%)
  starting transfers between devices  62.3 us (25%)
  Pallas kernels  48.4 us (20%)
  local copies, waits for them, and re-layouts  33.6 us (14%)
  other arithmetic  8.33 us (3%)
    pallas_call x8, Pallas kernels, call(): pl.pallas_call(body, out_shape=tuple((jax.ShapeDtypeStruct(o.shape, o.dty...  48.4 us
    ppermute x21, waiting for transfers between devices, along_narrow(): return lax.ppermute(x, 'narrow', [(i, i ^ k) for i in range(NARROW)])  41.6 us
    ppermute x21, starting transfers between devices, along_narrow(): return lax.ppermute(x, 'narrow', [(i, i ^ k) for i in range(NARROW)])  37.2 us
    ppermute x3, waiting for transfers between devices, per_device(): lax.ppermute(gains, 'wide', [(i, i ^ bit) for i in range(size)])  26.5 us
    unnamed x103, local copies, waits for them, and re-layouts  20 us
    all_to_all x1, waiting for transfers between devices, per_device(): lax.all_to_all(qkv_part.reshape(size, rows_d, 3 * COLS), 'wide', 0, 0)  12.9 us
    all_to_all x1, waiting for transfers between devices, per_device(): lax.all_to_all(out_part.reshape(size, rows_d, NARROW * COLS), 'wide', 0, 0)  9.98 us
    all_to_all x2, starting transfers between devices, in_plane(): return lax.all_to_all(copies, 'wide', 0, 0)  8.17 us
  transfers between devices with their start and end apart: 29, of which 15 were waited for; matrix products, arithmetic and copies ran while one was open for 9% of the time, Pallas kernels for 8%

profile of v1, /device:TPU:0, one launch (start us, length us, event | category | flops | bytes accessed | tf_op | source)
XLA Modules:
  0.0 244.8 jit_solution(11808301643821051508)
XLA Ops:
  1.4 5.0 %collective-permute-start.5 = (bf16[24,768]{1,0:T(8,128)(2,1)S(1)}, bf16[24,768]{1,0:T(8,128)(2,1)S(1)}, u32[]{:S(2)}, u32[]{:S(2)}) collective-permute-start(bf16[24,768]{1,0:T(8,128)(2,1)S(1)} %constant_dynamic-slice_fusion.1), channel_id=1, source_target_pairs={{0,3},{1,2},{2,1},{3,0},{4,7},{5,6},{6,5},{7,4},{8,11},{9,10},{10,... | collective-permute-start | bytes 110600 | tf_op jit(solution)/shard_map/ppermute | solution.py:325
  8.4 2.9 %collective-permute-done.4 = bf16[24,768]{1,0:T(8,128)(2,1)S(1)} collective-permute-done((bf16[24,768]{1,0:T(8,128)(2,1)S(1)}, bf16[24,768]{1,0:T(8,128)(2,1)S(1)}, u32[]{:S(2)}, u32[]{:S(2)}) %collective-permute-start.4) | collective-permute-done | bytes 36896 | tf_op jit(solution)/shard_map/ppermute | solution.py:325
  12.4 3.7 %all-to-all-start = ((bf16[8,3,24,768]{3,2,1,0:T(8,128)(2,1)}), bf16[8,3,24,768]{3,2,1,0:T(8,128)(2,1)S(1)}, u32[]{:S(2)}, u32[]{:S(2)}) async-start(bf16[8,3,24,768]{3,2,1,0:T(8,128)(2,1)} %broadcast_in_dim.9), calls=%async_computation | async-start | bytes 1769472 | tf_op jit(solution)/shard_map/all_to_all | solution.py:331
  18.3 2.1 collective-permute-start.6
  20.3 10.8 %collective-permute-done.6 = bf16[3,96,288]{1,2,0:T(8,128)(2,1)S(1)} collective-permute-done((bf16[3,96,288]{1,2,0:T(8,128)(2,1)S(1)}, bf16[3,96,288]{1,2,0:T(8,128)(2,1)S(1)}, u32[]{:S(2)}, u32[]{:S(2)}) %collective-permute-start.6) | collective-permute-done | bytes 165920 | tf_op jit(solution)/shard_map/ppermute | solution.py:325
  32.9 4.4 %all-to-all-start.1 = ((bf16[8,3,96,288]{3,2,1,0:T(8,128)(2,1)}), bf16[8,3,96,288]{3,2,1,0:T(8,128)(2,1)}, u32[]{:S(2)}, u32[]{:S(2)}) async-start(bf16[8,3,96,288]{3,2,1,0:T(8,128)(2,1)} %broadcast_in_dim.21), calls=%async_computation.1 | async-start | bytes 3538944 | tf_op jit(solution)/shard_map/all_to_all | solution.py:331
  38.4 12.6 %shard_map.161 = (bf16[256,384]{1,0:T(8,128)(2,1)S(1)}, bf16[256,384]{1,0:T(8,128)(2,1)}, bf16[256,384]{1,0:T(8,128)(2,1)}, bf16[256,384]{1,0:T(8,128)(2,1)}, bf...) custom-call(s32[1]{0:T(128)} %bitcast.z_ref, ...), custom_call_target="tpu_custom_call" | custom-call | flops 5000000000 | bytes 10066948 | tf_op jit(solution)/shard_map/pallas_call | solution.py:42
  55.1 2.7 %collective-permute-start.1 = (bf16[256,384]{1,0:T(8,128)(2,1)}, bf16[256,384]{1,0:T(8,128)(2,1)S(1)}, u32[]{:S(2)}, u32[]{:S(2)}) collective-permute-start(bf16[256,384]{1,0:T(8,128)(2,1)} %get-tuple-element.43), channel_id=1, source_target_pairs={{0,2},{1,3},{2,0},{3,1},{4,6},{5,7},{6,4},{7,5},{8,10},{9,11},{10,... | collective-permute-start | bytes 589832 | tf_op jit(solution)/shard_map/ppermute | solution.py:325
  60.9 2.5 %copy.35.gw_ref = bf16[2,768,288]{2,1,0:T(8,128)(2,1)} copy(bf16[2,768,288]{1,2,0:T(8,128)(2,1)} %param.16) | data formatting | bytes 1769472 | tf_op args[6]
  65.9 3.0 %copy.34 = bf16[3,8,96,288]{3,2,1,0:T(8,128)(2,1)} copy(bf16[3,8,96,288]{3,2,0,1:T(8,128)(2,1)} %bitcast.9) | data formatting | bytes 2654208 | tf_op jit(solution)/shard_map/transpose | solution.py:354
  68.9 3.5 %collective-permute-done.1.c2 = bf16[256,384]{1,0:T(8,128)(2,1)S(1)} collective-permute-done((bf16[256,384]{1,0:T(8,128)(2,1)}, bf16[256,384]{1,0:T(8,128)(2,1)S(1)}, u32[]{:S(2)}, u32[]{:S(2)}) %collective-permute-start.1) | collective-permute-done | bytes 196640 | tf_op jit(solution)/shard_map/ppermute | solution.py:325
  72.4 11.1 %shard_map.162 = (f32[512,768]{1,0:T(8,128)}, bf16[512,768]{1,0:T(8,128)(2,1)S(1)}, bf16[2,512,288]{2,1,0:T(8,128)(2,1)S(1)}, bf16[2,2,512,288]{3,2,1,0:T(8,128)...) custom-call(bf16[256,768]{1,0:T(8,128)(2,1)S(1)} %get-tuple-element., ...), custom_call_target="tpu_custom_call" | custom-call | flops 8000000000 | bytes 12684288 | tf_op jit(solution)/shard_map/pallas_call | solution.py:42
  85.2 4.2 %collective-permute-start.8 = (bf16[256,768]{1,0:T(8,128)(2,1)S(1)}, bf16[256,768]{1,0:T(8,128)(2,1)S(1)}, u32[]{:S(2)}, u32[]{:S(2)}) collective-permute-start(bf16[256,768]{1,0:T(8,128)(2,1)S(1)} %get-tuple-element.48), channel_id=1, source_target_pairs={{0,1},{1,0},{2,3},{3,2},{4,5},{5,4},{6,7},{7,6},{8,9},{9,8},{10,11... | collective-permute-start | bytes 1179656 | tf_op jit(solution)/shard_map/ppermute | solution.py:325
  89.3 8.8 %collective-permute-done.8.recv_ref = bf16[256,768]{1,0:T(8,128)(2,1)S(1)} collective-permute-done((bf16[256,768]{1,0:T(8,128)(2,1)S(1)}, bf16[256,768]{1,0:T(8,128)(2,1)S(1)}, u32[]{:S(2)}, u32[]{:S(2)}) %collective-permute-start.8) | collective-permute-done | bytes 393248 | tf_op jit(solution)/shard_map/ppermute | solution.py:325
  106.8 5.8 %collective-permute-done.10.b2 = bf16[128,384]{1,0:T(8,128)(2,1)S(1)} collective-permute-done((bf16[128,384]{1,0:T(8,128)(2,1)S(1)}, bf16[128,384]{1,0:T(8,128)(2,1)S(1)}, u32[]{:S(2)}, u32[]{:S(2)}) %collective-permute-start.10) | collective-permute-done | bytes 98336 | tf_op jit(solution)/shard_map/ppermute | solution.py:325
  112.6 12.7 %shard_map.164 = (bf16[1024,576]{1,0:T(8,128)(2,1)}, f32[256,768]{1,0:T(8,128)S(1)}, bf16[256,768]{1,0:T(8,128)(2,1)S(1)}, bf16[256,768]{1,0:T(8,128)(2,1)S(1)}, bf16[256,768]{1,0:T(8,128)(2,1)S(1)}) custom-call(s32[1]{0:T(128)} %bitcast.z_ref, s32[1,1024]{1,0:T(1,128)S(1)} %copy-done.26, f32[1024,128]{1,0:T(8,128)S(1)} %copy-done.42, ...), custom_call_target="tpu_custom_call" | custom-call | flops 6000000000 | bytes 9146372 | tf_op jit(solution)/shard_map/pallas_call | solution.py:42
  128.2 3.2 %shard_map.166 = (bf16[768,576]{1,0:T(8,128)(2,1)}, f32[768,128]{1,0:T(8,128)S(1)}) custom-call(bf16[1024,768]{1,0:T(8,128)(2,1)S(1)} %copy-done.2, bf16[1024,576]{1,0:T(8,128)(2,1)S(1)} %copy-done.3, bf16[3,768,192]{2,1,0:T(8,128)(2,1)S(1)} %copy.31.w_ref), custom_call_target="tpu_custom_call" | custom-call | flops 1000000000 | bytes 4915200 | tf_op jit(solution)/shard_map/pallas_call | solution.py:42
  132.2 4.4 %all-to-all-start.2 = ((bf16[8,96,576]{2,1,0:T(8,128)(2,1)}), bf16[8,96,576]{2,1,0:T(8,128)(2,1)}, u32[]{:S(2)}, u32[]{:S(2)}) async-start(bf16[8,96,576]{2,1,0:T(8,128)(2,1)} %bitcast.11), calls=%async_computation.2 | async-start | bytes 1966080 | tf_op jit(solution)/shard_map/all_to_all | solution.py:433
  138.4 12.9 %all-to-all-done.2 = bf16[8,96,576]{2,1,0:T(8,128)(2,1)} async-done(((bf16[8,96,576]{2,1,0:T(8,128)(2,1)}), bf16[8,96,576]{2,1,0:T(8,128)(2,1)}, u32[]{:S(2)}, u32[]{:S(2)}) %all-to-all-start.2) | async-done | bytes 884768 | tf_op jit(solution)/shard_map/all_to_all | solution.py:433
  151.3 4.3 %all-to-all-start.3 = ((bf16[8,96,768]{2,1,0:T(8,128)(2,1)}), bf16[8,96,768]{2,1,0:T(8,128)(2,1)}, u32[]{:S(2)}, u32[]{:S(2)}) async-start(bf16[8,96,768]{2,1,0:T(8,128)(2,1)} %bitcast.14), calls=%async_computation.3 | async-start | bytes 2359296 | tf_op jit(solution)/shard_map/all_to_all | solution.py:416
  158.1 4.3 %shard_map.168 = bf16[768,1728]{1,0:T(8,128)(2,1)} custom-call(bf16[512,768]{1,0:T(8,128)(2,1)S(1)} %copy-done.30, bf16[2,512,288]{2,1,0:T(8,128)(2,1)S(1)} %copy-done.32, bf16[2,2,512,288]{3,2,1,0:T(8,128)(2,1)S(1)} %copy-done.28, bf16[256,768]{1,0:T(8,128)(2,1)S(1)} %get-tuple-element.93.cot_own.cot_ref, bf16[256,768]{1,0:T(8,128)(2,1)S(1)} %copy-done.9), custom_call_target="tpu_custom_call" | custom-call | flops 4000000000 | bytes 5996544 | tf_op jit(solution)/shard_map/pallas_call | solution.py:42
  162.4 10.0 %all-to-all-done.3 = bf16[8,96,768]{2,1,0:T(8,128)(2,1)} async-done(((bf16[8,96,768]{2,1,0:T(8,128)(2,1)}), bf16[8,96,768]{2,1,0:T(8,128)(2,1)}, u32[]{:S(2)}, u32[]{:S(2)}) %all-to-all-start.3) | async-done | bytes 1179680 | tf_op jit(solution)/shard_map/all_to_all | solution.py:416
  172.4 4.8 %all-to-all-start.4 = ((bf16[8,96,1728]{2,1,0:T(8,128)(2,1)}), bf16[8,96,1728]{2,1,0:T(8,128)(2,1)}, u32[]{:S(2)}, u32[]{:S(2)}) async-start(bf16[8,96,1728]{2,1,0:T(8,128)(2,1)} %bitcast.28), calls=%async_computation.4 | async-start | bytes 5505024 | tf_op jit(solution)/shard_map/all_to_all | solution.py:398
  185.4 24.3 %collective-permute-done.16 = f32[2,768]{1,0:T(2,128)S(1)} collective-permute-done((f32[2,768]{1,0:T(2,128)S(1)}, f32[2,768]{1,0:T(2,128)S(1)}, u32[]{:S(2)}, u32[]{:S(2)}) %collective-permute-start.16) | collective-permute-done | bytes 6176 | tf_op jit(solution)/shard_map/ppermute | solution.py:437
  211.3 2.1 collective-permute-done.17
  215.1 2.0 collective-permute-done.18
  217.1 2.2 collective-permute-start.19
  229.5 2.1 collective-permute-start.22
  231.6 2.2 convert_reduce_fusion
  233.9 3.0 %collective-permute-start.23 = (bf16[96,864]{1,0:T(8,128)(2,1)S(1)}, bf16[96,864]{1,0:T(8,128)(2,1)S(1)}, u32[]{:S(2)}, u32[]{:S(2)}) collective-permute-start(bf16[96,864]{1,0:T(8,128)(2,1)S(1)} %slice.71), channel_id=1, source_target_pairs={{0,2},{1,3},{2,0},{3,1},{4,6},{5,7},{6,4},{7,5},{8,10},{9,11},{10,... | collective-permute-start | bytes 497672 | tf_op jit(solution)/shard_map/ppermute | solution.py:325
  236.9 2.0 collective-permute-done.21
  239.7 3.1 %collective-permute-done.23 = bf16[96,864]{1,0:T(8,128)(2,1)S(1)} collective-permute-done((bf16[96,864]{1,0:T(8,128)(2,1)S(1)}, bf16[96,864]{1,0:T(8,128)(2,1)S(1)}, u32[]{:S(2)}, u32[]{:S(2)}) %collective-permute-start.23) | collective-permute-done | bytes 165920 | tf_op jit(solution)/shard_map/ppermute | solution.py:325
  (175 shorter events, 60.7 us)
Async XLA Ops:
  1.4 7.0 %collective-permute-start.5 = (bf16[24,768]{1,0:T(8,128)(2,1)S(1)}, bf16[24,768]{1,0:T(8,128)(2,1)S(1)}, u32[]{:S(2)}, u32[]{:S(2)}) collective-permute-start(bf16[24,768]{1,0:T(8,128)(2,1)S(1)} %constant_dynamic-slice_fusion.1), channel_id=1, source_target_pairs={{0,3},{1,2},{2,1},{3,0},{4,7},{5,6},{6,5},{7,4},{8,11},{9,10},{10,... | collective-permute-start | bytes 110600 | tf_op jit(solution)/shard_map/ppermute | solution.py:325
  6.5 4.9 %collective-permute-start.4 = (bf16[24,768]{1,0:T(8,128)(2,1)S(1)}, bf16[24,768]{1,0:T(8,128)(2,1)S(1)}, u32[]{:S(2)}, u32[]{:S(2)}) collective-permute-start(bf16[24,768]{1,0:T(8,128)(2,1)S(1)} %constant_dynamic-slice_fusion.1), channel_id=1, source_target_pairs={{0,2},{1,3},{2,0},{3,1},{4,6},{5,7},{6,4},{7,5},{8,10},{9,11},{10,... | collective-permute-start | bytes 110600 | tf_op jit(solution)/shard_map/ppermute | solution.py:325
  6.5 4.9 %collective-permute-start.3 = (bf16[24,768]{1,0:T(8,128)(2,1)S(1)}, bf16[24,768]{1,0:T(8,128)(2,1)S(1)}, u32[]{:S(2)}, u32[]{:S(2)}) collective-permute-start(bf16[24,768]{1,0:T(8,128)(2,1)S(1)} %constant_dynamic-slice_fusion.1), channel_id=1, source_target_pairs={{0,1},{1,0},{2,3},{3,2},{4,5},{5,4},{6,7},{7,6},{8,9},{9,8},{10,11... | collective-permute-start | bytes 110600 | tf_op jit(solution)/shard_map/ppermute | solution.py:325
  12.4 19.0 %all-to-all-start = ((bf16[8,3,24,768]{3,2,1,0:T(8,128)(2,1)}), bf16[8,3,24,768]{3,2,1,0:T(8,128)(2,1)S(1)}, u32[]{:S(2)}, u32[]{:S(2)}) async-start(bf16[8,3,24,768]{3,2,1,0:T(8,128)(2,1)} %broadcast_in_dim.9), calls=%async_computation | async-start | bytes 1769472 | tf_op jit(solution)/shard_map/all_to_all | solution.py:331
  18.3 12.9 %collective-permute-start.6 = (bf16[3,96,288]{1,2,0:T(8,128)(2,1)S(1)}, bf16[3,96,288]{1,2,0:T(8,128)(2,1)S(1)}, u32[]{:S(2)}, u32[]{:S(2)}) collective-permute-start(bf16[3,96,288]{1,2,0:T(8,128)(2,1)S(1)} %pad_maximum_fusion.1), channel_id=1, source_target_pairs={{0,2},{1,3},{2,0},{3,1},{4,6},{5,7},{6,4},{7,5},{8,10},{9,11},{10,... | collective-permute-start | bytes 497672 | tf_op jit(solution)/shard_map/ppermute | solution.py:325
  32.9 32.9 %all-to-all-start.1 = ((bf16[8,3,96,288]{3,2,1,0:T(8,128)(2,1)}), bf16[8,3,96,288]{3,2,1,0:T(8,128)(2,1)}, u32[]{:S(2)}, u32[]{:S(2)}) async-start(bf16[8,3,96,288]{3,2,1,0:T(8,128)(2,1)} %broadcast_in_dim.21), calls=%async_computation.1 | async-start | bytes 3538944 | tf_op jit(solution)/shard_map/all_to_all | solution.py:331
  55.1 17.3 %copy-start.10 = (bf16[256,384]{1,0:T(8,128)(2,1)}, bf16[256,384]{1,0:T(8,128)(2,1)S(1)}, u32[]{:S(2)}) copy-start(bf16[256,384]{1,0:T(8,128)(2,1)S(1)} %get-tuple-element.41.c0) | copy-start | bytes 589828
  55.1 13.8 %collective-permute-start = (bf16[256,384]{1,0:T(8,128)(2,1)}, bf16[256,384]{1,0:T(8,128)(2,1)S(1)}, u32[]{:S(2)}, u32[]{:S(2)}) collective-permute-start(bf16[256,384]{1,0:T(8,128)(2,1)} %get-tuple-element.42), channel_id=1, source_target_pairs={{0,1},{1,0},{2,3},{3,2},{4,5},{5,4},{6,7},{7,6},{8,9},{9,8},{10,11... | collective-permute-start | bytes 589832 | tf_op jit(solution)/shard_map/ppermute | solution.py:325
  55.1 17.3 %collective-permute-start.1 = (bf16[256,384]{1,0:T(8,128)(2,1)}, bf16[256,384]{1,0:T(8,128)(2,1)S(1)}, u32[]{:S(2)}, u32[]{:S(2)}) collective-permute-start(bf16[256,384]{1,0:T(8,128)(2,1)} %get-tuple-element.43), channel_id=1, source_target_pairs={{0,2},{1,3},{2,0},{3,1},{4,6},{5,7},{6,4},{7,5},{8,10},{9,11},{10,... | collective-permute-start | bytes 589832 | tf_op jit(solution)/shard_map/ppermute | solution.py:325
  57.7 14.7 %collective-permute-start.2 = (bf16[256,384]{1,0:T(8,128)(2,1)}, bf16[256,384]{1,0:T(8,128)(2,1)S(1)}, u32[]{:S(2)}, u32[]{:S(2)}) collective-permute-start(bf16[256,384]{1,0:T(8,128)(2,1)} %get-tuple-element.44), channel_id=1, source_target_pairs={{0,3},{1,2},{2,1},{3,0},{4,7},{5,6},{6,5},{7,4},{8,11},{9,10},{10,... | collective-permute-start | bytes 589832 | tf_op jit(solution)/shard_map/ppermute | solution.py:325
  72.4 25.8 %copy-start = (bf16[4,192,768]{2,1,0:T(8,128)(2,1)S(1)}, bf16[4,192,768]{2,1,0:T(8,128)(2,1)}, u32[]{:S(2)}) copy-start(bf16[4,192,768]{2,1,0:T(8,128)(2,1)} %pad_maximum_fusion.wo_ref) | copy-start | bytes 3538948
  85.2 13.0 %collective-permute-start.8 = (bf16[256,768]{1,0:T(8,128)(2,1)S(1)}, bf16[256,768]{1,0:T(8,128)(2,1)S(1)}, u32[]{:S(2)}, u32[]{:S(2)}) collective-permute-start(bf16[256,768]{1,0:T(8,128)(2,1)S(1)} %get-tuple-element.48), channel_id=1, source_target_pairs={{0,1},{1,0},{2,3},{3,2},{4,5},{5,4},{6,7},{7,6},{8,9},{9,8},{10,11... | collective-permute-start | bytes 1179656 | tf_op jit(solution)/shard_map/ppermute | solution.py:325
  101.6 5.2 %collective-permute-start.9 = (bf16[128,384]{1,0:T(8,128)(2,1)S(1)}, bf16[128,384]{1,0:T(8,128)(2,1)S(1)}, u32[]{:S(2)}, u32[]{:S(2)}) collective-permute-start(bf16[128,384]{1,0:T(8,128)(2,1)S(1)} %get-tuple-element.58), channel_id=1, source_target_pairs={{0,1},{1,0},{2,3},{3,2},{4,5},{5,4},{6,7},{7,6},{8,9},{9,8},{10,11... | collective-permute-start | bytes 294920 | tf_op jit(solution)/shard_map/ppermute | solution.py:325
  103.3 9.2 %collective-permute-start.10 = (bf16[128,384]{1,0:T(8,128)(2,1)S(1)}, bf16[128,384]{1,0:T(8,128)(2,1)S(1)}, u32[]{:S(2)}, u32[]{:S(2)}) collective-permute-start(bf16[128,384]{1,0:T(8,128)(2,1)S(1)} %get-tuple-element.59), channel_id=1, source_target_pairs={{0,2},{1,3},{2,0},{3,1},{4,6},{5,7},{6,4},{7,5},{8,10},{9,11},{10,... | collective-permute-start | bytes 294920 | tf_op jit(solution)/shard_map/ppermute | solution.py:325
  104.2 8.3 %collective-permute-start.11 = (bf16[128,384]{1,0:T(8,128)(2,1)S(1)}, bf16[128,384]{1,0:T(8,128)(2,1)S(1)}, u32[]{:S(2)}, u32[]{:S(2)}) collective-permute-start(bf16[128,384]{1,0:T(8,128)(2,1)S(1)} %get-tuple-element.60), channel_id=1, source_target_pairs={{0,3},{1,2},{2,1},{3,0},{4,7},{5,6},{6,5},{7,4},{8,11},{9,10},{10,... | collective-permute-start | bytes 294920 | tf_op jit(solution)/shard_map/ppermute | solution.py:325
  132.2 19.1 %all-to-all-start.2 = ((bf16[8,96,576]{2,1,0:T(8,128)(2,1)}), bf16[8,96,576]{2,1,0:T(8,128)(2,1)}, u32[]{:S(2)}, u32[]{:S(2)}) async-start(bf16[8,96,576]{2,1,0:T(8,128)(2,1)} %bitcast.11), calls=%async_computation.2 | async-start | bytes 1966080 | tf_op jit(solution)/shard_map/all_to_all | solution.py:433
  138.4 17.2 %copy-start.30 = (bf16[512,768]{1,0:T(8,128)(2,1)S(1)}, bf16[512,768]{1,0:T(8,128)(2,1)}, u32[]{:S(2)}) copy-start(bf16[512,768]{1,0:T(8,128)(2,1)} %copy-done.29) | copy-start | bytes 2359300
  151.3 21.1 %all-to-all-start.3 = ((bf16[8,96,768]{2,1,0:T(8,128)(2,1)}), bf16[8,96,768]{2,1,0:T(8,128)(2,1)}, u32[]{:S(2)}, u32[]{:S(2)}) async-start(bf16[8,96,768]{2,1,0:T(8,128)(2,1)} %bitcast.14), calls=%async_computation.3 | async-start | bytes 2359296 | tf_op jit(solution)/shard_map/all_to_all | solution.py:416
  172.4 59.1 %all-to-all-start.4 = ((bf16[8,96,1728]{2,1,0:T(8,128)(2,1)}), bf16[8,96,1728]{2,1,0:T(8,128)(2,1)}, u32[]{:S(2)}, u32[]{:S(2)}) async-start(bf16[8,96,1728]{2,1,0:T(8,128)(2,1)} %bitcast.28), calls=%async_computation.4 | async-start | bytes 5505024 | tf_op jit(solution)/shard_map/all_to_all | solution.py:398
  177.5 1.8 collective-permute-start.15
  177.7 41.7 %collective-permute-start.7 = (bf16[256,768]{1,0:T(8,128)(2,1)S(1)}, bf16[256,768]{1,0:T(8,128)(2,1)S(1)}, u32[]{:S(2)}, u32[]{:S(2)}) collective-permute-start(bf16[256,768]{1,0:T(8,128)(2,1)S(1)} %copy-done.20), channel_id=1, source_target_pairs={{0,1},{1,0},{2,3},{3,2},{4,5},{5,4},{6,7},{7,6},{8,9},{9,8},{10,11... | collective-permute-start | bytes 1179656 | tf_op jit(solution)/shard_map/ppermute | solution.py:325
  179.3 30.5 %collective-permute-start.16 = (f32[2,768]{1,0:T(2,128)S(1)}, f32[2,768]{1,0:T(2,128)S(1)}, u32[]{:S(2)}, u32[]{:S(2)}) collective-permute-start(f32[2,768]{1,0:T(2,128)S(1)} %fusion.3), channel_id=1, source_target_pairs={{0,8},{4,12},{8,0},{12,4},{16,24},{20,28},{24,16},{28,20},{1,9},{5... | collective-permute-start | bytes 18440 | tf_op jit(solution)/shard_map/ppermute | solution.py:437
  181.0 41.2 %collective-permute-start.12 = (bf16[256,768]{1,0:T(8,128)(2,1)}, bf16[256,768]{1,0:T(8,128)(2,1)S(1)}, u32[]{:S(2)}, u32[]{:S(2)}) collective-permute-start(bf16[256,768]{1,0:T(8,128)(2,1)} %copy-done.25), channel_id=1, source_target_pairs={{0,1},{1,0},{2,3},{3,2},{4,5},{5,4},{6,7},{7,6},{8,9},{9,8},{10,11... | collective-permute-start | bytes 1179656 | tf_op jit(solution)/shard_map/ppermute | solution.py:325
  182.0 40.2 %collective-permute-start.13 = (bf16[256,768]{1,0:T(8,128)(2,1)S(1)}, bf16[256,768]{1,0:T(8,128)(2,1)S(1)}, u32[]{:S(2)}, u32[]{:S(2)}) collective-permute-start(bf16[256,768]{1,0:T(8,128)(2,1)S(1)} %copy-done.24), channel_id=1, source_target_pairs={{0,2},{1,3},{2,0},{3,1},{4,6},{5,7},{6,4},{7,5},{8,10},{9,11},{10,... | collective-permute-start | bytes 1179656 | tf_op jit(solution)/shard_map/ppermute | solution.py:325
  183.7 38.6 %collective-permute-start.14 = (bf16[256,768]{1,0:T(8,128)(2,1)S(1)}, bf16[256,768]{1,0:T(8,128)(2,1)S(1)}, u32[]{:S(2)}, u32[]{:S(2)}) collective-permute-start(bf16[256,768]{1,0:T(8,128)(2,1)S(1)} %copy-done.22), channel_id=1, source_target_pairs={{0,3},{1,2},{2,1},{3,0},{4,7},{5,6},{6,5},{7,4},{8,11},{9,10},{10,... | collective-permute-start | bytes 1179656 | tf_op jit(solution)/shard_map/ppermute | solution.py:325
  209.8 3.7 %collective-permute-start.17 = (f32[2,768]{1,0:T(2,128)S(1)}, f32[2,768]{1,0:T(2,128)S(1)}, u32[]{:S(2)}, u32[]{:S(2)}) collective-permute-start(f32[2,768]{1,0:T(2,128)S(1)} %fusion.5), channel_id=1, source_target_pairs={{0,16},{4,20},{8,24},{12,28},{16,0},{20,4},{24,8},{28,12},{1,17},{... | collective-permute-start | bytes 18440 | tf_op jit(solution)/shard_map/ppermute | solution.py:437
  213.5 3.6 %collective-permute-start.18 = (f32[2,768]{1,0:T(2,128)S(1)}, f32[2,768]{1,0:T(2,128)S(1)}, u32[]{:S(2)}, u32[]{:S(2)}) collective-permute-start(f32[2,768]{1,0:T(2,128)S(1)} %add.52), channel_id=1, source_target_pairs={{0,1},{1,0},{2,3},{3,2},{4,5},{5,4},{6,7},{7,6},{8,9},{9,8},{10,11... | collective-permute-start | bytes 18440 | tf_op jit(solution)/shard_map/ppermute | solution.py:325
  217.1 4.5 %collective-permute-start.19 = (f32[2,768]{1,0:T(2,128)S(1)}, f32[2,768]{1,0:T(2,128)S(1)}, u32[]{:S(2)}, u32[]{:S(2)}) collective-permute-start(f32[2,768]{1,0:T(2,128)S(1)} %add.53), channel_id=1, source_target_pairs={{0,2},{1,3},{2,0},{3,1},{4,6},{5,7},{6,4},{7,5},{8,10},{9,11},{10,... | collective-permute-start | bytes 18440 | tf_op jit(solution)/shard_map/ppermute | solution.py:325
  227.8 9.1 %collective-permute-start.20 = (bf16[96,192]{1,0:T(8,128)(2,1)S(1)}, bf16[96,192]{1,0:T(8,128)(2,1)S(1)}, u32[]{:S(2)}, u32[]{:S(2)}) collective-permute-start(bf16[96,192]{1,0:T(8,128)(2,1)S(1)} %get-tuple-element.96), channel_id=1, source_target_pairs={{0,1},{1,0},{2,3},{3,2},{4,5},{5,4},{6,7},{7,6},{8,9},{9,8},{10,11... | collective-permute-start | bytes 110600 | tf_op jit(solution)/shard_map/ppermute | solution.py:325
  229.5 7.4 %collective-permute-start.22 = (bf16[96,192]{1,0:T(8,128)(2,1)S(1)}, bf16[96,192]{1,0:T(8,128)(2,1)S(1)}, u32[]{:S(2)}, u32[]{:S(2)}) collective-permute-start(bf16[96,192]{1,0:T(8,128)(2,1)S(1)} %get-tuple-element.97), channel_id=1, source_target_pairs={{0,3},{1,2},{2,1},{3,0},{4,7},{5,6},{6,5},{7,4},{8,11},{9,10},{10,... | collective-permute-start | bytes 110600 | tf_op jit(solution)/shard_map/ppermute | solution.py:325
  231.5 7.4 %collective-permute-start.21 = (bf16[96,192]{1,0:T(8,128)(2,1)S(1)}, bf16[96,192]{1,0:T(8,128)(2,1)S(1)}, u32[]{:S(2)}, u32[]{:S(2)}) collective-permute-start(bf16[96,192]{1,0:T(8,128)(2,1)S(1)} %get-tuple-element.98), channel_id=1, source_target_pairs={{0,2},{1,3},{2,0},{3,1},{4,6},{5,7},{6,4},{7,5},{8,10},{9,11},{10,... | collective-permute-start | bytes 110600 | tf_op jit(solution)/shard_map/ppermute | solution.py:325
  233.9 8.9 %collective-permute-start.23 = (bf16[96,864]{1,0:T(8,128)(2,1)S(1)}, bf16[96,864]{1,0:T(8,128)(2,1)S(1)}, u32[]{:S(2)}, u32[]{:S(2)}) collective-permute-start(bf16[96,864]{1,0:T(8,128)(2,1)S(1)} %slice.71), channel_id=1, source_target_pairs={{0,2},{1,3},{2,0},{3,1},{4,6},{5,7},{6,4},{7,5},{8,10},{9,11},{10,... | collective-permute-start | bytes 497672 | tf_op jit(solution)/shard_map/ppermute | solution.py:325
  (46 other events, 264.8 us)

commit v2 on v1

v2 whole, which is shorter than its diff:
```python
import functools
import math

import jax
import jax.numpy as jnp
import numpy as np
from jax import lax
from jax.experimental import pallas as pl
from jax.experimental.pallas import tpu as pltpu
from jax.sharding import PartitionSpec as P

HEAD = 64
LEN = 1024
D = 768
HEADS_HERE = 3
COLS = HEADS_HERE * HEAD
LANES = 256
DOC = 256
QB = 128
WINDOW = QB + 2 * DOC
EPSILON = 1e-05
ROPE_BASE = 160000.0
NARROW = 4
BLOCK = LEN // NARROW
F32 = jnp.float32
GAIN_ROWS = 16
BF16 = jnp.bfloat16
NEGATIVE = -1e30
MIB = 1024 * 1024
COST = {
    "finish_kernel": 1,
    "qkv_sum_kernel": 1,
    "pack_kernel": 1,
    "arrived_kernel": 1,
    "pairs_kernel": 1,
    "quads_kernel": 1,
    "project_kernel": 6,
    "attend_kernel": 10000,
    "middle_kernel": 10000,
    "partner_kernel": 3,
    "own_kernel": 10,
    "residual_kernel": 10000,
    "output_grad_kernel": 2,
    "fold_kernel": 2,
    "backward_far_kernel": 10000,
    "backward_near_kernel": 10000,
    "add_kernel": 10000,
    "qkv_grad_kernel": 1,
    "collect_kernel": 1,
    "final_kernel": 10000,
}

NN = (((1,), (0,)), ((), ()))
NT = (((1,), (1,)), ((), ()))
TN = (((0,), (0,)), ((), ()))


def dot(a, b, dims=NN):
    return lax.dot_general(a, b, dims, preferred_element_type=F32)


def call(body, ins, outs, scratch=(), scalars=1):
    name = getattr(body, "func", body).__name__
    specs = [pl.BlockSpec(memory_space=pltpu.SMEM)] * scalars
    specs += [pl.BlockSpec(memory_space=pltpu.VMEM)] * (len(ins) - scalars)
    size = sum(math.prod(x.shape) * x.dtype.itemsize for x in (*ins, *outs))
    held = sum(math.prod(x.shape) * x.dtype.itemsize for x in scratch)
    return pl.pallas_call(
        body,
        name=name,
        out_shape=tuple(jax.ShapeDtypeStruct(o.shape, o.dtype) for o in outs),
        in_specs=specs,
        out_specs=tuple(pl.BlockSpec(memory_space=pltpu.VMEM) for _ in outs),
        scratch_shapes=list(scratch),
        compiler_params=pltpu.CompilerParams(vmem_limit_bytes=size + size // 4 + held + 8 * MIB),
        cost_estimate=pl.CostEstimate(flops=COST[name] * 10**9, bytes_accessed=size, transcendentals=0),
    )(*ins)


def sds(shape, dtype):
    return jax.ShapeDtypeStruct(shape, dtype)


def rotary_table():
    position = np.arange(DOC, dtype=np.float64)
    frequency = ROPE_BASE ** (-2.0 * np.arange(HEAD // 2, dtype=np.float64) / HEAD)
    angle = position[:, None] * frequency[None, :]
    cosine, sine = np.cos(angle), np.sin(angle)
    table = np.zeros((DOC, 2 * LANES), np.float32)
    for h in range(HEADS_HERE):
        base = h * HEAD
        table[:, base : base + 32] = cosine
        table[:, base + 32 : base + 64] = cosine
        table[:, LANES + base : LANES + base + 32] = -sine
        table[:, LANES + base + 32 : LANES + base + 64] = sine
    high = table.astype(jnp.bfloat16)
    low = (table - high.astype(np.float32)).astype(jnp.bfloat16)
    return np.stack([high, low])


def normalize(values):
    centre = values - jnp.mean(values, axis=-1, keepdims=True)
    spread = jnp.mean(centre * centre, axis=-1, keepdims=True)
    inverse = lax.rsqrt(spread + EPSILON)
    return centre * inverse, inverse


def norm_back(upstream, unit_rows, inverse, gain):
    scaled = upstream * gain
    first_mean = jnp.mean(scaled, axis=-1, keepdims=True)
    second_mean = jnp.mean(scaled * unit_rows, axis=-1, keepdims=True)
    return inverse * (scaled - first_mean - unit_rows * second_mean)


def lane_head(rows):
    return lax.broadcasted_iota(jnp.int32, (rows, LANES), 1) // HEAD


def swap_halves(x):
    lane = lax.broadcasted_iota(jnp.int32, x.shape, 1)
    return jnp.where(
        lane % HEAD < HEAD // 2,
        pltpu.roll(x, LANES - HEAD // 2, 1),
        pltpu.roll(x, HEAD // 2, 1),
    )


def by_head(block, head):
    return jnp.concatenate(
        [jnp.where(head == h, block, jnp.zeros_like(block)) for h in range(HEADS_HERE)], axis=0
    )


def merge_heads(stacked, head):
    parts = jnp.split(stacked, HEADS_HERE, axis=0)
    return jnp.where(head == 0, parts[0], jnp.where(head == 1, parts[1], parts[2]))


def own_window(i):
    return jnp.clip(i - DOC // QB, 0, (LEN - WINDOW) // QB) * QB


def static_window(i):
    reach = DOC // QB
    return max(0, i - reach) * QB, min(LEN // QB, i + reach + 1) * QB


def project_kernel(
    tok_ref, seg_ref, gain_ref, w_ref, table_ref,
    q_ref, k_ref, v_ref, normed_ref, trig_ref, segc_ref,
    proj_ref,
):
    seg = jnp.broadcast_to(seg_ref[...].astype(F32), (8, LEN))
    index = lax.broadcasted_iota(jnp.int32, (8, LEN), 1)
    first = jnp.where(seg != pltpu.roll(seg, 1, 1), index, 0)
    first = jnp.where(index == 0, 0, first).astype(F32)
    shift = 1
    while shift < DOC:
        first = jnp.maximum(first, jnp.where(index >= shift, pltpu.roll(first, shift, 1), 0.0))
        shift *= 2
    place = index.astype(F32) - first
    segc_ref[...] = jnp.transpose(jnp.broadcast_to(seg[:1], (128, LEN)))
    placec = jnp.transpose(jnp.broadcast_to(place[:1], (128, LEN)))
    lane = lax.broadcasted_iota(jnp.int32, (LEN, 128), 1).astype(F32)
    hot = jnp.concatenate(
        [jnp.where(placec == lane + 128.0 * j, 1.0, 0.0) for j in range(DOC // 128)], axis=1
    ).astype(BF16)
    trig_ref[...] = dot(hot, table_ref[0]) + dot(hot, table_ref[1])

    def norm_rows(i, carry):
        rows = pl.ds(pl.multiple_of(i * 128, 128), 128)
        unit, _ = normalize(tok_ref[rows, :].astype(F32))
        normed_ref[rows, :] = (unit * gain_ref[...]).astype(BF16)
        return carry

    lax.fori_loop(0, LEN // 128, norm_rows, 0)
    proj_ref[:, COLS:] = jnp.zeros((LEN, LANES - COLS), F32)
    for s, out in enumerate((q_ref, k_ref)):
        proj_ref[:, :COLS] = dot(normed_ref[...], w_ref[s], NT)
        x = proj_ref[...]
        out[...] = (x * trig_ref[:, :LANES] + swap_halves(x) * trig_ref[:, LANES:]).astype(BF16)
    proj_ref[:, :COLS] = dot(normed_ref[...], w_ref[2], NT)
    v_ref[...] = proj_ref[...].astype(BF16)


def attend_kernel(
    s_ref, seg_ref, segc_ref, q_ref, k_ref, v_ref, c0_ref, c1_ref, c2_ref, c3_ref, lse_ref, ctx_ref
):
    z = s_ref[0]
    head = lane_head(QB)
    column = lax.broadcasted_iota(jnp.int32, (QB, 128), 1)
    for i in range(LEN // QB):
        low, high = static_window(i)
        rows = slice(i * QB, (i + 1) * QB)
        stacked = by_head(q_ref[rows, :] * jnp.asarray(1.0 / math.sqrt(HEAD), BF16), head)
        scores = dot(stacked, k_ref[low:high, :], NT)
        same = segc_ref[rows, 0:1] == seg_ref[0:1, low:high].astype(F32)
        parts, logs = [], []
        for h in range(HEADS_HERE):
            mine = jnp.where(same, scores[h * QB : (h + 1) * QB], NEGATIVE)
            top = jnp.max(mine, axis=-1, keepdims=True)
            weights = jnp.exp(mine - top)
            total = jnp.sum(weights, axis=-1, keepdims=True)
            parts.append((weights * (1.0 / total)).astype(BF16))
            logs.append(top + jnp.log(total))
        lse_ref[rows, :] = jnp.where(column == 0, logs[0], jnp.where(column == 1, logs[1], logs[2]))
        mixed = dot(jnp.concatenate(parts, axis=0), v_ref[low:high, :])
        context = merge_heads(mixed, head)[:, :COLS].astype(BF16)
        block, r = i * QB // BLOCK, i * QB % BLOCK
        ctx_ref[block, r : r + QB, :COLS] = context
        ctx_ref[block ^ 1, r : r + QB, COLS:] = context
    for k, out in enumerate((c0_ref, c1_ref, c2_ref, c3_ref)):
        out[...] = ctx_ref[z ^ k]


def place_slots(s_ref, even_ref, odd_ref, out_ref, first, rows):
    cols = D // 2
    for i in range(8):
        slot = s_ref[2 + i]
        piece = even_ref[i, first : first + rows, :] if i < 4 else odd_ref[i - 4, first : first + rows, :]
        there = pl.ds(pl.multiple_of((slot // 2) * rows, 16), rows)
        out_ref[there, pl.ds(pl.multiple_of((slot % 2) * cols, 128), cols)] = piece


def gated(normed, cot, w_in, w_down, act_ref, gb_ref, width):
    both = dot(normed, w_in, NT)
    gate, linear = both[:, :width], both[:, width:]
    act_back = dot(cot, w_down, NT)
    cdf = 0.5 * (1.0 + lax.erf(gate * math.sqrt(0.5)))
    slope = cdf + gate * (jnp.exp(-0.5 * gate * gate) * (1.0 / math.sqrt(2.0 * math.pi)))
    gelu = gate * cdf
    act_ref[...] = (gelu * linear).astype(BF16)
    gb_ref[:, :width] = (act_back * linear * slope).astype(BF16)
    gb_ref[:, width:] = (act_back * gelu).astype(BF16)
    return dot(act_ref[...], w_down), dot(gb_ref[...], w_in)


def middle_kernel(
    s_ref, tok_ref, cot_ref, c0, c1, c2, c3, w_ref, here_ref, there_ref, gain_ref, gw_ref, dw_ref,
    res_ref, normed_ref, act_ref, gb_ref, branch_ref, back_ref, wo_ref, cot_out,
):
    z = s_ref[0]
    wo_ref[0] = w_ref[...]
    few = COLS // 4
    pieces = ((0, here_ref, 0), (2, here_ref, 1), (1, there_ref, 0), (3, there_ref, 1))
    for chip, ref, i in pieces:
        there = pl.ds(pl.multiple_of(s_ref[10 + chip] * few, 16), few)
        for k in range(3):
            for side in range(2):
                first = (2 * k + side) * few
                lanes = slice(side * (D // 2), (side + 1) * (D // 2))
                wo_ref[k + 1, there, lanes] = ref[i, first : first + few, :]
    for half in range(2):
        base = (z if half == 0 else z ^ 1) * BLOCK
        there = pl.ds(pl.multiple_of(base, BLOCK), BLOCK)
        rows = slice(half * BLOCK, (half + 1) * BLOCK)
        attended = jnp.zeros((BLOCK, D), F32)
        for k, c in enumerate((c0, c1, c2, c3)):
            attended += dot(c[:, half * COLS : (half + 1) * COLS], wo_ref[k])
        residual = tok_ref[there, :].astype(F32) + attended
        if half == 0:
            res_ref[...] = residual
            branch_ref[rows, :] = residual
        else:
            branch_ref[rows, :] = jnp.zeros_like(residual)
        unit, _ = normalize(residual)
        normed_ref[rows, :] = (unit * gain_ref[...]).astype(BF16)
        cot_out[rows, :] = cot_ref[there, :]
    branch, back = gated(
        normed_ref[...], cot_out[...], gw_ref[...], dw_ref[...], act_ref, gb_ref, dw_ref.shape[0]
    )
    branch_ref[...] += branch
    back_ref[...] = back


def partner_kernel(
    s_ref, normed_ref, cot_ref, branch_in, back_in, fe_ref, fo_ref,
    act_ref, gb_ref, branch_ref, back_ref, other_ref,
):
    width = act_ref.shape[1]
    place_slots(s_ref, fe_ref, fo_ref, other_ref, 0, other_ref.shape[0] // 4)
    branch, back = gated(
        normed_ref[BLOCK:, :], cot_ref[BLOCK:, :], other_ref[: 2 * width, :],
        other_ref[2 * width : 3 * width, :], act_ref, gb_ref, width,
    )
    branch_ref[...] = (branch_in[BLOCK:, :] + branch).astype(BF16)
    back_ref[...] = (back_in[BLOCK:, :] + back).astype(BF16)


def own_kernel(
    s_ref, normed_ref, cot_ref, branch_in, back_in, other_ref, act_ref, gb_ref, act_par, gb_par,
    branch_ref, back_ref, whole_ref,
    act_own, gb_own,
):
    width = act_ref.shape[1]
    branch, back = gated(
        normed_ref[:BLOCK, :], cot_ref[:BLOCK, :], other_ref[: 2 * width, :],
        other_ref[2 * width : 3 * width, :], act_own, gb_own, width,
    )
    branch_ref[...] = branch_in[:BLOCK, :] + branch
    back_ref[...] = back_in[:BLOCK, :] + back
    half = whole_ref.shape[1] // 2
    whole_ref[:, : 2 * width] = dot(normed_ref[...], gb_ref[...], TN).astype(BF16)
    whole_ref[:, 2 * width : 3 * width] = dot(cot_ref[...], act_ref[...], TN).astype(BF16)
    part = dot(normed_ref[:BLOCK, :], gb_own[...], TN) + dot(normed_ref[BLOCK:, :], gb_par[...], TN)
    whole_ref[:, half : half + 2 * width] = part.astype(BF16)
    part = dot(cot_ref[:BLOCK, :], act_own[...], TN) + dot(cot_ref[BLOCK:, :], act_par[...], TN)
    whole_ref[:, half + 2 * width : half + 3 * width] = part.astype(BF16)
    pad = jnp.zeros((D, half - 3 * width), BF16)
    whole_ref[:, 3 * width : half] = pad
    whole_ref[:, half + 3 * width :] = pad


def finish_kernel(keep_ref, r1, r2, r3, geglu_ref, down_ref, out_ref, pad_ref):
    half = r2.shape[1] - COLS
    rows, width = geglu_ref.shape[1:]
    ff = keep_ref[:, :half] + r2[:, :half].astype(F32)
    geglu_ref[0] = ff[:, :width]
    geglu_ref[1] = ff[:, width : 2 * width]
    out = keep_ref[:, half:] + r1[...].astype(F32) + r2[:, half:].astype(F32) + r3[...].astype(F32)
    pad_ref[...] = jnp.zeros_like(pad_ref)
    pad_ref[:rows, :width] = ff[:, 2 * width : 3 * width]
    down_ref[...] = jnp.transpose(pad_ref[...])[:width, :rows]
    pad_ref[:rows, :COLS] = out
    out_ref[...] = jnp.transpose(pad_ref[...])[:COLS, :rows]


def qkv_sum_kernel(parts_ref, grad_ref, gains_ref):
    rows = grad_ref.shape[1]
    total = jnp.sum(parts_ref[...].astype(F32), axis=0)
    for s in range(3):
        grad_ref[s] = total[:rows, s * COLS : (s + 1) * COLS]
    for gain in range(2):
        for side in range(2):
            first = rows + 6 * gain + side
            part = total[first : first + 1] + total[first + 2 : first + 3] + total[first + 4 : first + 5]
            gains_ref[gain : gain + 1, side * (D // 2) : (side + 1) * (D // 2)] = part[:, : D // 2]


def residual_kernel(
    keep_ref, recv_ref, res_ref, gain_ref, cot_ref, wo_ref,
    back_ref, low_ref, gain_out, b0, b1, b2, b3,
):
    unit, inverse = normalize(res_ref[...])
    upstream = keep_ref[...] + recv_ref[...].astype(F32)
    back = cot_ref[:BLOCK, :].astype(F32) + norm_back(upstream, unit, inverse, gain_ref[...])
    back_ref[...] = back
    gain_out[...] = jnp.sum(upstream * unit, axis=0, keepdims=True)
    low = back.astype(BF16)
    low_ref[...] = low
    for k, out in enumerate((b0, b1, b2, b3)):
        part = dot(low, wo_ref[k], NT).astype(BF16)
        out[:, :COLS] = part[: BLOCK // 2]
        out[:, COLS:] = part[BLOCK // 2 :]


def output_grad_kernel(s_ref, low_ref, c0, c1, c2, c3, ff_ref, even_ref, odd_ref, whole_ref):
    for k, c in enumerate((c0, c1, c2, c3)):
        whole_ref[:, k * COLS : (k + 1) * COLS] = dot(low_ref[...], c[:, :COLS], TN).astype(BF16)
    rows, ff = even_ref.shape[1], ff_ref.shape[1]
    for i in range(8):
        there = pl.ds(pl.multiple_of(s_ref[2 + i] * rows, 16), rows)
        out = even_ref.at[i] if i < 4 else odd_ref.at[i - 4]
        out[:, :ff] = ff_ref[there, :]
        out[:, ff:] = whole_ref[there, :]


def collect_kernel(own_ref, r1, r2, r3, keep_ref, s1, s2, s3):
    total = own_ref[...] + r1[...].astype(F32) + r2[...].astype(F32) + r3[...].astype(F32)
    half = keep_ref.shape[1] - COLS
    keep_ref[:, :half] = total[:, :half]
    keep_ref[:, half:] = total[:, 2 * half : 2 * half + COLS]
    s2[:, :half] = total[:, half : 2 * half].astype(BF16)
    for k, out in ((1, s1), (2, s2), (3, s3)):
        first = 2 * half + k * COLS
        out[:, out.shape[1] - COLS :] = total[:, first : first + COLS].astype(BF16)


def pack_kernel(s_ref, w_in_ref, w_down_ref, w_out_ref, out_ref, both_ref, whole_ref):
    slot = s_ref[1]
    there, cols = slot // 2, pl.ds(pl.multiple_of((slot % 2) * (D // 2), 128), D // 2)
    n_in, n_down = w_in_ref.shape[0], w_down_ref.shape[0]
    whole_ref[:n_in, :] = w_in_ref[...]
    whole_ref[n_in : n_in + n_down, :] = w_down_ref[...]
    whole_ref[n_in + n_down :, :] = jnp.zeros((whole_ref.shape[0] - n_in - n_down, D), BF16)
    rows = whole_ref.shape[0] // 4
    few = w_out_ref.shape[0] // 4
    here = pl.ds(pl.multiple_of(there * few, 16), few)
    both_ref[:rows, :] = whole_ref[pl.ds(pl.multiple_of(there * rows, 16), rows), cols]
    for side in range(2):
        mine = w_out_ref[here, side * (D // 2) : (side + 1) * (D // 2)]
        out_ref[side * few : (side + 1) * few, :] = mine
        both_ref[rows + side * few : rows + (side + 1) * few, :] = mine


def arrived_kernel(s_ref, f1, f2, f3, ff_ref, out_ref):
    ff, few = ff_ref.shape[0], f1.shape[0]
    ff_ref[...] = f2[:ff, :]
    for i, piece in enumerate((f1[...], f2[ff:, :], f3[...])):
        out_ref[i * few : (i + 1) * few, :] = piece


def pairs_kernel(s_ref, a0, a1, b0, b1, a_ref, b_ref):
    for i, (a, b) in enumerate(((a0, b0), (a1, b1))):
        a_ref[i] = a[...]
        b_ref[i] = b[...]


def quads_kernel(a0, a1, out_ref):
    out_ref[:2] = a0[...]
    out_ref[2:] = a1[...]


def backward_steps(
    first, count, seg_ref, segc_ref, q_ref, k_ref, v_ref, lse_ref, back_ref, dq_ref, dk_ref, dv_ref
):
    head = lane_head(QB)
    scale = jnp.asarray(1.0 / math.sqrt(HEAD), BF16)
    for j in range(count):
        i = first + j
        rows = pl.ds(pl.multiple_of(i * QB, QB), QB)
        keys = pl.ds(pl.multiple_of(own_window(i), QB), WINDOW)
        stacked = by_head(q_ref[rows, :] * scale, head)
        upstream = by_head(back_ref[rows, :], head)
        scores = dot(stacked, k_ref[keys, :], NT)
        prob_back = dot(upstream, v_ref[keys, :], NT)
        same = segc_ref[rows, 0:1] == seg_ref[0:1, keys].astype(F32)
        probs, grads = [], []
        for h in range(HEADS_HERE):
            at = slice(h * QB, (h + 1) * QB)
            prob = jnp.exp(jnp.where(same, scores[at], NEGATIVE) - lse_ref[rows, h : h + 1])
            inner = jnp.sum(prob * prob_back[at], axis=-1, keepdims=True)
            probs.append(prob.astype(BF16))
            grads.append((prob * (prob_back[at] - inner)).astype(BF16))
        prob = jnp.concatenate(probs, axis=0)
        grad = jnp.concatenate(grads, axis=0)
        dv_ref[keys, :] += dot(prob, upstream, TN)
        dk_ref[keys, :] += dot(grad, stacked, TN)
        dq_ref[rows, :] = merge_heads(dot(grad, k_ref[keys, :]), head) * (1.0 / math.sqrt(HEAD))


def rows_back(base, dq_ref, dk_ref, dv_ref, trig_ref, w_ref, qkv_ref):
    rows = pl.ds(pl.multiple_of(base, BLOCK), BLOCK)
    cosine, signed = trig_ref[rows, :LANES], trig_ref[rows, LANES:]
    total = None
    for part, grad_ref in enumerate((dq_ref, dk_ref, dv_ref)):
        g = grad_ref[rows, :]
        if part < 2:
            g = g * cosine - swap_halves(g) * signed
        low = g[:, :COLS].astype(BF16)
        qkv_ref[:, part * COLS : (part + 1) * COLS] = low
        product = dot(low, w_ref[part])
        total = product if total is None else total + product
    return total


def backward_far_kernel(
    s_ref, seg_ref, segc_ref, q_ref, k_ref, v_ref, lse_ref, trig_ref, b0, b1, b2, b3, w_ref,
    n2, n3, qkv_ref, back_ref, dq_ref, dk_ref, dv_ref,
):
    z = s_ref[0]
    pair = z // 2
    half = BLOCK // 2
    back_ref[:, COLS:] = jnp.zeros((LEN, LANES - COLS), BF16)
    for k, b in enumerate((b0, b1, b2, b3)):
        base = pl.multiple_of((z ^ k) * BLOCK, BLOCK)
        back_ref[pl.ds(base, half), :COLS] = b[:, :COLS]
        back_ref[pl.ds(pl.multiple_of(base + half, half), half), :COLS] = b[:, COLS:]
    dk_ref[...] = jnp.zeros_like(dk_ref)
    dv_ref[...] = jnp.zeros_like(dv_ref)
    refs = (seg_ref, segc_ref, q_ref, k_ref, v_ref, lse_ref, back_ref, dq_ref, dk_ref, dv_ref)
    steps = LEN // QB
    reach = DOC // QB
    backward_steps((1 - pair) * (steps // 2 - reach), steps // 2 + reach, *refs)
    for k, out in ((2, n2), (3, n3)):
        at = qkv_ref.at[(k - 2) * BLOCK : (k - 1) * BLOCK]
        part = rows_back((z ^ k) * BLOCK, dq_ref, dk_ref, dv_ref, trig_ref, w_ref, at)
        out[...] = part.astype(out.dtype)


def add_kernel(mine_ref, recv_ref, out_ref):
    out_ref[...] = (mine_ref[...] + recv_ref[...].astype(F32)).astype(out_ref.dtype)


def backward_near_kernel(
    s_ref, seg_ref, segc_ref, q_ref, k_ref, v_ref, lse_ref, trig_ref, back_ref, dq_in, dk_in, dv_in,
    w_ref, n0, n1, qkv_ref, dq_ref, dk_ref, dv_ref,
):
    z = s_ref[0]
    pair = z // 2
    dq_ref[...] = dq_in[...]
    dk_ref[...] = dk_in[...]
    dv_ref[...] = dv_in[...]
    refs = (seg_ref, segc_ref, q_ref, k_ref, v_ref, lse_ref, back_ref, dq_ref, dk_ref, dv_ref)
    steps = LEN // QB
    reach = DOC // QB
    backward_steps(pair * (steps // 2 + reach), steps // 2 - reach, *refs)
    for k, out in ((0, n0), (1, n1)):
        at = qkv_ref.at[k * BLOCK : (k + 1) * BLOCK]
        part = rows_back((z ^ k) * BLOCK, dq_ref, dk_ref, dv_ref, trig_ref, w_ref, at)
        out[...] = part.astype(out.dtype)


def qkv_grad_kernel(
    s_ref, normed_ref, near_ref, far_ref, w_ref, gain_ref, gain_two_ref, out_ref, whole_ref, rows_ref
):
    for k in range(NARROW):
        base = pl.multiple_of((s_ref[0] ^ k) * BLOCK, BLOCK)
        rows_ref[k * BLOCK : (k + 1) * BLOCK, :] = normed_ref[pl.ds(base, BLOCK), :]
    pair = 2 * BLOCK
    total = None
    for s in range(3):
        cols = slice(s * COLS, (s + 1) * COLS)
        part = dot(rows_ref[:pair, :], near_ref[:, cols], TN)
        part += dot(rows_ref[pair:, :], far_ref[:, cols], TN)
        whole_ref[:, cols] = part.astype(BF16)
        weighted = part * jnp.transpose(w_ref[s].astype(F32))
        total = weighted if total is None else total + weighted
    column = jnp.broadcast_to(jnp.sum(total, axis=1, keepdims=True), (D, 128))
    gains = (jnp.transpose(column)[:1, :] / gain_ref[...], gain_two_ref[...])
    extra = jnp.zeros((GAIN_ROWS, D // 2), F32)
    row = lax.broadcasted_iota(jnp.int32, extra.shape, 0)
    at = 0
    for gain in gains:
        rest = gain
        for _ in range(3):
            term = rest.astype(BF16).astype(F32)
            rest = rest - term
            for side in range(2):
                extra = jnp.where(row == at, term[:, side * (D // 2) : (side + 1) * (D // 2)], extra)
                at += 1
    blocks, rows, cols = out_ref.shape
    rows -= GAIN_ROWS
    for i in range(blocks):
        if rows % 16 == 0:
            out_ref[i, :rows, :] = whole_ref[i * rows : (i + 1) * rows, :]
            out_ref[i, rows:, :] = jnp.zeros((GAIN_ROWS, cols), BF16)
            out_ref[i, rows:, : D // 2] = extra.astype(BF16)
        else:
            lines = [whole_ref[i * rows : (i + 1) * rows, :].astype(F32)]
            pad = jnp.zeros((GAIN_ROWS, cols - D // 2), F32)
            lines.append(jnp.concatenate([extra, pad], axis=1))
            out_ref[i] = jnp.concatenate(lines, axis=0).astype(BF16)


def final_kernel(s_ref, tok_ref, gain_ref, back_ref, n0, n1, n2, out_ref):
    upstream = n0[...] + n1[:BLOCK, :].astype(F32) + n2[...].astype(F32)
    rows = pl.ds(pl.multiple_of(s_ref[0] * BLOCK, BLOCK), BLOCK)
    unit, inverse = normalize(tok_ref[rows, :].astype(F32))
    out_ref[...] = back_ref[...] + norm_back(upstream, unit, inverse, gain_ref[...])


def fold_kernel(even_ref, recv_ref, own_ref, s1_ref, s2_ref, s3_ref):
    for i, out in enumerate((own_ref, s1_ref, s2_ref, s3_ref)):
        out[...] = (even_ref[i].astype(F32) + recv_ref[i].astype(F32)).astype(out.dtype)


def along_narrow(x, k):
    return lax.ppermute(x, "narrow", [(i, i ^ k) for i in range(NARROW)])


def along_wide(x, k):
    return lax.ppermute(x, "wide", [(i, i ^ k) for i in range(lax.axis_size("wide"))])


def tie(x, *others):
    return lax.optimization_barrier((x, *others))[0]


def quarter_slice(x, slot):
    rows, cols = x.shape[-2] // 4, x.shape[-1] // 2
    x = lax.dynamic_slice_in_dim(x, (slot // 2) * rows, rows, x.ndim - 2)
    return lax.dynamic_slice_in_dim(x, (slot % 2) * cols, cols, x.ndim - 1)


def all_slots(x, hops):
    whole = jnp.stack([along_narrow(x, k) for k in hops])
    slots = jnp.stack([quarter_slice(whole, i) for i in range(8)])
    return slots[:4], slots[4:]


def sum_wide(x):
    return jnp.sum(lax.all_to_all(x, "wide", 0, 0).astype(F32), axis=0)


def per_device(
    tokens, segments, first_gain, qkv_weight, output_weight, second_gain, geglu_weight, down_weight,
    cotangent,
):
    size = lax.axis_size("wide")
    plane = size == 8
    mine = lax.axis_index("wide").astype(jnp.int32)
    z = lax.axis_index("narrow").astype(jnp.int32)
    order = jnp.asarray([0, 2, 4, 6, 1, 3, 5, 7], jnp.int32)
    slots = (mine ^ order) if plane else jnp.arange(8, dtype=jnp.int32)
    chips = ((mine // 2) ^ jnp.arange(4, dtype=jnp.int32)) if plane else jnp.arange(4, dtype=jnp.int32)
    scalars = jnp.concatenate([z[None], mine[None], slots, chips])
    hidden = geglu_weight.shape[2]
    padded = -(-3 * hidden // 64) * 64
    rows_d = D // size
    gain_one = first_gain.reshape(1, D)
    gain_two = second_gain.reshape(1, D)
    w_qkv = qkv_weight.transpose(0, 2, 1)
    w_in = geglu_weight.transpose(0, 2, 1).reshape(2 * hidden, D)

    few, many = COLS // 4, padded // 4
    if plane:
        slot_out, slot_both = call(
            pack_kernel,
            (scalars, w_in, down_weight, output_weight),
            (sds((2 * few, D // 2), BF16), sds((many + 2 * few, D // 2), BF16)),
            [pltpu.VMEM((padded, D), BF16)],
        )
        fetched = [along_narrow(x, k) for k, x in ((1, slot_out), (2, slot_both), (3, slot_out))]
    else:
        whole = jnp.concatenate(
            [w_in, down_weight, jnp.zeros((padded - 3 * hidden, D), BF16)], axis=0
        )
        even, odd = (x[:, 0] for x in all_slots(whole, (2,)))
        quarters = jnp.stack([along_narrow(output_weight, k) for k in (1, 2, 3)])
        quarters = quarters.reshape(3, 4, few, 2, D // 2).transpose(1, 0, 3, 2, 4)
        quarters = quarters.reshape(4, 6 * few, D // 2)
        b_pair, b_there = quarters[::2], quarters[1::2]

    wide_rows = sds((LEN, LANES), BF16)
    q, k, v, normed_one, trig, segc = call(
        project_kernel,
        (tokens, segments, gain_one, w_qkv, jnp.asarray(rotary_table())),
        (wide_rows, wide_rows, wide_rows, sds((LEN, D), BF16), sds((LEN, 2 * LANES), F32),
         sds((LEN, 128), F32)),
        [pltpu.VMEM((LEN, LANES), F32)],
        scalars=0,
    )
    now = scalars
    if plane:
        a0, b0 = call(
            arrived_kernel,
            (tie(scalars, q), *fetched),
            (sds((many, D // 2), BF16), sds((6 * few, D // 2), BF16)),
        )
        a1, b1 = along_wide(a0, 2), along_wide(b0, 4)
        now = tie(scalars, a0)
    piece = sds((BLOCK, 2 * COLS), BF16)
    c0, c1, c2, c3, lse = call(
        attend_kernel,
        (now, segments, segc, q, k, v),
        (piece, piece, piece, piece, sds((LEN, 128), F32)),
        [pltpu.VMEM((NARROW, BLOCK, 2 * COLS), BF16)],
    )
    context = (c0, *(along_narrow(c, k) for k, c in ((1, c1), (2, c2), (3, c3))))
    if plane:
        a_pair, b_pair = call(
            pairs_kernel,
            (tie(scalars, lse), a0, a1, b0, b1),
            (sds((2, many, D // 2), BF16), sds((2, 6 * few, D // 2), BF16)),
        )
        b_there = along_wide(b_pair, 2)
        (even,) = call(
            quads_kernel, (a_pair, along_wide(a_pair, 4)), (sds((4, many, D // 2), BF16),), scalars=0
        )
        odd = along_wide(even, 1)

    whole = sds((2 * BLOCK, D), F32)
    own = sds((BLOCK, D), F32)
    own_low = sds((BLOCK, D), BF16)
    res, normed_two, act, gb, branch, back, wo, cot = call(
        middle_kernel,
        (scalars, tokens, cotangent, *context, output_weight, b_pair, b_there, gain_two,
         w_in, down_weight),
        (own, sds((2 * BLOCK, D), BF16), sds((2 * BLOCK, hidden), BF16),
         sds((2 * BLOCK, 2 * hidden), BF16), whole, whole, sds((NARROW, COLS, D), BF16),
         sds((2 * BLOCK, D), BF16)),
    )
    part_act, part_gb = sds((BLOCK, hidden), BF16), sds((BLOCK, 2 * hidden), BF16)
    act_par, gb_par, out_send, send, other = call(
        partner_kernel,
        (scalars, normed_two, cot, branch, back, even, odd),
        (part_act, part_gb, own_low, own_low, sds((padded, D), BF16)),
    )
    recv = along_narrow(send, 1)
    half = -(-3 * hidden // 128) * 128
    out_keep, keep, ff_part = call(
        own_kernel,
        (scalars, normed_two, cot, branch, back, other, act, gb, act_par, gb_par),
        (own, own, sds((D, 2 * half), BF16)),
        [pltpu.VMEM((BLOCK, hidden), BF16), pltpu.VMEM((BLOCK, 2 * hidden), BF16)],
    )
    low_piece = sds((BLOCK // 2, 2 * COLS), BF16)
    back, low, gain_two_part, b0, b1, b2, b3 = call(
        residual_kernel,
        (keep, recv, res, gain_two, cot, wo),
        (own, own_low, sds((1, D), F32), low_piece, low_piece, low_piece, low_piece),
        scalars=0,
    )
    upstream = (b0, *(along_narrow(b, k) for k, b in ((1, b1), (2, b2), (3, b3))))
    grad_cols = 2 * half + NARROW * COLS
    even_part, odd_part = call(
        output_grad_kernel,
        (scalars, low, *context, ff_part),
        (sds((4, D // 8, grad_cols), BF16),) * 2,
        [pltpu.VMEM((D, NARROW * COLS), BF16)],
    )
    block = sds((rows_d, grad_cols), F32)
    if plane:
        block_low = sds((rows_d, grad_cols), BF16)
        grad_sum, *grad_sends = call(
            fold_kernel,
            (even_part, along_wide(odd_part, 1)),
            (block, block_low, block_low, block_low),
            scalars=0,
        )
        grad_recv = [along_wide(x, 2 * (i + 1)) for i, x in enumerate(grad_sends)]
        now = tie(scalars, *grad_sends)
    else:
        blocks = jnp.concatenate([even_part, odd_part], axis=0)
        grad_sum = sum_wide(blocks.reshape(size, rows_d, grad_cols))
        grad_recv = [jnp.zeros((rows_d, grad_cols), BF16)] * 3
        now = tie(scalars, even_part)

    rows_f32 = sds((LEN, LANES), F32)
    pair_qkv = sds((2 * BLOCK, 3 * COLS), BF16)
    n2, n3, qkv_far, back_rows, *grads = call(
        backward_far_kernel,
        (now, segments, segc, q, k, v, lse, trig, *upstream, w_qkv),
        (own, own_low, pair_qkv, wide_rows, rows_f32, rows_f32, rows_f32),
    )
    exchanged = along_narrow(n3, 1)
    n0, n1, qkv_near = call(
        backward_near_kernel,
        (scalars, segments, segc, q, k, v, lse, trig, back_rows, *grads, w_qkv),
        (own, own_low, pair_qkv),
        [pltpu.VMEM((LEN, LANES), F32)] * 3,
    )
    (qkv_part,) = call(
        qkv_grad_kernel,
        (tie(scalars, n1), normed_one, qkv_near, qkv_far, w_qkv, gain_one, gain_two_part),
        (sds((size, rows_d + GAIN_ROWS, 3 * COLS), BF16),),
        [pltpu.VMEM((D, 3 * COLS), BF16), pltpu.VMEM((LEN, D), BF16)],
    )
    near_recv = along_narrow(jnp.concatenate([n1, out_send], axis=0), 1)
    (pair_sum,) = call(add_kernel, (tie(n2, qkv_part), exchanged), (own_low,), scalars=0)
    far_recv = along_narrow(pair_sum, 2)
    qkv_grad, gains = call(
        qkv_sum_kernel,
        (lax.all_to_all(tie(qkv_part, pair_sum), "wide", 0, 0),),
        (sds((3, rows_d, COLS), F32), sds((2, D), F32)),
        scalars=0,
    )
    few_cols = sds((rows_d, COLS), BF16)
    grad_keep, *there = call(
        collect_kernel,
        (tie(grad_sum, near_recv, pair_sum), *grad_recv),
        (sds((rows_d, half + COLS), F32), few_cols, sds((rows_d, half + COLS), BF16), few_cols),
        scalars=0,
    )
    there = [along_narrow(x, k) for k, x in zip((1, 2, 3), there)]
    geglu_grad, down_grad, out_grad = call(
        finish_kernel,
        (grad_keep, *there),
        (sds((2, rows_d, hidden), F32), sds((hidden, rows_d), F32), sds((COLS, rows_d), F32)),
        [pltpu.VMEM((128, -(-hidden // 128) * 128), F32)],
        scalars=0,
    )
    (tokens_grad,) = call(
        final_kernel,
        (scalars, tokens, gain_one, back, n0, near_recv, far_recv),
        (own,),
    )
    gains = gains + along_narrow(gains, 1) + along_narrow(gains, 2) + along_narrow(gains, 3)
    layer_out = (out_keep + near_recv[BLOCK:].astype(F32)).astype(BF16)
    return (
        layer_out, tokens_grad, gains[0], qkv_grad, out_grad, gains[1], geglu_grad, down_grad,
    )


def solution(mesh):
    return jax.shard_map(
        per_device,
        mesh=mesh,
        in_specs=(
            P("wide", None),
            P("wide", None),
            P(),
            P(None, None, "narrow"),
            P("narrow", None),
            P(),
            P(None, None, "narrow"),
            P("narrow", None),
            P("wide", None),
        ),
        out_specs=(
            P(("wide", "narrow"), None),
            P(("wide", "narrow"), None),
            P(),
            P(None, "wide", "narrow"),
            P("narrow", "wide"),
            P(),
            P(None, "wide", "narrow"),
            P("narrow", "wide"),
        ),
        check_vma=False,
    )
```

time: 246 us -> 155 us (0.63)
  waiting for transfers between devices: 90.9 us -> 44.2 us
  local copies, waits for them, and re-layouts: 33.6 us -> 3.91 us
  starting transfers between devices: 62.3 us -> 42.9 us
  Pallas kernels: 48.4 us -> 58.9 us
  other arithmetic: 8.33 us -> 3.5 us
    ppermute x3 -> x9, waiting for transfers between devices: 26.5 us -> 2.2 us  [along_wide(): lax.ppermute(x, 'wide', [(i, i ^ k) for i in range(lax.axis_size('wide'))])]
    all_to_all x5 -> x1, waiting for transfers between devices: 22.9 us -> 0.01 us  [per_device(): lax.all_to_all(tie(qkv_part, pair_sum), 'wide', 0, 0)]
    all_to_all x5 -> x1, starting transfers between devices: 21.6 us -> 4.24 us  [per_device(): lax.all_to_all(tie(qkv_part, pair_sum), 'wide', 0, 0)]
    unnamed x103 -> x72, local copies, waits for them, and re-layouts: 20 us -> 3.29 us
    pallas_call x8 -> x20, Pallas kernels: 48.4 us -> 58.9 us  [call(): pl.pallas_call(body, name=name, out_shape=tuple((jax.ShapeDtypeStruct(o.s...]
    ppermute x21 -> x19, starting transfers between devices: 37.2 us -> 30.1 us  [along_narrow(): return lax.ppermute(x, 'narrow', [(i, i ^ k) for i in range(NARROW)])]
    ppermute x3 -> x9, starting transfers between devices: 3.48 us -> 8.53 us  [along_wide(): lax.ppermute(x, 'wide', [(i, i ^ k) for i in range(lax.axis_size('wide'))])]
    reduce_sum x3 -> x0, other arithmetic: 5.05 us -> none  [the longest x1 2.23 us: per_device(): ff_sum = jnp.sum(ff_blocks.astype(F32), axis=0)]
  transfers between devices with their start and end apart: 29 -> 29, of which waited for: 15 -> 7; matrix products, arithmetic and copies ran while one was open for 9% -> 2% of each run, Pallas kernels for 8% -> 32%
where the time goes in v2:
time: 155 us
  Pallas kernels  58.9 us (38%)
  waiting for transfers between devices  44.2 us (29%)
  starting transfers between devices  42.9 us (28%)
  local copies, waits for them, and re-layouts  3.91 us (3%)
  other arithmetic  3.5 us (2%)
    pallas_call x20, Pallas kernels, call(): pl.pallas_call(body, name=name, out_shape=tuple((jax.ShapeDtypeStruct(o.s...  58.9 us
    ppermute x19, waiting for transfers between devices, along_narrow(): return lax.ppermute(x, 'narrow', [(i, i ^ k) for i in range(NARROW)])  42 us
    ppermute x19, starting transfers between devices, along_narrow(): return lax.ppermute(x, 'narrow', [(i, i ^ k) for i in range(NARROW)])  30.1 us
    ppermute x9, starting transfers between devices, along_wide(): lax.ppermute(x, 'wide', [(i, i ^ k) for i in range(lax.axis_size('wide'))])  8.53 us
    all_to_all x1, starting transfers between devices, per_device(): lax.all_to_all(tie(qkv_part, pair_sum), 'wide', 0, 0)  4.24 us
    unnamed x72, local copies, waits for them, and re-layouts  3.29 us
  transfers between devices with their start and end apart: 29, of which 7 were waited for; matrix products, arithmetic and copies ran while one was open for 2% of the time, Pallas kernels for 32%

profile of v2, /device:TPU:0, one launch (start us, length us, event | category | flops | bytes accessed | tf_op | source)
XLA Modules:
  0.0 154.6 jit_solution(2703840469836693775)
XLA Ops:
  5.2 5.1 %collective-permute-start.2 = (bf16[96,384]{1,0:T(8,128)(2,1)S(1)}, bf16[96,384]{1,0:T(8,128)(2,1)S(1)}, u32[]{:S(2)}, u32[]{:S(2)}) collective-permute-start(bf16[96,384]{1,0:T(8,128)(2,1)S(1)} %get-tuple-element.83), channel_id=1, source_target_pairs={{0,3},{1,2},{2,1},{3,0},{4,7},{5,6},{6,5},{7,4},{8,11},{9,10},{10,... | collective-permute-start | bytes 221192 | tf_op jit(solution)/shard_map/ppermute | solution.py:559
  11.0 5.9 %project_kernel.1 = (bf16[1024,256]{1,0:T(8,128)(2,1)S(1)}, bf16[1024,256]{1,0:T(8,128)(2,1)S(1)}, bf16[1024,256]{1,0:T(8,128)(2,1)S(1)}, bf16[1024,768]{1,0:T(8...) custom-call(bf16[1024,768]{1,0:T(8,128)(2,1)S(1)} %copy-done.8, s32[1,1024]{1,0:T(1,128)S(1)} %copy-done.19, ...), custom_call_target="tpu_custom_call" | custom-call | flops 6000000000 | bytes 8756224 | tf_op jit(solution)/shard_map/project_kernel/pallas_call | solution.py:68
  17.0 6.9 %collective-permute-done.1.f2 = bf16[320,384]{1,0:T(8,128)(2,1)S(1)} collective-permute-done((bf16[320,384]{1,0:T(8,128)(2,1)S(1)}, bf16[320,384]{1,0:T(8,128)(2,1)S(1)}, u32[]{:S(2)}, u32[]{:S(2)}) %collective-permute-start.1) | collective-permute-done | bytes 245792 | tf_op jit(solution)/shard_map/ppermute | solution.py:559
  26.8 1.5 collective-permute-start.7
  28.3 4.8 %attend_kernel.1 = (bf16[256,384]{1,0:T(8,128)(2,1)S(1)}, bf16[256,384]{1,0:T(8,128)(2,1)S(1)}, bf16[256,384]{1,0:T(8,128)(2,1)S(1)}, bf16[256,384]{1,0:T(8,128)(2,1)S(1)}, f32[1024,128]{1,0:T(8,128)S(1)}) custom-call(s32[14]{0:T(128)S(1)} %pad_add_fusion.s_ref, s32[1,1024]{1,0:T(1,128)S(1)} %copy-done.19, f32[1024,128]{1,0:T(8,128)S(1)} %get-tuple-element.87.segc_ref, ...), custom_call_target="tpu_custom_call" | custom-call | flops 9999999827968 | bytes 3412024 | tf_op jit(solution)/shard_map/attend_kernel/pallas_call | solution.py:68
  37.1 3.4 %collective-permute-start.4 = (bf16[256,384]{1,0:T(8,128)(2,1)S(1)}, bf16[256,384]{1,0:T(8,128)(2,1)S(1)}, u32[]{:S(2)}, u32[]{:S(2)}) collective-permute-start(bf16[256,384]{1,0:T(8,128)(2,1)S(1)} %get-tuple-element.92), channel_id=1, source_target_pairs={{0,2},{1,3},{2,0},{3,1},{4,6},{5,7},{6,4},{7,5},{8,10},{9,11},{10,... | collective-permute-start | bytes 589832 | tf_op jit(solution)/shard_map/ppermute | solution.py:559
  41.0 2.2 %collective-permute-done.9.a1 = bf16[2,224,384]{2,1,0:T(8,128)(2,1)S(1)} collective-permute-done((bf16[2,224,384]{2,1,0:T(8,128)(2,1)S(1)}, bf16[2,224,384]{2,1,0:T(8,128)(2,1)S(1)}, u32[]{:S(2)}, u32[]{:S(2)}) %collective-permute-start.9) | collective-permute-done | bytes 344096 | tf_op jit(solution)/shard_map/ppermute | solution.py:563
  44.1 9.4 %collective-permute-done.4.c2 = bf16[256,384]{1,0:T(8,128)(2,1)S(1)} collective-permute-done((bf16[256,384]{1,0:T(8,128)(2,1)S(1)}, bf16[256,384]{1,0:T(8,128)(2,1)S(1)}, u32[]{:S(2)}, u32[]{:S(2)}) %collective-permute-start.4) | collective-permute-done | bytes 196640 | tf_op jit(solution)/shard_map/ppermute | solution.py:559
  53.5 4.6 %middle_kernel.1 = (f32[256,768]{1,0:T(8,128)S(1)}, bf16[512,768]{1,0:T(8,128)(2,1)S(1)}, bf16[512,288]{1,0:T(8,128)(2,1)S(1)}, bf16[512,576]{1,0:T(8,128)(2,1)S...) custom-call(s32[14]{0:T(128)S(1)} %pad_add_fusion.s_ref, ...), custom_call_target="tpu_custom_call" | custom-call | flops 9999999827968 | bytes 14011448 | tf_op jit(solution)/shard_map/middle_kernel/pallas_call | solution.py:68
  58.1 3.0 %partner_kernel.1 = (bf16[256,288]{1,0:T(8,128)(2,1)S(1)}, bf16[256,576]{1,0:T(8,128)(2,1)S(1)}, bf16[256,768]{1,0:T(8,128)(2,1)S(1)}, bf16[256,768]{1,0:T(8,128)(2,1)S(1)}, bf16[896,768]{1,0:T(8,128)(2,1)S(1)}) custom-call(s32[14]{0:T(128)S(1)} %pad_add_fusion.s_ref, bf16[512,768]{1,0:T(8,128)(2,1)S(1)} %get-tuple-element.98.normed_ref, ...), custom_call_target="tpu_custom_call" | custom-call | flops 3000000000 | bytes 8699960 | tf_op jit(solution)/shard_map/partner_kernel/pallas_call | solution.py:68
  61.2 2.7 %collective-permute-start.11 = (bf16[256,768]{1,0:T(8,128)(2,1)S(1)}, bf16[256,768]{1,0:T(8,128)(2,1)S(1)}, u32[]{:S(2)}, u32[]{:S(2)}) collective-permute-start(bf16[256,768]{1,0:T(8,128)(2,1)S(1)} %get-tuple-element.111), channel_id=1, source_target_pairs={{0,1},{1,0},{2,3},{3,2},{4,5},{5,4},{6,7},{7,6},{8,9},{9,8},{10,11... | collective-permute-start | bytes 1179656 | tf_op jit(solution)/shard_map/ppermute | solution.py:559
  63.9 4.5 %own_kernel.1 = (f32[256,768]{1,0:T(8,128)S(1)}, f32[256,768]{1,0:T(8,128)S(1)}, bf16[768,1792]{1,0:T(8,128)(2,1)S(1)}) custom-call(s32[14]{0:T(128)S(1)} %pad_add_fusion.s_ref, bf16[512,768]{1,0:T(8,128)(2,1)S(1)} %get-tuple-element.98.normed_ref, bf16[512,768]{1,0:T(8,128)(2,1)S(1)} %get-tuple-element.99.cot_ref, ...), custom_call_target="tpu_custom_call" | custom-call | flops 10000000000 | bytes 11747384 | tf_op jit(solution)/shard_map/own_kernel/pallas_call | solution.py:68
  68.3 2.5 %collective-permute-done.11.recv_ref = bf16[256,768]{1,0:T(8,128)(2,1)S(1)} collective-permute-done((bf16[256,768]{1,0:T(8,128)(2,1)S(1)}, bf16[256,768]{1,0:T(8,128)(2,1)S(1)}, u32[]{:S(2)}, u32[]{:S(2)}) %collective-permute-start.11) | collective-permute-done | bytes 393248 | tf_op jit(solution)/shard_map/ppermute | solution.py:559
  72.0 1.5 output_grad_kernel.1
  73.7 1.8 %collective-permute-start.13 = (bf16[128,384]{1,0:T(8,128)(2,1)S(1)}, bf16[128,384]{1,0:T(8,128)(2,1)S(1)}, u32[]{:S(2)}, u32[]{:S(2)}) collective-permute-start(bf16[128,384]{1,0:T(8,128)(2,1)S(1)} %get-tuple-element.123), channel_id=1, source_target_pairs={{0,1},{1,0},{2,3},{3,2},{4,5},{5,4},{6,7},{7,6},{8,9},{9,8},{10,11... | collective-permute-start | bytes 294920 | tf_op jit(solution)/shard_map/ppermute | solution.py:559
  79.5 1.5 collective-permute-start.22
  83.0 3.2 %collective-permute-done.14.b2 = bf16[128,384]{1,0:T(8,128)(2,1)S(1)} collective-permute-done((bf16[128,384]{1,0:T(8,128)(2,1)S(1)}, bf16[128,384]{1,0:T(8,128)(2,1)S(1)}, u32[]{:S(2)}, u32[]{:S(2)}) %collective-permute-start.14) | collective-permute-done | bytes 98336 | tf_op jit(solution)/shard_map/ppermute | solution.py:559
  86.3 9.3 %backward_far_kernel.1 = (f32[256,768]{1,0:T(8,128)S(1)}, bf16[256,768]{1,0:T(8,128)(2,1)}, bf16[512,576]{1,0:T(8,128)(2,1)S(1)}, bf16[1024,256]{1,0:T(8,128)(2,...) custom-call(s32[14]{0:T(128)S(1)} %pad_add_fusion.s_ref, ...), custom_call_target="tpu_custom_call" | custom-call | flops 9999999827968 | bytes 11440184 | tf_op jit(solution)/shard_map/backward_far_kernel/pallas_call | solution.py:68
  95.6 1.9 %collective-permute-start.17 = (bf16[256,768]{1,0:T(8,128)(2,1)}, bf16[256,768]{1,0:T(8,128)(2,1)}, u32[]{:S(2)}, u32[]{:S(2)}) collective-permute-start(bf16[256,768]{1,0:T(8,128)(2,1)} %get-tuple-element.141), channel_id=1, source_target_pairs={{0,1},{1,0},{2,3},{3,2},{4,5},{5,4},{6,7},{7,6},{8,9},{9,8},{10,11... | collective-permute-start | bytes 1179656 | tf_op jit(solution)/shard_map/ppermute | solution.py:559
  97.5 4.2 %backward_near_kernel.1 = (f32[256,768]{1,0:T(8,128)S(1)}, bf16[256,768]{1,0:T(8,128)(2,1)S(1)}, bf16[512,576]{1,0:T(8,128)(2,1)S(1)}) custom-call(s32[14]{0:T(128)S(1)} %pad_add_fusion.s_ref, s32[1,1024]{1,0:T(1,128)S(1)} %copy-done.20, f32[1024,128]{1,0:T(8,128)S(1)} %copy-done.29, bf16[1024,256]{1,0:T(8,128)(2,1)S(1)} %copy-done.23, ...), custom_call_target="tpu_custom_call" | custom-call | flops 9999999827968 | bytes 11046968 | tf_op jit(solution)/shard_map/backward_near_kernel/pallas_call | solution.py:68
  101.7 4.1 %qkv_grad_kernel.1 = bf16[8,112,576]{2,1,0:T(8,128)(2,1)} custom-call(s32[14]{0:T(128)S(1)} %pad_add_fusion.s_ref, bf16[1024,768]{1,0:T(8,128)(2,1)S(1)} %get-tuple-element.136.normed_ref, bf16[512,576]{1,0:T(8,128)(2,1)S(1)} %get-tuple-element.137.near_ref, bf16[512,576]{1,0:T(8,128)(2,1)S(1)} %get-tuple-element.138.far_ref, ...), custom_call_target="tpu_custom_call" | custom-call | flops 1000000000 | bytes 4675640 | tf_op jit(solution)/shard_map/qkv_grad_kernel/pallas_call | solution.py:68
  107.9 2.9 %collective-permute-start.18 = (bf16[256,768]{1,0:T(8,128)(2,1)S(1)}, bf16[256,768]{1,0:T(8,128)(2,1)S(1)}, u32[]{:S(2)}, u32[]{:S(2)}) collective-permute-start(bf16[256,768]{1,0:T(8,128)(2,1)S(1)} %add_kernel.1), channel_id=1, source_target_pairs={{0,2},{1,3},{2,0},{3,1},{4,6},{5,7},{6,4},{7,5},{8,10},{9,11},{10,... | collective-permute-start | bytes 1179656 | tf_op jit(solution)/shard_map/ppermute | solution.py:559
  110.8 4.2 %all-to-all-start = ((bf16[8,112,576]{2,1,0:T(8,128)(2,1)}), bf16[8,112,576]{2,1,0:T(8,128)(2,1)}, u32[]{:S(2)}, u32[]{:S(2)}) async-start(bf16[8,112,576]{2,1,0:T(8,128)(2,1)} %qkv_grad_kernel.1), calls=%async_computation | async-start | bytes 2293760 | tf_op jit(solution)/shard_map/all_to_all | solution.py:745
  115.1 19.0 %collective-permute-done.16.n1 = bf16[512,768]{1,0:T(8,128)(2,1)} collective-permute-done((bf16[512,768]{1,0:T(8,128)(2,1)}, bf16[512,768]{1,0:T(8,128)(2,1)}, u32[]{:S(2)}, u32[]{:S(2)}) %collective-permute-start.16) | collective-permute-done | bytes 786464 | tf_op jit(solution)/shard_map/ppermute | solution.py:559
  134.1 2.4 %collect_kernel.1 = (f32[96,1088]{1,0:T(8,128)S(1)}, bf16[96,192]{1,0:T(8,128)(2,1)}, bf16[96,1088]{1,0:T(8,128)(2,1)}, bf16[96,192]{1,0:T(8,128)(2,1)}) custom-call(f32[96,2560]{1,0:T(8,128)S(1)} %get-tuple-element.146.own_ref, bf16[96,2560]{1,0:T(8,128)(2,1)} %collective-permute-done.22.r1, bf16[96,2560]{1,0:T(8,128)(2,1)} %collective-permute-done.23.r2, ...), custom_call_target="tpu_custom_call" | custom-call | flops 1000000000 | bytes 3158016 | tf_op jit(solution)/shard_map/collect_kernel/pallas_call | solution.py:68
  136.6 2.7 %collective-permute-start.27 = (bf16[96,192]{1,0:T(8,128)(2,1)}, bf16[96,192]{1,0:T(8,128)(2,1)}, u32[]{:S(2)}, u32[]{:S(2)}) collective-permute-start(bf16[96,192]{1,0:T(8,128)(2,1)} %get-tuple-element.150), channel_id=1, source_target_pairs={{0,3},{1,2},{2,1},{3,0},{4,7},{5,6},{6,5},{7,4},{8,11},{9,10},{10,... | collective-permute-start | bytes 110600 | tf_op jit(solution)/shard_map/ppermute | solution.py:559
  140.0 1.8 %add_convert_fusion = bf16[256,768]{1,0:T(8,128)(2,1)} fusion(f32[256,768]{1,0:T(8,128)S(1)} %get-tuple-element.108, bf16[512,768]{1,0:T(8,128)(2,1)} %collective-permute-done.16.n1), kind=kLoop, calls=%fused_computation.1 | loop fusion | flops 589824 | bytes 1572864 | tf_op jit(solution)/shard_map/convert_element_type | solution.py:770
  141.9 2.7 %final_kernel.1 = f32[256,768]{1,0:T(8,128)} custom-call(s32[14]{0:T(128)S(1)} %copy-done.6, bf16[1024,768]{1,0:T(8,128)(2,1)S(1)} %copy-done.10, f32[1,768]{1,0:T(1,128)S(1)} %copy-done.4, f32[256,768]{1,0:T(8,128)S(1)} %copy-done.33, f32[256,768]{1,0:T(8,128)S(1)} %copy-done.31, bf16[512,768]{1,0:T(8,128)(2,1)} %collective-permute-done.16.n1, ...), custom_call_target="tpu_custom_call" | custom-call | flops 9999999827968 | bytes 5114936 | tf_op jit(solution)/shard_map/final_kernel/pallas_call | solution.py:68
  144.5 2.2 %qkv_sum_kernel.1 = (f32[3,96,192]{2,1,0:T(8,128)}, f32[2,768]{1,0:T(2,128)S(1)}) custom-call(bf16[8,112,576]{2,1,0:T(8,128)(2,1)} %all-to-all-done.parts_ref), custom_call_target="tpu_custom_call" | custom-call | flops 1000000000 | bytes 1259520 | tf_op jit(solution)/shard_map/qkv_sum_kernel/pallas_call | solution.py:68
  146.7 2.6 %collective-permute-start.21 = (f32[2,768]{1,0:T(2,128)S(1)}, f32[2,768]{1,0:T(2,128)S(1)}, u32[]{:S(2)}, u32[]{:S(2)}) collective-permute-start(f32[2,768]{1,0:T(2,128)S(1)} %get-tuple-element.143), channel_id=1, source_target_pairs={{0,3},{1,2},{2,1},{3,0},{4,7},{5,6},{6,5},{7,4},{8,11},{9,10},{10,... | collective-permute-start | bytes 18440 | tf_op jit(solution)/shard_map/ppermute | solution.py:559
  149.3 1.8 %collective-permute-start.19 = (f32[2,768]{1,0:T(2,128)S(1)}, f32[2,768]{1,0:T(2,128)S(1)}, u32[]{:S(2)}, u32[]{:S(2)}) collective-permute-start(f32[2,768]{1,0:T(2,128)S(1)} %get-tuple-element.143), channel_id=1, source_target_pairs={{0,1},{1,0},{2,3},{3,2},{4,5},{5,4},{6,7},{7,6},{8,9},{9,8},{10,11... | collective-permute-start | bytes 18440 | tf_op jit(solution)/shard_map/ppermute | solution.py:559
  152.0 1.9 %finish_kernel.1 = (f32[2,96,288]{2,1,0:T(8,128)}, f32[288,96]{1,0:T(8,128)}, f32[192,96]{1,0:T(8,128)}) custom-call(f32[96,1088]{1,0:T(8,128)S(1)} %get-tuple-element.147.keep_ref, bf16[96,192]{1,0:T(8,128)(2,1)} %collective-permute-done.25.r1, bf16[96,1088]{1,0:T(8,128)(2,1)} %collective-permute-done.26.r2, bf16[96,192]{1,0:T(8,128)(2,1)} %collective-permute-done.27.r3), custom_call_target="tpu_custom_call" | custom-call | flops 1000000000 | bytes 1105920 | tf_op jit(solution)/shard_map/finish_kernel/pallas_call | solution.py:68
  (127 shorter events, 25.3 us)
Async XLA Ops:
  1.4 100.3 %copy-start.5 = (s32[14]{0:T(128)}, s32[14]{0:T(128)S(1)}, u32[]{:S(2)}) copy-start(s32[14]{0:T(128)S(1)} %pad_add_fusion.s_ref) | copy-start | bytes 172
  5.2 11.8 %collective-permute-start.2 = (bf16[96,384]{1,0:T(8,128)(2,1)S(1)}, bf16[96,384]{1,0:T(8,128)(2,1)S(1)}, u32[]{:S(2)}, u32[]{:S(2)}) collective-permute-start(bf16[96,384]{1,0:T(8,128)(2,1)S(1)} %get-tuple-element.83), channel_id=1, source_target_pairs={{0,3},{1,2},{2,1},{3,0},{4,7},{5,6},{6,5},{7,4},{8,11},{9,10},{10,... | collective-permute-start | bytes 221192 | tf_op jit(solution)/shard_map/ppermute | solution.py:559
  10.4 6.7 %collective-permute-start = (bf16[96,384]{1,0:T(8,128)(2,1)S(1)}, bf16[96,384]{1,0:T(8,128)(2,1)S(1)}, u32[]{:S(2)}, u32[]{:S(2)}) collective-permute-start(bf16[96,384]{1,0:T(8,128)(2,1)S(1)} %get-tuple-element.83), channel_id=1, source_target_pairs={{0,1},{1,0},{2,3},{3,2},{4,5},{5,4},{6,7},{7,6},{8,9},{9,8},{10,11... | collective-permute-start | bytes 221192 | tf_op jit(solution)/shard_map/ppermute | solution.py:559
  10.4 13.6 %collective-permute-start.1 = (bf16[320,384]{1,0:T(8,128)(2,1)S(1)}, bf16[320,384]{1,0:T(8,128)(2,1)S(1)}, u32[]{:S(2)}, u32[]{:S(2)}) collective-permute-start(bf16[320,384]{1,0:T(8,128)(2,1)S(1)} %get-tuple-element.84), channel_id=1, source_target_pairs={{0,2},{1,3},{2,0},{3,1},{4,6},{5,7},{6,4},{7,5},{8,10},{9,11},{10,... | collective-permute-start | bytes 737288 | tf_op jit(solution)/shard_map/ppermute | solution.py:559
  25.3 7.9 %collective-permute-start.6 = (bf16[224,384]{1,0:T(8,128)(2,1)}, bf16[224,384]{1,0:T(8,128)(2,1)}, u32[]{:S(2)}, u32[]{:S(2)}) collective-permute-start(bf16[224,384]{1,0:T(8,128)(2,1)} %get-tuple-element.85.a0), channel_id=1, source_target_pairs={{0,8},{4,12},{8,0},{12,4},{16,24},{20,28},{24,16},{28,20},{1,9},{5... | collective-permute-start | bytes 516104 | tf_op jit(solution)/shard_map/ppermute | solution.py:563
  26.8 6.4 %collective-permute-start.7 = (bf16[288,384]{1,0:T(8,128)(2,1)}, bf16[288,384]{1,0:T(8,128)(2,1)}, u32[]{:S(2)}, u32[]{:S(2)}) collective-permute-start(bf16[288,384]{1,0:T(8,128)(2,1)} %get-tuple-element.96.b0), channel_id=1, source_target_pairs={{0,16},{4,20},{8,24},{12,28},{16,0},{20,4},{24,8},{28,12},{1,17},{... | collective-permute-start | bytes 663560 | tf_op jit(solution)/shard_map/ppermute | solution.py:563
  33.2 20.3 %copy-start.12 = (bf16[2,768,288]{1,2,0:T(8,128)(2,1)S(1)}, bf16[2,768,288]{1,2,0:T(8,128)(2,1)}, u32[]{:S(2)}) copy-start(bf16[2,768,288]{1,2,0:T(8,128)(2,1)} %param.17) | copy-start | bytes 2654212
  33.2 20.3 %copy-start.16 = (bf16[192,768]{1,0:T(8,128)(2,1)S(1)}, bf16[192,768]{1,0:T(8,128)(2,1)}, u32[]{:S(2)}) copy-start(bf16[192,768]{1,0:T(8,128)(2,1)} %w_ref.1) | copy-start | bytes 884740
  34.6 18.9 %collective-permute-start.8 = (bf16[2,288,384]{2,1,0:T(8,128)(2,1)S(1)}, bf16[2,288,384]{2,1,0:T(8,128)(2,1)S(1)}, u32[]{:S(2)}, u32[]{:S(2)}) collective-permute-start(bf16[2,288,384]{2,1,0:T(8,128)(2,1)S(1)} %get-tuple-element.97.here_ref), channel_id=1, source_target_pairs={{0,8},{4,12},{8,0},{12,4},{16,24},{20,28},{24,16},{28,20},{1,9},{5... | collective-permute-start | bytes 1327112 | tf_op jit(solution)/shard_map/ppermute | solution.py:563
  35.2 8.0 %collective-permute-start.9 = (bf16[2,224,384]{2,1,0:T(8,128)(2,1)S(1)}, bf16[2,224,384]{2,1,0:T(8,128)(2,1)S(1)}, u32[]{:S(2)}, u32[]{:S(2)}) collective-permute-start(bf16[2,224,384]{2,1,0:T(8,128)(2,1)S(1)} %get-tuple-element.102.a0), channel_id=1, source_target_pairs={{0,16},{4,20},{8,24},{12,28},{16,0},{20,4},{24,8},{28,12},{1,17},{... | collective-permute-start | bytes 1032200 | tf_op jit(solution)/shard_map/ppermute | solution.py:563
  36.6 7.5 %collective-permute-start.3 = (bf16[256,384]{1,0:T(8,128)(2,1)S(1)}, bf16[256,384]{1,0:T(8,128)(2,1)S(1)}, u32[]{:S(2)}, u32[]{:S(2)}) collective-permute-start(bf16[256,384]{1,0:T(8,128)(2,1)S(1)} %get-tuple-element.91), channel_id=1, source_target_pairs={{0,1},{1,0},{2,3},{3,2},{4,5},{5,4},{6,7},{7,6},{8,9},{9,8},{10,11... | collective-permute-start | bytes 589832 | tf_op jit(solution)/shard_map/ppermute | solution.py:559
  37.1 16.4 %collective-permute-start.4 = (bf16[256,384]{1,0:T(8,128)(2,1)S(1)}, bf16[256,384]{1,0:T(8,128)(2,1)S(1)}, u32[]{:S(2)}, u32[]{:S(2)}) collective-permute-start(bf16[256,384]{1,0:T(8,128)(2,1)S(1)} %get-tuple-element.92), channel_id=1, source_target_pairs={{0,2},{1,3},{2,0},{3,1},{4,6},{5,7},{6,4},{7,5},{8,10},{9,11},{10,... | collective-permute-start | bytes 589832 | tf_op jit(solution)/shard_map/ppermute | solution.py:559
  40.5 13.0 %collective-permute-start.5 = (bf16[256,384]{1,0:T(8,128)(2,1)S(1)}, bf16[256,384]{1,0:T(8,128)(2,1)S(1)}, u32[]{:S(2)}, u32[]{:S(2)}) collective-permute-start(bf16[256,384]{1,0:T(8,128)(2,1)S(1)} %get-tuple-element.93), channel_id=1, source_target_pairs={{0,3},{1,2},{2,1},{3,0},{4,7},{5,6},{6,5},{7,4},{8,11},{9,10},{10,... | collective-permute-start | bytes 589832 | tf_op jit(solution)/shard_map/ppermute | solution.py:559
  44.1 14.1 %collective-permute-start.10 = (bf16[4,224,384]{2,1,0:T(8,128)(2,1)}, bf16[4,224,384]{2,1,0:T(8,128)(2,1)}, u32[]{:S(2)}, u32[]{:S(2)}) collective-permute-start(bf16[4,224,384]{2,1,0:T(8,128)(2,1)} %quads_kernel.1.fe_ref), channel_id=1, source_target_pairs={{0,4},{4,0},{8,12},{12,8},{16,20},{20,16},{24,28},{28,24},{1,5},{5... | collective-permute-start | bytes 2064392 | tf_op jit(solution)/shard_map/ppermute | solution.py:563
  61.2 9.7 %collective-permute-start.11 = (bf16[256,768]{1,0:T(8,128)(2,1)S(1)}, bf16[256,768]{1,0:T(8,128)(2,1)S(1)}, u32[]{:S(2)}, u32[]{:S(2)}) collective-permute-start(bf16[256,768]{1,0:T(8,128)(2,1)S(1)} %get-tuple-element.111), channel_id=1, source_target_pairs={{0,1},{1,0},{2,3},{3,2},{4,5},{5,4},{6,7},{7,6},{8,9},{9,8},{10,11... | collective-permute-start | bytes 1179656 | tf_op jit(solution)/shard_map/ppermute | solution.py:559
  73.6 4.5 %collective-permute-start.12 = (bf16[4,96,2560]{2,1,0:T(8,128)(2,1)S(1)}, bf16[4,96,2560]{2,1,0:T(8,128)(2,1)S(1)}, u32[]{:S(2)}, u32[]{:S(2)}) collective-permute-start(bf16[4,96,2560]{2,1,0:T(8,128)(2,1)S(1)} %get-tuple-element.117), channel_id=1, source_target_pairs={{0,4},{4,0},{8,12},{12,8},{16,20},{20,16},{24,28},{28,24},{1,5},{5... | collective-permute-start | bytes 5898248 | tf_op jit(solution)/shard_map/ppermute | solution.py:563
  73.7 8.5 %collective-permute-start.13 = (bf16[128,384]{1,0:T(8,128)(2,1)S(1)}, bf16[128,384]{1,0:T(8,128)(2,1)S(1)}, u32[]{:S(2)}, u32[]{:S(2)}) collective-permute-start(bf16[128,384]{1,0:T(8,128)(2,1)S(1)} %get-tuple-element.123), channel_id=1, source_target_pairs={{0,1},{1,0},{2,3},{3,2},{4,5},{5,4},{6,7},{7,6},{8,9},{9,8},{10,11... | collective-permute-start | bytes 294920 | tf_op jit(solution)/shard_map/ppermute | solution.py:559
  75.5 10.8 %collective-permute-start.14 = (bf16[128,384]{1,0:T(8,128)(2,1)S(1)}, bf16[128,384]{1,0:T(8,128)(2,1)S(1)}, u32[]{:S(2)}, u32[]{:S(2)}) collective-permute-start(bf16[128,384]{1,0:T(8,128)(2,1)S(1)} %get-tuple-element.124), channel_id=1, source_target_pairs={{0,2},{1,3},{2,0},{3,1},{4,6},{5,7},{6,4},{7,5},{8,10},{9,11},{10,... | collective-permute-start | bytes 294920 | tf_op jit(solution)/shard_map/ppermute | solution.py:559
  76.7 9.5 %collective-permute-start.15 = (bf16[128,384]{1,0:T(8,128)(2,1)S(1)}, bf16[128,384]{1,0:T(8,128)(2,1)S(1)}, u32[]{:S(2)}, u32[]{:S(2)}) collective-permute-start(bf16[128,384]{1,0:T(8,128)(2,1)S(1)} %get-tuple-element.125), channel_id=1, source_target_pairs={{0,3},{1,2},{2,1},{3,0},{4,7},{5,6},{6,5},{7,4},{8,11},{9,10},{10,... | collective-permute-start | bytes 294920 | tf_op jit(solution)/shard_map/ppermute | solution.py:559
  79.5 54.5 %collective-permute-start.22 = (bf16[96,2560]{1,0:T(8,128)(2,1)}, bf16[96,2560]{1,0:T(8,128)(2,1)}, u32[]{:S(2)}, u32[]{:S(2)}) collective-permute-start(bf16[96,2560]{1,0:T(8,128)(2,1)} %get-tuple-element.118), channel_id=1, source_target_pairs={{0,8},{4,12},{8,0},{12,4},{16,24},{20,28},{24,16},{28,20},{1,9},{5... | collective-permute-start | bytes 1474568 | tf_op jit(solution)/shard_map/ppermute | solution.py:563
  81.0 53.0 %collective-permute-start.23 = (bf16[96,2560]{1,0:T(8,128)(2,1)}, bf16[96,2560]{1,0:T(8,128)(2,1)}, u32[]{:S(2)}, u32[]{:S(2)}) collective-permute-start(bf16[96,2560]{1,0:T(8,128)(2,1)} %get-tuple-element.119), channel_id=1, source_target_pairs={{0,16},{4,20},{8,24},{12,28},{16,0},{20,4},{24,8},{28,12},{1,17},{... | collective-permute-start | bytes 1474568 | tf_op jit(solution)/shard_map/ppermute | solution.py:563
  82.1 51.9 %collective-permute-start.24 = (bf16[96,2560]{1,0:T(8,128)(2,1)}, bf16[96,2560]{1,0:T(8,128)(2,1)}, u32[]{:S(2)}, u32[]{:S(2)}) collective-permute-start(bf16[96,2560]{1,0:T(8,128)(2,1)} %get-tuple-element.120), channel_id=1, source_target_pairs={{0,24},{4,28},{8,16},{12,20},{16,8},{20,12},{24,0},{28,4},{1,25},{... | collective-permute-start | bytes 1474568 | tf_op jit(solution)/shard_map/ppermute | solution.py:563
  95.6 11.2 %collective-permute-start.17 = (bf16[256,768]{1,0:T(8,128)(2,1)}, bf16[256,768]{1,0:T(8,128)(2,1)}, u32[]{:S(2)}, u32[]{:S(2)}) collective-permute-start(bf16[256,768]{1,0:T(8,128)(2,1)} %get-tuple-element.141), channel_id=1, source_target_pairs={{0,1},{1,0},{2,3},{3,2},{4,5},{5,4},{6,7},{7,6},{8,9},{9,8},{10,11... | collective-permute-start | bytes 1179656 | tf_op jit(solution)/shard_map/ppermute | solution.py:559
  106.7 27.3 %collective-permute-start.16 = (bf16[512,768]{1,0:T(8,128)(2,1)}, bf16[512,768]{1,0:T(8,128)(2,1)}, u32[]{:S(2)}, u32[]{:S(2)}) collective-permute-start(bf16[512,768]{1,0:T(8,128)(2,1)} %pad_maximum_fusion), channel_id=1, source_target_pairs={{0,1},{1,0},{2,3},{3,2},{4,5},{5,4},{6,7},{7,6},{8,9},{9,8},{10,11... | collective-permute-start | bytes 2359304 | tf_op jit(solution)/shard_map/ppermute | solution.py:559
  107.9 33.9 %collective-permute-start.18 = (bf16[256,768]{1,0:T(8,128)(2,1)S(1)}, bf16[256,768]{1,0:T(8,128)(2,1)S(1)}, u32[]{:S(2)}, u32[]{:S(2)}) collective-permute-start(bf16[256,768]{1,0:T(8,128)(2,1)S(1)} %add_kernel.1), channel_id=1, source_target_pairs={{0,2},{1,3},{2,0},{3,1},{4,6},{5,7},{6,4},{7,5},{8,10},{9,11},{10,... | collective-permute-start | bytes 1179656 | tf_op jit(solution)/shard_map/ppermute | solution.py:559
  110.8 33.7 %all-to-all-start = ((bf16[8,112,576]{2,1,0:T(8,128)(2,1)}), bf16[8,112,576]{2,1,0:T(8,128)(2,1)}, u32[]{:S(2)}, u32[]{:S(2)}) async-start(bf16[8,112,576]{2,1,0:T(8,128)(2,1)} %qkv_grad_kernel.1), calls=%async_computation | async-start | bytes 2293760 | tf_op jit(solution)/shard_map/all_to_all | solution.py:745
  136.5 12.8 %collective-permute-start.25 = (bf16[96,192]{1,0:T(8,128)(2,1)}, bf16[96,192]{1,0:T(8,128)(2,1)}, u32[]{:S(2)}, u32[]{:S(2)}) collective-permute-start(bf16[96,192]{1,0:T(8,128)(2,1)} %get-tuple-element.148), channel_id=1, source_target_pairs={{0,1},{1,0},{2,3},{3,2},{4,5},{5,4},{6,7},{7,6},{8,9},{9,8},{10,11... | collective-permute-start | bytes 110600 | tf_op jit(solution)/shard_map/ppermute | solution.py:559
  136.6 14.5 %collective-permute-start.27 = (bf16[96,192]{1,0:T(8,128)(2,1)}, bf16[96,192]{1,0:T(8,128)(2,1)}, u32[]{:S(2)}, u32[]{:S(2)}) collective-permute-start(bf16[96,192]{1,0:T(8,128)(2,1)} %get-tuple-element.150), channel_id=1, source_target_pairs={{0,3},{1,2},{2,1},{3,0},{4,7},{5,6},{6,5},{7,4},{8,11},{9,10},{10,... | collective-permute-start | bytes 110600 | tf_op jit(solution)/shard_map/ppermute | solution.py:559
  139.2 12.8 %collective-permute-start.26 = (bf16[96,1088]{1,0:T(8,128)(2,1)}, bf16[96,1088]{1,0:T(8,128)(2,1)}, u32[]{:S(2)}, u32[]{:S(2)}) collective-permute-start(bf16[96,1088]{1,0:T(8,128)(2,1)} %get-tuple-element.149), channel_id=1, source_target_pairs={{0,2},{1,3},{2,0},{3,1},{4,6},{5,7},{6,4},{7,5},{8,10},{9,11},{10,... | collective-permute-start | bytes 626696 | tf_op jit(solution)/shard_map/ppermute | solution.py:559
  146.7 7.2 %collective-permute-start.21 = (f32[2,768]{1,0:T(2,128)S(1)}, f32[2,768]{1,0:T(2,128)S(1)}, u32[]{:S(2)}, u32[]{:S(2)}) collective-permute-start(f32[2,768]{1,0:T(2,128)S(1)} %get-tuple-element.143), channel_id=1, source_target_pairs={{0,3},{1,2},{2,1},{3,0},{4,7},{5,6},{6,5},{7,4},{8,11},{9,10},{10,... | collective-permute-start | bytes 18440 | tf_op jit(solution)/shard_map/ppermute | solution.py:559
  149.3 4.6 %collective-permute-start.20 = (f32[2,768]{1,0:T(2,128)S(1)}, f32[2,768]{1,0:T(2,128)S(1)}, u32[]{:S(2)}, u32[]{:S(2)}) collective-permute-start(f32[2,768]{1,0:T(2,128)S(1)} %get-tuple-element.143), channel_id=1, source_target_pairs={{0,2},{1,3},{2,0},{3,1},{4,6},{5,7},{6,4},{7,5},{8,10},{9,11},{10,... | collective-permute-start | bytes 18440 | tf_op jit(solution)/shard_map/ppermute | solution.py:559
  149.3 4.6 %collective-permute-start.19 = (f32[2,768]{1,0:T(2,128)S(1)}, f32[2,768]{1,0:T(2,128)S(1)}, u32[]{:S(2)}, u32[]{:S(2)}) collective-permute-start(f32[2,768]{1,0:T(2,128)S(1)} %get-tuple-element.143), channel_id=1, source_target_pairs={{0,1},{1,0},{2,3},{3,2},{4,5},{5,4},{6,7},{7,6},{8,9},{9,8},{10,11... | collective-permute-start | bytes 18440 | tf_op jit(solution)/shard_map/ppermute | solution.py:559
  (33 other events, 265.2 us)

commit v3 on v2

--- a/solution.py
+++ b/solution.py
@@ -32,8 +32,8 @@
     "qkv_sum_kernel": 1,
     "pack_kernel": 1,
     "arrived_kernel": 1,
-    "pairs_kernel": 1,
-    "quads_kernel": 1,
+    "pair_kernel": 1,
+    "begin_kernel": 10000,
     "project_kernel": 6,
     "attend_kernel": 10000,
     "middle_kernel": 10000,
@@ -213,19 +213,18 @@
         out[...] = ctx_ref[z ^ k]
 
 
-def place_slots(s_ref, even_ref, odd_ref, out_ref, first, rows):
-    cols = D // 2
-    for i in range(8):
-        slot = s_ref[2 + i]
-        piece = even_ref[i, first : first + rows, :] if i < 4 else odd_ref[i - 4, first : first + rows, :]
-        there = pl.ds(pl.multiple_of((slot // 2) * rows, 16), rows)
-        out_ref[there, pl.ds(pl.multiple_of((slot % 2) * cols, 128), cols)] = piece
-
-
-def gated(normed, cot, w_in, w_down, act_ref, gb_ref, width):
+def place_slots(s_ref, refs, out_ref):
+    rows, cols = refs[0].shape[1:]
+    for group, ref in enumerate(refs):
+        for i in range(2):
+            slot = s_ref[2 + 4 * (group // 2) + 2 * i + group % 2]
+            there = pl.ds(pl.multiple_of((slot // 2) * rows, 16), rows)
+            out_ref[there, pl.ds(pl.multiple_of((slot % 2) * cols, 128), cols)] = ref[i]
+
+
+def gated(normed, act_back, w_in, w_down, act_ref, gb_ref, width):
     both = dot(normed, w_in, NT)
     gate, linear = both[:, :width], both[:, width:]
-    act_back = dot(cot, w_down, NT)
     cdf = 0.5 * (1.0 + lax.erf(gate * math.sqrt(0.5)))
     slope = cdf + gate * (jnp.exp(-0.5 * gate * gate) * (1.0 / math.sqrt(2.0 * math.pi)))
     gelu = gate * cdf
@@ -235,52 +234,59 @@
     return dot(act_ref[...], w_down), dot(gb_ref[...], w_in)
 
 
+def begin_kernel(
+    s_ref, tok_ref, cot_ref, c0, c1, c2, c3, w_ref, dw_ref, res_ref, context_ref, cot_out, back_ref
+):
+    z = s_ref[0]
+    for half in range(2):
+        base = (z if half == 0 else z ^ 1) * BLOCK
+        there = pl.ds(pl.multiple_of(base, BLOCK), BLOCK)
+        rows = slice(half * BLOCK, (half + 1) * BLOCK)
+        mine = slice(half * COLS, (half + 1) * COLS)
+        res_ref[rows, :] = tok_ref[there, :].astype(F32) + dot(c0[:, mine], w_ref[...])
+        for k, c in enumerate((c1, c2, c3)):
+            context_ref[k, rows, :] = c[:, mine]
+        cot_out[rows, :] = cot_ref[there, :]
+    back_ref[...] = dot(cot_out[...], dw_ref[...], NT)
+
+
 def middle_kernel(
-    s_ref, tok_ref, cot_ref, c0, c1, c2, c3, w_ref, here_ref, there_ref, gain_ref, gw_ref, dw_ref,
-    res_ref, normed_ref, act_ref, gb_ref, branch_ref, back_ref, wo_ref, cot_out,
-):
-    z = s_ref[0]
+    s_ref, part_ref, context_ref, cot_ref, act_back_ref, w_ref, here_ref, there_ref, gain_ref, gw_ref, dw_ref,
+    res_ref, normed_ref, act_ref, gb_ref, branch_ref, back_ref, wo_ref,
+):
     wo_ref[0] = w_ref[...]
     few = COLS // 4
-    pieces = ((0, here_ref, 0), (2, here_ref, 1), (1, there_ref, 0), (3, there_ref, 1))
-    for chip, ref, i in pieces:
-        there = pl.ds(pl.multiple_of(s_ref[10 + chip] * few, 16), few)
+    pieces = ((0, here_ref, 0), (1, here_ref, 1), (2, there_ref, 0), (3, there_ref, 1))
+    for slot, ref, i in pieces:
+        there = pl.ds(pl.multiple_of(s_ref[10 + slot] * few, 16), few)
         for k in range(3):
             for side in range(2):
                 first = (2 * k + side) * few
                 lanes = slice(side * (D // 2), (side + 1) * (D // 2))
                 wo_ref[k + 1, there, lanes] = ref[i, first : first + few, :]
-    for half in range(2):
-        base = (z if half == 0 else z ^ 1) * BLOCK
-        there = pl.ds(pl.multiple_of(base, BLOCK), BLOCK)
-        rows = slice(half * BLOCK, (half + 1) * BLOCK)
-        attended = jnp.zeros((BLOCK, D), F32)
-        for k, c in enumerate((c0, c1, c2, c3)):
-            attended += dot(c[:, half * COLS : (half + 1) * COLS], wo_ref[k])
-        residual = tok_ref[there, :].astype(F32) + attended
-        if half == 0:
-            res_ref[...] = residual
-            branch_ref[rows, :] = residual
-        else:
-            branch_ref[rows, :] = jnp.zeros_like(residual)
-        unit, _ = normalize(residual)
-        normed_ref[rows, :] = (unit * gain_ref[...]).astype(BF16)
-        cot_out[rows, :] = cot_ref[there, :]
+    residual = part_ref[...]
+    for k in range(3):
+        residual += dot(context_ref[k], wo_ref[k + 1])
+    res_ref[...] = residual[:BLOCK]
+    branch_ref[:BLOCK, :] = residual[:BLOCK]
+    branch_ref[BLOCK:, :] = jnp.zeros((BLOCK, D), F32)
+    unit, _ = normalize(residual)
+    normed_ref[...] = (unit * gain_ref[...]).astype(BF16)
     branch, back = gated(
-        normed_ref[...], cot_out[...], gw_ref[...], dw_ref[...], act_ref, gb_ref, dw_ref.shape[0]
+        normed_ref[...], act_back_ref[...], gw_ref[...], dw_ref[...], act_ref, gb_ref, dw_ref.shape[0]
     )
     branch_ref[...] += branch
     back_ref[...] = back
 
 
 def partner_kernel(
-    s_ref, normed_ref, cot_ref, branch_in, back_in, fe_ref, fo_ref,
+    s_ref, normed_ref, cot_ref, branch_in, back_in, f0, f1, f2, f3,
     act_ref, gb_ref, branch_ref, back_ref, other_ref,
 ):
     width = act_ref.shape[1]
-    place_slots(s_ref, fe_ref, fo_ref, other_ref, 0, other_ref.shape[0] // 4)
+    place_slots(s_ref, (f0, f1, f2, f3), other_ref)
     branch, back = gated(
-        normed_ref[BLOCK:, :], cot_ref[BLOCK:, :], other_ref[: 2 * width, :],
+        normed_ref[BLOCK:, :], dot(cot_ref[BLOCK:, :], other_ref[2 * width : 3 * width, :], NT), other_ref[: 2 * width, :],
         other_ref[2 * width : 3 * width, :], act_ref, gb_ref, width,
     )
     branch_ref[...] = (branch_in[BLOCK:, :] + branch).astype(BF16)
@@ -294,7 +300,7 @@
 ):
     width = act_ref.shape[1]
     branch, back = gated(
-        normed_ref[:BLOCK, :], cot_ref[:BLOCK, :], other_ref[: 2 * width, :],
+        normed_ref[:BLOCK, :], dot(cot_ref[:BLOCK, :], other_ref[2 * width : 3 * width, :], NT), other_ref[: 2 * width, :],
         other_ref[2 * width : 3 * width, :], act_own, gb_own, width,
     )
     branch_ref[...] = branch_in[:BLOCK, :] + branch
@@ -376,7 +382,7 @@
         out[:, out.shape[1] - COLS :] = total[:, first : first + COLS].astype(BF16)
 
 
-def pack_kernel(s_ref, w_in_ref, w_down_ref, w_out_ref, out_ref, both_ref, whole_ref):
+def pack_kernel(s_ref, w_in_ref, w_down_ref, w_out_ref, out_ref, ff_ref, whole_ref):
     slot = s_ref[1]
     there, cols = slot // 2, pl.ds(pl.multiple_of((slot % 2) * (D // 2), 128), D // 2)
     n_in, n_down = w_in_ref.shape[0], w_down_ref.shape[0]
@@ -385,30 +391,22 @@
     whole_ref[n_in + n_down :, :] = jnp.zeros((whole_ref.shape[0] - n_in - n_down, D), BF16)
     rows = whole_ref.shape[0] // 4
     few = w_out_ref.shape[0] // 4
-    here = pl.ds(pl.multiple_of(there * few, 16), few)
-    both_ref[:rows, :] = whole_ref[pl.ds(pl.multiple_of(there * rows, 16), rows), cols]
+    here = pl.ds(pl.multiple_of(slot % 4 * few, 16), few)
+    ff_ref[...] = whole_ref[pl.ds(pl.multiple_of(there * rows, 16), rows), cols]
     for side in range(2):
         mine = w_out_ref[here, side * (D // 2) : (side + 1) * (D // 2)]
         out_ref[side * few : (side + 1) * few, :] = mine
-        both_ref[rows + side * few : rows + (side + 1) * few, :] = mine
-
-
-def arrived_kernel(s_ref, f1, f2, f3, ff_ref, out_ref):
-    ff, few = ff_ref.shape[0], f1.shape[0]
-    ff_ref[...] = f2[:ff, :]
-    for i, piece in enumerate((f1[...], f2[ff:, :], f3[...])):
-        out_ref[i * few : (i + 1) * few, :] = piece
-
-
-def pairs_kernel(s_ref, a0, a1, b0, b1, a_ref, b_ref):
-    for i, (a, b) in enumerate(((a0, b0), (a1, b1))):
-        a_ref[i] = a[...]
-        b_ref[i] = b[...]
-
-
-def quads_kernel(a0, a1, out_ref):
-    out_ref[:2] = a0[...]
-    out_ref[2:] = a1[...]
+
+
+def arrived_kernel(s_ref, f1, f2, f3, out_ref):
+    few = f1.shape[0]
+    for i, piece in enumerate((f1, f2, f3)):
+        out_ref[i * few : (i + 1) * few, :] = piece[...]
+
+
+def pair_kernel(s_ref, a0, a1, out_ref):
+    out_ref[0] = a0[...]
+    out_ref[1] = a1[...]
 
 
 def backward_steps(
@@ -544,7 +542,7 @@
 
 
 def final_kernel(s_ref, tok_ref, gain_ref, back_ref, n0, n1, n2, out_ref):
-    upstream = n0[...] + n1[:BLOCK, :].astype(F32) + n2[...].astype(F32)
+    upstream = n0[...] + n1[...].astype(F32) + n2[...].astype(F32)
     rows = pl.ds(pl.multiple_of(s_ref[0] * BLOCK, BLOCK), BLOCK)
     unit, inverse = normalize(tok_ref[rows, :].astype(F32))
     out_ref[...] = back_ref[...] + norm_back(upstream, unit, inverse, gain_ref[...])
@@ -593,8 +591,9 @@
     z = lax.axis_index("narrow").astype(jnp.int32)
     order = jnp.asarray([0, 2, 4, 6, 1, 3, 5, 7], jnp.int32)
     slots = (mine ^ order) if plane else jnp.arange(8, dtype=jnp.int32)
-    chips = ((mine // 2) ^ jnp.arange(4, dtype=jnp.int32)) if plane else jnp.arange(4, dtype=jnp.int32)
-    scalars = jnp.concatenate([z[None], mine[None], slots, chips])
+    quarters = jnp.asarray([0, 2, 1, 3], jnp.int32)
+    quarters = ((mine % 4) ^ quarters) if plane else jnp.arange(4, dtype=jnp.int32)
+    scalars = jnp.concatenate([z[None], mine[None], slots, quarters])
     hidden = geglu_weight.shape[2]
     padded = -(-3 * hidden // 64) * 64
     rows_d = D // size
@@ -604,24 +603,16 @@
     w_in = geglu_weight.transpose(0, 2, 1).reshape(2 * hidden, D)
 
     few, many = COLS // 4, padded // 4
+    now = scalars
     if plane:
-        slot_out, slot_both = call(
+        slot_out, slot_ff = call(
             pack_kernel,
             (scalars, w_in, down_weight, output_weight),
-            (sds((2 * few, D // 2), BF16), sds((many + 2 * few, D // 2), BF16)),
+            (sds((2 * few, D // 2), BF16), sds((many, D // 2), BF16)),
             [pltpu.VMEM((padded, D), BF16)],
         )
-        fetched = [along_narrow(x, k) for k, x in ((1, slot_out), (2, slot_both), (3, slot_out))]
-    else:
-        whole = jnp.concatenate(
-            [w_in, down_weight, jnp.zeros((padded - 3 * hidden, D), BF16)], axis=0
-        )
-        even, odd = (x[:, 0] for x in all_slots(whole, (2,)))
-        quarters = jnp.stack([along_narrow(output_weight, k) for k in (1, 2, 3)])
-        quarters = quarters.reshape(3, 4, few, 2, D // 2).transpose(1, 0, 3, 2, 4)
-        quarters = quarters.reshape(4, 6 * few, D // 2)
-        b_pair, b_there = quarters[::2], quarters[1::2]
-
+        out_fetched = [along_narrow(slot_out, k) for k in (1, 2, 3)]
+        ff_fetched = along_narrow(slot_ff, 2)
     wide_rows = sds((LEN, LANES), BF16)
     q, k, v, normed_one, trig, segc = call(
         project_kernel,
@@ -631,15 +622,6 @@
         [pltpu.VMEM((LEN, LANES), F32)],
         scalars=0,
     )
-    now = scalars
-    if plane:
-        a0, b0 = call(
-            arrived_kernel,
-            (tie(scalars, q), *fetched),
-            (sds((many, D // 2), BF16), sds((6 * few, D // 2), BF16)),
-        )
-        a1, b1 = along_wide(a0, 2), along_wide(b0, 4)
-        now = tie(scalars, a0)
     piece = sds((BLOCK, 2 * COLS), BF16)
     c0, c1, c2, c3, lse = call(
         attend_kernel,
@@ -649,32 +631,49 @@
     )
     context = (c0, *(along_narrow(c, k) for k, c in ((1, c1), (2, c2), (3, c3))))
     if plane:
-        a_pair, b_pair = call(
-            pairs_kernel,
-            (tie(scalars, lse), a0, a1, b0, b1),
-            (sds((2, many, D // 2), BF16), sds((2, 6 * few, D // 2), BF16)),
+        ff0 = tie(ff_fetched, lse)
+        slots_two = sds((2, many, D // 2), BF16)
+        (out0,) = call(
+            arrived_kernel, (tie(scalars, lse), *out_fetched), (sds((6 * few, D // 2), BF16),)
         )
-        b_there = along_wide(b_pair, 2)
-        (even,) = call(
-            quads_kernel, (a_pair, along_wide(a_pair, 4)), (sds((4, many, D // 2), BF16),), scalars=0
+        (out_here,) = call(
+            pair_kernel, (scalars, out0, along_wide(out0, 2)), (sds((2, 6 * few, D // 2), BF16),)
         )
-        odd = along_wide(even, 1)
+        out_there = along_wide(out_here, 1)
+        (ff_pair,) = call(pair_kernel, (scalars, ff0, along_wide(ff0, 4)), (slots_two,))
+        ff_x = along_wide(ff_pair, 2)
+        ff_slots = (ff_pair, ff_x, along_wide(ff_pair, 1), along_wide(ff_x, 1))
+    else:
+        everything = jnp.concatenate(
+            [w_in, down_weight, jnp.zeros((padded - 3 * hidden, D), BF16)], axis=0
+        )
+        even, odd = (x[:, 0] for x in all_slots(everything, (2,)))
+        ff_slots = (even[::2], even[1::2], odd[::2], odd[1::2])
+        others = jnp.stack([along_narrow(output_weight, k) for k in (1, 2, 3)])
+        others = others.reshape(3, 4, few, 2, D // 2).transpose(1, 0, 3, 2, 4)
+        others = others.reshape(4, 6 * few, D // 2)
+        out_here, out_there = others[:2], others[2:]
 
     whole = sds((2 * BLOCK, D), F32)
     own = sds((BLOCK, D), F32)
     own_low = sds((BLOCK, D), BF16)
-    res, normed_two, act, gb, branch, back, wo, cot = call(
+    part, contexts, cot, act_back = call(
+        begin_kernel,
+        (scalars, tokens, cotangent, *context, output_weight, down_weight),
+        (whole, sds((3, 2 * BLOCK, COLS), BF16), sds((2 * BLOCK, D), BF16),
+         sds((2 * BLOCK, hidden), F32)),
+    )
+    res, normed_two, act, gb, branch, back, wo = call(
         middle_kernel,
-        (scalars, tokens, cotangent, *context, output_weight, b_pair, b_there, gain_two,
-         w_in, down_weight),
+        (scalars, part, contexts, cot, act_back, output_weight, out_here, out_there, gain_two, w_in,
+         down_weight),
         (own, sds((2 * BLOCK, D), BF16), sds((2 * BLOCK, hidden), BF16),
-         sds((2 * BLOCK, 2 * hidden), BF16), whole, whole, sds((NARROW, COLS, D), BF16),
-         sds((2 * BLOCK, D), BF16)),
+         sds((2 * BLOCK, 2 * hidden), BF16), whole, whole, sds((NARROW, COLS, D), BF16)),
     )
     part_act, part_gb = sds((BLOCK, hidden), BF16), sds((BLOCK, 2 * hidden), BF16)
     act_par, gb_par, out_send, send, other = call(
         partner_kernel,
-        (scalars, normed_two, cot, branch, back, even, odd),
+        (scalars, normed_two, cot, branch, back, *ff_slots),
         (part_act, part_gb, own_low, own_low, sds((padded, D), BF16)),
     )
     recv = along_narrow(send, 1)
@@ -714,7 +713,7 @@
     else:
         blocks = jnp.concatenate([even_part, odd_part], axis=0)
         grad_sum = sum_wide(blocks.reshape(size, rows_d, grad_cols))
-        grad_recv = [jnp.zeros((rows_d, grad_cols), BF16)] * 3
+        grad_recv, grad_sends = [jnp.zeros((rows_d, grad_cols), BF16)] * 3, ()
         now = tie(scalars, even_part)
 
     rows_f32 = sds((LEN, LANES), F32)
@@ -725,6 +724,7 @@
         (own, own_low, pair_qkv, wide_rows, rows_f32, rows_f32, rows_f32),
     )
     exchanged = along_narrow(n3, 1)
+    branch_recv = along_narrow(tie(out_send, upstream[1], *grad_sends), 1)
     n0, n1, qkv_near = call(
         backward_near_kernel,
         (scalars, segments, segc, q, k, v, lse, trig, back_rows, *grads, w_qkv),
@@ -733,16 +733,16 @@
     )
     (qkv_part,) = call(
         qkv_grad_kernel,
-        (tie(scalars, n1), normed_one, qkv_near, qkv_far, w_qkv, gain_one, gain_two_part),
+        (tie(scalars, n1, branch_recv), normed_one, qkv_near, qkv_far, w_qkv, gain_one, gain_two_part),
         (sds((size, rows_d + GAIN_ROWS, 3 * COLS), BF16),),
         [pltpu.VMEM((D, 3 * COLS), BF16), pltpu.VMEM((LEN, D), BF16)],
     )
-    near_recv = along_narrow(jnp.concatenate([n1, out_send], axis=0), 1)
+    near_recv = along_narrow(n1, 1)
     (pair_sum,) = call(add_kernel, (tie(n2, qkv_part), exchanged), (own_low,), scalars=0)
     far_recv = along_narrow(pair_sum, 2)
     qkv_grad, gains = call(
         qkv_sum_kernel,
-        (lax.all_to_all(tie(qkv_part, pair_sum), "wide", 0, 0),),
+        (lax.all_to_all(qkv_part, "wide", 0, 0),),
         (sds((3, rows_d, COLS), F32), sds((2, D), F32)),
         scalars=0,
     )
@@ -754,20 +754,20 @@
         scalars=0,
     )
     there = [along_narrow(x, k) for k, x in zip((1, 2, 3), there)]
-    geglu_grad, down_grad, out_grad = call(
-        finish_kernel,
-        (grad_keep, *there),
-        (sds((2, rows_d, hidden), F32), sds((hidden, rows_d), F32), sds((COLS, rows_d), F32)),
-        [pltpu.VMEM((128, -(-hidden // 128) * 128), F32)],
-        scalars=0,
-    )
     (tokens_grad,) = call(
         final_kernel,
         (scalars, tokens, gain_one, back, n0, near_recv, far_recv),
         (own,),
     )
     gains = gains + along_narrow(gains, 1) + along_narrow(gains, 2) + along_narrow(gains, 3)
-    layer_out = (out_keep + near_recv[BLOCK:].astype(F32)).astype(BF16)
+    geglu_grad, down_grad, out_grad = call(
+        finish_kernel,
+        (tie(grad_keep, tokens_grad), *there),
+        (sds((2, rows_d, hidden), F32), sds((hidden, rows_d), F32), sds((COLS, rows_d), F32)),
+        [pltpu.VMEM((128, -(-hidden // 128) * 128), F32)],
+        scalars=0,
+    )
+    layer_out = (out_keep + branch_recv.astype(F32)).astype(BF16)
     return (
         layer_out, tokens_grad, gains[0], qkv_grad, out_grad, gains[1], geglu_grad, down_grad,
     )

time: 155 us -> 144 us (0.929)
  waiting for transfers between devices: 44.2 us -> 27.4 us
  Pallas kernels: 58.9 us -> 63 us
    ppermute x19 -> x21, waiting for transfers between devices: 42 us -> 26.9 us  [along_narrow(): return lax.ppermute(x, 'narrow', [(i, i ^ k) for i in range(NARROW)])]
    pallas_call x20 -> x21, Pallas kernels: 58.9 us -> 63 us  [call(): pl.pallas_call(body, name=name, out_shape=tuple((jax.ShapeDtypeStruct(o.s...]
    ppermute x9 -> x10, waiting for transfers between devices: 2.2 us -> 0.03 us  [along_wide(): lax.ppermute(x, 'wide', [(i, i ^ k) for i in range(lax.axis_size('wide'))])]
    ppermute x19 -> x21, starting transfers between devices: 30.1 us -> 31.9 us  [along_narrow(): return lax.ppermute(x, 'narrow', [(i, i ^ k) for i in range(NARROW)])]
    unnamed x72 -> x82, local copies, waits for them, and re-layouts: 3.29 us -> 4.18 us
    ppermute x9 -> x10, starting transfers between devices: 8.53 us -> 7.74 us  [along_wide(): lax.ppermute(x, 'wide', [(i, i ^ k) for i in range(lax.axis_size('wide'))])]
  transfers between devices with their start and end apart: 29 -> 32, of which waited for: 7 -> 8; matrix products, arithmetic and copies ran while one was open for 2% -> 1% of each run, Pallas kernels for 32% -> 39%
where the time goes in v3:
time: 144 us; the launch traced here: 143 us
  Pallas kernels  63 us (44%)
  starting transfers between devices  43.8 us (30%)
  waiting for transfers between devices  27.4 us (19%)
  local copies, waits for them, and re-layouts  4.8 us (3%)
  other arithmetic  3.22 us (2%)
    pallas_call x21, Pallas kernels, call(): pl.pallas_call(body, name=name, out_shape=tuple((jax.ShapeDtypeStruct(o.s...  63 us
    ppermute x21, starting transfers between devices, along_narrow(): return lax.ppermute(x, 'narrow', [(i, i ^ k) for i in range(NARROW)])  31.9 us
    ppermute x21, waiting for transfers between devices, along_narrow(): return lax.ppermute(x, 'narrow', [(i, i ^ k) for i in range(NARROW)])  26.9 us
    ppermute x10, starting transfers between devices, along_wide(): lax.ppermute(x, 'wide', [(i, i ^ k) for i in range(lax.axis_size('wide'))])  7.74 us
    all_to_all x1, starting transfers between devices, per_device(): lax.all_to_all(qkv_part, 'wide', 0, 0)  4.25 us
    unnamed x82, local copies, waits for them, and re-layouts  4.18 us
  transfers between devices with their start and end apart: 32, of which 8 were waited for; matrix products, arithmetic and copies ran while one was open for 1% of the time, Pallas kernels for 39%

profile of v3, /device:TPU:0, one launch (start us, length us, event | category | flops | bytes accessed | tf_op | source)
XLA Modules:
  0.0 143.5 jit_solution(11243558807303469893)
XLA Ops:
  6.6 5.0 %collective-permute-start.5 = (bf16[96,384]{1,0:T(8,128)(2,1)}, bf16[96,384]{1,0:T(8,128)(2,1)}, u32[]{:S(2)}, u32[]{:S(2)}) collective-permute-start(bf16[96,384]{1,0:T(8,128)(2,1)} %get-tuple-element.94), channel_id=1, source_target_pairs={{0,3},{1,2},{2,1},{3,0},{4,7},{5,6},{6,5},{7,4},{8,11},{9,10},{10,... | collective-permute-start | bytes 221192 | tf_op jit(solution)/shard_map/ppermute | solution.py:557
  12.2 2.4 %collective-permute-start.8 = (bf16[224,384]{1,0:T(8,128)(2,1)}, bf16[224,384]{1,0:T(8,128)(2,1)}, u32[]{:S(2)}, u32[]{:S(2)}) collective-permute-start(bf16[224,384]{1,0:T(8,128)(2,1)} %get-tuple-element.98), channel_id=1, source_target_pairs={{0,2},{1,3},{2,0},{3,1},{4,6},{5,7},{6,4},{7,5},{8,10},{9,11},{10,... | collective-permute-start | bytes 516104 | tf_op jit(solution)/shard_map/ppermute | solution.py:557
  14.6 5.9 %project_kernel.1 = (bf16[1024,256]{1,0:T(8,128)(2,1)S(1)}, bf16[1024,256]{1,0:T(8,128)(2,1)S(1)}, bf16[1024,256]{1,0:T(8,128)(2,1)S(1)}, bf16[1024,768]{1,0:T(8...) custom-call(bf16[1024,768]{1,0:T(8,128)(2,1)S(1)} %copy-done.9, s32[1,1024]{1,0:T(1,128)S(1)} %copy-done.24, ...), custom_call_target="tpu_custom_call" | custom-call | flops 6000000000 | bytes 8756224 | tf_op jit(solution)/shard_map/project_kernel/pallas_call | solution.py:68
  20.6 4.7 %attend_kernel.1 = (bf16[256,384]{1,0:T(8,128)(2,1)S(1)}, bf16[256,384]{1,0:T(8,128)(2,1)S(1)}, bf16[256,384]{1,0:T(8,128)(2,1)S(1)}, bf16[256,384]{1,0:T(8,128)(2,1)S(1)}, f32[1024,128]{1,0:T(8,128)S(1)}) custom-call(s32[14]{0:T(128)S(1)} %pad_add_fusion.s_ref, s32[1,1024]{1,0:T(1,128)S(1)} %copy-done.24, f32[1024,128]{1,0:T(8,128)S(1)} %get-tuple-element.80.segc_ref, ...), custom_call_target="tpu_custom_call" | custom-call | flops 9999999827968 | bytes 3412024 | tf_op jit(solution)/shard_map/attend_kernel/pallas_call | solution.py:68
  26.4 1.6 %collective-permute-start.6 = (bf16[288,384]{1,0:T(8,128)(2,1)S(1)}, bf16[288,384]{1,0:T(8,128)(2,1)S(1)}, u32[]{:S(2)}, u32[]{:S(2)}) collective-permute-start(bf16[288,384]{1,0:T(8,128)(2,1)S(1)} %arrived_kernel.1.a0), channel_id=1, source_target_pairs={{0,8},{4,12},{8,0},{12,4},{16,24},{20,28},{24,16},{28,20},{1,9},{5... | collective-permute-start | bytes 663560 | tf_op jit(solution)/shard_map/ppermute | solution.py:561
  29.5 2.0 %collective-permute-start = (bf16[256,384]{1,0:T(8,128)(2,1)S(1)}, bf16[256,384]{1,0:T(8,128)(2,1)S(1)}, u32[]{:S(2)}, u32[]{:S(2)}) collective-permute-start(bf16[256,384]{1,0:T(8,128)(2,1)S(1)} %get-tuple-element.85), channel_id=1, source_target_pairs={{0,1},{1,0},{2,3},{3,2},{4,5},{5,4},{6,7},{7,6},{8,9},{9,8},{10,11... | collective-permute-start | bytes 589832 | tf_op jit(solution)/shard_map/ppermute | solution.py:557
  31.6 2.3 %collective-permute-start.2 = (bf16[256,384]{1,0:T(8,128)(2,1)S(1)}, bf16[256,384]{1,0:T(8,128)(2,1)S(1)}, u32[]{:S(2)}, u32[]{:S(2)}) collective-permute-start(bf16[256,384]{1,0:T(8,128)(2,1)S(1)} %get-tuple-element.87), channel_id=1, source_target_pairs={{0,3},{1,2},{2,1},{3,0},{4,7},{5,6},{6,5},{7,4},{8,11},{9,10},{10,... | collective-permute-start | bytes 589832 | tf_op jit(solution)/shard_map/ppermute | solution.py:557
  35.3 1.8 %pair_kernel.3.f0 = bf16[2,224,384]{2,1,0:T(8,128)(2,1)} custom-call(s32[14]{0:T(128)S(1)} %pad_add_fusion.s_ref, bf16[224,384]{1,0:T(8,128)(2,1)} %collective-permute-done.8.a0, bf16[224,384]{1,0:T(8,128)(2,1)S(1)} %collective-permute-done.9.a1), custom_call_target="tpu_custom_call" | custom-call | flops 1000000000 | bytes 688184 | tf_op jit(solution)/shard_map/pair_kernel/pallas_call | solution.py:68
  38.3 8.4 %collective-permute-done.1.c2 = bf16[256,384]{1,0:T(8,128)(2,1)S(1)} collective-permute-done((bf16[256,384]{1,0:T(8,128)(2,1)S(1)}, bf16[256,384]{1,0:T(8,128)(2,1)S(1)}, u32[]{:S(2)}, u32[]{:S(2)}) %collective-permute-start.1) | collective-permute-done | bytes 196640 | tf_op jit(solution)/shard_map/ppermute | solution.py:557
  48.7 4.8 %middle_kernel.1 = (f32[256,768]{1,0:T(8,128)S(1)}, bf16[512,768]{1,0:T(8,128)(2,1)S(1)}, bf16[512,288]{1,0:T(8,128)(2,1)S(1)}, bf16[512,576]{1,0:T(8,128)(2,1)S...) custom-call(s32[14]{0:T(128)S(1)} %pad_add_fusion.s_ref, ...), custom_call_target="tpu_custom_call" | custom-call | flops 9999999827968 | bytes 12831800 | tf_op jit(solution)/shard_map/middle_kernel/pallas_call | solution.py:68
  53.5 3.7 %partner_kernel.1 = (bf16[256,288]{1,0:T(8,128)(2,1)S(1)}, bf16[256,576]{1,0:T(8,128)(2,1)S(1)}, bf16[256,768]{1,0:T(8,128)(2,1)}, bf16[256,768]{1,0:T(8,128)(2,1)S(1)}, bf16[896,768]{1,0:T(8,128)(2,1)S(1)}) custom-call(s32[14]{0:T(128)S(1)} %pad_add_fusion.s_ref, bf16[512,768]{1,0:T(8,128)(2,1)S(1)} %get-tuple-element.95.normed_ref, ...), custom_call_target="tpu_custom_call" | custom-call | flops 3000000000 | bytes 8699960 | tf_op jit(solution)/shard_map/partner_kernel/pallas_call | solution.py:68
  57.2 3.4 %collective-permute-start.13 = (bf16[256,768]{1,0:T(8,128)(2,1)S(1)}, bf16[256,768]{1,0:T(8,128)(2,1)S(1)}, u32[]{:S(2)}, u32[]{:S(2)}) collective-permute-start(bf16[256,768]{1,0:T(8,128)(2,1)S(1)} %get-tuple-element.108), channel_id=1, source_target_pairs={{0,1},{1,0},{2,3},{3,2},{4,5},{5,4},{6,7},{7,6},{8,9},{9,8},{10,11... | collective-permute-start | bytes 1179656 | tf_op jit(solution)/shard_map/ppermute | solution.py:557
  60.6 4.4 %own_kernel.1 = (f32[256,768]{1,0:T(8,128)S(1)}, f32[256,768]{1,0:T(8,128)S(1)}, bf16[768,1792]{1,0:T(8,128)(2,1)S(1)}) custom-call(s32[14]{0:T(128)S(1)} %pad_add_fusion.s_ref, bf16[512,768]{1,0:T(8,128)(2,1)S(1)} %get-tuple-element.95.normed_ref, bf16[512,768]{1,0:T(8,128)(2,1)S(1)} %get-tuple-element.90.cot_ref, ...), custom_call_target="tpu_custom_call" | custom-call | flops 10000000000 | bytes 11747384 | tf_op jit(solution)/shard_map/own_kernel/pallas_call | solution.py:68
  65.1 4.9 %collective-permute-done.13.recv_ref = bf16[256,768]{1,0:T(8,128)(2,1)S(1)} collective-permute-done((bf16[256,768]{1,0:T(8,128)(2,1)S(1)}, bf16[256,768]{1,0:T(8,128)(2,1)S(1)}, u32[]{:S(2)}, u32[]{:S(2)}) %collective-permute-start.13) | collective-permute-done | bytes 393248 | tf_op jit(solution)/shard_map/ppermute | solution.py:557
  73.7 1.8 %collective-permute-start.14 = (bf16[128,384]{1,0:T(8,128)(2,1)S(1)}, bf16[128,384]{1,0:T(8,128)(2,1)S(1)}, u32[]{:S(2)}, u32[]{:S(2)}) collective-permute-start(bf16[128,384]{1,0:T(8,128)(2,1)S(1)} %get-tuple-element.111), channel_id=1, source_target_pairs={{0,1},{1,0},{2,3},{3,2},{4,5},{5,4},{6,7},{7,6},{8,9},{9,8},{10,11... | collective-permute-start | bytes 294920 | tf_op jit(solution)/shard_map/ppermute | solution.py:557
  75.6 2.6 %collective-permute-start.18 = (bf16[128,384]{1,0:T(8,128)(2,1)S(1)}, bf16[128,384]{1,0:T(8,128)(2,1)S(1)}, u32[]{:S(2)}, u32[]{:S(2)}) collective-permute-start(bf16[128,384]{1,0:T(8,128)(2,1)S(1)} %get-tuple-element.125), channel_id=1, source_target_pairs={{0,3},{1,2},{2,1},{3,0},{4,7},{5,6},{6,5},{7,4},{8,11},{9,10},{10,... | collective-permute-start | bytes 294920 | tf_op jit(solution)/shard_map/ppermute | solution.py:557
  80.6 2.4 %collective-permute-start.27 = (bf16[96,2560]{1,0:T(8,128)(2,1)}, bf16[96,2560]{1,0:T(8,128)(2,1)}, u32[]{:S(2)}, u32[]{:S(2)}) collective-permute-start(bf16[96,2560]{1,0:T(8,128)(2,1)} %get-tuple-element.118), channel_id=1, source_target_pairs={{0,24},{4,28},{8,16},{12,20},{16,8},{20,12},{24,0},{28,4},{1,25},{... | collective-permute-start | bytes 1474568 | tf_op jit(solution)/shard_map/ppermute | solution.py:561
  83.1 2.7 %collective-permute-done.17.b2 = bf16[128,384]{1,0:T(8,128)(2,1)S(1)} collective-permute-done((bf16[128,384]{1,0:T(8,128)(2,1)S(1)}, bf16[128,384]{1,0:T(8,128)(2,1)S(1)}, u32[]{:S(2)}, u32[]{:S(2)}) %collective-permute-start.17) | collective-permute-done | bytes 98336 | tf_op jit(solution)/shard_map/ppermute | solution.py:557
  85.9 9.4 %backward_far_kernel.1 = (f32[256,768]{1,0:T(8,128)S(1)}, bf16[256,768]{1,0:T(8,128)(2,1)}, bf16[512,576]{1,0:T(8,128)(2,1)S(1)}, bf16[1024,256]{1,0:T(8,128)(2,...) custom-call(s32[14]{0:T(128)S(1)} %copy-done.6, s32[1,1024]{1,0:T(1,128)S(1)} %copy-done.25, ...), custom_call_target="tpu_custom_call" | custom-call | flops 9999999827968 | bytes 11440184 | tf_op jit(solution)/shard_map/backward_far_kernel/pallas_call | solution.py:68
  95.3 2.3 %collective-permute-start.20 = (bf16[256,768]{1,0:T(8,128)(2,1)}, bf16[256,768]{1,0:T(8,128)(2,1)}, u32[]{:S(2)}, u32[]{:S(2)}) collective-permute-start(bf16[256,768]{1,0:T(8,128)(2,1)} %get-tuple-element.139), channel_id=1, source_target_pairs={{0,1},{1,0},{2,3},{3,2},{4,5},{5,4},{6,7},{7,6},{8,9},{9,8},{10,11... | collective-permute-start | bytes 1179656 | tf_op jit(solution)/shard_map/ppermute | solution.py:557
  97.5 4.9 %backward_near_kernel.1 = (f32[256,768]{1,0:T(8,128)S(1)}, bf16[256,768]{1,0:T(8,128)(2,1)}, bf16[512,576]{1,0:T(8,128)(2,1)S(1)}) custom-call(s32[14]{0:T(128)S(1)} %copy-done.6, s32[1,1024]{1,0:T(1,128)S(1)} %copy-done.25, f32[1024,128]{1,0:T(8,128)S(1)} %copy-done.36, bf16[1024,256]{1,0:T(8,128)(2,1)S(1)} %copy-done.30, bf16[1024,256]{1,0:T(8,128)(2,1)S(1)} %copy-done.32, ...), custom_call_target="tpu_custom_call" | custom-call | flops 9999999827968 | bytes 11046968 | tf_op jit(solution)/shard_map/backward_near_kernel/pallas_call | solution.py:68
  102.5 4.0 %qkv_grad_kernel.1 = bf16[8,112,576]{2,1,0:T(8,128)(2,1)} custom-call(s32[14]{0:T(128)S(1)} %copy-done.6, bf16[1024,768]{1,0:T(8,128)(2,1)S(1)} %get-tuple-element.134.normed_ref, bf16[512,576]{1,0:T(8,128)(2,1)S(1)} %get-tuple-element.135.near_ref, bf16[512,576]{1,0:T(8,128)(2,1)S(1)} %get-tuple-element.136.far_ref, bf16[3,192,768]{2,1,0:T(8,128)(2,1)S(1)} %bitcast.9, ...), custom_call_target="tpu_custom_call" | custom-call | flops 1000000000 | bytes 4675640 | tf_op jit(solution)/shard_map/qkv_grad_kernel/pallas_call | solution.py:68
  110.4 4.2 %all-to-all-start = ((bf16[8,112,576]{2,1,0:T(8,128)(2,1)}), bf16[8,112,576]{2,1,0:T(8,128)(2,1)}, u32[]{:S(2)}, u32[]{:S(2)}) async-start(bf16[8,112,576]{2,1,0:T(8,128)(2,1)} %qkv_grad_kernel.1), calls=%async_computation | async-start | bytes 2293760 | tf_op jit(solution)/shard_map/all_to_all | solution.py:745
  114.7 5.7 %collective-permute-done.19.n1 = bf16[256,768]{1,0:T(8,128)(2,1)} collective-permute-done((bf16[256,768]{1,0:T(8,128)(2,1)}, bf16[256,768]{1,0:T(8,128)(2,1)}, u32[]{:S(2)}, u32[]{:S(2)}) %collective-permute-start.19) | collective-permute-done | bytes 393248 | tf_op jit(solution)/shard_map/ppermute | solution.py:557
  120.4 1.8 %add_convert_fusion = bf16[256,768]{1,0:T(8,128)(2,1)} fusion(f32[256,768]{1,0:T(8,128)S(1)} %get-tuple-element.105, bf16[256,768]{1,0:T(8,128)(2,1)} %collective-permute-done.16), kind=kLoop, calls=%fused_computation | loop fusion | flops 589824 | bytes 1572864 | tf_op jit(solution)/shard_map/convert_element_type | solution.py:770
  122.2 2.4 %collect_kernel.1 = (f32[96,1088]{1,0:T(8,128)S(1)}, bf16[96,192]{1,0:T(8,128)(2,1)}, bf16[96,1088]{1,0:T(8,128)(2,1)}, bf16[96,192]{1,0:T(8,128)(2,1)}) custom-call(f32[96,2560]{1,0:T(8,128)S(1)} %get-tuple-element.143.own_ref, bf16[96,2560]{1,0:T(8,128)(2,1)} %collective-permute-done.25.r1, bf16[96,2560]{1,0:T(8,128)(2,1)} %collective-permute-done.26.r2, ...), custom_call_target="tpu_custom_call" | custom-call | flops 1000000000 | bytes 3158016 | tf_op jit(solution)/shard_map/collect_kernel/pallas_call | solution.py:68
  124.7 2.5 %collective-permute-start.30 = (bf16[96,192]{1,0:T(8,128)(2,1)}, bf16[96,192]{1,0:T(8,128)(2,1)}, u32[]{:S(2)}, u32[]{:S(2)}) collective-permute-start(bf16[96,192]{1,0:T(8,128)(2,1)} %get-tuple-element.148), channel_id=1, source_target_pairs={{0,3},{1,2},{2,1},{3,0},{4,7},{5,6},{6,5},{7,4},{8,11},{9,10},{10,... | collective-permute-start | bytes 110600 | tf_op jit(solution)/shard_map/ppermute | solution.py:557
  128.2 2.5 %final_kernel.1 = f32[256,768]{1,0:T(8,128)} custom-call(s32[14]{0:T(128)S(1)} %copy-done.7, bf16[1024,768]{1,0:T(8,128)(2,1)S(1)} %copy-done.11, f32[1,768]{1,0:T(1,128)S(1)} %copy-done.4, f32[256,768]{1,0:T(8,128)S(1)} %copy-done.38, f32[256,768]{1,0:T(8,128)S(1)} %get-tuple-element.130.n0, bf16[256,768]{1,0:T(8,128)(2,1)} %collective-permute-done.19.n1, ...), custom_call_target="tpu_custom_call" | custom-call | flops 9999999827968 | bytes 4721720 | tf_op jit(solution)/shard_map/final_kernel/pallas_call | solution.py:68
  131.1 2.2 %qkv_sum_kernel.1 = (f32[3,96,192]{2,1,0:T(8,128)}, f32[2,768]{1,0:T(2,128)S(1)}) custom-call(bf16[8,112,576]{2,1,0:T(8,128)(2,1)} %all-to-all-done.parts_ref), custom_call_target="tpu_custom_call" | custom-call | flops 1000000000 | bytes 1259520 | tf_op jit(solution)/shard_map/qkv_sum_kernel/pallas_call | solution.py:68
  133.3 3.0 %collective-permute-start.24 = (f32[2,768]{1,0:T(2,128)S(1)}, f32[2,768]{1,0:T(2,128)S(1)}, u32[]{:S(2)}, u32[]{:S(2)}) collective-permute-start(f32[2,768]{1,0:T(2,128)S(1)} %get-tuple-element.140), channel_id=1, source_target_pairs={{0,3},{1,2},{2,1},{3,0},{4,7},{5,6},{6,5},{7,4},{8,11},{9,10},{10,... | collective-permute-start | bytes 18440 | tf_op jit(solution)/shard_map/ppermute | solution.py:557
  137.7 3.2 %collective-permute-done.29.r2 = bf16[96,1088]{1,0:T(8,128)(2,1)} collective-permute-done((bf16[96,1088]{1,0:T(8,128)(2,1)}, bf16[96,1088]{1,0:T(8,128)(2,1)}, u32[]{:S(2)}, u32[]{:S(2)}) %collective-permute-start.29) | collective-permute-done | bytes 208928 | tf_op jit(solution)/shard_map/ppermute | solution.py:557
  140.9 1.9 %finish_kernel.1 = (f32[2,96,288]{2,1,0:T(8,128)}, f32[288,96]{1,0:T(8,128)}, f32[192,96]{1,0:T(8,128)}) custom-call(f32[96,1088]{1,0:T(8,128)S(1)} %get-tuple-element.145.keep_ref, bf16[96,192]{1,0:T(8,128)(2,1)} %collective-permute-done.28.r1, bf16[96,1088]{1,0:T(8,128)(2,1)} %collective-permute-done.29.r2, bf16[96,192]{1,0:T(8,128)(2,1)} %collective-permute-done.30.r3), custom_call_target="tpu_custom_call" | custom-call | flops 1000000000 | bytes 1105920 | tf_op jit(solution)/shard_map/finish_kernel/pallas_call | solution.py:68
  (143 shorter events, 27.1 us)
Async XLA Ops:
  6.6 18.8 %collective-permute-start.5 = (bf16[96,384]{1,0:T(8,128)(2,1)}, bf16[96,384]{1,0:T(8,128)(2,1)}, u32[]{:S(2)}, u32[]{:S(2)}) collective-permute-start(bf16[96,384]{1,0:T(8,128)(2,1)} %get-tuple-element.94), channel_id=1, source_target_pairs={{0,3},{1,2},{2,1},{3,0},{4,7},{5,6},{6,5},{7,4},{8,11},{9,10},{10,... | collective-permute-start | bytes 221192 | tf_op jit(solution)/shard_map/ppermute | solution.py:557
  11.6 13.8 %collective-permute-start.4 = (bf16[96,384]{1,0:T(8,128)(2,1)}, bf16[96,384]{1,0:T(8,128)(2,1)}, u32[]{:S(2)}, u32[]{:S(2)}) collective-permute-start(bf16[96,384]{1,0:T(8,128)(2,1)} %get-tuple-element.94), channel_id=1, source_target_pairs={{0,2},{1,3},{2,0},{3,1},{4,6},{5,7},{6,4},{7,5},{8,10},{9,11},{10,... | collective-permute-start | bytes 221192 | tf_op jit(solution)/shard_map/ppermute | solution.py:557
  11.6 13.8 %collective-permute-start.3 = (bf16[96,384]{1,0:T(8,128)(2,1)}, bf16[96,384]{1,0:T(8,128)(2,1)}, u32[]{:S(2)}, u32[]{:S(2)}) collective-permute-start(bf16[96,384]{1,0:T(8,128)(2,1)} %get-tuple-element.94), channel_id=1, source_target_pairs={{0,1},{1,0},{2,3},{3,2},{4,5},{5,4},{6,7},{7,6},{8,9},{9,8},{10,11... | collective-permute-start | bytes 221192 | tf_op jit(solution)/shard_map/ppermute | solution.py:557
  12.2 15.8 %collective-permute-start.8 = (bf16[224,384]{1,0:T(8,128)(2,1)}, bf16[224,384]{1,0:T(8,128)(2,1)}, u32[]{:S(2)}, u32[]{:S(2)}) collective-permute-start(bf16[224,384]{1,0:T(8,128)(2,1)} %get-tuple-element.98), channel_id=1, source_target_pairs={{0,2},{1,3},{2,0},{3,1},{4,6},{5,7},{6,4},{7,5},{8,10},{9,11},{10,... | collective-permute-start | bytes 516104 | tf_op jit(solution)/shard_map/ppermute | solution.py:557
  26.4 7.5 %collective-permute-start.6 = (bf16[288,384]{1,0:T(8,128)(2,1)S(1)}, bf16[288,384]{1,0:T(8,128)(2,1)S(1)}, u32[]{:S(2)}, u32[]{:S(2)}) collective-permute-start(bf16[288,384]{1,0:T(8,128)(2,1)S(1)} %arrived_kernel.1.a0), channel_id=1, source_target_pairs={{0,8},{4,12},{8,0},{12,4},{16,24},{20,28},{24,16},{28,20},{1,9},{5... | collective-permute-start | bytes 663560 | tf_op jit(solution)/shard_map/ppermute | solution.py:561
  28.0 7.3 %collective-permute-start.9 = (bf16[224,384]{1,0:T(8,128)(2,1)}, bf16[224,384]{1,0:T(8,128)(2,1)S(1)}, u32[]{:S(2)}, u32[]{:S(2)}) collective-permute-start(bf16[224,384]{1,0:T(8,128)(2,1)} %collective-permute-done.8.a0), channel_id=1, source_target_pairs={{0,16},{4,20},{8,24},{12,28},{16,0},{20,4},{24,8},{28,12},{1,17},{... | collective-permute-start | bytes 516104 | tf_op jit(solution)/shard_map/ppermute | solution.py:561
  29.5 8.8 %collective-permute-start = (bf16[256,384]{1,0:T(8,128)(2,1)S(1)}, bf16[256,384]{1,0:T(8,128)(2,1)S(1)}, u32[]{:S(2)}, u32[]{:S(2)}) collective-permute-start(bf16[256,384]{1,0:T(8,128)(2,1)S(1)} %get-tuple-element.85), channel_id=1, source_target_pairs={{0,1},{1,0},{2,3},{3,2},{4,5},{5,4},{6,7},{7,6},{8,9},{9,8},{10,11... | collective-permute-start | bytes 589832 | tf_op jit(solution)/shard_map/ppermute | solution.py:557
  31.5 15.2 %collective-permute-start.1 = (bf16[256,384]{1,0:T(8,128)(2,1)S(1)}, bf16[256,384]{1,0:T(8,128)(2,1)S(1)}, u32[]{:S(2)}, u32[]{:S(2)}) collective-permute-start(bf16[256,384]{1,0:T(8,128)(2,1)S(1)} %get-tuple-element.86), channel_id=1, source_target_pairs={{0,2},{1,3},{2,0},{3,1},{4,6},{5,7},{6,4},{7,5},{8,10},{9,11},{10,... | collective-permute-start | bytes 589832 | tf_op jit(solution)/shard_map/ppermute | solution.py:557
  31.6 15.2 %collective-permute-start.2 = (bf16[256,384]{1,0:T(8,128)(2,1)S(1)}, bf16[256,384]{1,0:T(8,128)(2,1)S(1)}, u32[]{:S(2)}, u32[]{:S(2)}) collective-permute-start(bf16[256,384]{1,0:T(8,128)(2,1)S(1)} %get-tuple-element.87), channel_id=1, source_target_pairs={{0,3},{1,2},{2,1},{3,0},{4,7},{5,6},{6,5},{7,4},{8,11},{9,10},{10,... | collective-permute-start | bytes 589832 | tf_op jit(solution)/shard_map/ppermute | solution.py:557
  35.3 13.5 %collective-permute-start.7 = (bf16[2,288,384]{2,1,0:T(8,128)(2,1)}, bf16[2,288,384]{2,1,0:T(8,128)(2,1)}, u32[]{:S(2)}, u32[]{:S(2)}) collective-permute-start(bf16[2,288,384]{2,1,0:T(8,128)(2,1)} %pair_kernel.2.here_ref), channel_id=1, source_target_pairs={{0,4},{4,0},{8,12},{12,8},{16,20},{20,16},{24,28},{28,24},{1,5},{5... | collective-permute-start | bytes 1327112 | tf_op jit(solution)/shard_map/ppermute | solution.py:561
  37.1 11.1 %collective-permute-start.10 = (bf16[2,224,384]{2,1,0:T(8,128)(2,1)}, bf16[2,224,384]{2,1,0:T(8,128)(2,1)}, u32[]{:S(2)}, u32[]{:S(2)}) collective-permute-start(bf16[2,224,384]{2,1,0:T(8,128)(2,1)} %pair_kernel.3.f0), channel_id=1, source_target_pairs={{0,8},{4,12},{8,0},{12,4},{16,24},{20,28},{24,16},{28,20},{1,9},{5... | collective-permute-start | bytes 1032200 | tf_op jit(solution)/shard_map/ppermute | solution.py:561
  48.1 5.4 %collective-permute-start.11 = (bf16[2,224,384]{2,1,0:T(8,128)(2,1)}, bf16[2,224,384]{2,1,0:T(8,128)(2,1)}, u32[]{:S(2)}, u32[]{:S(2)}) collective-permute-start(bf16[2,224,384]{2,1,0:T(8,128)(2,1)} %pair_kernel.3.f0), channel_id=1, source_target_pairs={{0,4},{4,0},{8,12},{12,8},{16,20},{20,16},{24,28},{28,24},{1,5},{5... | collective-permute-start | bytes 1032200 | tf_op jit(solution)/shard_map/ppermute | solution.py:561
  48.2 5.3 %collective-permute-start.12 = (bf16[2,224,384]{2,1,0:T(8,128)(2,1)}, bf16[2,224,384]{2,1,0:T(8,128)(2,1)}, u32[]{:S(2)}, u32[]{:S(2)}) collective-permute-start(bf16[2,224,384]{2,1,0:T(8,128)(2,1)} %collective-permute-done.10.f1), channel_id=1, source_target_pairs={{0,4},{4,0},{8,12},{12,8},{16,20},{20,16},{24,28},{28,24},{1,5},{5... | collective-permute-start | bytes 1032200 | tf_op jit(solution)/shard_map/ppermute | solution.py:561
  57.2 12.7 %collective-permute-start.13 = (bf16[256,768]{1,0:T(8,128)(2,1)S(1)}, bf16[256,768]{1,0:T(8,128)(2,1)S(1)}, u32[]{:S(2)}, u32[]{:S(2)}) collective-permute-start(bf16[256,768]{1,0:T(8,128)(2,1)S(1)} %get-tuple-element.108), channel_id=1, source_target_pairs={{0,1},{1,0},{2,3},{3,2},{4,5},{5,4},{6,7},{7,6},{8,9},{9,8},{10,11... | collective-permute-start | bytes 1179656 | tf_op jit(solution)/shard_map/ppermute | solution.py:557
  73.7 4.5 %collective-permute-start.15 = (bf16[4,96,2560]{2,1,0:T(8,128)(2,1)S(1)}, bf16[4,96,2560]{2,1,0:T(8,128)(2,1)S(1)}, u32[]{:S(2)}, u32[]{:S(2)}) collective-permute-start(bf16[4,96,2560]{2,1,0:T(8,128)(2,1)S(1)} %get-tuple-element.115), channel_id=1, source_target_pairs={{0,4},{4,0},{8,12},{12,8},{16,20},{20,16},{24,28},{28,24},{1,5},{5... | collective-permute-start | bytes 5898248 | tf_op jit(solution)/shard_map/ppermute | solution.py:561
  73.7 6.9 %collective-permute-start.14 = (bf16[128,384]{1,0:T(8,128)(2,1)S(1)}, bf16[128,384]{1,0:T(8,128)(2,1)S(1)}, u32[]{:S(2)}, u32[]{:S(2)}) collective-permute-start(bf16[128,384]{1,0:T(8,128)(2,1)S(1)} %get-tuple-element.111), channel_id=1, source_target_pairs={{0,1},{1,0},{2,3},{3,2},{4,5},{5,4},{6,7},{7,6},{8,9},{9,8},{10,11... | collective-permute-start | bytes 294920 | tf_op jit(solution)/shard_map/ppermute | solution.py:557
  75.5 10.3 %collective-permute-start.17 = (bf16[128,384]{1,0:T(8,128)(2,1)S(1)}, bf16[128,384]{1,0:T(8,128)(2,1)S(1)}, u32[]{:S(2)}, u32[]{:S(2)}) collective-permute-start(bf16[128,384]{1,0:T(8,128)(2,1)S(1)} %get-tuple-element.124), channel_id=1, source_target_pairs={{0,2},{1,3},{2,0},{3,1},{4,6},{5,7},{6,4},{7,5},{8,10},{9,11},{10,... | collective-permute-start | bytes 294920 | tf_op jit(solution)/shard_map/ppermute | solution.py:557
  75.6 10.3 %collective-permute-start.18 = (bf16[128,384]{1,0:T(8,128)(2,1)S(1)}, bf16[128,384]{1,0:T(8,128)(2,1)S(1)}, u32[]{:S(2)}, u32[]{:S(2)}) collective-permute-start(bf16[128,384]{1,0:T(8,128)(2,1)S(1)} %get-tuple-element.125), channel_id=1, source_target_pairs={{0,3},{1,2},{2,1},{3,0},{4,7},{5,6},{6,5},{7,4},{8,11},{9,10},{10,... | collective-permute-start | bytes 294920 | tf_op jit(solution)/shard_map/ppermute | solution.py:557
  79.6 42.6 %collective-permute-start.25 = (bf16[96,2560]{1,0:T(8,128)(2,1)}, bf16[96,2560]{1,0:T(8,128)(2,1)}, u32[]{:S(2)}, u32[]{:S(2)}) collective-permute-start(bf16[96,2560]{1,0:T(8,128)(2,1)} %get-tuple-element.116), channel_id=1, source_target_pairs={{0,8},{4,12},{8,0},{12,4},{16,24},{20,28},{24,16},{28,20},{1,9},{5... | collective-permute-start | bytes 1474568 | tf_op jit(solution)/shard_map/ppermute | solution.py:561
  80.1 42.1 %collective-permute-start.26 = (bf16[96,2560]{1,0:T(8,128)(2,1)}, bf16[96,2560]{1,0:T(8,128)(2,1)}, u32[]{:S(2)}, u32[]{:S(2)}) collective-permute-start(bf16[96,2560]{1,0:T(8,128)(2,1)} %get-tuple-element.117), channel_id=1, source_target_pairs={{0,16},{4,20},{8,24},{12,28},{16,0},{20,4},{24,8},{28,12},{1,17},{... | collective-permute-start | bytes 1474568 | tf_op jit(solution)/shard_map/ppermute | solution.py:561
  80.6 41.6 %collective-permute-start.27 = (bf16[96,2560]{1,0:T(8,128)(2,1)}, bf16[96,2560]{1,0:T(8,128)(2,1)}, u32[]{:S(2)}, u32[]{:S(2)}) collective-permute-start(bf16[96,2560]{1,0:T(8,128)(2,1)} %get-tuple-element.118), channel_id=1, source_target_pairs={{0,24},{4,28},{8,16},{12,20},{16,8},{20,12},{24,0},{28,4},{1,25},{... | collective-permute-start | bytes 1474568 | tf_op jit(solution)/shard_map/ppermute | solution.py:561
  85.8 16.6 %collective-permute-start.16 = (bf16[256,768]{1,0:T(8,128)(2,1)}, bf16[256,768]{1,0:T(8,128)(2,1)}, u32[]{:S(2)}, u32[]{:S(2)}) collective-permute-start(bf16[256,768]{1,0:T(8,128)(2,1)} %get-tuple-element.119), channel_id=1, source_target_pairs={{0,1},{1,0},{2,3},{3,2},{4,5},{5,4},{6,7},{7,6},{8,9},{9,8},{10,11... | collective-permute-start | bytes 1179656 | tf_op jit(solution)/shard_map/ppermute | solution.py:557
  95.3 12.5 %collective-permute-start.20 = (bf16[256,768]{1,0:T(8,128)(2,1)}, bf16[256,768]{1,0:T(8,128)(2,1)}, u32[]{:S(2)}, u32[]{:S(2)}) collective-permute-start(bf16[256,768]{1,0:T(8,128)(2,1)} %get-tuple-element.139), channel_id=1, source_target_pairs={{0,1},{1,0},{2,3},{3,2},{4,5},{5,4},{6,7},{7,6},{8,9},{9,8},{10,11... | collective-permute-start | bytes 1179656 | tf_op jit(solution)/shard_map/ppermute | solution.py:557
  102.5 17.9 %collective-permute-start.19 = (bf16[256,768]{1,0:T(8,128)(2,1)}, bf16[256,768]{1,0:T(8,128)(2,1)}, u32[]{:S(2)}, u32[]{:S(2)}) collective-permute-start(bf16[256,768]{1,0:T(8,128)(2,1)} %get-tuple-element.131), channel_id=1, source_target_pairs={{0,1},{1,0},{2,3},{3,2},{4,5},{5,4},{6,7},{7,6},{8,9},{9,8},{10,11... | collective-permute-start | bytes 1179656 | tf_op jit(solution)/shard_map/ppermute | solution.py:557
  108.9 19.3 %collective-permute-start.21 = (bf16[256,768]{1,0:T(8,128)(2,1)S(1)}, bf16[256,768]{1,0:T(8,128)(2,1)S(1)}, u32[]{:S(2)}, u32[]{:S(2)}) collective-permute-start(bf16[256,768]{1,0:T(8,128)(2,1)S(1)} %add_kernel.1), channel_id=1, source_target_pairs={{0,2},{1,3},{2,0},{3,1},{4,6},{5,7},{6,4},{7,5},{8,10},{9,11},{10,... | collective-permute-start | bytes 1179656 | tf_op jit(solution)/shard_map/ppermute | solution.py:557
  110.4 20.7 %all-to-all-start = ((bf16[8,112,576]{2,1,0:T(8,128)(2,1)}), bf16[8,112,576]{2,1,0:T(8,128)(2,1)}, u32[]{:S(2)}, u32[]{:S(2)}) async-start(bf16[8,112,576]{2,1,0:T(8,128)(2,1)} %qkv_grad_kernel.1), calls=%async_computation | async-start | bytes 2293760 | tf_op jit(solution)/shard_map/all_to_all | solution.py:745
  124.7 11.6 %collective-permute-start.28 = (bf16[96,192]{1,0:T(8,128)(2,1)}, bf16[96,192]{1,0:T(8,128)(2,1)}, u32[]{:S(2)}, u32[]{:S(2)}) collective-permute-start(bf16[96,192]{1,0:T(8,128)(2,1)} %get-tuple-element.146), channel_id=1, source_target_pairs={{0,1},{1,0},{2,3},{3,2},{4,5},{5,4},{6,7},{7,6},{8,9},{9,8},{10,11... | collective-permute-start | bytes 110600 | tf_op jit(solution)/shard_map/ppermute | solution.py:557
  124.7 13.0 %collective-permute-start.30 = (bf16[96,192]{1,0:T(8,128)(2,1)}, bf16[96,192]{1,0:T(8,128)(2,1)}, u32[]{:S(2)}, u32[]{:S(2)}) collective-permute-start(bf16[96,192]{1,0:T(8,128)(2,1)} %get-tuple-element.148), channel_id=1, source_target_pairs={{0,3},{1,2},{2,1},{3,0},{4,7},{5,6},{6,5},{7,4},{8,11},{9,10},{10,... | collective-permute-start | bytes 110600 | tf_op jit(solution)/shard_map/ppermute | solution.py:557
  127.2 13.7 %collective-permute-start.29 = (bf16[96,1088]{1,0:T(8,128)(2,1)}, bf16[96,1088]{1,0:T(8,128)(2,1)}, u32[]{:S(2)}, u32[]{:S(2)}) collective-permute-start(bf16[96,1088]{1,0:T(8,128)(2,1)} %get-tuple-element.147), channel_id=1, source_target_pairs={{0,2},{1,3},{2,0},{3,1},{4,6},{5,7},{6,4},{7,5},{8,10},{9,11},{10,... | collective-permute-start | bytes 626696 | tf_op jit(solution)/shard_map/ppermute | solution.py:557
  133.3 9.5 %collective-permute-start.24 = (f32[2,768]{1,0:T(2,128)S(1)}, f32[2,768]{1,0:T(2,128)S(1)}, u32[]{:S(2)}, u32[]{:S(2)}) collective-permute-start(f32[2,768]{1,0:T(2,128)S(1)} %get-tuple-element.140), channel_id=1, source_target_pairs={{0,3},{1,2},{2,1},{3,0},{4,7},{5,6},{6,5},{7,4},{8,11},{9,10},{10,... | collective-permute-start | bytes 18440 | tf_op jit(solution)/shard_map/ppermute | solution.py:557
  136.3 6.6 %collective-permute-start.23 = (f32[2,768]{1,0:T(2,128)S(1)}, f32[2,768]{1,0:T(2,128)S(1)}, u32[]{:S(2)}, u32[]{:S(2)}) collective-permute-start(f32[2,768]{1,0:T(2,128)S(1)} %get-tuple-element.140), channel_id=1, source_target_pairs={{0,2},{1,3},{2,0},{3,1},{4,6},{5,7},{6,4},{7,5},{8,10},{9,11},{10,... | collective-permute-start | bytes 18440 | tf_op jit(solution)/shard_map/ppermute | solution.py:557
  136.3 6.6 %collective-permute-start.22 = (f32[2,768]{1,0:T(2,128)S(1)}, f32[2,768]{1,0:T(2,128)S(1)}, u32[]{:S(2)}, u32[]{:S(2)}) collective-permute-start(f32[2,768]{1,0:T(2,128)S(1)} %get-tuple-element.140), channel_id=1, source_target_pairs={{0,1},{1,0},{2,3},{3,2},{4,5},{5,4},{6,7},{7,6},{8,9},{9,8},{10,11... | collective-permute-start | bytes 18440 | tf_op jit(solution)/shard_map/ppermute | solution.py:557
  (41 other events, 360.6 us)

commit v4 on v3

--- a/solution.py
+++ b/solution.py
@@ -22,6 +22,7 @@
 ROPE_BASE = 160000.0
 NARROW = 4
 BLOCK = LEN // NARROW
+ORDER = (0, 2, 4, 6, 1, 3, 5, 7)
 F32 = jnp.float32
 GAIN_ROWS = 16
 BF16 = jnp.bfloat16
@@ -33,21 +34,21 @@
     "pack_kernel": 1,
     "arrived_kernel": 1,
     "pair_kernel": 1,
-    "begin_kernel": 10000,
+    "begin_kernel": 100,
     "project_kernel": 6,
-    "attend_kernel": 10000,
-    "middle_kernel": 10000,
+    "attend_kernel": 100,
+    "middle_kernel": 5,
     "partner_kernel": 3,
     "own_kernel": 10,
-    "residual_kernel": 10000,
+    "residual_kernel": 100,
     "output_grad_kernel": 2,
     "fold_kernel": 2,
-    "backward_far_kernel": 10000,
-    "backward_near_kernel": 10000,
-    "add_kernel": 10000,
+    "backward_far_kernel": 100,
+    "backward_near_kernel": 100,
+    "add_kernel": 100,
     "qkv_grad_kernel": 1,
     "collect_kernel": 1,
-    "final_kernel": 10000,
+    "final_kernel": 100,
 }
 
 NN = (((1,), (0,)), ((), ()))
@@ -86,13 +87,13 @@
     frequency = ROPE_BASE ** (-2.0 * np.arange(HEAD // 2, dtype=np.float64) / HEAD)
     angle = position[:, None] * frequency[None, :]
     cosine, sine = np.cos(angle), np.sin(angle)
-    table = np.zeros((DOC, 2 * LANES), np.float32)
-    for h in range(HEADS_HERE):
+    table = np.zeros((DOC, 2 * 128), np.float32)
+    for h in range(2):
         base = h * HEAD
         table[:, base : base + 32] = cosine
         table[:, base + 32 : base + 64] = cosine
-        table[:, LANES + base : LANES + base + 32] = -sine
-        table[:, LANES + base + 32 : LANES + base + 64] = sine
+        table[:, 128 + base : 128 + base + 32] = -sine
+        table[:, 128 + base + 32 : 128 + base + 64] = sine
     high = table.astype(jnp.bfloat16)
     low = (table - high.astype(np.float32)).astype(jnp.bfloat16)
     return np.stack([high, low])
@@ -125,6 +126,15 @@
     )
 
 
+def turn(x, trig, sign):
+    swapped = swap_halves(x)
+    cosine, sine = trig[:, :128], sign * trig[:, 128:]
+    parts = [
+        x[:, i : i + 128] * cosine + swapped[:, i : i + 128] * sine for i in range(0, LANES, 128)
+    ]
+    return jnp.concatenate(parts, axis=1)
+
+
 def by_head(block, head):
     return jnp.concatenate(
         [jnp.where(head == h, block, jnp.zeros_like(block)) for h in range(HEADS_HERE)], axis=0
@@ -134,10 +144,6 @@
 def merge_heads(stacked, head):
     parts = jnp.split(stacked, HEADS_HERE, axis=0)
     return jnp.where(head == 0, parts[0], jnp.where(head == 1, parts[1], parts[2]))
-
-
-def own_window(i):
-    return jnp.clip(i - DOC // QB, 0, (LEN - WINDOW) // QB) * QB
 
 
 def static_window(i):
@@ -167,20 +173,17 @@
     ).astype(BF16)
     trig_ref[...] = dot(hot, table_ref[0]) + dot(hot, table_ref[1])
 
-    def norm_rows(i, carry):
-        rows = pl.ds(pl.multiple_of(i * 128, 128), 128)
+    step = LEN // 4
+    proj_ref[:, COLS:] = jnp.zeros((step, LANES - COLS), F32)
+    for i in range(4):
+        rows = slice(i * step, (i + 1) * step)
         unit, _ = normalize(tok_ref[rows, :].astype(F32))
-        normed_ref[rows, :] = (unit * gain_ref[...]).astype(BF16)
-        return carry
-
-    lax.fori_loop(0, LEN // 128, norm_rows, 0)
-    proj_ref[:, COLS:] = jnp.zeros((LEN, LANES - COLS), F32)
-    for s, out in enumerate((q_ref, k_ref)):
-        proj_ref[:, :COLS] = dot(normed_ref[...], w_ref[s], NT)
-        x = proj_ref[...]
-        out[...] = (x * trig_ref[:, :LANES] + swap_halves(x) * trig_ref[:, LANES:]).astype(BF16)
-    proj_ref[:, :COLS] = dot(normed_ref[...], w_ref[2], NT)
-    v_ref[...] = proj_ref[...].astype(BF16)
+        normed = (unit * gain_ref[...]).astype(BF16)
+        normed_ref[rows, :] = normed
+        for s, out in enumerate((q_ref, k_ref, v_ref)):
+            proj_ref[:, :COLS] = dot(normed, w_ref[s], NT)
+            x = proj_ref[...]
+            out[rows, :] = (turn(x, trig_ref[rows, :], 1.0) if s < 2 else x).astype(BF16)
 
 
 def attend_kernel(
@@ -217,7 +220,7 @@
     rows, cols = refs[0].shape[1:]
     for group, ref in enumerate(refs):
         for i in range(2):
-            slot = s_ref[2 + 4 * (group // 2) + 2 * i + group % 2]
+            slot = s_ref[1] ^ ORDER[4 * (group // 2) + 2 * i + group % 2]
             there = pl.ds(pl.multiple_of((slot // 2) * rows, 16), rows)
             out_ref[there, pl.ds(pl.multiple_of((slot % 2) * cols, 128), cols)] = ref[i]
 
@@ -256,9 +259,9 @@
 ):
     wo_ref[0] = w_ref[...]
     few = COLS // 4
-    pieces = ((0, here_ref, 0), (1, here_ref, 1), (2, there_ref, 0), (3, there_ref, 1))
+    pieces = ((0, here_ref, 0), (2, here_ref, 1), (1, there_ref, 0), (3, there_ref, 1))
     for slot, ref, i in pieces:
-        there = pl.ds(pl.multiple_of(s_ref[10 + slot] * few, 16), few)
+        there = pl.ds(pl.multiple_of((s_ref[1] % 4 ^ slot) * few, 16), few)
         for k in range(3):
             for side in range(2):
                 first = (2 * k + side) * few
@@ -268,15 +271,11 @@
     for k in range(3):
         residual += dot(context_ref[k], wo_ref[k + 1])
     res_ref[...] = residual[:BLOCK]
-    branch_ref[:BLOCK, :] = residual[:BLOCK]
-    branch_ref[BLOCK:, :] = jnp.zeros((BLOCK, D), F32)
     unit, _ = normalize(residual)
     normed_ref[...] = (unit * gain_ref[...]).astype(BF16)
-    branch, back = gated(
-        normed_ref[...], act_back_ref[...], gw_ref[...], dw_ref[...], act_ref, gb_ref, dw_ref.shape[0]
-    )
-    branch_ref[...] += branch
-    back_ref[...] = back
+    branch_ref[...], back_ref[...] = gated(
+        normed_ref[BLOCK:, :], act_back_ref[BLOCK:, :], gw_ref[...], dw_ref[...], act_ref, gb_ref, dw_ref.shape[0]
+    )
 
 
 def partner_kernel(
@@ -289,32 +288,32 @@
         normed_ref[BLOCK:, :], dot(cot_ref[BLOCK:, :], other_ref[2 * width : 3 * width, :], NT), other_ref[: 2 * width, :],
         other_ref[2 * width : 3 * width, :], act_ref, gb_ref, width,
     )
-    branch_ref[...] = (branch_in[BLOCK:, :] + branch).astype(BF16)
-    back_ref[...] = (back_in[BLOCK:, :] + back).astype(BF16)
+    branch_ref[...] = (branch_in[...] + branch).astype(BF16)
+    back_ref[...] = (back_in[...] + back).astype(BF16)
 
 
 def own_kernel(
-    s_ref, normed_ref, cot_ref, branch_in, back_in, other_ref, act_ref, gb_ref, act_par, gb_par,
+    s_ref, normed_ref, cot_ref, act_back_ref, res_ref, gw_ref, dw_ref, other_ref,
+    act_par, gb_par, act_par_two, gb_par_two,
     branch_ref, back_ref, whole_ref,
-    act_own, gb_own,
-):
-    width = act_ref.shape[1]
-    branch, back = gated(
-        normed_ref[:BLOCK, :], dot(cot_ref[:BLOCK, :], other_ref[2 * width : 3 * width, :], NT), other_ref[: 2 * width, :],
-        other_ref[2 * width : 3 * width, :], act_own, gb_own, width,
-    )
-    branch_ref[...] = branch_in[:BLOCK, :] + branch
-    back_ref[...] = back_in[:BLOCK, :] + back
+    act_one, gb_one, act_two, gb_two,
+):
+    width = act_par.shape[1]
+    normed, cot = normed_ref[:BLOCK, :], cot_ref[:BLOCK, :]
+    w_down = other_ref[2 * width : 3 * width, :]
+    branch, back = gated(normed, act_back_ref[:BLOCK, :], gw_ref[...], dw_ref[...], act_one, gb_one, width)
+    more, back_more = gated(normed, dot(cot, w_down, NT), other_ref[: 2 * width, :], w_down, act_two, gb_two, width)
+    branch_ref[...] = res_ref[...] + branch + more
+    back_ref[...] = back + back_more
     half = whole_ref.shape[1] // 2
-    whole_ref[:, : 2 * width] = dot(normed_ref[...], gb_ref[...], TN).astype(BF16)
-    whole_ref[:, 2 * width : 3 * width] = dot(cot_ref[...], act_ref[...], TN).astype(BF16)
-    part = dot(normed_ref[:BLOCK, :], gb_own[...], TN) + dot(normed_ref[BLOCK:, :], gb_par[...], TN)
-    whole_ref[:, half : half + 2 * width] = part.astype(BF16)
-    part = dot(cot_ref[:BLOCK, :], act_own[...], TN) + dot(cot_ref[BLOCK:, :], act_par[...], TN)
-    whole_ref[:, half + 2 * width : half + 3 * width] = part.astype(BF16)
-    pad = jnp.zeros((D, half - 3 * width), BF16)
-    whole_ref[:, 3 * width : half] = pad
-    whole_ref[:, half + 3 * width :] = pad
+    shards = ((act_one, gb_one, act_par, gb_par), (act_two, gb_two, act_par_two, gb_par_two))
+    for shard, (act, gb, act_there, gb_there) in enumerate(shards):
+        at = shard * half
+        part = dot(normed, gb[...], TN) + dot(normed_ref[BLOCK:, :], gb_there[...], TN)
+        whole_ref[:, at : at + 2 * width] = part.astype(BF16)
+        part = dot(cot, act[...], TN) + dot(cot_ref[BLOCK:, :], act_there[...], TN)
+        whole_ref[:, at + 2 * width : at + 3 * width] = part.astype(BF16)
+        whole_ref[:, at + 3 * width : at + half] = jnp.zeros((D, half - 3 * width), BF16)
 
 
 def finish_kernel(keep_ref, r1, r2, r3, geglu_ref, down_ref, out_ref, pad_ref):
@@ -365,7 +364,7 @@
         whole_ref[:, k * COLS : (k + 1) * COLS] = dot(low_ref[...], c[:, :COLS], TN).astype(BF16)
     rows, ff = even_ref.shape[1], ff_ref.shape[1]
     for i in range(8):
-        there = pl.ds(pl.multiple_of(s_ref[2 + i] * rows, 16), rows)
+        there = pl.ds(pl.multiple_of((s_ref[1] ^ ORDER[i]) * rows, 16), rows)
         out = even_ref.at[i] if i < 4 else odd_ref.at[i - 4]
         out[:, :ff] = ff_ref[there, :]
         out[:, ff:] = whole_ref[there, :]
@@ -410,14 +409,17 @@
 
 
 def backward_steps(
-    first, count, seg_ref, segc_ref, q_ref, k_ref, v_ref, lse_ref, back_ref, dq_ref, dk_ref, dv_ref
-):
+    mirror, steps, seg_ref, segc_ref, q_ref, k_ref, v_ref, lse_ref, back_ref, dq_ref, dk_ref, dv_ref
+):
+    last = LEN // QB - 1
     head = lane_head(QB)
     scale = jnp.asarray(1.0 / math.sqrt(HEAD), BF16)
-    for j in range(count):
-        i = first + j
+    for step in steps:
+        low, high = static_window(step)
+        i = jnp.where(mirror == 1, last - step, step)
         rows = pl.ds(pl.multiple_of(i * QB, QB), QB)
-        keys = pl.ds(pl.multiple_of(own_window(i), QB), WINDOW)
+        keys = jnp.where(mirror == 1, LEN - high, low)
+        keys = pl.ds(pl.multiple_of(keys, QB), high - low)
         stacked = by_head(q_ref[rows, :] * scale, head)
         upstream = by_head(back_ref[rows, :], head)
         scores = dot(stacked, k_ref[keys, :], NT)
@@ -439,12 +441,12 @@
 
 def rows_back(base, dq_ref, dk_ref, dv_ref, trig_ref, w_ref, qkv_ref):
     rows = pl.ds(pl.multiple_of(base, BLOCK), BLOCK)
-    cosine, signed = trig_ref[rows, :LANES], trig_ref[rows, LANES:]
+    trig = trig_ref[rows, :]
     total = None
     for part, grad_ref in enumerate((dq_ref, dk_ref, dv_ref)):
         g = grad_ref[rows, :]
         if part < 2:
-            g = g * cosine - swap_halves(g) * signed
+            g = turn(g, trig, -1.0)
         low = g[:, :COLS].astype(BF16)
         qkv_ref[:, part * COLS : (part + 1) * COLS] = low
         product = dot(low, w_ref[part])
@@ -469,7 +471,7 @@
     refs = (seg_ref, segc_ref, q_ref, k_ref, v_ref, lse_ref, back_ref, dq_ref, dk_ref, dv_ref)
     steps = LEN // QB
     reach = DOC // QB
-    backward_steps((1 - pair) * (steps // 2 - reach), steps // 2 + reach, *refs)
+    backward_steps(1 - pair, range(steps // 2 + reach), *refs)
     for k, out in ((2, n2), (3, n3)):
         at = qkv_ref.at[(k - 2) * BLOCK : (k - 1) * BLOCK]
         part = rows_back((z ^ k) * BLOCK, dq_ref, dk_ref, dv_ref, trig_ref, w_ref, at)
@@ -492,7 +494,7 @@
     refs = (seg_ref, segc_ref, q_ref, k_ref, v_ref, lse_ref, back_ref, dq_ref, dk_ref, dv_ref)
     steps = LEN // QB
     reach = DOC // QB
-    backward_steps(pair * (steps // 2 + reach), steps // 2 - reach, *refs)
+    backward_steps(pair, range(steps // 2 - reach), *refs)
     for k, out in ((0, n0), (1, n1)):
         at = qkv_ref.at[k * BLOCK : (k + 1) * BLOCK]
         part = rows_back((z ^ k) * BLOCK, dq_ref, dk_ref, dv_ref, trig_ref, w_ref, at)
@@ -573,7 +575,7 @@
 
 def all_slots(x, hops):
     whole = jnp.stack([along_narrow(x, k) for k in hops])
-    slots = jnp.stack([quarter_slice(whole, i) for i in range(8)])
+    slots = jnp.stack([quarter_slice(whole, i) for i in ORDER])
     return slots[:4], slots[4:]
 
 
@@ -589,11 +591,7 @@
     plane = size == 8
     mine = lax.axis_index("wide").astype(jnp.int32)
     z = lax.axis_index("narrow").astype(jnp.int32)
-    order = jnp.asarray([0, 2, 4, 6, 1, 3, 5, 7], jnp.int32)
-    slots = (mine ^ order) if plane else jnp.arange(8, dtype=jnp.int32)
-    quarters = jnp.asarray([0, 2, 1, 3], jnp.int32)
-    quarters = ((mine % 4) ^ quarters) if plane else jnp.arange(4, dtype=jnp.int32)
-    scalars = jnp.concatenate([z[None], mine[None], slots, quarters])
+    scalars = jnp.stack([z, mine if plane else jnp.zeros_like(mine)])
     hidden = geglu_weight.shape[2]
     padded = -(-3 * hidden // 64) * 64
     rows_d = D // size
@@ -617,9 +615,9 @@
     q, k, v, normed_one, trig, segc = call(
         project_kernel,
         (tokens, segments, gain_one, w_qkv, jnp.asarray(rotary_table())),
-        (wide_rows, wide_rows, wide_rows, sds((LEN, D), BF16), sds((LEN, 2 * LANES), F32),
+        (wide_rows, wide_rows, wide_rows, sds((LEN, D), BF16), sds((LEN, 2 * 128), F32),
          sds((LEN, 128), F32)),
-        [pltpu.VMEM((LEN, LANES), F32)],
+        [pltpu.VMEM((LEN // 4, LANES), F32)],
         scalars=0,
     )
     piece = sds((BLOCK, 2 * COLS), BF16)
@@ -652,7 +650,7 @@
         others = jnp.stack([along_narrow(output_weight, k) for k in (1, 2, 3)])
         others = others.reshape(3, 4, few, 2, D // 2).transpose(1, 0, 3, 2, 4)
         others = others.reshape(4, 6 * few, D // 2)
-        out_here, out_there = others[:2], others[2:]
+        out_here, out_there = others[::2], others[1::2]
 
     whole = sds((2 * BLOCK, D), F32)
     own = sds((BLOCK, D), F32)
@@ -663,15 +661,14 @@
         (whole, sds((3, 2 * BLOCK, COLS), BF16), sds((2 * BLOCK, D), BF16),
          sds((2 * BLOCK, hidden), F32)),
     )
-    res, normed_two, act, gb, branch, back, wo = call(
+    part_act, part_gb = sds((BLOCK, hidden), BF16), sds((BLOCK, 2 * hidden), BF16)
+    res, normed_two, act_par, gb_par, branch, back, wo = call(
         middle_kernel,
         (scalars, part, contexts, cot, act_back, output_weight, out_here, out_there, gain_two, w_in,
          down_weight),
-        (own, sds((2 * BLOCK, D), BF16), sds((2 * BLOCK, hidden), BF16),
-         sds((2 * BLOCK, 2 * hidden), BF16), whole, whole, sds((NARROW, COLS, D), BF16)),
-    )
-    part_act, part_gb = sds((BLOCK, hidden), BF16), sds((BLOCK, 2 * hidden), BF16)
-    act_par, gb_par, out_send, send, other = call(
+        (own, sds((2 * BLOCK, D), BF16), part_act, part_gb, own, own, sds((NARROW, COLS, D), BF16)),
+    )
+    act_par_two, gb_par_two, out_send, send, other = call(
         partner_kernel,
         (scalars, normed_two, cot, branch, back, *ff_slots),
         (part_act, part_gb, own_low, own_low, sds((padded, D), BF16)),
@@ -680,9 +677,10 @@
     half = -(-3 * hidden // 128) * 128
     out_keep, keep, ff_part = call(
         own_kernel,
-        (scalars, normed_two, cot, branch, back, other, act, gb, act_par, gb_par),
+        (scalars, normed_two, cot, act_back, res, w_in, down_weight, other, act_par, gb_par,
+         act_par_two, gb_par_two),
         (own, own, sds((D, 2 * half), BF16)),
-        [pltpu.VMEM((BLOCK, hidden), BF16), pltpu.VMEM((BLOCK, 2 * hidden), BF16)],
+        [pltpu.VMEM((BLOCK, hidden), BF16), pltpu.VMEM((BLOCK, 2 * hidden), BF16)] * 2,
     )
     low_piece = sds((BLOCK // 2, 2 * COLS), BF16)
     back, low, gain_two_part, b0, b1, b2, b3 = call(
@@ -711,7 +709,7 @@
         grad_recv = [along_wide(x, 2 * (i + 1)) for i, x in enumerate(grad_sends)]
         now = tie(scalars, *grad_sends)
     else:
-        blocks = jnp.concatenate([even_part, odd_part], axis=0)
+        blocks = jnp.stack([even_part, odd_part], axis=1)
         grad_sum = sum_wide(blocks.reshape(size, rows_d, grad_cols))
         grad_recv, grad_sends = [jnp.zeros((rows_d, grad_cols), BF16)] * 3, ()
         now = tie(scalars, even_part)

time: 144 us -> 134 us (0.931)
  Pallas kernels: 63 us -> 49.3 us
  waiting for transfers between devices: 27.4 us -> 31.7 us
    pallas_call x21, Pallas kernels: 63 us -> 49.3 us  [call(): pl.pallas_call(body, name=name, out_shape=tuple((jax.ShapeDtypeStruct(o.s...]
    ppermute x21, waiting for transfers between devices: 26.9 us -> 31.7 us  [along_narrow(): return lax.ppermute(x, 'narrow', [(i, i ^ k) for i in range(NARROW)])]
    unnamed x82 -> x68, local copies, waits for them, and re-layouts: 4.18 us -> 4.27 us
  transfers between devices with their start and end apart: 32 -> 32, of which waited for: 8 -> 8; matrix products, arithmetic and copies ran while one was open for 1% -> 1% of each run, Pallas kernels for 39% -> 32%
where the time goes in v4:
time: 134 us
  Pallas kernels  49.3 us (37%)
  starting transfers between devices  44.7 us (33%)
  waiting for transfers between devices  31.7 us (24%)
  local copies, waits for them, and re-layouts  4.89 us (4%)
  other arithmetic  1.9 us (1%)
    pallas_call x21, Pallas kernels, call(): pl.pallas_call(body, name=name, out_shape=tuple((jax.ShapeDtypeStruct(o.s...  49.3 us
    ppermute x21, starting transfers between devices, along_narrow(): return lax.ppermute(x, 'narrow', [(i, i ^ k) for i in range(NARROW)])  32.3 us
    ppermute x21, waiting for transfers between devices, along_narrow(): return lax.ppermute(x, 'narrow', [(i, i ^ k) for i in range(NARROW)])  31.7 us
    ppermute x10, starting transfers between devices, along_wide(): lax.ppermute(x, 'wide', [(i, i ^ k) for i in range(lax.axis_size('wide'))])  8.83 us
    unnamed x68, local copies, waits for them, and re-layouts  4.27 us
    all_to_all x1, starting transfers between devices, per_device(): lax.all_to_all(qkv_part, 'wide', 0, 0)  3.56 us
  transfers between devices with their start and end apart: 32, of which 8 were waited for; matrix products, arithmetic and copies ran while one was open for 1% of the time, Pallas kernels for 32%

profile of v4, /device:TPU:0, one launch (start us, length us, event | category | flops | bytes accessed | tf_op | source)
XLA Modules:
  0.0 133.8 jit_solution(6677948601861782085)
XLA Ops:
  4.5 5.1 %collective-permute-start.5 = (bf16[96,384]{1,0:T(8,128)(2,1)S(1)}, bf16[96,384]{1,0:T(8,128)(2,1)S(1)}, u32[]{:S(2)}, u32[]{:S(2)}) collective-permute-start(bf16[96,384]{1,0:T(8,128)(2,1)S(1)} %get-tuple-element.94), channel_id=1, source_target_pairs={{0,3},{1,2},{2,1},{3,0},{4,7},{5,6},{6,5},{7,4},{8,11},{9,10},{10,... | collective-permute-start | bytes 221192 | tf_op jit(solution)/shard_map/ppermute | solution.py:559
  10.3 2.3 %collective-permute-start.8 = (bf16[224,384]{1,0:T(8,128)(2,1)S(1)}, bf16[224,384]{1,0:T(8,128)(2,1)S(1)}, u32[]{:S(2)}, u32[]{:S(2)}) collective-permute-start(bf16[224,384]{1,0:T(8,128)(2,1)S(1)} %get-tuple-element.99), channel_id=1, source_target_pairs={{0,2},{1,3},{2,0},{3,1},{4,6},{5,7},{6,4},{7,5},{8,10},{9,11},{10,... | collective-permute-start | bytes 516104 | tf_op jit(solution)/shard_map/ppermute | solution.py:559
  12.6 3.2 %project_kernel.1 = (bf16[1024,256]{1,0:T(8,128)(2,1)S(1)}, bf16[1024,256]{1,0:T(8,128)(2,1)S(1)}, bf16[1024,256]{1,0:T(8,128)(2,1)S(1)}, bf16[1024,768]{1,0:T(8...) custom-call(bf16[1024,768]{1,0:T(8,128)(2,1)S(1)} %copy-done.5, s32[1,1024]{1,0:T(1,128)S(1)} %copy-done.13, ...), custom_call_target="tpu_custom_call" | custom-call | flops 6000000000 | bytes 7445504 | tf_op jit(solution)/shard_map/project_kernel/pallas_call | solution.py:69
  15.9 4.9 %attend_kernel.1 = (bf16[256,384]{1,0:T(8,128)(2,1)S(1)}, bf16[256,384]{1,0:T(8,128)(2,1)S(1)}, bf16[256,384]{1,0:T(8,128)(2,1)S(1)}, bf16[256,384]{1,0:T(8,128)(2,1)S(1)}, f32[1024,128]{1,0:T(8,128)S(1)}) custom-call(s32[2]{0:T(128)S(1)} %pad_add_fusion.s_ref, s32[1,1024]{1,0:T(1,128)S(1)} %copy-done.13, f32[1024,128]{1,0:T(8,128)S(1)} %get-tuple-element.80.segc_ref, ...), custom_call_target="tpu_custom_call" | custom-call | flops 99999997952 | bytes 3411976 | tf_op jit(solution)/shard_map/attend_kernel/pallas_call | solution.py:69
  24.8 1.8 %collective-permute-start = (bf16[256,384]{1,0:T(8,128)(2,1)S(1)}, bf16[256,384]{1,0:T(8,128)(2,1)S(1)}, u32[]{:S(2)}, u32[]{:S(2)}) collective-permute-start(bf16[256,384]{1,0:T(8,128)(2,1)S(1)} %get-tuple-element.85), channel_id=1, source_target_pairs={{0,1},{1,0},{2,3},{3,2},{4,5},{5,4},{6,7},{7,6},{8,9},{9,8},{10,11... | collective-permute-start | bytes 589832 | tf_op jit(solution)/shard_map/ppermute | solution.py:559
  32.0 1.6 %collective-permute-done.c1 = bf16[256,384]{1,0:T(8,128)(2,1)S(1)} collective-permute-done((bf16[256,384]{1,0:T(8,128)(2,1)S(1)}, bf16[256,384]{1,0:T(8,128)(2,1)S(1)}, u32[]{:S(2)}, u32[]{:S(2)}) %collective-permute-start) | collective-permute-done | bytes 196640 | tf_op jit(solution)/shard_map/ppermute | solution.py:559
  33.7 9.0 %collective-permute-done.1.c2 = bf16[256,384]{1,0:T(8,128)(2,1)S(1)} collective-permute-done((bf16[256,384]{1,0:T(8,128)(2,1)S(1)}, bf16[256,384]{1,0:T(8,128)(2,1)S(1)}, u32[]{:S(2)}, u32[]{:S(2)}) %collective-permute-start.1) | collective-permute-done | bytes 196640 | tf_op jit(solution)/shard_map/ppermute | solution.py:559
  44.6 3.3 %middle_kernel.1 = (f32[256,768]{1,0:T(8,128)S(1)}, bf16[512,768]{1,0:T(8,128)(2,1)S(1)}, bf16[256,288]{1,0:T(8,128)(2,1)S(1)}, bf16[256,576]{1,0:T(8,128)(2,1)S...) custom-call(s32[2]{0:T(128)S(1)} %pad_add_fusion.s_ref, ...), custom_call_target="tpu_custom_call" | custom-call | flops 5000000000 | bytes 10816520 | tf_op jit(solution)/shard_map/middle_kernel/pallas_call | solution.py:69
  48.0 3.1 %partner_kernel.1 = (bf16[256,288]{1,0:T(8,128)(2,1)S(1)}, bf16[256,576]{1,0:T(8,128)(2,1)S(1)}, bf16[256,768]{1,0:T(8,128)(2,1)}, bf16[256,768]{1,0:T(8,128)(2,1)S(1)}, bf16[896,768]{1,0:T(8,128)(2,1)S(1)}) custom-call(s32[2]{0:T(128)S(1)} %pad_add_fusion.s_ref, bf16[512,768]{1,0:T(8,128)(2,1)S(1)} %get-tuple-element.95.normed_ref, ...), custom_call_target="tpu_custom_call" | custom-call | flops 3000000000 | bytes 7127048 | tf_op jit(solution)/shard_map/partner_kernel/pallas_call | solution.py:69
  51.1 2.7 %collective-permute-start.13 = (bf16[256,768]{1,0:T(8,128)(2,1)S(1)}, bf16[256,768]{1,0:T(8,128)(2,1)S(1)}, u32[]{:S(2)}, u32[]{:S(2)}) collective-permute-start(bf16[256,768]{1,0:T(8,128)(2,1)S(1)} %get-tuple-element.109), channel_id=1, source_target_pairs={{0,1},{1,0},{2,3},{3,2},{4,5},{5,4},{6,7},{7,6},{8,9},{9,8},{10,11... | collective-permute-start | bytes 1179656 | tf_op jit(solution)/shard_map/ppermute | solution.py:559
  53.8 5.4 %own_kernel.1 = (f32[256,768]{1,0:T(8,128)S(1)}, f32[256,768]{1,0:T(8,128)S(1)}, bf16[768,1792]{1,0:T(8,128)(2,1)S(1)}) custom-call(s32[2]{0:T(128)S(1)} %pad_add_fusion.s_ref, bf16[512,768]{1,0:T(8,128)(2,1)S(1)} %get-tuple-element.95.normed_ref, bf16[512,768]{1,0:T(8,128)(2,1)S(1)} %get-tuple-element.90.cot_ref, ...), custom_call_target="tpu_custom_call" | custom-call | flops 10000000000 | bytes 10862600 | tf_op jit(solution)/shard_map/own_kernel/pallas_call | solution.py:69
  59.2 3.9 %collective-permute-done.13.recv_ref = bf16[256,768]{1,0:T(8,128)(2,1)S(1)} collective-permute-done((bf16[256,768]{1,0:T(8,128)(2,1)S(1)}, bf16[256,768]{1,0:T(8,128)(2,1)S(1)}, u32[]{:S(2)}, u32[]{:S(2)}) %collective-permute-start.13) | collective-permute-done | bytes 393248 | tf_op jit(solution)/shard_map/ppermute | solution.py:559
  65.9 1.8 %collective-permute-start.14 = (bf16[128,384]{1,0:T(8,128)(2,1)S(1)}, bf16[128,384]{1,0:T(8,128)(2,1)S(1)}, u32[]{:S(2)}, u32[]{:S(2)}) collective-permute-start(bf16[128,384]{1,0:T(8,128)(2,1)S(1)} %get-tuple-element.111), channel_id=1, source_target_pairs={{0,1},{1,0},{2,3},{3,2},{4,5},{5,4},{6,7},{7,6},{8,9},{9,8},{10,11... | collective-permute-start | bytes 294920 | tf_op jit(solution)/shard_map/ppermute | solution.py:559
  68.7 1.7 %collective-permute-start.18 = (bf16[128,384]{1,0:T(8,128)(2,1)S(1)}, bf16[128,384]{1,0:T(8,128)(2,1)S(1)}, u32[]{:S(2)}, u32[]{:S(2)}) collective-permute-start(bf16[128,384]{1,0:T(8,128)(2,1)S(1)} %get-tuple-element.125), channel_id=1, source_target_pairs={{0,3},{1,2},{2,1},{3,0},{4,7},{5,6},{6,5},{7,4},{8,11},{9,10},{10,... | collective-permute-start | bytes 294920 | tf_op jit(solution)/shard_map/ppermute | solution.py:559
  74.6 1.7 %collective-permute-start.27 = (bf16[96,2560]{1,0:T(8,128)(2,1)}, bf16[96,2560]{1,0:T(8,128)(2,1)}, u32[]{:S(2)}, u32[]{:S(2)}) collective-permute-start(bf16[96,2560]{1,0:T(8,128)(2,1)} %get-tuple-element.118), channel_id=1, source_target_pairs={{0,24},{4,28},{8,16},{12,20},{16,8},{20,12},{24,0},{28,4},{1,25},{... | collective-permute-start | bytes 1474568 | tf_op jit(solution)/shard_map/ppermute | solution.py:563
  76.3 2.2 %collective-permute-done.17.b2 = bf16[128,384]{1,0:T(8,128)(2,1)S(1)} collective-permute-done((bf16[128,384]{1,0:T(8,128)(2,1)S(1)}, bf16[128,384]{1,0:T(8,128)(2,1)S(1)}, u32[]{:S(2)}, u32[]{:S(2)}) %collective-permute-start.17) | collective-permute-done | bytes 98336 | tf_op jit(solution)/shard_map/ppermute | solution.py:559
  78.6 7.9 %backward_far_kernel.1 = (f32[256,768]{1,0:T(8,128)S(1)}, bf16[256,768]{1,0:T(8,128)(2,1)S(1)}, bf16[512,576]{1,0:T(8,128)(2,1)S(1)}, bf16[1024,256]{1,0:T(8,128...) custom-call(s32[2]{0:T(128)S(1)} %pad_add_fusion.s_ref, ...), custom_call_target="tpu_custom_call" | custom-call | flops 99999997952 | bytes 10391560 | tf_op jit(solution)/shard_map/backward_far_kernel/pallas_call | solution.py:69
  86.5 2.1 %collective-permute-start.20 = (bf16[256,768]{1,0:T(8,128)(2,1)S(1)}, bf16[256,768]{1,0:T(8,128)(2,1)S(1)}, u32[]{:S(2)}, u32[]{:S(2)}) collective-permute-start(bf16[256,768]{1,0:T(8,128)(2,1)S(1)} %get-tuple-element.139), channel_id=1, source_target_pairs={{0,1},{1,0},{2,3},{3,2},{4,5},{5,4},{6,7},{7,6},{8,9},{9,8},{10,11... | collective-permute-start | bytes 1179656 | tf_op jit(solution)/shard_map/ppermute | solution.py:559
  88.6 3.8 %backward_near_kernel.1 = (f32[256,768]{1,0:T(8,128)S(1)}, bf16[256,768]{1,0:T(8,128)(2,1)S(1)}, bf16[512,576]{1,0:T(8,128)(2,1)S(1)}) custom-call(s32[2]{0:T(128)S(1)} %pad_add_fusion.s_ref, s32[1,1024]{1,0:T(1,128)S(1)} %copy-done.14, f32[1024,128]{1,0:T(8,128)S(1)} %copy-done.27, bf16[1024,256]{1,0:T(8,128)(2,1)S(1)} %copy-done.21, ...), custom_call_target="tpu_custom_call" | custom-call | flops 99999997952 | bytes 9998344 | tf_op jit(solution)/shard_map/backward_near_kernel/pallas_call | solution.py:69
  92.5 4.1 %qkv_grad_kernel.1 = bf16[8,112,576]{2,1,0:T(8,128)(2,1)} custom-call(s32[2]{0:T(128)S(1)} %pad_add_fusion.s_ref, bf16[1024,768]{1,0:T(8,128)(2,1)S(1)} %get-tuple-element.134.normed_ref, bf16[512,576]{1,0:T(8,128)(2,1)S(1)} %get-tuple-element.135.near_ref, bf16[512,576]{1,0:T(8,128)(2,1)S(1)} %get-tuple-element.136.far_ref, ...), custom_call_target="tpu_custom_call" | custom-call | flops 1000000000 | bytes 4675592 | tf_op jit(solution)/shard_map/qkv_grad_kernel/pallas_call | solution.py:69
  96.5 2.1 %collective-permute-done.20.recv_ref = bf16[256,768]{1,0:T(8,128)(2,1)S(1)} collective-permute-done((bf16[256,768]{1,0:T(8,128)(2,1)S(1)}, bf16[256,768]{1,0:T(8,128)(2,1)S(1)}, u32[]{:S(2)}, u32[]{:S(2)}) %collective-permute-start.20) | collective-permute-done | bytes 393248 | tf_op jit(solution)/shard_map/ppermute | solution.py:559
  98.7 2.7 %collective-permute-start.21 = (bf16[256,768]{1,0:T(8,128)(2,1)S(1)}, bf16[256,768]{1,0:T(8,128)(2,1)S(1)}, u32[]{:S(2)}, u32[]{:S(2)}) collective-permute-start(bf16[256,768]{1,0:T(8,128)(2,1)S(1)} %add_kernel.1), channel_id=1, source_target_pairs={{0,2},{1,3},{2,0},{3,1},{4,6},{5,7},{6,4},{7,5},{8,10},{9,11},{10,... | collective-permute-start | bytes 1179656 | tf_op jit(solution)/shard_map/ppermute | solution.py:559
  101.4 3.6 %all-to-all-start = ((bf16[8,112,576]{2,1,0:T(8,128)(2,1)}), bf16[8,112,576]{2,1,0:T(8,128)(2,1)S(1)}, u32[]{:S(2)}, u32[]{:S(2)}) async-start(bf16[8,112,576]{2,1,0:T(8,128)(2,1)} %qkv_grad_kernel.1), calls=%async_computation | async-start | bytes 2293760 | tf_op jit(solution)/shard_map/all_to_all | solution.py:743
  104.9 8.6 %collective-permute-done.19.n1 = bf16[256,768]{1,0:T(8,128)(2,1)S(1)} collective-permute-done((bf16[256,768]{1,0:T(8,128)(2,1)S(1)}, bf16[256,768]{1,0:T(8,128)(2,1)S(1)}, u32[]{:S(2)}, u32[]{:S(2)}) %collective-permute-start.19) | collective-permute-done | bytes 393248 | tf_op jit(solution)/shard_map/ppermute | solution.py:559
  113.5 1.8 %add_convert_fusion = bf16[256,768]{1,0:T(8,128)(2,1)} fusion(f32[256,768]{1,0:T(8,128)S(1)} %get-tuple-element.106, bf16[256,768]{1,0:T(8,128)(2,1)} %collective-permute-done.16), kind=kLoop, calls=%fused_computation | loop fusion | flops 589824 | bytes 1572864 | tf_op jit(solution)/shard_map/convert_element_type | solution.py:768
  115.4 1.8 %collect_kernel.1 = (f32[96,1088]{1,0:T(8,128)S(1)}, bf16[96,192]{1,0:T(8,128)(2,1)S(1)}, bf16[96,1088]{1,0:T(8,128)(2,1)S(1)}, bf16[96,192]{1,0:T(8,128)(2,1)S(1)}) custom-call(f32[96,2560]{1,0:T(8,128)S(1)} %copy-done.17, bf16[96,2560]{1,0:T(8,128)(2,1)} %collective-permute-done.25.r1, bf16[96,2560]{1,0:T(8,128)(2,1)} %collective-permute-done.26.r2, ...), custom_call_target="tpu_custom_call" | custom-call | flops 1000000000 | bytes 3158016 | tf_op jit(solution)/shard_map/collect_kernel/pallas_call | solution.py:69
  117.3 1.7 %collective-permute-start.30 = (bf16[96,192]{1,0:T(8,128)(2,1)S(1)}, bf16[96,192]{1,0:T(8,128)(2,1)S(1)}, u32[]{:S(2)}, u32[]{:S(2)}) collective-permute-start(bf16[96,192]{1,0:T(8,128)(2,1)S(1)} %get-tuple-element.148), channel_id=1, source_target_pairs={{0,3},{1,2},{2,1},{3,0},{4,7},{5,6},{6,5},{7,4},{8,11},{9,10},{10,... | collective-permute-start | bytes 110600 | tf_op jit(solution)/shard_map/ppermute | solution.py:559
  119.0 1.8 %collective-permute-start.29 = (bf16[96,1088]{1,0:T(8,128)(2,1)S(1)}, bf16[96,1088]{1,0:T(8,128)(2,1)S(1)}, u32[]{:S(2)}, u32[]{:S(2)}) collective-permute-start(bf16[96,1088]{1,0:T(8,128)(2,1)S(1)} %get-tuple-element.147), channel_id=1, source_target_pairs={{0,2},{1,3},{2,0},{3,1},{4,6},{5,7},{6,4},{7,5},{8,10},{9,11},{10,... | collective-permute-start | bytes 626696 | tf_op jit(solution)/shard_map/ppermute | solution.py:559
  120.8 2.1 %final_kernel.1 = f32[256,768]{1,0:T(8,128)} custom-call(s32[2]{0:T(128)S(1)} %pad_add_fusion.s_ref, bf16[1024,768]{1,0:T(8,128)(2,1)S(1)} %copy-done.6, f32[1,768]{1,0:T(1,128)S(1)} %copy-done.3, f32[256,768]{1,0:T(8,128)S(1)} %copy-done.31, f32[256,768]{1,0:T(8,128)S(1)} %copy-done.29, bf16[256,768]{1,0:T(8,128)(2,1)S(1)} %collective-permute-done.19.n1, ...), custom_call_target="tpu_custom_call" | custom-call | flops 99999997952 | bytes 4721672 | tf_op jit(solution)/shard_map/final_kernel/pallas_call | solution.py:69
  123.8 1.6 %collective-permute-start.24 = (f32[2,768]{1,0:T(2,128)S(1)}, f32[2,768]{1,0:T(2,128)S(1)}, u32[]{:S(2)}, u32[]{:S(2)}) collective-permute-start(f32[2,768]{1,0:T(2,128)S(1)} %get-tuple-element.140), channel_id=1, source_target_pairs={{0,3},{1,2},{2,1},{3,0},{4,7},{5,6},{6,5},{7,4},{8,11},{9,10},{10,... | collective-permute-start | bytes 18440 | tf_op jit(solution)/shard_map/ppermute | solution.py:559
  126.2 1.9 %collective-permute-start.22 = (f32[2,768]{1,0:T(2,128)S(1)}, f32[2,768]{1,0:T(2,128)S(1)}, u32[]{:S(2)}, u32[]{:S(2)}) collective-permute-start(f32[2,768]{1,0:T(2,128)S(1)} %get-tuple-element.140), channel_id=1, source_target_pairs={{0,1},{1,0},{2,3},{3,2},{4,5},{5,4},{6,7},{7,6},{8,9},{9,8},{10,11... | collective-permute-start | bytes 18440 | tf_op jit(solution)/shard_map/ppermute | solution.py:559
  128.1 4.0 %collective-permute-done.29.r2 = bf16[96,1088]{1,0:T(8,128)(2,1)S(1)} collective-permute-done((bf16[96,1088]{1,0:T(8,128)(2,1)S(1)}, bf16[96,1088]{1,0:T(8,128)(2,1)S(1)}, u32[]{:S(2)}, u32[]{:S(2)}) %collective-permute-start.29) | collective-permute-done | bytes 208928 | tf_op jit(solution)/shard_map/ppermute | solution.py:559
  (127 shorter events, 27.3 us)
Async XLA Ops:
  4.5 16.3 %collective-permute-start.5 = (bf16[96,384]{1,0:T(8,128)(2,1)S(1)}, bf16[96,384]{1,0:T(8,128)(2,1)S(1)}, u32[]{:S(2)}, u32[]{:S(2)}) collective-permute-start(bf16[96,384]{1,0:T(8,128)(2,1)S(1)} %get-tuple-element.94), channel_id=1, source_target_pairs={{0,3},{1,2},{2,1},{3,0},{4,7},{5,6},{6,5},{7,4},{8,11},{9,10},{10,... | collective-permute-start | bytes 221192 | tf_op jit(solution)/shard_map/ppermute | solution.py:559
  9.7 11.2 %collective-permute-start.4 = (bf16[96,384]{1,0:T(8,128)(2,1)S(1)}, bf16[96,384]{1,0:T(8,128)(2,1)S(1)}, u32[]{:S(2)}, u32[]{:S(2)}) collective-permute-start(bf16[96,384]{1,0:T(8,128)(2,1)S(1)} %get-tuple-element.94), channel_id=1, source_target_pairs={{0,2},{1,3},{2,0},{3,1},{4,6},{5,7},{6,4},{7,5},{8,10},{9,11},{10,... | collective-permute-start | bytes 221192 | tf_op jit(solution)/shard_map/ppermute | solution.py:559
  9.7 11.2 %collective-permute-start.3 = (bf16[96,384]{1,0:T(8,128)(2,1)S(1)}, bf16[96,384]{1,0:T(8,128)(2,1)S(1)}, u32[]{:S(2)}, u32[]{:S(2)}) collective-permute-start(bf16[96,384]{1,0:T(8,128)(2,1)S(1)} %get-tuple-element.94), channel_id=1, source_target_pairs={{0,1},{1,0},{2,3},{3,2},{4,5},{5,4},{6,7},{7,6},{8,9},{9,8},{10,11... | collective-permute-start | bytes 221192 | tf_op jit(solution)/shard_map/ppermute | solution.py:559
  10.3 12.9 %collective-permute-start.8 = (bf16[224,384]{1,0:T(8,128)(2,1)S(1)}, bf16[224,384]{1,0:T(8,128)(2,1)S(1)}, u32[]{:S(2)}, u32[]{:S(2)}) collective-permute-start(bf16[224,384]{1,0:T(8,128)(2,1)S(1)} %get-tuple-element.99), channel_id=1, source_target_pairs={{0,2},{1,3},{2,0},{3,1},{4,6},{5,7},{6,4},{7,5},{8,10},{9,11},{10,... | collective-permute-start | bytes 516104 | tf_op jit(solution)/shard_map/ppermute | solution.py:559
  21.4 7.8 %collective-permute-start.6 = (bf16[288,384]{1,0:T(8,128)(2,1)S(1)}, bf16[288,384]{1,0:T(8,128)(2,1)S(1)}, u32[]{:S(2)}, u32[]{:S(2)}) collective-permute-start(bf16[288,384]{1,0:T(8,128)(2,1)S(1)} %arrived_kernel.1.a0), channel_id=1, source_target_pairs={{0,8},{4,12},{8,0},{12,4},{16,24},{20,28},{24,16},{28,20},{1,9},{5... | collective-permute-start | bytes 663560 | tf_op jit(solution)/shard_map/ppermute | solution.py:563
  23.2 6.6 %collective-permute-start.9 = (bf16[224,384]{1,0:T(8,128)(2,1)S(1)}, bf16[224,384]{1,0:T(8,128)(2,1)S(1)}, u32[]{:S(2)}, u32[]{:S(2)}) collective-permute-start(bf16[224,384]{1,0:T(8,128)(2,1)S(1)} %collective-permute-done.8.a0), channel_id=1, source_target_pairs={{0,16},{4,20},{8,24},{12,28},{16,0},{20,4},{24,8},{28,12},{1,17},{... | collective-permute-start | bytes 516104 | tf_op jit(solution)/shard_map/ppermute | solution.py:563
  24.8 8.9 %collective-permute-start = (bf16[256,384]{1,0:T(8,128)(2,1)S(1)}, bf16[256,384]{1,0:T(8,128)(2,1)S(1)}, u32[]{:S(2)}, u32[]{:S(2)}) collective-permute-start(bf16[256,384]{1,0:T(8,128)(2,1)S(1)} %get-tuple-element.85), channel_id=1, source_target_pairs={{0,1},{1,0},{2,3},{3,2},{4,5},{5,4},{6,7},{7,6},{8,9},{9,8},{10,11... | collective-permute-start | bytes 589832 | tf_op jit(solution)/shard_map/ppermute | solution.py:559
  26.5 16.2 %collective-permute-start.1 = (bf16[256,384]{1,0:T(8,128)(2,1)S(1)}, bf16[256,384]{1,0:T(8,128)(2,1)S(1)}, u32[]{:S(2)}, u32[]{:S(2)}) collective-permute-start(bf16[256,384]{1,0:T(8,128)(2,1)S(1)} %get-tuple-element.86), channel_id=1, source_target_pairs={{0,2},{1,3},{2,0},{3,1},{4,6},{5,7},{6,4},{7,5},{8,10},{9,11},{10,... | collective-permute-start | bytes 589832 | tf_op jit(solution)/shard_map/ppermute | solution.py:559
  28.0 14.6 %collective-permute-start.2 = (bf16[256,384]{1,0:T(8,128)(2,1)S(1)}, bf16[256,384]{1,0:T(8,128)(2,1)S(1)}, u32[]{:S(2)}, u32[]{:S(2)}) collective-permute-start(bf16[256,384]{1,0:T(8,128)(2,1)S(1)} %get-tuple-element.87), channel_id=1, source_target_pairs={{0,3},{1,2},{2,1},{3,0},{4,7},{5,6},{6,5},{7,4},{8,11},{9,10},{10,... | collective-permute-start | bytes 589832 | tf_op jit(solution)/shard_map/ppermute | solution.py:559
  29.8 14.8 %collective-permute-start.7 = (bf16[2,288,384]{2,1,0:T(8,128)(2,1)S(1)}, bf16[2,288,384]{2,1,0:T(8,128)(2,1)S(1)}, u32[]{:S(2)}, u32[]{:S(2)}) collective-permute-start(bf16[2,288,384]{2,1,0:T(8,128)(2,1)S(1)} %pair_kernel.2.here_ref), channel_id=1, source_target_pairs={{0,4},{4,0},{8,12},{12,8},{16,20},{20,16},{24,28},{28,24},{1,5},{5... | collective-permute-start | bytes 1327112 | tf_op jit(solution)/shard_map/ppermute | solution.py:563
  30.5 13.7 %collective-permute-start.10 = (bf16[2,224,384]{2,1,0:T(8,128)(2,1)S(1)}, bf16[2,224,384]{2,1,0:T(8,128)(2,1)S(1)}, u32[]{:S(2)}, u32[]{:S(2)}) collective-permute-start(bf16[2,224,384]{2,1,0:T(8,128)(2,1)S(1)} %pair_kernel.3.f0), channel_id=1, source_target_pairs={{0,8},{4,12},{8,0},{12,4},{16,24},{20,28},{24,16},{28,20},{1,9},{5... | collective-permute-start | bytes 1032200 | tf_op jit(solution)/shard_map/ppermute | solution.py:563
  44.0 3.9 %collective-permute-start.11 = (bf16[2,224,384]{2,1,0:T(8,128)(2,1)S(1)}, bf16[2,224,384]{2,1,0:T(8,128)(2,1)S(1)}, u32[]{:S(2)}, u32[]{:S(2)}) collective-permute-start(bf16[2,224,384]{2,1,0:T(8,128)(2,1)S(1)} %pair_kernel.3.f0), channel_id=1, source_target_pairs={{0,4},{4,0},{8,12},{12,8},{16,20},{20,16},{24,28},{28,24},{1,5},{5... | collective-permute-start | bytes 1032200 | tf_op jit(solution)/shard_map/ppermute | solution.py:563
  44.1 3.8 %collective-permute-start.12 = (bf16[2,224,384]{2,1,0:T(8,128)(2,1)S(1)}, bf16[2,224,384]{2,1,0:T(8,128)(2,1)S(1)}, u32[]{:S(2)}, u32[]{:S(2)}) collective-permute-start(bf16[2,224,384]{2,1,0:T(8,128)(2,1)S(1)} %collective-permute-done.10.f1), channel_id=1, source_target_pairs={{0,4},{4,0},{8,12},{12,8},{16,20},{20,16},{24,28},{28,24},{1,5},{5... | collective-permute-start | bytes 1032200 | tf_op jit(solution)/shard_map/ppermute | solution.py:563
  51.1 12.0 %collective-permute-start.13 = (bf16[256,768]{1,0:T(8,128)(2,1)S(1)}, bf16[256,768]{1,0:T(8,128)(2,1)S(1)}, u32[]{:S(2)}, u32[]{:S(2)}) collective-permute-start(bf16[256,768]{1,0:T(8,128)(2,1)S(1)} %get-tuple-element.109), channel_id=1, source_target_pairs={{0,1},{1,0},{2,3},{3,2},{4,5},{5,4},{6,7},{7,6},{8,9},{9,8},{10,11... | collective-permute-start | bytes 1179656 | tf_op jit(solution)/shard_map/ppermute | solution.py:559
  65.9 4.5 %collective-permute-start.15 = (bf16[4,96,2560]{2,1,0:T(8,128)(2,1)S(1)}, bf16[4,96,2560]{2,1,0:T(8,128)(2,1)S(1)}, u32[]{:S(2)}, u32[]{:S(2)}) collective-permute-start(bf16[4,96,2560]{2,1,0:T(8,128)(2,1)S(1)} %get-tuple-element.115), channel_id=1, source_target_pairs={{0,4},{4,0},{8,12},{12,8},{16,20},{20,16},{24,28},{28,24},{1,5},{5... | collective-permute-start | bytes 5898248 | tf_op jit(solution)/shard_map/ppermute | solution.py:563
  65.9 8.6 %collective-permute-start.14 = (bf16[128,384]{1,0:T(8,128)(2,1)S(1)}, bf16[128,384]{1,0:T(8,128)(2,1)S(1)}, u32[]{:S(2)}, u32[]{:S(2)}) collective-permute-start(bf16[128,384]{1,0:T(8,128)(2,1)S(1)} %get-tuple-element.111), channel_id=1, source_target_pairs={{0,1},{1,0},{2,3},{3,2},{4,5},{5,4},{6,7},{7,6},{8,9},{9,8},{10,11... | collective-permute-start | bytes 294920 | tf_op jit(solution)/shard_map/ppermute | solution.py:559
  67.8 10.8 %collective-permute-start.17 = (bf16[128,384]{1,0:T(8,128)(2,1)S(1)}, bf16[128,384]{1,0:T(8,128)(2,1)S(1)}, u32[]{:S(2)}, u32[]{:S(2)}) collective-permute-start(bf16[128,384]{1,0:T(8,128)(2,1)S(1)} %get-tuple-element.124), channel_id=1, source_target_pairs={{0,2},{1,3},{2,0},{3,1},{4,6},{5,7},{6,4},{7,5},{8,10},{9,11},{10,... | collective-permute-start | bytes 294920 | tf_op jit(solution)/shard_map/ppermute | solution.py:559
  68.7 9.8 %collective-permute-start.18 = (bf16[128,384]{1,0:T(8,128)(2,1)S(1)}, bf16[128,384]{1,0:T(8,128)(2,1)S(1)}, u32[]{:S(2)}, u32[]{:S(2)}) collective-permute-start(bf16[128,384]{1,0:T(8,128)(2,1)S(1)} %get-tuple-element.125), channel_id=1, source_target_pairs={{0,3},{1,2},{2,1},{3,0},{4,7},{5,6},{6,5},{7,4},{8,11},{9,10},{10,... | collective-permute-start | bytes 294920 | tf_op jit(solution)/shard_map/ppermute | solution.py:559
  72.8 42.5 %collective-permute-start.25 = (bf16[96,2560]{1,0:T(8,128)(2,1)}, bf16[96,2560]{1,0:T(8,128)(2,1)}, u32[]{:S(2)}, u32[]{:S(2)}) collective-permute-start(bf16[96,2560]{1,0:T(8,128)(2,1)} %get-tuple-element.116), channel_id=1, source_target_pairs={{0,8},{4,12},{8,0},{12,4},{16,24},{20,28},{24,16},{28,20},{1,9},{5... | collective-permute-start | bytes 1474568 | tf_op jit(solution)/shard_map/ppermute | solution.py:563
  74.1 41.3 %collective-permute-start.26 = (bf16[96,2560]{1,0:T(8,128)(2,1)}, bf16[96,2560]{1,0:T(8,128)(2,1)}, u32[]{:S(2)}, u32[]{:S(2)}) collective-permute-start(bf16[96,2560]{1,0:T(8,128)(2,1)} %get-tuple-element.117), channel_id=1, source_target_pairs={{0,16},{4,20},{8,24},{12,28},{16,0},{20,4},{24,8},{28,12},{1,17},{... | collective-permute-start | bytes 1474568 | tf_op jit(solution)/shard_map/ppermute | solution.py:563
  74.6 40.8 %collective-permute-start.27 = (bf16[96,2560]{1,0:T(8,128)(2,1)}, bf16[96,2560]{1,0:T(8,128)(2,1)}, u32[]{:S(2)}, u32[]{:S(2)}) collective-permute-start(bf16[96,2560]{1,0:T(8,128)(2,1)} %get-tuple-element.118), channel_id=1, source_target_pairs={{0,24},{4,28},{8,16},{12,20},{16,8},{20,12},{24,0},{28,4},{1,25},{... | collective-permute-start | bytes 1474568 | tf_op jit(solution)/shard_map/ppermute | solution.py:563
  78.5 13.9 %collective-permute-start.16 = (bf16[256,768]{1,0:T(8,128)(2,1)}, bf16[256,768]{1,0:T(8,128)(2,1)}, u32[]{:S(2)}, u32[]{:S(2)}) collective-permute-start(bf16[256,768]{1,0:T(8,128)(2,1)} %get-tuple-element.119), channel_id=1, source_target_pairs={{0,1},{1,0},{2,3},{3,2},{4,5},{5,4},{6,7},{7,6},{8,9},{9,8},{10,11... | collective-permute-start | bytes 1179656 | tf_op jit(solution)/shard_map/ppermute | solution.py:559
  86.5 12.1 %collective-permute-start.20 = (bf16[256,768]{1,0:T(8,128)(2,1)S(1)}, bf16[256,768]{1,0:T(8,128)(2,1)S(1)}, u32[]{:S(2)}, u32[]{:S(2)}) collective-permute-start(bf16[256,768]{1,0:T(8,128)(2,1)S(1)} %get-tuple-element.139), channel_id=1, source_target_pairs={{0,1},{1,0},{2,3},{3,2},{4,5},{5,4},{6,7},{7,6},{8,9},{9,8},{10,11... | collective-permute-start | bytes 1179656 | tf_op jit(solution)/shard_map/ppermute | solution.py:559
  92.4 21.2 %collective-permute-start.19 = (bf16[256,768]{1,0:T(8,128)(2,1)S(1)}, bf16[256,768]{1,0:T(8,128)(2,1)S(1)}, u32[]{:S(2)}, u32[]{:S(2)}) collective-permute-start(bf16[256,768]{1,0:T(8,128)(2,1)S(1)} %get-tuple-element.131), channel_id=1, source_target_pairs={{0,1},{1,0},{2,3},{3,2},{4,5},{5,4},{6,7},{7,6},{8,9},{9,8},{10,11... | collective-permute-start | bytes 1179656 | tf_op jit(solution)/shard_map/ppermute | solution.py:559
  98.7 22.1 %collective-permute-start.21 = (bf16[256,768]{1,0:T(8,128)(2,1)S(1)}, bf16[256,768]{1,0:T(8,128)(2,1)S(1)}, u32[]{:S(2)}, u32[]{:S(2)}) collective-permute-start(bf16[256,768]{1,0:T(8,128)(2,1)S(1)} %add_kernel.1), channel_id=1, source_target_pairs={{0,2},{1,3},{2,0},{3,1},{4,6},{5,7},{6,4},{7,5},{8,10},{9,11},{10,... | collective-permute-start | bytes 1179656 | tf_op jit(solution)/shard_map/ppermute | solution.py:559
  101.4 21.5 %all-to-all-start = ((bf16[8,112,576]{2,1,0:T(8,128)(2,1)}), bf16[8,112,576]{2,1,0:T(8,128)(2,1)S(1)}, u32[]{:S(2)}, u32[]{:S(2)}) async-start(bf16[8,112,576]{2,1,0:T(8,128)(2,1)} %qkv_grad_kernel.1), calls=%async_computation | async-start | bytes 2293760 | tf_op jit(solution)/shard_map/all_to_all | solution.py:743
  117.2 9.0 %collective-permute-start.28 = (bf16[96,192]{1,0:T(8,128)(2,1)S(1)}, bf16[96,192]{1,0:T(8,128)(2,1)S(1)}, u32[]{:S(2)}, u32[]{:S(2)}) collective-permute-start(bf16[96,192]{1,0:T(8,128)(2,1)S(1)} %get-tuple-element.146), channel_id=1, source_target_pairs={{0,1},{1,0},{2,3},{3,2},{4,5},{5,4},{6,7},{7,6},{8,9},{9,8},{10,11... | collective-permute-start | bytes 110600 | tf_op jit(solution)/shard_map/ppermute | solution.py:559
  117.3 10.8 %collective-permute-start.30 = (bf16[96,192]{1,0:T(8,128)(2,1)S(1)}, bf16[96,192]{1,0:T(8,128)(2,1)S(1)}, u32[]{:S(2)}, u32[]{:S(2)}) collective-permute-start(bf16[96,192]{1,0:T(8,128)(2,1)S(1)} %get-tuple-element.148), channel_id=1, source_target_pairs={{0,3},{1,2},{2,1},{3,0},{4,7},{5,6},{6,5},{7,4},{8,11},{9,10},{10,... | collective-permute-start | bytes 110600 | tf_op jit(solution)/shard_map/ppermute | solution.py:559
  119.0 13.2 %collective-permute-start.29 = (bf16[96,1088]{1,0:T(8,128)(2,1)S(1)}, bf16[96,1088]{1,0:T(8,128)(2,1)S(1)}, u32[]{:S(2)}, u32[]{:S(2)}) collective-permute-start(bf16[96,1088]{1,0:T(8,128)(2,1)S(1)} %get-tuple-element.147), channel_id=1, source_target_pairs={{0,2},{1,3},{2,0},{3,1},{4,6},{5,7},{6,4},{7,5},{8,10},{9,11},{10,... | collective-permute-start | bytes 626696 | tf_op jit(solution)/shard_map/ppermute | solution.py:559
  123.8 9.4 %collective-permute-start.24 = (f32[2,768]{1,0:T(2,128)S(1)}, f32[2,768]{1,0:T(2,128)S(1)}, u32[]{:S(2)}, u32[]{:S(2)}) collective-permute-start(f32[2,768]{1,0:T(2,128)S(1)} %get-tuple-element.140), channel_id=1, source_target_pairs={{0,3},{1,2},{2,1},{3,0},{4,7},{5,6},{6,5},{7,4},{8,11},{9,10},{10,... | collective-permute-start | bytes 18440 | tf_op jit(solution)/shard_map/ppermute | solution.py:559
  125.3 7.8 %collective-permute-start.23 = (f32[2,768]{1,0:T(2,128)S(1)}, f32[2,768]{1,0:T(2,128)S(1)}, u32[]{:S(2)}, u32[]{:S(2)}) collective-permute-start(f32[2,768]{1,0:T(2,128)S(1)} %get-tuple-element.140), channel_id=1, source_target_pairs={{0,2},{1,3},{2,0},{3,1},{4,6},{5,7},{6,4},{7,5},{8,10},{9,11},{10,... | collective-permute-start | bytes 18440 | tf_op jit(solution)/shard_map/ppermute | solution.py:559
  126.2 7.0 %collective-permute-start.22 = (f32[2,768]{1,0:T(2,128)S(1)}, f32[2,768]{1,0:T(2,128)S(1)}, u32[]{:S(2)}, u32[]{:S(2)}) collective-permute-start(f32[2,768]{1,0:T(2,128)S(1)} %get-tuple-element.140), channel_id=1, source_target_pairs={{0,1},{1,0},{2,3},{3,2},{4,5},{5,4},{6,7},{7,6},{8,9},{9,8},{10,11... | collective-permute-start | bytes 18440 | tf_op jit(solution)/shard_map/ppermute | solution.py:559
  (34 other events, 219.8 us)

commit v5 on v4

--- a/solution.py
+++ b/solution.py
@@ -17,6 +17,7 @@
 LANES = 256
 DOC = 256
 QB = 128
+PART = 32
 WINDOW = QB + 2 * DOC
 EPSILON = 1e-05
 ROPE_BASE = 160000.0
@@ -60,12 +61,12 @@
     return lax.dot_general(a, b, dims, preferred_element_type=F32)
 
 
-def call(body, ins, outs, scratch=(), scalars=1):
+def call(body, ins, outs, scratch=(), scalars=1, place=pltpu.VMEM):
     name = getattr(body, "func", body).__name__
     specs = [pl.BlockSpec(memory_space=pltpu.SMEM)] * scalars
-    specs += [pl.BlockSpec(memory_space=pltpu.VMEM)] * (len(ins) - scalars)
+    specs += [pl.BlockSpec(memory_space=place)] * (len(ins) - scalars)
     size = sum(math.prod(x.shape) * x.dtype.itemsize for x in (*ins, *outs))
-    held = sum(math.prod(x.shape) * x.dtype.itemsize for x in scratch)
+    held = sum(math.prod(x.shape) * x.dtype.itemsize for x in scratch if hasattr(x.dtype, "itemsize"))
     return pl.pallas_call(
         body,
         name=name,
@@ -192,11 +193,19 @@
     z = s_ref[0]
     head = lane_head(QB)
     column = lax.broadcasted_iota(jnp.int32, (QB, 128), 1)
+
+    def products(i):
+        low, high = static_window(i)
+        block = q_ref[i * QB : (i + 1) * QB, :] * jnp.asarray(1.0 / math.sqrt(HEAD), BF16)
+        return dot(by_head(block, head), k_ref[low:high, :], NT)
+
+    ahead = products(0)
     for i in range(LEN // QB):
         low, high = static_window(i)
         rows = slice(i * QB, (i + 1) * QB)
-        stacked = by_head(q_ref[rows, :] * jnp.asarray(1.0 / math.sqrt(HEAD), BF16), head)
-        scores = dot(stacked, k_ref[low:high, :], NT)
+        scores = ahead
+        if (i + 1) * QB < LEN:
+            ahead = products(i + 1)
         same = segc_ref[rows, 0:1] == seg_ref[0:1, low:high].astype(F32)
         parts, logs = [], []
         for h in range(HEADS_HERE):
@@ -381,20 +390,51 @@
         out[:, out.shape[1] - COLS :] = total[:, first : first + COLS].astype(BF16)
 
 
-def pack_kernel(s_ref, w_in_ref, w_down_ref, w_out_ref, out_ref, ff_ref, whole_ref):
+def pack_kernel(s_ref, w_in_ref, w_down_ref, w_out_ref, out_ref, ff_ref, sems, out_sems):
     slot = s_ref[1]
-    there, cols = slot // 2, pl.ds(pl.multiple_of((slot % 2) * (D // 2), 128), D // 2)
-    n_in, n_down = w_in_ref.shape[0], w_down_ref.shape[0]
-    whole_ref[:n_in, :] = w_in_ref[...]
-    whole_ref[n_in : n_in + n_down, :] = w_down_ref[...]
-    whole_ref[n_in + n_down :, :] = jnp.zeros((whole_ref.shape[0] - n_in - n_down, D), BF16)
-    rows = whole_ref.shape[0] // 4
-    few = w_out_ref.shape[0] // 4
+    cols = pl.ds(pl.multiple_of((slot % 2) * (D // 2), 128), D // 2)
+    few = out_ref.shape[0] // 2
     here = pl.ds(pl.multiple_of(slot % 4 * few, 16), few)
-    ff_ref[...] = whole_ref[pl.ds(pl.multiple_of(there * rows, 16), rows), cols]
-    for side in range(2):
-        mine = w_out_ref[here, side * (D // 2) : (side + 1) * (D // 2)]
-        out_ref[side * few : (side + 1) * few, :] = mine
+    copies = [
+        pltpu.make_async_copy(
+            w_out_ref.at[here, side * (D // 2) : (side + 1) * (D // 2)],
+            out_ref.at[side * few : (side + 1) * few, :],
+            out_sems.at[side],
+        )
+        for side in range(2)
+    ]
+    for copy in copies:
+        copy.start()
+    n_in, n_down = w_in_ref.shape[0] // PART, w_down_ref.shape[0] // PART
+    parts = ff_ref.shape[0] // PART
+    for i in range(parts):
+        at = (slot // 2) * parts + i
+        there = ff_ref.at[i * PART : (i + 1) * PART, :]
+
+        def fetch(ref, first):
+            rows = pl.ds(pl.multiple_of((at - first) * PART, PART), PART)
+            return pltpu.make_async_copy(ref.at[rows, cols], there, sems.at[i])
+
+        @pl.when(at < n_in)
+        def _():
+            fetch(w_in_ref, 0).start()
+
+        @pl.when((at >= n_in) & (at < n_in + n_down))
+        def _():
+            fetch(w_down_ref, n_in).start()
+
+        @pl.when(at >= n_in + n_down)
+        def _():
+            there[...] = jnp.zeros(there.shape, BF16)
+
+    for copy in copies:
+        copy.wait()
+    for i in range(parts):
+        there = ff_ref.at[i * PART : (i + 1) * PART, :]
+
+        @pl.when((slot // 2) * parts + i < n_in + n_down)
+        def _():
+            pltpu.make_async_copy(w_in_ref.at[:PART, : D // 2], there, sems.at[i]).wait()
 
 
 def arrived_kernel(s_ref, f1, f2, f3, out_ref):
@@ -414,7 +454,8 @@
     last = LEN // QB - 1
     head = lane_head(QB)
     scale = jnp.asarray(1.0 / math.sqrt(HEAD), BF16)
-    for step in steps:
+
+    def products(step):
         low, high = static_window(step)
         i = jnp.where(mirror == 1, last - step, step)
         rows = pl.ds(pl.multiple_of(i * QB, QB), QB)
@@ -424,6 +465,13 @@
         upstream = by_head(back_ref[rows, :], head)
         scores = dot(stacked, k_ref[keys, :], NT)
         prob_back = dot(upstream, v_ref[keys, :], NT)
+        return rows, keys, stacked, upstream, scores, prob_back
+
+    ahead = products(steps[0])
+    for step in steps:
+        rows, keys, stacked, upstream, scores, prob_back = ahead
+        if step + 1 in steps:
+            ahead = products(step + 1)
         same = segc_ref[rows, 0:1] == seg_ref[0:1, keys].astype(F32)
         probs, grads = [], []
         for h in range(HEADS_HERE):
@@ -434,8 +482,8 @@
             grads.append((prob * (prob_back[at] - inner)).astype(BF16))
         prob = jnp.concatenate(probs, axis=0)
         grad = jnp.concatenate(grads, axis=0)
-        dv_ref[keys, :] += dot(prob, upstream, TN)
-        dk_ref[keys, :] += dot(grad, stacked, TN)
+        dv_ref[:, keys] += dot(upstream, prob, TN)
+        dk_ref[:, keys] += dot(stacked, grad, TN)
         dq_ref[rows, :] = merge_heads(dot(grad, k_ref[keys, :]), head) * (1.0 / math.sqrt(HEAD))
 
 
@@ -444,7 +492,7 @@
     trig = trig_ref[rows, :]
     total = None
     for part, grad_ref in enumerate((dq_ref, dk_ref, dv_ref)):
-        g = grad_ref[rows, :]
+        g = jnp.transpose(grad_ref[:, rows]) if part else grad_ref[rows, :]
         if part < 2:
             g = turn(g, trig, -1.0)
         low = g[:, :COLS].astype(BF16)
@@ -543,11 +591,14 @@
             out_ref[i] = jnp.concatenate(lines, axis=0).astype(BF16)
 
 
-def final_kernel(s_ref, tok_ref, gain_ref, back_ref, n0, n1, n2, out_ref):
+def final_kernel(
+    s_ref, tok_ref, gain_ref, back_ref, n0, n1, n2, own_ref, branch_ref, out_ref, layer_ref
+):
     upstream = n0[...] + n1[...].astype(F32) + n2[...].astype(F32)
     rows = pl.ds(pl.multiple_of(s_ref[0] * BLOCK, BLOCK), BLOCK)
     unit, inverse = normalize(tok_ref[rows, :].astype(F32))
     out_ref[...] = back_ref[...] + norm_back(upstream, unit, inverse, gain_ref[...])
+    layer_ref[...] = (own_ref[...] + branch_ref[...].astype(F32)).astype(BF16)
 
 
 def fold_kernel(even_ref, recv_ref, own_ref, s1_ref, s2_ref, s3_ref):
@@ -605,9 +656,10 @@
     if plane:
         slot_out, slot_ff = call(
             pack_kernel,
-            (scalars, w_in, down_weight, output_weight),
+            (scalars, *(pltpu.with_memory_space_constraint(w, pltpu.HBM) for w in (w_in, down_weight, output_weight))),
             (sds((2 * few, D // 2), BF16), sds((many, D // 2), BF16)),
-            [pltpu.VMEM((padded, D), BF16)],
+            [pltpu.SemaphoreType.DMA((many // PART,)), pltpu.SemaphoreType.DMA((2,))],
+            place=pltpu.HBM,
         )
         out_fetched = [along_narrow(slot_out, k) for k in (1, 2, 3)]
         ff_fetched = along_narrow(slot_ff, 2)
@@ -715,11 +767,12 @@
         now = tie(scalars, even_part)
 
     rows_f32 = sds((LEN, LANES), F32)
+    columns_f32 = sds((LANES, LEN), F32)
     pair_qkv = sds((2 * BLOCK, 3 * COLS), BF16)
     n2, n3, qkv_far, back_rows, *grads = call(
         backward_far_kernel,
         (now, segments, segc, q, k, v, lse, trig, *upstream, w_qkv),
-        (own, own_low, pair_qkv, wide_rows, rows_f32, rows_f32, rows_f32),
+        (own, own_low, pair_qkv, wide_rows, rows_f32, columns_f32, columns_f32),
     )
     exchanged = along_narrow(n3, 1)
     branch_recv = along_narrow(tie(out_send, upstream[1], *grad_sends), 1)
@@ -727,7 +780,7 @@
         backward_near_kernel,
         (scalars, segments, segc, q, k, v, lse, trig, back_rows, *grads, w_qkv),
         (own, own_low, pair_qkv),
-        [pltpu.VMEM((LEN, LANES), F32)] * 3,
+        [pltpu.VMEM((LEN, LANES), F32)] + [pltpu.VMEM((LANES, LEN), F32)] * 2,
     )
     (qkv_part,) = call(
         qkv_grad_kernel,
@@ -752,10 +805,10 @@
         scalars=0,
     )
     there = [along_narrow(x, k) for k, x in zip((1, 2, 3), there)]
-    (tokens_grad,) = call(
+    tokens_grad, layer_out = call(
         final_kernel,
-        (scalars, tokens, gain_one, back, n0, near_recv, far_recv),
-        (own,),
+        (scalars, tokens, gain_one, back, n0, near_recv, far_recv, out_keep, branch_recv),
+        (own, own_low),
     )
     gains = gains + along_narrow(gains, 1) + along_narrow(gains, 2) + along_narrow(gains, 3)
     geglu_grad, down_grad, out_grad = call(
@@ -765,7 +818,6 @@
         [pltpu.VMEM((128, -(-hidden // 128) * 128), F32)],
         scalars=0,
     )
-    layer_out = (out_keep + branch_recv.astype(F32)).astype(BF16)
     return (
         layer_out, tokens_grad, gains[0], qkv_grad, out_grad, gains[1], geglu_grad, down_grad,
     )

time: 134 us -> 131 us (0.978)
  other arithmetic: 1.9 us -> 0.09 us
  waiting for transfers between devices: 31.7 us -> 30.2 us
    convert_element_type x1 -> x0, other arithmetic: 1.81 us -> none  [per_device(): layer_out = (out_keep + branch_recv.astype(F32)).astype(BF16)]
    ppermute x21, waiting for transfers between devices: 31.7 us -> 30.2 us  [along_narrow(): return lax.ppermute(x, 'narrow', [(i, i ^ k) for i in range(NARROW)])]
    unnamed x68 -> x62, local copies, waits for them, and re-layouts: 4.27 us -> 3.52 us
  transfers between devices with their start and end apart: 32 -> 32, of which waited for: 8 -> 8; matrix products, arithmetic and copies ran while one was open for 1% -> 0% of each run, Pallas kernels for 32% -> 33%
where the time goes in v5:
time: 131 us
  Pallas kernels  50.4 us (38%)
  starting transfers between devices  44.8 us (34%)
  waiting for transfers between devices  30.2 us (23%)
  local copies, waits for them, and re-layouts  4.14 us (3%)
    pallas_call x21, Pallas kernels, call(): pl.pallas_call(body, name=name, out_shape=tuple((jax.ShapeDtypeStruct(o.s...  50.4 us
    ppermute x21, starting transfers between devices, along_narrow(): return lax.ppermute(x, 'narrow', [(i, i ^ k) for i in range(NARROW)])  32.5 us
    ppermute x21, waiting for transfers between devices, along_narrow(): return lax.ppermute(x, 'narrow', [(i, i ^ k) for i in range(NARROW)])  30.2 us
    ppermute x10, starting transfers between devices, along_wide(): lax.ppermute(x, 'wide', [(i, i ^ k) for i in range(lax.axis_size('wide'))])  8.82 us
    all_to_all x1, starting transfers between devices, per_device(): lax.all_to_all(qkv_part, 'wide', 0, 0)  3.56 us
    unnamed x62, local copies, waits for them, and re-layouts  3.52 us
  transfers between devices with their start and end apart: 32, of which 8 were waited for; matrix products, arithmetic and copies ran while one was open for 0% of the time, Pallas kernels for 33%

profile of v5, /device:TPU:0, one launch (start us, length us, event | category | flops | bytes accessed | tf_op | source)
XLA Modules:
  0.0 130.9 jit_solution(18095772661990182667)
XLA Ops:
  0.7 1.7 %pack_kernel.1 = (bf16[96,384]{1,0:T(8,128)(2,1)S(1)}, bf16[224,384]{1,0:T(8,128)(2,1)S(1)}) custom-call(s32[2]{0:T(128)S(1)} %pad_add_fusion.s_ref, bf16[576,768]{1,0:T(8,128)(2,1)} %bitcast.10, bf16[288,768]{1,0:T(8,128)(2,1)} %dw_ref.5, bf16[192,768]{1,0:T(8,128)(2,1)} %w_ref.3), custom_call_target="tpu_custom_call" | custom-call | flops 1000000000 | bytes 1867784 | tf_op jit(solution)/shard_map/pack_kernel/pallas_call | solution.py:70
  2.5 5.1 %collective-permute-start.5 = (bf16[96,384]{1,0:T(8,128)(2,1)S(1)}, bf16[96,384]{1,0:T(8,128)(2,1)S(1)}, u32[]{:S(2)}, u32[]{:S(2)}) collective-permute-start(bf16[96,384]{1,0:T(8,128)(2,1)S(1)} %get-tuple-element.96), channel_id=1, source_target_pairs={{0,3},{1,2},{2,1},{3,0},{4,7},{5,6},{6,5},{7,4},{8,11},{9,10},{10,... | collective-permute-start | bytes 221192 | tf_op jit(solution)/shard_map/ppermute | solution.py:610
  8.2 2.3 %collective-permute-start.8 = (bf16[224,384]{1,0:T(8,128)(2,1)S(1)}, bf16[224,384]{1,0:T(8,128)(2,1)S(1)}, u32[]{:S(2)}, u32[]{:S(2)}) collective-permute-start(bf16[224,384]{1,0:T(8,128)(2,1)S(1)} %get-tuple-element.101), channel_id=1, source_target_pairs={{0,2},{1,3},{2,0},{3,1},{4,6},{5,7},{6,4},{7,5},{8,10},{9,11},{10,... | collective-permute-start | bytes 516104 | tf_op jit(solution)/shard_map/ppermute | solution.py:610
  10.6 3.2 %project_kernel.1 = (bf16[1024,256]{1,0:T(8,128)(2,1)S(1)}, bf16[1024,256]{1,0:T(8,128)(2,1)S(1)}, bf16[1024,256]{1,0:T(8,128)(2,1)S(1)}, bf16[1024,768]{1,0:T(8...) custom-call(bf16[1024,768]{1,0:T(8,128)(2,1)S(1)} %copy-done.5, s32[1,1024]{1,0:T(1,128)S(1)} %copy-done.10, ...), custom_call_target="tpu_custom_call" | custom-call | flops 6000000000 | bytes 7445504 | tf_op jit(solution)/shard_map/project_kernel/pallas_call | solution.py:70
  13.8 4.3 %attend_kernel.1 = (bf16[256,384]{1,0:T(8,128)(2,1)S(1)}, bf16[256,384]{1,0:T(8,128)(2,1)S(1)}, bf16[256,384]{1,0:T(8,128)(2,1)S(1)}, bf16[256,384]{1,0:T(8,128)(2,1)S(1)}, f32[1024,128]{1,0:T(8,128)S(1)}) custom-call(s32[2]{0:T(128)S(1)} %pad_add_fusion.s_ref, s32[1,1024]{1,0:T(1,128)S(1)} %copy-done.10, f32[1024,128]{1,0:T(8,128)S(1)} %get-tuple-element.82.segc_ref, ...), custom_call_target="tpu_custom_call" | custom-call | flops 99999997952 | bytes 3411976 | tf_op jit(solution)/shard_map/attend_kernel/pallas_call | solution.py:70
  18.8 1.6 %collective-permute-start.6 = (bf16[288,384]{1,0:T(8,128)(2,1)S(1)}, bf16[288,384]{1,0:T(8,128)(2,1)S(1)}, u32[]{:S(2)}, u32[]{:S(2)}) collective-permute-start(bf16[288,384]{1,0:T(8,128)(2,1)S(1)} %arrived_kernel.1.a0), channel_id=1, source_target_pairs={{0,8},{4,12},{8,0},{12,4},{16,24},{20,28},{24,16},{28,20},{1,9},{5... | collective-permute-start | bytes 663560 | tf_op jit(solution)/shard_map/ppermute | solution.py:614
  21.2 1.5 %collective-permute-start.9 = (bf16[224,384]{1,0:T(8,128)(2,1)S(1)}, bf16[224,384]{1,0:T(8,128)(2,1)S(1)}, u32[]{:S(2)}, u32[]{:S(2)}) collective-permute-start(bf16[224,384]{1,0:T(8,128)(2,1)S(1)} %collective-permute-done.8.a0), channel_id=1, source_target_pairs={{0,16},{4,20},{8,24},{12,28},{16,0},{20,4},{24,8},{28,12},{1,17},{... | collective-permute-start | bytes 516104 | tf_op jit(solution)/shard_map/ppermute | solution.py:614
  23.9 2.1 %collective-permute-start.1 = (bf16[256,384]{1,0:T(8,128)(2,1)S(1)}, bf16[256,384]{1,0:T(8,128)(2,1)S(1)}, u32[]{:S(2)}, u32[]{:S(2)}) collective-permute-start(bf16[256,384]{1,0:T(8,128)(2,1)S(1)} %get-tuple-element.88), channel_id=1, source_target_pairs={{0,2},{1,3},{2,0},{3,1},{4,6},{5,7},{6,4},{7,5},{8,10},{9,11},{10,... | collective-permute-start | bytes 589832 | tf_op jit(solution)/shard_map/ppermute | solution.py:610
  28.4 1.5 %collective-permute-start.10 = (bf16[2,224,384]{2,1,0:T(8,128)(2,1)S(1)}, bf16[2,224,384]{2,1,0:T(8,128)(2,1)S(1)}, u32[]{:S(2)}, u32[]{:S(2)}) collective-permute-start(bf16[2,224,384]{2,1,0:T(8,128)(2,1)S(1)} %pair_kernel.3.f0), channel_id=1, source_target_pairs={{0,8},{4,12},{8,0},{12,4},{16,24},{20,28},{24,16},{28,20},{1,9},{5... | collective-permute-start | bytes 1032200 | tf_op jit(solution)/shard_map/ppermute | solution.py:614
  30.0 1.8 %collective-permute-done.c1 = bf16[256,384]{1,0:T(8,128)(2,1)S(1)} collective-permute-done((bf16[256,384]{1,0:T(8,128)(2,1)S(1)}, bf16[256,384]{1,0:T(8,128)(2,1)S(1)}, u32[]{:S(2)}, u32[]{:S(2)}) %collective-permute-start) | collective-permute-done | bytes 196640 | tf_op jit(solution)/shard_map/ppermute | solution.py:610
  31.7 8.6 %collective-permute-done.1.c2 = bf16[256,384]{1,0:T(8,128)(2,1)S(1)} collective-permute-done((bf16[256,384]{1,0:T(8,128)(2,1)S(1)}, bf16[256,384]{1,0:T(8,128)(2,1)S(1)}, u32[]{:S(2)}, u32[]{:S(2)}) %collective-permute-start.1) | collective-permute-done | bytes 196640 | tf_op jit(solution)/shard_map/ppermute | solution.py:610
  42.3 3.4 %middle_kernel.1 = (f32[256,768]{1,0:T(8,128)S(1)}, bf16[512,768]{1,0:T(8,128)(2,1)S(1)}, bf16[256,288]{1,0:T(8,128)(2,1)S(1)}, bf16[256,576]{1,0:T(8,128)(2,1)S...) custom-call(s32[2]{0:T(128)S(1)} %pad_add_fusion.s_ref, ...), custom_call_target="tpu_custom_call" | custom-call | flops 5000000000 | bytes 10816520 | tf_op jit(solution)/shard_map/middle_kernel/pallas_call | solution.py:70
  45.7 3.0 %partner_kernel.1 = (bf16[256,288]{1,0:T(8,128)(2,1)S(1)}, bf16[256,576]{1,0:T(8,128)(2,1)S(1)}, bf16[256,768]{1,0:T(8,128)(2,1)}, bf16[256,768]{1,0:T(8,128)(2,1)S(1)}, bf16[896,768]{1,0:T(8,128)(2,1)S(1)}) custom-call(s32[2]{0:T(128)S(1)} %pad_add_fusion.s_ref, bf16[512,768]{1,0:T(8,128)(2,1)S(1)} %get-tuple-element.97.normed_ref, ...), custom_call_target="tpu_custom_call" | custom-call | flops 3000000000 | bytes 7127048 | tf_op jit(solution)/shard_map/partner_kernel/pallas_call | solution.py:70
  48.7 2.7 %collective-permute-start.13 = (bf16[256,768]{1,0:T(8,128)(2,1)S(1)}, bf16[256,768]{1,0:T(8,128)(2,1)S(1)}, u32[]{:S(2)}, u32[]{:S(2)}) collective-permute-start(bf16[256,768]{1,0:T(8,128)(2,1)S(1)} %get-tuple-element.109), channel_id=1, source_target_pairs={{0,1},{1,0},{2,3},{3,2},{4,5},{5,4},{6,7},{7,6},{8,9},{9,8},{10,11... | collective-permute-start | bytes 1179656 | tf_op jit(solution)/shard_map/ppermute | solution.py:610
  51.3 5.7 %own_kernel.1 = (f32[256,768]{1,0:T(8,128)S(1)}, f32[256,768]{1,0:T(8,128)S(1)}, bf16[768,1792]{1,0:T(8,128)(2,1)S(1)}) custom-call(s32[2]{0:T(128)S(1)} %pad_add_fusion.s_ref, bf16[512,768]{1,0:T(8,128)(2,1)S(1)} %get-tuple-element.97.normed_ref, bf16[512,768]{1,0:T(8,128)(2,1)S(1)} %get-tuple-element.92.cot_ref, ...), custom_call_target="tpu_custom_call" | custom-call | flops 10000000000 | bytes 10862600 | tf_op jit(solution)/shard_map/own_kernel/pallas_call | solution.py:70
  57.0 3.7 %collective-permute-done.13.recv_ref = bf16[256,768]{1,0:T(8,128)(2,1)S(1)} collective-permute-done((bf16[256,768]{1,0:T(8,128)(2,1)S(1)}, bf16[256,768]{1,0:T(8,128)(2,1)S(1)}, u32[]{:S(2)}, u32[]{:S(2)}) %collective-permute-start.13) | collective-permute-done | bytes 393248 | tf_op jit(solution)/shard_map/ppermute | solution.py:610
  63.5 1.8 %collective-permute-start.15 = (bf16[128,384]{1,0:T(8,128)(2,1)S(1)}, bf16[128,384]{1,0:T(8,128)(2,1)S(1)}, u32[]{:S(2)}, u32[]{:S(2)}) collective-permute-start(bf16[128,384]{1,0:T(8,128)(2,1)S(1)} %get-tuple-element.122), channel_id=1, source_target_pairs={{0,1},{1,0},{2,3},{3,2},{4,5},{5,4},{6,7},{7,6},{8,9},{9,8},{10,11... | collective-permute-start | bytes 294920 | tf_op jit(solution)/shard_map/ppermute | solution.py:610
  72.4 1.5 %collective-permute-start.27 = (bf16[96,2560]{1,0:T(8,128)(2,1)}, bf16[96,2560]{1,0:T(8,128)(2,1)}, u32[]{:S(2)}, u32[]{:S(2)}) collective-permute-start(bf16[96,2560]{1,0:T(8,128)(2,1)} %get-tuple-element.119), channel_id=1, source_target_pairs={{0,24},{4,28},{8,16},{12,20},{16,8},{20,12},{24,0},{28,4},{1,25},{... | collective-permute-start | bytes 1474568 | tf_op jit(solution)/shard_map/ppermute | solution.py:614
  73.9 2.2 %collective-permute-done.16.b2 = bf16[128,384]{1,0:T(8,128)(2,1)S(1)} collective-permute-done((bf16[128,384]{1,0:T(8,128)(2,1)S(1)}, bf16[128,384]{1,0:T(8,128)(2,1)S(1)}, u32[]{:S(2)}, u32[]{:S(2)}) %collective-permute-start.16) | collective-permute-done | bytes 98336 | tf_op jit(solution)/shard_map/ppermute | solution.py:610
  76.1 8.0 %backward_far_kernel.1 = (f32[256,768]{1,0:T(8,128)S(1)}, bf16[256,768]{1,0:T(8,128)(2,1)S(1)}, bf16[512,576]{1,0:T(8,128)(2,1)S(1)}, bf16[1024,256]{1,0:T(8,128...) custom-call(s32[2]{0:T(128)S(1)} %pad_add_fusion.s_ref, ...), custom_call_target="tpu_custom_call" | custom-call | flops 99999997952 | bytes 10391560 | tf_op jit(solution)/shard_map/backward_far_kernel/pallas_call | solution.py:70
  84.1 2.1 %collective-permute-start.20 = (bf16[256,768]{1,0:T(8,128)(2,1)S(1)}, bf16[256,768]{1,0:T(8,128)(2,1)S(1)}, u32[]{:S(2)}, u32[]{:S(2)}) collective-permute-start(bf16[256,768]{1,0:T(8,128)(2,1)S(1)} %get-tuple-element.140), channel_id=1, source_target_pairs={{0,1},{1,0},{2,3},{3,2},{4,5},{5,4},{6,7},{7,6},{8,9},{9,8},{10,11... | collective-permute-start | bytes 1179656 | tf_op jit(solution)/shard_map/ppermute | solution.py:610
  86.2 3.7 %backward_near_kernel.1 = (f32[256,768]{1,0:T(8,128)S(1)}, bf16[256,768]{1,0:T(8,128)(2,1)S(1)}, bf16[512,576]{1,0:T(8,128)(2,1)S(1)}) custom-call(s32[2]{0:T(128)S(1)} %pad_add_fusion.s_ref, s32[1,1024]{1,0:T(1,128)S(1)} %copy-done.11, f32[1024,128]{1,0:T(8,128)S(1)} %copy-done.22, bf16[1024,256]{1,0:T(8,128)(2,1)S(1)} %copy-done.16, ...), custom_call_target="tpu_custom_call" | custom-call | flops 99999997952 | bytes 9998344 | tf_op jit(solution)/shard_map/backward_near_kernel/pallas_call | solution.py:70
  90.0 4.0 %qkv_grad_kernel.1 = bf16[8,112,576]{2,1,0:T(8,128)(2,1)} custom-call(s32[2]{0:T(128)S(1)} %pad_add_fusion.s_ref, bf16[1024,768]{1,0:T(8,128)(2,1)S(1)} %get-tuple-element.135.normed_ref, bf16[512,576]{1,0:T(8,128)(2,1)S(1)} %get-tuple-element.136.near_ref, bf16[512,576]{1,0:T(8,128)(2,1)S(1)} %get-tuple-element.137.far_ref, ...), custom_call_target="tpu_custom_call" | custom-call | flops 1000000000 | bytes 4675592 | tf_op jit(solution)/shard_map/qkv_grad_kernel/pallas_call | solution.py:70
  94.0 2.2 %collective-permute-done.20.recv_ref = bf16[256,768]{1,0:T(8,128)(2,1)S(1)} collective-permute-done((bf16[256,768]{1,0:T(8,128)(2,1)S(1)}, bf16[256,768]{1,0:T(8,128)(2,1)S(1)}, u32[]{:S(2)}, u32[]{:S(2)}) %collective-permute-start.20) | collective-permute-done | bytes 393248 | tf_op jit(solution)/shard_map/ppermute | solution.py:610
  96.3 2.8 %collective-permute-start.21 = (bf16[256,768]{1,0:T(8,128)(2,1)S(1)}, bf16[256,768]{1,0:T(8,128)(2,1)S(1)}, u32[]{:S(2)}, u32[]{:S(2)}) collective-permute-start(bf16[256,768]{1,0:T(8,128)(2,1)S(1)} %add_kernel.1), channel_id=1, source_target_pairs={{0,2},{1,3},{2,0},{3,1},{4,6},{5,7},{6,4},{7,5},{8,10},{9,11},{10,... | collective-permute-start | bytes 1179656 | tf_op jit(solution)/shard_map/ppermute | solution.py:610
  99.1 3.6 %all-to-all-start = ((bf16[8,112,576]{2,1,0:T(8,128)(2,1)}), bf16[8,112,576]{2,1,0:T(8,128)(2,1)S(1)}, u32[]{:S(2)}, u32[]{:S(2)}) async-start(bf16[8,112,576]{2,1,0:T(8,128)(2,1)} %qkv_grad_kernel.1), calls=%async_computation | async-start | bytes 2293760 | tf_op jit(solution)/shard_map/all_to_all | solution.py:796
  102.7 8.7 %collective-permute-done.18.n1 = bf16[256,768]{1,0:T(8,128)(2,1)S(1)} collective-permute-done((bf16[256,768]{1,0:T(8,128)(2,1)S(1)}, bf16[256,768]{1,0:T(8,128)(2,1)S(1)}, u32[]{:S(2)}, u32[]{:S(2)}) %collective-permute-start.18) | collective-permute-done | bytes 393248 | tf_op jit(solution)/shard_map/ppermute | solution.py:610
  112.7 1.8 %collect_kernel.1 = (f32[96,1088]{1,0:T(8,128)S(1)}, bf16[96,192]{1,0:T(8,128)(2,1)S(1)}, bf16[96,1088]{1,0:T(8,128)(2,1)S(1)}, bf16[96,192]{1,0:T(8,128)(2,1)S(1)}) custom-call(f32[96,2560]{1,0:T(8,128)S(1)} %copy-done.14, bf16[96,2560]{1,0:T(8,128)(2,1)} %collective-permute-done.25.r1, bf16[96,2560]{1,0:T(8,128)(2,1)} %collective-permute-done.26.r2, ...), custom_call_target="tpu_custom_call" | custom-call | flops 1000000000 | bytes 3158016 | tf_op jit(solution)/shard_map/collect_kernel/pallas_call | solution.py:70
  115.8 2.3 %collective-permute-start.29 = (bf16[96,1088]{1,0:T(8,128)(2,1)S(1)}, bf16[96,1088]{1,0:T(8,128)(2,1)S(1)}, u32[]{:S(2)}, u32[]{:S(2)}) collective-permute-start(bf16[96,1088]{1,0:T(8,128)(2,1)S(1)} %get-tuple-element.151), channel_id=1, source_target_pairs={{0,2},{1,3},{2,0},{3,1},{4,6},{5,7},{6,4},{7,5},{8,10},{9,11},{10,... | collective-permute-start | bytes 626696 | tf_op jit(solution)/shard_map/ppermute | solution.py:610
  119.2 2.6 %final_kernel.1 = (f32[256,768]{1,0:T(8,128)}, bf16[256,768]{1,0:T(8,128)(2,1)}) custom-call(s32[2]{0:T(128)S(1)} %pad_add_fusion.s_ref, bf16[1024,768]{1,0:T(8,128)(2,1)S(1)} %copy-done.6, f32[1,768]{1,0:T(1,128)S(1)} %copy-done.3, f32[256,768]{1,0:T(8,128)S(1)} %copy-done.28, f32[256,768]{1,0:T(8,128)S(1)} %copy-done.26, ...), custom_call_target="tpu_custom_call" | custom-call | flops 99999997952 | bytes 6294536 | tf_op jit(solution)/shard_map/final_kernel/pallas_call | solution.py:70
  125.2 1.9 %collective-permute-start.22 = (f32[2,768]{1,0:T(2,128)S(1)}, f32[2,768]{1,0:T(2,128)S(1)}, u32[]{:S(2)}, u32[]{:S(2)}) collective-permute-start(f32[2,768]{1,0:T(2,128)S(1)} %get-tuple-element.144), channel_id=1, source_target_pairs={{0,1},{1,0},{2,3},{3,2},{4,5},{5,4},{6,7},{7,6},{8,9},{9,8},{10,11... | collective-permute-start | bytes 18440 | tf_op jit(solution)/shard_map/ppermute | solution.py:610
  127.1 2.2 %collective-permute-done.29.r2 = bf16[96,1088]{1,0:T(8,128)(2,1)S(1)} collective-permute-done((bf16[96,1088]{1,0:T(8,128)(2,1)S(1)}, bf16[96,1088]{1,0:T(8,128)(2,1)S(1)}, u32[]{:S(2)}, u32[]{:S(2)}) %collective-permute-start.29) | collective-permute-done | bytes 208928 | tf_op jit(solution)/shard_map/ppermute | solution.py:610
  (120 shorter events, 26.3 us)
Async XLA Ops:
  2.5 15.7 %collective-permute-start.5 = (bf16[96,384]{1,0:T(8,128)(2,1)S(1)}, bf16[96,384]{1,0:T(8,128)(2,1)S(1)}, u32[]{:S(2)}, u32[]{:S(2)}) collective-permute-start(bf16[96,384]{1,0:T(8,128)(2,1)S(1)} %get-tuple-element.96), channel_id=1, source_target_pairs={{0,3},{1,2},{2,1},{3,0},{4,7},{5,6},{6,5},{7,4},{8,11},{9,10},{10,... | collective-permute-start | bytes 221192 | tf_op jit(solution)/shard_map/ppermute | solution.py:610
  7.6 10.6 %collective-permute-start.4 = (bf16[96,384]{1,0:T(8,128)(2,1)S(1)}, bf16[96,384]{1,0:T(8,128)(2,1)S(1)}, u32[]{:S(2)}, u32[]{:S(2)}) collective-permute-start(bf16[96,384]{1,0:T(8,128)(2,1)S(1)} %get-tuple-element.96), channel_id=1, source_target_pairs={{0,2},{1,3},{2,0},{3,1},{4,6},{5,7},{6,4},{7,5},{8,10},{9,11},{10,... | collective-permute-start | bytes 221192 | tf_op jit(solution)/shard_map/ppermute | solution.py:610
  7.6 10.6 %collective-permute-start.3 = (bf16[96,384]{1,0:T(8,128)(2,1)S(1)}, bf16[96,384]{1,0:T(8,128)(2,1)S(1)}, u32[]{:S(2)}, u32[]{:S(2)}) collective-permute-start(bf16[96,384]{1,0:T(8,128)(2,1)S(1)} %get-tuple-element.96), channel_id=1, source_target_pairs={{0,1},{1,0},{2,3},{3,2},{4,5},{5,4},{6,7},{7,6},{8,9},{9,8},{10,11... | collective-permute-start | bytes 221192 | tf_op jit(solution)/shard_map/ppermute | solution.py:610
  8.2 12.9 %collective-permute-start.8 = (bf16[224,384]{1,0:T(8,128)(2,1)S(1)}, bf16[224,384]{1,0:T(8,128)(2,1)S(1)}, u32[]{:S(2)}, u32[]{:S(2)}) collective-permute-start(bf16[224,384]{1,0:T(8,128)(2,1)S(1)} %get-tuple-element.101), channel_id=1, source_target_pairs={{0,2},{1,3},{2,0},{3,1},{4,6},{5,7},{6,4},{7,5},{8,10},{9,11},{10,... | collective-permute-start | bytes 516104 | tf_op jit(solution)/shard_map/ppermute | solution.py:610
  18.8 8.3 %collective-permute-start.6 = (bf16[288,384]{1,0:T(8,128)(2,1)S(1)}, bf16[288,384]{1,0:T(8,128)(2,1)S(1)}, u32[]{:S(2)}, u32[]{:S(2)}) collective-permute-start(bf16[288,384]{1,0:T(8,128)(2,1)S(1)} %arrived_kernel.1.a0), channel_id=1, source_target_pairs={{0,8},{4,12},{8,0},{12,4},{16,24},{20,28},{24,16},{28,20},{1,9},{5... | collective-permute-start | bytes 663560 | tf_op jit(solution)/shard_map/ppermute | solution.py:614
  21.2 6.6 %collective-permute-start.9 = (bf16[224,384]{1,0:T(8,128)(2,1)S(1)}, bf16[224,384]{1,0:T(8,128)(2,1)S(1)}, u32[]{:S(2)}, u32[]{:S(2)}) collective-permute-start(bf16[224,384]{1,0:T(8,128)(2,1)S(1)} %collective-permute-done.8.a0), channel_id=1, source_target_pairs={{0,16},{4,20},{8,24},{12,28},{16,0},{20,4},{24,8},{28,12},{1,17},{... | collective-permute-start | bytes 516104 | tf_op jit(solution)/shard_map/ppermute | solution.py:614
  22.7 9.0 %collective-permute-start = (bf16[256,384]{1,0:T(8,128)(2,1)S(1)}, bf16[256,384]{1,0:T(8,128)(2,1)S(1)}, u32[]{:S(2)}, u32[]{:S(2)}) collective-permute-start(bf16[256,384]{1,0:T(8,128)(2,1)S(1)} %get-tuple-element.87), channel_id=1, source_target_pairs={{0,1},{1,0},{2,3},{3,2},{4,5},{5,4},{6,7},{7,6},{8,9},{9,8},{10,11... | collective-permute-start | bytes 589832 | tf_op jit(solution)/shard_map/ppermute | solution.py:610
  23.9 16.5 %collective-permute-start.1 = (bf16[256,384]{1,0:T(8,128)(2,1)S(1)}, bf16[256,384]{1,0:T(8,128)(2,1)S(1)}, u32[]{:S(2)}, u32[]{:S(2)}) collective-permute-start(bf16[256,384]{1,0:T(8,128)(2,1)S(1)} %get-tuple-element.88), channel_id=1, source_target_pairs={{0,2},{1,3},{2,0},{3,1},{4,6},{5,7},{6,4},{7,5},{8,10},{9,11},{10,... | collective-permute-start | bytes 589832 | tf_op jit(solution)/shard_map/ppermute | solution.py:610
  26.0 14.4 %collective-permute-start.2 = (bf16[256,384]{1,0:T(8,128)(2,1)S(1)}, bf16[256,384]{1,0:T(8,128)(2,1)S(1)}, u32[]{:S(2)}, u32[]{:S(2)}) collective-permute-start(bf16[256,384]{1,0:T(8,128)(2,1)S(1)} %get-tuple-element.89), channel_id=1, source_target_pairs={{0,3},{1,2},{2,1},{3,0},{4,7},{5,6},{6,5},{7,4},{8,11},{9,10},{10,... | collective-permute-start | bytes 589832 | tf_op jit(solution)/shard_map/ppermute | solution.py:610
  27.7 14.6 %collective-permute-start.7 = (bf16[2,288,384]{2,1,0:T(8,128)(2,1)S(1)}, bf16[2,288,384]{2,1,0:T(8,128)(2,1)S(1)}, u32[]{:S(2)}, u32[]{:S(2)}) collective-permute-start(bf16[2,288,384]{2,1,0:T(8,128)(2,1)S(1)} %pair_kernel.2.here_ref), channel_id=1, source_target_pairs={{0,4},{4,0},{8,12},{12,8},{16,20},{20,16},{24,28},{28,24},{1,5},{5... | collective-permute-start | bytes 1327112 | tf_op jit(solution)/shard_map/ppermute | solution.py:614
  28.4 13.4 %collective-permute-start.10 = (bf16[2,224,384]{2,1,0:T(8,128)(2,1)S(1)}, bf16[2,224,384]{2,1,0:T(8,128)(2,1)S(1)}, u32[]{:S(2)}, u32[]{:S(2)}) collective-permute-start(bf16[2,224,384]{2,1,0:T(8,128)(2,1)S(1)} %pair_kernel.3.f0), channel_id=1, source_target_pairs={{0,8},{4,12},{8,0},{12,4},{16,24},{20,28},{24,16},{28,20},{1,9},{5... | collective-permute-start | bytes 1032200 | tf_op jit(solution)/shard_map/ppermute | solution.py:614
  41.7 4.0 %collective-permute-start.11 = (bf16[2,224,384]{2,1,0:T(8,128)(2,1)S(1)}, bf16[2,224,384]{2,1,0:T(8,128)(2,1)S(1)}, u32[]{:S(2)}, u32[]{:S(2)}) collective-permute-start(bf16[2,224,384]{2,1,0:T(8,128)(2,1)S(1)} %pair_kernel.3.f0), channel_id=1, source_target_pairs={{0,4},{4,0},{8,12},{12,8},{16,20},{20,16},{24,28},{28,24},{1,5},{5... | collective-permute-start | bytes 1032200 | tf_op jit(solution)/shard_map/ppermute | solution.py:614
  41.8 3.9 %collective-permute-start.12 = (bf16[2,224,384]{2,1,0:T(8,128)(2,1)S(1)}, bf16[2,224,384]{2,1,0:T(8,128)(2,1)S(1)}, u32[]{:S(2)}, u32[]{:S(2)}) collective-permute-start(bf16[2,224,384]{2,1,0:T(8,128)(2,1)S(1)} %collective-permute-done.10.f1), channel_id=1, source_target_pairs={{0,4},{4,0},{8,12},{12,8},{16,20},{20,16},{24,28},{28,24},{1,5},{5... | collective-permute-start | bytes 1032200 | tf_op jit(solution)/shard_map/ppermute | solution.py:614
  48.7 12.0 %collective-permute-start.13 = (bf16[256,768]{1,0:T(8,128)(2,1)S(1)}, bf16[256,768]{1,0:T(8,128)(2,1)S(1)}, u32[]{:S(2)}, u32[]{:S(2)}) collective-permute-start(bf16[256,768]{1,0:T(8,128)(2,1)S(1)} %get-tuple-element.109), channel_id=1, source_target_pairs={{0,1},{1,0},{2,3},{3,2},{4,5},{5,4},{6,7},{7,6},{8,9},{9,8},{10,11... | collective-permute-start | bytes 1179656 | tf_op jit(solution)/shard_map/ppermute | solution.py:610
  63.4 4.5 %collective-permute-start.14 = (bf16[4,96,2560]{2,1,0:T(8,128)(2,1)S(1)}, bf16[4,96,2560]{2,1,0:T(8,128)(2,1)S(1)}, u32[]{:S(2)}, u32[]{:S(2)}) collective-permute-start(bf16[4,96,2560]{2,1,0:T(8,128)(2,1)S(1)} %get-tuple-element.116), channel_id=1, source_target_pairs={{0,4},{4,0},{8,12},{12,8},{16,20},{20,16},{24,28},{28,24},{1,5},{5... | collective-permute-start | bytes 5898248 | tf_op jit(solution)/shard_map/ppermute | solution.py:614
  63.5 8.8 %collective-permute-start.15 = (bf16[128,384]{1,0:T(8,128)(2,1)S(1)}, bf16[128,384]{1,0:T(8,128)(2,1)S(1)}, u32[]{:S(2)}, u32[]{:S(2)}) collective-permute-start(bf16[128,384]{1,0:T(8,128)(2,1)S(1)} %get-tuple-element.122), channel_id=1, source_target_pairs={{0,1},{1,0},{2,3},{3,2},{4,5},{5,4},{6,7},{7,6},{8,9},{9,8},{10,11... | collective-permute-start | bytes 294920 | tf_op jit(solution)/shard_map/ppermute | solution.py:610
  65.3 10.8 %collective-permute-start.16 = (bf16[128,384]{1,0:T(8,128)(2,1)S(1)}, bf16[128,384]{1,0:T(8,128)(2,1)S(1)}, u32[]{:S(2)}, u32[]{:S(2)}) collective-permute-start(bf16[128,384]{1,0:T(8,128)(2,1)S(1)} %get-tuple-element.123), channel_id=1, source_target_pairs={{0,2},{1,3},{2,0},{3,1},{4,6},{5,7},{6,4},{7,5},{8,10},{9,11},{10,... | collective-permute-start | bytes 294920 | tf_op jit(solution)/shard_map/ppermute | solution.py:610
  66.5 9.6 %collective-permute-start.17 = (bf16[128,384]{1,0:T(8,128)(2,1)S(1)}, bf16[128,384]{1,0:T(8,128)(2,1)S(1)}, u32[]{:S(2)}, u32[]{:S(2)}) collective-permute-start(bf16[128,384]{1,0:T(8,128)(2,1)S(1)} %get-tuple-element.124), channel_id=1, source_target_pairs={{0,3},{1,2},{2,1},{3,0},{4,7},{5,6},{6,5},{7,4},{8,11},{9,10},{10,... | collective-permute-start | bytes 294920 | tf_op jit(solution)/shard_map/ppermute | solution.py:610
  70.4 41.0 %collective-permute-start.25 = (bf16[96,2560]{1,0:T(8,128)(2,1)}, bf16[96,2560]{1,0:T(8,128)(2,1)}, u32[]{:S(2)}, u32[]{:S(2)}) collective-permute-start(bf16[96,2560]{1,0:T(8,128)(2,1)} %get-tuple-element.117), channel_id=1, source_target_pairs={{0,8},{4,12},{8,0},{12,4},{16,24},{20,28},{24,16},{28,20},{1,9},{5... | collective-permute-start | bytes 1474568 | tf_op jit(solution)/shard_map/ppermute | solution.py:614
  71.9 39.5 %collective-permute-start.26 = (bf16[96,2560]{1,0:T(8,128)(2,1)}, bf16[96,2560]{1,0:T(8,128)(2,1)}, u32[]{:S(2)}, u32[]{:S(2)}) collective-permute-start(bf16[96,2560]{1,0:T(8,128)(2,1)} %get-tuple-element.118), channel_id=1, source_target_pairs={{0,16},{4,20},{8,24},{12,28},{16,0},{20,4},{24,8},{28,12},{1,17},{... | collective-permute-start | bytes 1474568 | tf_op jit(solution)/shard_map/ppermute | solution.py:614
  72.4 39.0 %collective-permute-start.27 = (bf16[96,2560]{1,0:T(8,128)(2,1)}, bf16[96,2560]{1,0:T(8,128)(2,1)}, u32[]{:S(2)}, u32[]{:S(2)}) collective-permute-start(bf16[96,2560]{1,0:T(8,128)(2,1)} %get-tuple-element.119), channel_id=1, source_target_pairs={{0,24},{4,28},{8,16},{12,20},{16,8},{20,12},{24,0},{28,4},{1,25},{... | collective-permute-start | bytes 1474568 | tf_op jit(solution)/shard_map/ppermute | solution.py:614
  76.1 13.8 %collective-permute-start.19 = (bf16[256,768]{1,0:T(8,128)(2,1)}, bf16[256,768]{1,0:T(8,128)(2,1)}, u32[]{:S(2)}, u32[]{:S(2)}) collective-permute-start(bf16[256,768]{1,0:T(8,128)(2,1)} %get-tuple-element.133), channel_id=1, source_target_pairs={{0,1},{1,0},{2,3},{3,2},{4,5},{5,4},{6,7},{7,6},{8,9},{9,8},{10,11... | collective-permute-start | bytes 1179656 | tf_op jit(solution)/shard_map/ppermute | solution.py:610
  84.1 12.1 %collective-permute-start.20 = (bf16[256,768]{1,0:T(8,128)(2,1)S(1)}, bf16[256,768]{1,0:T(8,128)(2,1)S(1)}, u32[]{:S(2)}, u32[]{:S(2)}) collective-permute-start(bf16[256,768]{1,0:T(8,128)(2,1)S(1)} %get-tuple-element.140), channel_id=1, source_target_pairs={{0,1},{1,0},{2,3},{3,2},{4,5},{5,4},{6,7},{7,6},{8,9},{9,8},{10,11... | collective-permute-start | bytes 1179656 | tf_op jit(solution)/shard_map/ppermute | solution.py:610
  89.9 21.4 %collective-permute-start.18 = (bf16[256,768]{1,0:T(8,128)(2,1)S(1)}, bf16[256,768]{1,0:T(8,128)(2,1)S(1)}, u32[]{:S(2)}, u32[]{:S(2)}) collective-permute-start(bf16[256,768]{1,0:T(8,128)(2,1)S(1)} %get-tuple-element.130), channel_id=1, source_target_pairs={{0,1},{1,0},{2,3},{3,2},{4,5},{5,4},{6,7},{7,6},{8,9},{9,8},{10,11... | collective-permute-start | bytes 1179656 | tf_op jit(solution)/shard_map/ppermute | solution.py:610
  96.3 21.7 %collective-permute-start.21 = (bf16[256,768]{1,0:T(8,128)(2,1)S(1)}, bf16[256,768]{1,0:T(8,128)(2,1)S(1)}, u32[]{:S(2)}, u32[]{:S(2)}) collective-permute-start(bf16[256,768]{1,0:T(8,128)(2,1)S(1)} %add_kernel.1), channel_id=1, source_target_pairs={{0,2},{1,3},{2,0},{3,1},{4,6},{5,7},{6,4},{7,5},{8,10},{9,11},{10,... | collective-permute-start | bytes 1179656 | tf_op jit(solution)/shard_map/ppermute | solution.py:610
  99.1 22.7 %all-to-all-start = ((bf16[8,112,576]{2,1,0:T(8,128)(2,1)}), bf16[8,112,576]{2,1,0:T(8,128)(2,1)S(1)}, u32[]{:S(2)}, u32[]{:S(2)}) async-start(bf16[8,112,576]{2,1,0:T(8,128)(2,1)} %qkv_grad_kernel.1), calls=%async_computation | async-start | bytes 2293760 | tf_op jit(solution)/shard_map/all_to_all | solution.py:796
  114.5 10.7 %collective-permute-start.28 = (bf16[96,192]{1,0:T(8,128)(2,1)S(1)}, bf16[96,192]{1,0:T(8,128)(2,1)S(1)}, u32[]{:S(2)}, u32[]{:S(2)}) collective-permute-start(bf16[96,192]{1,0:T(8,128)(2,1)S(1)} %get-tuple-element.150), channel_id=1, source_target_pairs={{0,1},{1,0},{2,3},{3,2},{4,5},{5,4},{6,7},{7,6},{8,9},{9,8},{10,11... | collective-permute-start | bytes 110600 | tf_op jit(solution)/shard_map/ppermute | solution.py:610
  114.6 12.6 %collective-permute-start.30 = (bf16[96,192]{1,0:T(8,128)(2,1)S(1)}, bf16[96,192]{1,0:T(8,128)(2,1)S(1)}, u32[]{:S(2)}, u32[]{:S(2)}) collective-permute-start(bf16[96,192]{1,0:T(8,128)(2,1)S(1)} %get-tuple-element.152), channel_id=1, source_target_pairs={{0,3},{1,2},{2,1},{3,0},{4,7},{5,6},{6,5},{7,4},{8,11},{9,10},{10,... | collective-permute-start | bytes 110600 | tf_op jit(solution)/shard_map/ppermute | solution.py:610
  115.8 13.5 %collective-permute-start.29 = (bf16[96,1088]{1,0:T(8,128)(2,1)S(1)}, bf16[96,1088]{1,0:T(8,128)(2,1)S(1)}, u32[]{:S(2)}, u32[]{:S(2)}) collective-permute-start(bf16[96,1088]{1,0:T(8,128)(2,1)S(1)} %get-tuple-element.151), channel_id=1, source_target_pairs={{0,2},{1,3},{2,0},{3,1},{4,6},{5,7},{6,4},{7,5},{8,10},{9,11},{10,... | collective-permute-start | bytes 626696 | tf_op jit(solution)/shard_map/ppermute | solution.py:610
  122.7 7.6 %collective-permute-start.24 = (f32[2,768]{1,0:T(2,128)S(1)}, f32[2,768]{1,0:T(2,128)S(1)}, u32[]{:S(2)}, u32[]{:S(2)}) collective-permute-start(f32[2,768]{1,0:T(2,128)S(1)} %get-tuple-element.144), channel_id=1, source_target_pairs={{0,3},{1,2},{2,1},{3,0},{4,7},{5,6},{6,5},{7,4},{8,11},{9,10},{10,... | collective-permute-start | bytes 18440 | tf_op jit(solution)/shard_map/ppermute | solution.py:610
  123.9 6.4 %collective-permute-start.23 = (f32[2,768]{1,0:T(2,128)S(1)}, f32[2,768]{1,0:T(2,128)S(1)}, u32[]{:S(2)}, u32[]{:S(2)}) collective-permute-start(f32[2,768]{1,0:T(2,128)S(1)} %get-tuple-element.144), channel_id=1, source_target_pairs={{0,2},{1,3},{2,0},{3,1},{4,6},{5,7},{6,4},{7,5},{8,10},{9,11},{10,... | collective-permute-start | bytes 18440 | tf_op jit(solution)/shard_map/ppermute | solution.py:610
  125.2 5.1 %collective-permute-start.22 = (f32[2,768]{1,0:T(2,128)S(1)}, f32[2,768]{1,0:T(2,128)S(1)}, u32[]{:S(2)}, u32[]{:S(2)}) collective-permute-start(f32[2,768]{1,0:T(2,128)S(1)} %get-tuple-element.144), channel_id=1, source_target_pairs={{0,1},{1,0},{2,3},{3,2},{4,5},{5,4},{6,7},{7,6},{8,9},{9,8},{10,11... | collective-permute-start | bytes 18440 | tf_op jit(solution)/shard_map/ppermute | solution.py:610
  (31 other events, 202.6 us)

commit v6 on v5

--- a/solution.py
+++ b/solution.py
@@ -61,7 +61,7 @@
     return lax.dot_general(a, b, dims, preferred_element_type=F32)
 
 
-def call(body, ins, outs, scratch=(), scalars=1, place=pltpu.VMEM):
+def call(body, ins, outs, scratch=(), scalars=1, place=pltpu.VMEM, far=()):
     name = getattr(body, "func", body).__name__
     specs = [pl.BlockSpec(memory_space=pltpu.SMEM)] * scalars
     specs += [pl.BlockSpec(memory_space=place)] * (len(ins) - scalars)
@@ -70,7 +70,7 @@
     return pl.pallas_call(
         body,
         name=name,
-        out_shape=tuple(jax.ShapeDtypeStruct(o.shape, o.dtype) for o in outs),
+        out_shape=tuple(pltpu.HBM(o.shape, o.dtype) if i in far else sds(o.shape, o.dtype) for i, o in enumerate(outs)),
         in_specs=specs,
         out_specs=tuple(pl.BlockSpec(memory_space=pltpu.VMEM) for _ in outs),
         scratch_shapes=list(scratch),
@@ -614,6 +614,10 @@
     return lax.ppermute(x, "wide", [(i, i ^ k) for i in range(lax.axis_size("wide"))])
 
 
+def in_hbm(x):
+    return pltpu.with_memory_space_constraint(x, pltpu.HBM)
+
+
 def tie(x, *others):
     return lax.optimization_barrier((x, *others))[0]
 
@@ -656,7 +660,7 @@
     if plane:
         slot_out, slot_ff = call(
             pack_kernel,
-            (scalars, *(pltpu.with_memory_space_constraint(w, pltpu.HBM) for w in (w_in, down_weight, output_weight))),
+            (scalars, in_hbm(w_in), in_hbm(down_weight), in_hbm(output_weight)),
             (sds((2 * few, D // 2), BF16), sds((many, D // 2), BF16)),
             [pltpu.SemaphoreType.DMA((many // PART,)), pltpu.SemaphoreType.DMA((2,))],
             place=pltpu.HBM,
@@ -757,6 +761,7 @@
             (even_part, along_wide(odd_part, 1)),
             (block, block_low, block_low, block_low),
             scalars=0,
+            far=(0,),
         )
         grad_recv = [along_wide(x, 2 * (i + 1)) for i, x in enumerate(grad_sends)]
         now = tie(scalars, *grad_sends)
@@ -800,7 +805,7 @@
     few_cols = sds((rows_d, COLS), BF16)
     grad_keep, *there = call(
         collect_kernel,
-        (tie(grad_sum, near_recv, pair_sum), *grad_recv),
+        (in_hbm(tie(grad_sum, near_recv, pair_sum)), *grad_recv),
         (sds((rows_d, half + COLS), F32), few_cols, sds((rows_d, half + COLS), BF16), few_cols),
         scalars=0,
     )

time: 131 us -> 130 us (level)
  local copies, waits for them, and re-layouts: 4.14 us -> 1.88 us
    unnamed x62 -> x58, local copies, waits for them, and re-layouts: 3.52 us -> 1.26 us
  transfers between devices with their start and end apart: 32 -> 32, of which waited for: 8 -> 8; matrix products, arithmetic and copies ran while one was open for 0% -> 0% of each run, Pallas kernels for 33% -> 34%
where the time goes in v6:
time: 130 us
  Pallas kernels  51.1 us (39%)
  starting transfers between devices  44.9 us (35%)
  waiting for transfers between devices  30.7 us (24%)
  local copies, waits for them, and re-layouts  1.88 us (1%)
    pallas_call x21, Pallas kernels, call(): pl.pallas_call(body, name=name, out_shape=tuple((pltpu.HBM(o.shape, o.dty...  51.1 us
    ppermute x21, starting transfers between devices, along_narrow(): return lax.ppermute(x, 'narrow', [(i, i ^ k) for i in range(NARROW)])  32.5 us
    ppermute x21, waiting for transfers between devices, along_narrow(): return lax.ppermute(x, 'narrow', [(i, i ^ k) for i in range(NARROW)])  30.7 us
    ppermute x10, starting transfers between devices, along_wide(): lax.ppermute(x, 'wide', [(i, i ^ k) for i in range(lax.axis_size('wide'))])  8.82 us
    all_to_all x1, starting transfers between devices, per_device(): lax.all_to_all(qkv_part, 'wide', 0, 0)  3.56 us
  transfers between devices with their start and end apart: 32, of which 8 were waited for; matrix products, arithmetic and copies ran while one was open for 0% of the time, Pallas kernels for 34%

profile of v6, /device:TPU:0, one launch (start us, length us, event | category | flops | bytes accessed | tf_op | source)
XLA Modules:
  0.0 129.9 jit_solution(8198380705810364942)
XLA Ops:
  0.7 1.7 %pack_kernel.1 = (bf16[96,384]{1,0:T(8,128)(2,1)S(1)}, bf16[224,384]{1,0:T(8,128)(2,1)S(1)}) custom-call(s32[2]{0:T(128)S(1)} %pad_add_fusion.s_ref, bf16[576,768]{1,0:T(8,128)(2,1)} %bitcast.10, bf16[288,768]{1,0:T(8,128)(2,1)} %dw_ref.5, bf16[192,768]{1,0:T(8,128)(2,1)} %w_ref.3), custom_call_target="tpu_custom_call" | custom-call | flops 1000000000 | bytes 1867784 | tf_op jit(solution)/shard_map/pack_kernel/pallas_call | solution.py:70
  2.5 5.1 %collective-permute-start.5 = (bf16[96,384]{1,0:T(8,128)(2,1)S(1)}, bf16[96,384]{1,0:T(8,128)(2,1)S(1)}, u32[]{:S(2)}, u32[]{:S(2)}) collective-permute-start(bf16[96,384]{1,0:T(8,128)(2,1)S(1)} %get-tuple-element.96), channel_id=1, source_target_pairs={{0,3},{1,2},{2,1},{3,0},{4,7},{5,6},{6,5},{7,4},{8,11},{9,10},{10,... | collective-permute-start | bytes 221192 | tf_op jit(solution)/shard_map/ppermute | solution.py:610
  8.2 2.3 %collective-permute-start.8 = (bf16[224,384]{1,0:T(8,128)(2,1)S(1)}, bf16[224,384]{1,0:T(8,128)(2,1)S(1)}, u32[]{:S(2)}, u32[]{:S(2)}) collective-permute-start(bf16[224,384]{1,0:T(8,128)(2,1)S(1)} %get-tuple-element.101), channel_id=1, source_target_pairs={{0,2},{1,3},{2,0},{3,1},{4,6},{5,7},{6,4},{7,5},{8,10},{9,11},{10,... | collective-permute-start | bytes 516104 | tf_op jit(solution)/shard_map/ppermute | solution.py:610
  10.6 3.2 %project_kernel.1 = (bf16[1024,256]{1,0:T(8,128)(2,1)S(1)}, bf16[1024,256]{1,0:T(8,128)(2,1)S(1)}, bf16[1024,256]{1,0:T(8,128)(2,1)S(1)}, bf16[1024,768]{1,0:T(8...) custom-call(bf16[1024,768]{1,0:T(8,128)(2,1)S(1)} %copy-done.5, s32[1,1024]{1,0:T(1,128)S(1)} %copy-done.10, ...), custom_call_target="tpu_custom_call" | custom-call | flops 6000000000 | bytes 7445504 | tf_op jit(solution)/shard_map/project_kernel/pallas_call | solution.py:70
  13.8 4.3 %attend_kernel.1 = (bf16[256,384]{1,0:T(8,128)(2,1)S(1)}, bf16[256,384]{1,0:T(8,128)(2,1)S(1)}, bf16[256,384]{1,0:T(8,128)(2,1)S(1)}, bf16[256,384]{1,0:T(8,128)(2,1)S(1)}, f32[1024,128]{1,0:T(8,128)S(1)}) custom-call(s32[2]{0:T(128)S(1)} %pad_add_fusion.s_ref, s32[1,1024]{1,0:T(1,128)S(1)} %copy-done.10, f32[1024,128]{1,0:T(8,128)S(1)} %get-tuple-element.82.segc_ref, ...), custom_call_target="tpu_custom_call" | custom-call | flops 99999997952 | bytes 3411976 | tf_op jit(solution)/shard_map/attend_kernel/pallas_call | solution.py:70
  18.8 1.6 %collective-permute-start.6 = (bf16[288,384]{1,0:T(8,128)(2,1)S(1)}, bf16[288,384]{1,0:T(8,128)(2,1)S(1)}, u32[]{:S(2)}, u32[]{:S(2)}) collective-permute-start(bf16[288,384]{1,0:T(8,128)(2,1)S(1)} %arrived_kernel.1.a0), channel_id=1, source_target_pairs={{0,8},{4,12},{8,0},{12,4},{16,24},{20,28},{24,16},{28,20},{1,9},{5... | collective-permute-start | bytes 663560 | tf_op jit(solution)/shard_map/ppermute | solution.py:614
  21.2 1.5 %collective-permute-start.9 = (bf16[224,384]{1,0:T(8,128)(2,1)S(1)}, bf16[224,384]{1,0:T(8,128)(2,1)S(1)}, u32[]{:S(2)}, u32[]{:S(2)}) collective-permute-start(bf16[224,384]{1,0:T(8,128)(2,1)S(1)} %collective-permute-done.8.a0), channel_id=1, source_target_pairs={{0,16},{4,20},{8,24},{12,28},{16,0},{20,4},{24,8},{28,12},{1,17},{... | collective-permute-start | bytes 516104 | tf_op jit(solution)/shard_map/ppermute | solution.py:614
  23.9 2.1 %collective-permute-start.1 = (bf16[256,384]{1,0:T(8,128)(2,1)S(1)}, bf16[256,384]{1,0:T(8,128)(2,1)S(1)}, u32[]{:S(2)}, u32[]{:S(2)}) collective-permute-start(bf16[256,384]{1,0:T(8,128)(2,1)S(1)} %get-tuple-element.88), channel_id=1, source_target_pairs={{0,2},{1,3},{2,0},{3,1},{4,6},{5,7},{6,4},{7,5},{8,10},{9,11},{10,... | collective-permute-start | bytes 589832 | tf_op jit(solution)/shard_map/ppermute | solution.py:610
  28.4 1.5 %collective-permute-start.10 = (bf16[2,224,384]{2,1,0:T(8,128)(2,1)S(1)}, bf16[2,224,384]{2,1,0:T(8,128)(2,1)S(1)}, u32[]{:S(2)}, u32[]{:S(2)}) collective-permute-start(bf16[2,224,384]{2,1,0:T(8,128)(2,1)S(1)} %pair_kernel.3.f0), channel_id=1, source_target_pairs={{0,8},{4,12},{8,0},{12,4},{16,24},{20,28},{24,16},{28,20},{1,9},{5... | collective-permute-start | bytes 1032200 | tf_op jit(solution)/shard_map/ppermute | solution.py:614
  30.0 1.8 %collective-permute-done.c1 = bf16[256,384]{1,0:T(8,128)(2,1)S(1)} collective-permute-done((bf16[256,384]{1,0:T(8,128)(2,1)S(1)}, bf16[256,384]{1,0:T(8,128)(2,1)S(1)}, u32[]{:S(2)}, u32[]{:S(2)}) %collective-permute-start) | collective-permute-done | bytes 196640 | tf_op jit(solution)/shard_map/ppermute | solution.py:610
  31.7 8.6 %collective-permute-done.1.c2 = bf16[256,384]{1,0:T(8,128)(2,1)S(1)} collective-permute-done((bf16[256,384]{1,0:T(8,128)(2,1)S(1)}, bf16[256,384]{1,0:T(8,128)(2,1)S(1)}, u32[]{:S(2)}, u32[]{:S(2)}) %collective-permute-start.1) | collective-permute-done | bytes 196640 | tf_op jit(solution)/shard_map/ppermute | solution.py:610
  42.3 3.4 %middle_kernel.1 = (f32[256,768]{1,0:T(8,128)S(1)}, bf16[512,768]{1,0:T(8,128)(2,1)S(1)}, bf16[256,288]{1,0:T(8,128)(2,1)S(1)}, bf16[256,576]{1,0:T(8,128)(2,1)S...) custom-call(s32[2]{0:T(128)S(1)} %pad_add_fusion.s_ref, ...), custom_call_target="tpu_custom_call" | custom-call | flops 5000000000 | bytes 10816520 | tf_op jit(solution)/shard_map/middle_kernel/pallas_call | solution.py:70
  45.7 3.0 %partner_kernel.1 = (bf16[256,288]{1,0:T(8,128)(2,1)S(1)}, bf16[256,576]{1,0:T(8,128)(2,1)S(1)}, bf16[256,768]{1,0:T(8,128)(2,1)}, bf16[256,768]{1,0:T(8,128)(2,1)S(1)}, bf16[896,768]{1,0:T(8,128)(2,1)S(1)}) custom-call(s32[2]{0:T(128)S(1)} %pad_add_fusion.s_ref, bf16[512,768]{1,0:T(8,128)(2,1)S(1)} %get-tuple-element.97.normed_ref, ...), custom_call_target="tpu_custom_call" | custom-call | flops 3000000000 | bytes 7127048 | tf_op jit(solution)/shard_map/partner_kernel/pallas_call | solution.py:70
  48.7 2.7 %collective-permute-start.13 = (bf16[256,768]{1,0:T(8,128)(2,1)S(1)}, bf16[256,768]{1,0:T(8,128)(2,1)S(1)}, u32[]{:S(2)}, u32[]{:S(2)}) collective-permute-start(bf16[256,768]{1,0:T(8,128)(2,1)S(1)} %get-tuple-element.109), channel_id=1, source_target_pairs={{0,1},{1,0},{2,3},{3,2},{4,5},{5,4},{6,7},{7,6},{8,9},{9,8},{10,11... | collective-permute-start | bytes 1179656 | tf_op jit(solution)/shard_map/ppermute | solution.py:610
  51.3 5.7 %own_kernel.1 = (f32[256,768]{1,0:T(8,128)S(1)}, f32[256,768]{1,0:T(8,128)S(1)}, bf16[768,1792]{1,0:T(8,128)(2,1)S(1)}) custom-call(s32[2]{0:T(128)S(1)} %pad_add_fusion.s_ref, bf16[512,768]{1,0:T(8,128)(2,1)S(1)} %get-tuple-element.97.normed_ref, bf16[512,768]{1,0:T(8,128)(2,1)S(1)} %get-tuple-element.92.cot_ref, ...), custom_call_target="tpu_custom_call" | custom-call | flops 10000000000 | bytes 10862600 | tf_op jit(solution)/shard_map/own_kernel/pallas_call | solution.py:70
  57.0 3.7 %collective-permute-done.13.recv_ref = bf16[256,768]{1,0:T(8,128)(2,1)S(1)} collective-permute-done((bf16[256,768]{1,0:T(8,128)(2,1)S(1)}, bf16[256,768]{1,0:T(8,128)(2,1)S(1)}, u32[]{:S(2)}, u32[]{:S(2)}) %collective-permute-start.13) | collective-permute-done | bytes 393248 | tf_op jit(solution)/shard_map/ppermute | solution.py:610
  63.5 1.8 %collective-permute-start.15 = (bf16[128,384]{1,0:T(8,128)(2,1)S(1)}, bf16[128,384]{1,0:T(8,128)(2,1)S(1)}, u32[]{:S(2)}, u32[]{:S(2)}) collective-permute-start(bf16[128,384]{1,0:T(8,128)(2,1)S(1)} %get-tuple-element.122), channel_id=1, source_target_pairs={{0,1},{1,0},{2,3},{3,2},{4,5},{5,4},{6,7},{7,6},{8,9},{9,8},{10,11... | collective-permute-start | bytes 294920 | tf_op jit(solution)/shard_map/ppermute | solution.py:610
  68.0 1.8 %fold_kernel.1 = (f32[96,2560]{1,0:T(8,128)}, bf16[96,2560]{1,0:T(8,128)(2,1)}, bf16[96,2560]{1,0:T(8,128)(2,1)}, bf16[96,2560]{1,0:T(8,128)(2,1)}) custom-call(bf16[4,96,2560]{2,1,0:T(8,128)(2,1)S(1)} %get-tuple-element.115.even_ref, bf16[4,96,2560]{2,1,0:T(8,128)(2,1)S(1)} %collective-permute-done.14.recv_ref), custom_call_target="tpu_custom_call" | custom-call | flops 2000000000 | bytes 6389760 | tf_op jit(solution)/shard_map/fold_kernel/pallas_call | solution.py:70
  73.3 2.8 %collective-permute-done.16.b2 = bf16[128,384]{1,0:T(8,128)(2,1)S(1)} collective-permute-done((bf16[128,384]{1,0:T(8,128)(2,1)S(1)}, bf16[128,384]{1,0:T(8,128)(2,1)S(1)}, u32[]{:S(2)}, u32[]{:S(2)}) %collective-permute-start.16) | collective-permute-done | bytes 98336 | tf_op jit(solution)/shard_map/ppermute | solution.py:610
  76.1 7.9 %backward_far_kernel.1 = (f32[256,768]{1,0:T(8,128)S(1)}, bf16[256,768]{1,0:T(8,128)(2,1)S(1)}, bf16[512,576]{1,0:T(8,128)(2,1)S(1)}, bf16[1024,256]{1,0:T(8,128...) custom-call(s32[2]{0:T(128)S(1)} %pad_add_fusion.s_ref, ...), custom_call_target="tpu_custom_call" | custom-call | flops 99999997952 | bytes 10391560 | tf_op jit(solution)/shard_map/backward_far_kernel/pallas_call | solution.py:70
  84.1 2.1 %collective-permute-start.20 = (bf16[256,768]{1,0:T(8,128)(2,1)S(1)}, bf16[256,768]{1,0:T(8,128)(2,1)S(1)}, u32[]{:S(2)}, u32[]{:S(2)}) collective-permute-start(bf16[256,768]{1,0:T(8,128)(2,1)S(1)} %get-tuple-element.140), channel_id=1, source_target_pairs={{0,1},{1,0},{2,3},{3,2},{4,5},{5,4},{6,7},{7,6},{8,9},{9,8},{10,11... | collective-permute-start | bytes 1179656 | tf_op jit(solution)/shard_map/ppermute | solution.py:610
  86.2 3.7 %backward_near_kernel.1 = (f32[256,768]{1,0:T(8,128)S(1)}, bf16[256,768]{1,0:T(8,128)(2,1)S(1)}, bf16[512,576]{1,0:T(8,128)(2,1)S(1)}) custom-call(s32[2]{0:T(128)S(1)} %pad_add_fusion.s_ref, s32[1,1024]{1,0:T(1,128)S(1)} %copy-done.11, f32[1024,128]{1,0:T(8,128)S(1)} %copy-done.20, bf16[1024,256]{1,0:T(8,128)(2,1)S(1)} %copy-done.14, ...), custom_call_target="tpu_custom_call" | custom-call | flops 99999997952 | bytes 9998344 | tf_op jit(solution)/shard_map/backward_near_kernel/pallas_call | solution.py:70
  90.0 4.1 %qkv_grad_kernel.1 = bf16[8,112,576]{2,1,0:T(8,128)(2,1)} custom-call(s32[2]{0:T(128)S(1)} %pad_add_fusion.s_ref, bf16[1024,768]{1,0:T(8,128)(2,1)S(1)} %get-tuple-element.135.normed_ref, bf16[512,576]{1,0:T(8,128)(2,1)S(1)} %get-tuple-element.136.near_ref, bf16[512,576]{1,0:T(8,128)(2,1)S(1)} %get-tuple-element.137.far_ref, ...), custom_call_target="tpu_custom_call" | custom-call | flops 1000000000 | bytes 4675592 | tf_op jit(solution)/shard_map/qkv_grad_kernel/pallas_call | solution.py:70
  94.0 2.2 %collective-permute-done.20.recv_ref = bf16[256,768]{1,0:T(8,128)(2,1)S(1)} collective-permute-done((bf16[256,768]{1,0:T(8,128)(2,1)S(1)}, bf16[256,768]{1,0:T(8,128)(2,1)S(1)}, u32[]{:S(2)}, u32[]{:S(2)}) %collective-permute-start.20) | collective-permute-done | bytes 393248 | tf_op jit(solution)/shard_map/ppermute | solution.py:610
  96.3 2.8 %collective-permute-start.21 = (bf16[256,768]{1,0:T(8,128)(2,1)S(1)}, bf16[256,768]{1,0:T(8,128)(2,1)S(1)}, u32[]{:S(2)}, u32[]{:S(2)}) collective-permute-start(bf16[256,768]{1,0:T(8,128)(2,1)S(1)} %add_kernel.1), channel_id=1, source_target_pairs={{0,2},{1,3},{2,0},{3,1},{4,6},{5,7},{6,4},{7,5},{8,10},{9,11},{10,... | collective-permute-start | bytes 1179656 | tf_op jit(solution)/shard_map/ppermute | solution.py:610
  99.1 3.6 %all-to-all-start = ((bf16[8,112,576]{2,1,0:T(8,128)(2,1)}), bf16[8,112,576]{2,1,0:T(8,128)(2,1)S(1)}, u32[]{:S(2)}, u32[]{:S(2)}) async-start(bf16[8,112,576]{2,1,0:T(8,128)(2,1)} %qkv_grad_kernel.1), calls=%async_computation | async-start | bytes 2293760 | tf_op jit(solution)/shard_map/all_to_all | solution.py:801
  102.7 8.6 %collective-permute-done.18.n1 = bf16[256,768]{1,0:T(8,128)(2,1)S(1)} collective-permute-done((bf16[256,768]{1,0:T(8,128)(2,1)S(1)}, bf16[256,768]{1,0:T(8,128)(2,1)S(1)}, u32[]{:S(2)}, u32[]{:S(2)}) %collective-permute-start.18) | collective-permute-done | bytes 393248 | tf_op jit(solution)/shard_map/ppermute | solution.py:610
  111.3 2.1 %collect_kernel.1 = (f32[96,1088]{1,0:T(8,128)S(1)}, bf16[96,192]{1,0:T(8,128)(2,1)S(1)}, bf16[96,1088]{1,0:T(8,128)(2,1)S(1)}, bf16[96,192]{1,0:T(8,128)(2,1)S(1)}) custom-call(f32[96,2560]{1,0:T(8,128)} %get-tuple-element.147.own_ref, bf16[96,2560]{1,0:T(8,128)(2,1)} %collective-permute-done.25.r1, bf16[96,2560]{1,0:T(8,128)(2,1)} %collective-permute-done.26.r2, ...), custom_call_target="tpu_custom_call" | custom-call | flops 1000000000 | bytes 3158016 | tf_op jit(solution)/shard_map/collect_kernel/pallas_call | solution.py:70
  114.8 2.3 %collective-permute-start.29 = (bf16[96,1088]{1,0:T(8,128)(2,1)S(1)}, bf16[96,1088]{1,0:T(8,128)(2,1)S(1)}, u32[]{:S(2)}, u32[]{:S(2)}) collective-permute-start(bf16[96,1088]{1,0:T(8,128)(2,1)S(1)} %get-tuple-element.151), channel_id=1, source_target_pairs={{0,2},{1,3},{2,0},{3,1},{4,6},{5,7},{6,4},{7,5},{8,10},{9,11},{10,... | collective-permute-start | bytes 626696 | tf_op jit(solution)/shard_map/ppermute | solution.py:610
  118.2 2.6 %final_kernel.1 = (f32[256,768]{1,0:T(8,128)}, bf16[256,768]{1,0:T(8,128)(2,1)}) custom-call(s32[2]{0:T(128)S(1)} %pad_add_fusion.s_ref, bf16[1024,768]{1,0:T(8,128)(2,1)S(1)} %copy-done.6, f32[1,768]{1,0:T(1,128)S(1)} %copy-done.3, f32[256,768]{1,0:T(8,128)S(1)} %copy-done.26, f32[256,768]{1,0:T(8,128)S(1)} %copy-done.24, ...), custom_call_target="tpu_custom_call" | custom-call | flops 99999997952 | bytes 6294536 | tf_op jit(solution)/shard_map/final_kernel/pallas_call | solution.py:70
  124.2 1.9 %collective-permute-start.22 = (f32[2,768]{1,0:T(2,128)S(1)}, f32[2,768]{1,0:T(2,128)S(1)}, u32[]{:S(2)}, u32[]{:S(2)}) collective-permute-start(f32[2,768]{1,0:T(2,128)S(1)} %get-tuple-element.144), channel_id=1, source_target_pairs={{0,1},{1,0},{2,3},{3,2},{4,5},{5,4},{6,7},{7,6},{8,9},{9,8},{10,11... | collective-permute-start | bytes 18440 | tf_op jit(solution)/shard_map/ppermute | solution.py:610
  126.1 2.2 %collective-permute-done.29.r2 = bf16[96,1088]{1,0:T(8,128)(2,1)S(1)} collective-permute-done((bf16[96,1088]{1,0:T(8,128)(2,1)S(1)}, bf16[96,1088]{1,0:T(8,128)(2,1)S(1)}, u32[]{:S(2)}, u32[]{:S(2)}) %collective-permute-start.29) | collective-permute-done | bytes 208928 | tf_op jit(solution)/shard_map/ppermute | solution.py:610
  (116 shorter events, 24.1 us)
Async XLA Ops:
  2.5 15.7 %collective-permute-start.5 = (bf16[96,384]{1,0:T(8,128)(2,1)S(1)}, bf16[96,384]{1,0:T(8,128)(2,1)S(1)}, u32[]{:S(2)}, u32[]{:S(2)}) collective-permute-start(bf16[96,384]{1,0:T(8,128)(2,1)S(1)} %get-tuple-element.96), channel_id=1, source_target_pairs={{0,3},{1,2},{2,1},{3,0},{4,7},{5,6},{6,5},{7,4},{8,11},{9,10},{10,... | collective-permute-start | bytes 221192 | tf_op jit(solution)/shard_map/ppermute | solution.py:610
  7.6 10.6 %collective-permute-start.4 = (bf16[96,384]{1,0:T(8,128)(2,1)S(1)}, bf16[96,384]{1,0:T(8,128)(2,1)S(1)}, u32[]{:S(2)}, u32[]{:S(2)}) collective-permute-start(bf16[96,384]{1,0:T(8,128)(2,1)S(1)} %get-tuple-element.96), channel_id=1, source_target_pairs={{0,2},{1,3},{2,0},{3,1},{4,6},{5,7},{6,4},{7,5},{8,10},{9,11},{10,... | collective-permute-start | bytes 221192 | tf_op jit(solution)/shard_map/ppermute | solution.py:610
  7.6 10.6 %collective-permute-start.3 = (bf16[96,384]{1,0:T(8,128)(2,1)S(1)}, bf16[96,384]{1,0:T(8,128)(2,1)S(1)}, u32[]{:S(2)}, u32[]{:S(2)}) collective-permute-start(bf16[96,384]{1,0:T(8,128)(2,1)S(1)} %get-tuple-element.96), channel_id=1, source_target_pairs={{0,1},{1,0},{2,3},{3,2},{4,5},{5,4},{6,7},{7,6},{8,9},{9,8},{10,11... | collective-permute-start | bytes 221192 | tf_op jit(solution)/shard_map/ppermute | solution.py:610
  8.2 12.9 %collective-permute-start.8 = (bf16[224,384]{1,0:T(8,128)(2,1)S(1)}, bf16[224,384]{1,0:T(8,128)(2,1)S(1)}, u32[]{:S(2)}, u32[]{:S(2)}) collective-permute-start(bf16[224,384]{1,0:T(8,128)(2,1)S(1)} %get-tuple-element.101), channel_id=1, source_target_pairs={{0,2},{1,3},{2,0},{3,1},{4,6},{5,7},{6,4},{7,5},{8,10},{9,11},{10,... | collective-permute-start | bytes 516104 | tf_op jit(solution)/shard_map/ppermute | solution.py:610
  18.8 8.3 %collective-permute-start.6 = (bf16[288,384]{1,0:T(8,128)(2,1)S(1)}, bf16[288,384]{1,0:T(8,128)(2,1)S(1)}, u32[]{:S(2)}, u32[]{:S(2)}) collective-permute-start(bf16[288,384]{1,0:T(8,128)(2,1)S(1)} %arrived_kernel.1.a0), channel_id=1, source_target_pairs={{0,8},{4,12},{8,0},{12,4},{16,24},{20,28},{24,16},{28,20},{1,9},{5... | collective-permute-start | bytes 663560 | tf_op jit(solution)/shard_map/ppermute | solution.py:614
  21.2 6.6 %collective-permute-start.9 = (bf16[224,384]{1,0:T(8,128)(2,1)S(1)}, bf16[224,384]{1,0:T(8,128)(2,1)S(1)}, u32[]{:S(2)}, u32[]{:S(2)}) collective-permute-start(bf16[224,384]{1,0:T(8,128)(2,1)S(1)} %collective-permute-done.8.a0), channel_id=1, source_target_pairs={{0,16},{4,20},{8,24},{12,28},{16,0},{20,4},{24,8},{28,12},{1,17},{... | collective-permute-start | bytes 516104 | tf_op jit(solution)/shard_map/ppermute | solution.py:614
  22.7 9.0 %collective-permute-start = (bf16[256,384]{1,0:T(8,128)(2,1)S(1)}, bf16[256,384]{1,0:T(8,128)(2,1)S(1)}, u32[]{:S(2)}, u32[]{:S(2)}) collective-permute-start(bf16[256,384]{1,0:T(8,128)(2,1)S(1)} %get-tuple-element.87), channel_id=1, source_target_pairs={{0,1},{1,0},{2,3},{3,2},{4,5},{5,4},{6,7},{7,6},{8,9},{9,8},{10,11... | collective-permute-start | bytes 589832 | tf_op jit(solution)/shard_map/ppermute | solution.py:610
  23.9 16.5 %collective-permute-start.1 = (bf16[256,384]{1,0:T(8,128)(2,1)S(1)}, bf16[256,384]{1,0:T(8,128)(2,1)S(1)}, u32[]{:S(2)}, u32[]{:S(2)}) collective-permute-start(bf16[256,384]{1,0:T(8,128)(2,1)S(1)} %get-tuple-element.88), channel_id=1, source_target_pairs={{0,2},{1,3},{2,0},{3,1},{4,6},{5,7},{6,4},{7,5},{8,10},{9,11},{10,... | collective-permute-start | bytes 589832 | tf_op jit(solution)/shard_map/ppermute | solution.py:610
  26.0 14.4 %collective-permute-start.2 = (bf16[256,384]{1,0:T(8,128)(2,1)S(1)}, bf16[256,384]{1,0:T(8,128)(2,1)S(1)}, u32[]{:S(2)}, u32[]{:S(2)}) collective-permute-start(bf16[256,384]{1,0:T(8,128)(2,1)S(1)} %get-tuple-element.89), channel_id=1, source_target_pairs={{0,3},{1,2},{2,1},{3,0},{4,7},{5,6},{6,5},{7,4},{8,11},{9,10},{10,... | collective-permute-start | bytes 589832 | tf_op jit(solution)/shard_map/ppermute | solution.py:610
  27.7 14.6 %collective-permute-start.7 = (bf16[2,288,384]{2,1,0:T(8,128)(2,1)S(1)}, bf16[2,288,384]{2,1,0:T(8,128)(2,1)S(1)}, u32[]{:S(2)}, u32[]{:S(2)}) collective-permute-start(bf16[2,288,384]{2,1,0:T(8,128)(2,1)S(1)} %pair_kernel.2.here_ref), channel_id=1, source_target_pairs={{0,4},{4,0},{8,12},{12,8},{16,20},{20,16},{24,28},{28,24},{1,5},{5... | collective-permute-start | bytes 1327112 | tf_op jit(solution)/shard_map/ppermute | solution.py:614
  28.4 13.4 %collective-permute-start.10 = (bf16[2,224,384]{2,1,0:T(8,128)(2,1)S(1)}, bf16[2,224,384]{2,1,0:T(8,128)(2,1)S(1)}, u32[]{:S(2)}, u32[]{:S(2)}) collective-permute-start(bf16[2,224,384]{2,1,0:T(8,128)(2,1)S(1)} %pair_kernel.3.f0), channel_id=1, source_target_pairs={{0,8},{4,12},{8,0},{12,4},{16,24},{20,28},{24,16},{28,20},{1,9},{5... | collective-permute-start | bytes 1032200 | tf_op jit(solution)/shard_map/ppermute | solution.py:614
  41.7 4.0 %collective-permute-start.11 = (bf16[2,224,384]{2,1,0:T(8,128)(2,1)S(1)}, bf16[2,224,384]{2,1,0:T(8,128)(2,1)S(1)}, u32[]{:S(2)}, u32[]{:S(2)}) collective-permute-start(bf16[2,224,384]{2,1,0:T(8,128)(2,1)S(1)} %pair_kernel.3.f0), channel_id=1, source_target_pairs={{0,4},{4,0},{8,12},{12,8},{16,20},{20,16},{24,28},{28,24},{1,5},{5... | collective-permute-start | bytes 1032200 | tf_op jit(solution)/shard_map/ppermute | solution.py:614
  41.8 3.9 %collective-permute-start.12 = (bf16[2,224,384]{2,1,0:T(8,128)(2,1)S(1)}, bf16[2,224,384]{2,1,0:T(8,128)(2,1)S(1)}, u32[]{:S(2)}, u32[]{:S(2)}) collective-permute-start(bf16[2,224,384]{2,1,0:T(8,128)(2,1)S(1)} %collective-permute-done.10.f1), channel_id=1, source_target_pairs={{0,4},{4,0},{8,12},{12,8},{16,20},{20,16},{24,28},{28,24},{1,5},{5... | collective-permute-start | bytes 1032200 | tf_op jit(solution)/shard_map/ppermute | solution.py:614
  48.7 12.0 %collective-permute-start.13 = (bf16[256,768]{1,0:T(8,128)(2,1)S(1)}, bf16[256,768]{1,0:T(8,128)(2,1)S(1)}, u32[]{:S(2)}, u32[]{:S(2)}) collective-permute-start(bf16[256,768]{1,0:T(8,128)(2,1)S(1)} %get-tuple-element.109), channel_id=1, source_target_pairs={{0,1},{1,0},{2,3},{3,2},{4,5},{5,4},{6,7},{7,6},{8,9},{9,8},{10,11... | collective-permute-start | bytes 1179656 | tf_op jit(solution)/shard_map/ppermute | solution.py:610
  63.4 4.5 %collective-permute-start.14 = (bf16[4,96,2560]{2,1,0:T(8,128)(2,1)S(1)}, bf16[4,96,2560]{2,1,0:T(8,128)(2,1)S(1)}, u32[]{:S(2)}, u32[]{:S(2)}) collective-permute-start(bf16[4,96,2560]{2,1,0:T(8,128)(2,1)S(1)} %get-tuple-element.116), channel_id=1, source_target_pairs={{0,4},{4,0},{8,12},{12,8},{16,20},{20,16},{24,28},{28,24},{1,5},{5... | collective-permute-start | bytes 5898248 | tf_op jit(solution)/shard_map/ppermute | solution.py:614
  63.5 8.3 %collective-permute-start.15 = (bf16[128,384]{1,0:T(8,128)(2,1)S(1)}, bf16[128,384]{1,0:T(8,128)(2,1)S(1)}, u32[]{:S(2)}, u32[]{:S(2)}) collective-permute-start(bf16[128,384]{1,0:T(8,128)(2,1)S(1)} %get-tuple-element.122), channel_id=1, source_target_pairs={{0,1},{1,0},{2,3},{3,2},{4,5},{5,4},{6,7},{7,6},{8,9},{9,8},{10,11... | collective-permute-start | bytes 294920 | tf_op jit(solution)/shard_map/ppermute | solution.py:610
  65.3 10.8 %collective-permute-start.16 = (bf16[128,384]{1,0:T(8,128)(2,1)S(1)}, bf16[128,384]{1,0:T(8,128)(2,1)S(1)}, u32[]{:S(2)}, u32[]{:S(2)}) collective-permute-start(bf16[128,384]{1,0:T(8,128)(2,1)S(1)} %get-tuple-element.123), channel_id=1, source_target_pairs={{0,2},{1,3},{2,0},{3,1},{4,6},{5,7},{6,4},{7,5},{8,10},{9,11},{10,... | collective-permute-start | bytes 294920 | tf_op jit(solution)/shard_map/ppermute | solution.py:610
  66.5 9.6 %collective-permute-start.17 = (bf16[128,384]{1,0:T(8,128)(2,1)S(1)}, bf16[128,384]{1,0:T(8,128)(2,1)S(1)}, u32[]{:S(2)}, u32[]{:S(2)}) collective-permute-start(bf16[128,384]{1,0:T(8,128)(2,1)S(1)} %get-tuple-element.124), channel_id=1, source_target_pairs={{0,3},{1,2},{2,1},{3,0},{4,7},{5,6},{6,5},{7,4},{8,11},{9,10},{10,... | collective-permute-start | bytes 294920 | tf_op jit(solution)/shard_map/ppermute | solution.py:610
  69.8 41.5 %collective-permute-start.25 = (bf16[96,2560]{1,0:T(8,128)(2,1)}, bf16[96,2560]{1,0:T(8,128)(2,1)}, u32[]{:S(2)}, u32[]{:S(2)}) collective-permute-start(bf16[96,2560]{1,0:T(8,128)(2,1)} %get-tuple-element.117), channel_id=1, source_target_pairs={{0,8},{4,12},{8,0},{12,4},{16,24},{20,28},{24,16},{28,20},{1,9},{5... | collective-permute-start | bytes 1474568 | tf_op jit(solution)/shard_map/ppermute | solution.py:614
  71.3 40.0 %collective-permute-start.26 = (bf16[96,2560]{1,0:T(8,128)(2,1)}, bf16[96,2560]{1,0:T(8,128)(2,1)}, u32[]{:S(2)}, u32[]{:S(2)}) collective-permute-start(bf16[96,2560]{1,0:T(8,128)(2,1)} %get-tuple-element.118), channel_id=1, source_target_pairs={{0,16},{4,20},{8,24},{12,28},{16,0},{20,4},{24,8},{28,12},{1,17},{... | collective-permute-start | bytes 1474568 | tf_op jit(solution)/shard_map/ppermute | solution.py:614
  71.8 39.5 %collective-permute-start.27 = (bf16[96,2560]{1,0:T(8,128)(2,1)}, bf16[96,2560]{1,0:T(8,128)(2,1)}, u32[]{:S(2)}, u32[]{:S(2)}) collective-permute-start(bf16[96,2560]{1,0:T(8,128)(2,1)} %get-tuple-element.119), channel_id=1, source_target_pairs={{0,24},{4,28},{8,16},{12,20},{16,8},{20,12},{24,0},{28,4},{1,25},{... | collective-permute-start | bytes 1474568 | tf_op jit(solution)/shard_map/ppermute | solution.py:614
  76.1 13.8 %collective-permute-start.19 = (bf16[256,768]{1,0:T(8,128)(2,1)}, bf16[256,768]{1,0:T(8,128)(2,1)}, u32[]{:S(2)}, u32[]{:S(2)}) collective-permute-start(bf16[256,768]{1,0:T(8,128)(2,1)} %get-tuple-element.133), channel_id=1, source_target_pairs={{0,1},{1,0},{2,3},{3,2},{4,5},{5,4},{6,7},{7,6},{8,9},{9,8},{10,11... | collective-permute-start | bytes 1179656 | tf_op jit(solution)/shard_map/ppermute | solution.py:610
  84.1 12.1 %collective-permute-start.20 = (bf16[256,768]{1,0:T(8,128)(2,1)S(1)}, bf16[256,768]{1,0:T(8,128)(2,1)S(1)}, u32[]{:S(2)}, u32[]{:S(2)}) collective-permute-start(bf16[256,768]{1,0:T(8,128)(2,1)S(1)} %get-tuple-element.140), channel_id=1, source_target_pairs={{0,1},{1,0},{2,3},{3,2},{4,5},{5,4},{6,7},{7,6},{8,9},{9,8},{10,11... | collective-permute-start | bytes 1179656 | tf_op jit(solution)/shard_map/ppermute | solution.py:610
  89.9 21.4 %collective-permute-start.18 = (bf16[256,768]{1,0:T(8,128)(2,1)S(1)}, bf16[256,768]{1,0:T(8,128)(2,1)S(1)}, u32[]{:S(2)}, u32[]{:S(2)}) collective-permute-start(bf16[256,768]{1,0:T(8,128)(2,1)S(1)} %get-tuple-element.130), channel_id=1, source_target_pairs={{0,1},{1,0},{2,3},{3,2},{4,5},{5,4},{6,7},{7,6},{8,9},{9,8},{10,11... | collective-permute-start | bytes 1179656 | tf_op jit(solution)/shard_map/ppermute | solution.py:610
  96.3 20.8 %collective-permute-start.21 = (bf16[256,768]{1,0:T(8,128)(2,1)S(1)}, bf16[256,768]{1,0:T(8,128)(2,1)S(1)}, u32[]{:S(2)}, u32[]{:S(2)}) collective-permute-start(bf16[256,768]{1,0:T(8,128)(2,1)S(1)} %add_kernel.1), channel_id=1, source_target_pairs={{0,2},{1,3},{2,0},{3,1},{4,6},{5,7},{6,4},{7,5},{8,10},{9,11},{10,... | collective-permute-start | bytes 1179656 | tf_op jit(solution)/shard_map/ppermute | solution.py:610
  99.1 21.7 %all-to-all-start = ((bf16[8,112,576]{2,1,0:T(8,128)(2,1)}), bf16[8,112,576]{2,1,0:T(8,128)(2,1)S(1)}, u32[]{:S(2)}, u32[]{:S(2)}) async-start(bf16[8,112,576]{2,1,0:T(8,128)(2,1)} %qkv_grad_kernel.1), calls=%async_computation | async-start | bytes 2293760 | tf_op jit(solution)/shard_map/all_to_all | solution.py:801
  113.5 10.7 %collective-permute-start.28 = (bf16[96,192]{1,0:T(8,128)(2,1)S(1)}, bf16[96,192]{1,0:T(8,128)(2,1)S(1)}, u32[]{:S(2)}, u32[]{:S(2)}) collective-permute-start(bf16[96,192]{1,0:T(8,128)(2,1)S(1)} %get-tuple-element.150), channel_id=1, source_target_pairs={{0,1},{1,0},{2,3},{3,2},{4,5},{5,4},{6,7},{7,6},{8,9},{9,8},{10,11... | collective-permute-start | bytes 110600 | tf_op jit(solution)/shard_map/ppermute | solution.py:610
  113.5 12.6 %collective-permute-start.30 = (bf16[96,192]{1,0:T(8,128)(2,1)S(1)}, bf16[96,192]{1,0:T(8,128)(2,1)S(1)}, u32[]{:S(2)}, u32[]{:S(2)}) collective-permute-start(bf16[96,192]{1,0:T(8,128)(2,1)S(1)} %get-tuple-element.152), channel_id=1, source_target_pairs={{0,3},{1,2},{2,1},{3,0},{4,7},{5,6},{6,5},{7,4},{8,11},{9,10},{10,... | collective-permute-start | bytes 110600 | tf_op jit(solution)/shard_map/ppermute | solution.py:610
  114.8 13.5 %collective-permute-start.29 = (bf16[96,1088]{1,0:T(8,128)(2,1)S(1)}, bf16[96,1088]{1,0:T(8,128)(2,1)S(1)}, u32[]{:S(2)}, u32[]{:S(2)}) collective-permute-start(bf16[96,1088]{1,0:T(8,128)(2,1)S(1)} %get-tuple-element.151), channel_id=1, source_target_pairs={{0,2},{1,3},{2,0},{3,1},{4,6},{5,7},{6,4},{7,5},{8,10},{9,11},{10,... | collective-permute-start | bytes 626696 | tf_op jit(solution)/shard_map/ppermute | solution.py:610
  121.7 7.6 %collective-permute-start.24 = (f32[2,768]{1,0:T(2,128)S(1)}, f32[2,768]{1,0:T(2,128)S(1)}, u32[]{:S(2)}, u32[]{:S(2)}) collective-permute-start(f32[2,768]{1,0:T(2,128)S(1)} %get-tuple-element.144), channel_id=1, source_target_pairs={{0,3},{1,2},{2,1},{3,0},{4,7},{5,6},{6,5},{7,4},{8,11},{9,10},{10,... | collective-permute-start | bytes 18440 | tf_op jit(solution)/shard_map/ppermute | solution.py:610
  122.8 6.4 %collective-permute-start.23 = (f32[2,768]{1,0:T(2,128)S(1)}, f32[2,768]{1,0:T(2,128)S(1)}, u32[]{:S(2)}, u32[]{:S(2)}) collective-permute-start(f32[2,768]{1,0:T(2,128)S(1)} %get-tuple-element.144), channel_id=1, source_target_pairs={{0,2},{1,3},{2,0},{3,1},{4,6},{5,7},{6,4},{7,5},{8,10},{9,11},{10,... | collective-permute-start | bytes 18440 | tf_op jit(solution)/shard_map/ppermute | solution.py:610
  124.2 5.1 %collective-permute-start.22 = (f32[2,768]{1,0:T(2,128)S(1)}, f32[2,768]{1,0:T(2,128)S(1)}, u32[]{:S(2)}, u32[]{:S(2)}) collective-permute-start(f32[2,768]{1,0:T(2,128)S(1)} %get-tuple-element.144), channel_id=1, source_target_pairs={{0,1},{1,0},{2,3},{3,2},{4,5},{5,4},{6,7},{7,6},{8,9},{9,8},{10,11... | collective-permute-start | bytes 18440 | tf_op jit(solution)/shard_map/ppermute | solution.py:610
  (29 other events, 200.1 us)

commit v7 on v6

--- a/solution.py
+++ b/solution.py
@@ -17,7 +17,6 @@
 LANES = 256
 DOC = 256
 QB = 128
-PART = 32
 WINDOW = QB + 2 * DOC
 EPSILON = 1e-05
 ROPE_BASE = 160000.0
@@ -405,36 +404,29 @@
     ]
     for copy in copies:
         copy.start()
-    n_in, n_down = w_in_ref.shape[0] // PART, w_down_ref.shape[0] // PART
-    parts = ff_ref.shape[0] // PART
-    for i in range(parts):
-        at = (slot // 2) * parts + i
-        there = ff_ref.at[i * PART : (i + 1) * PART, :]
-
-        def fetch(ref, first):
-            rows = pl.ds(pl.multiple_of((at - first) * PART, PART), PART)
-            return pltpu.make_async_copy(ref.at[rows, cols], there, sems.at[i])
-
-        @pl.when(at < n_in)
+    n_in, n_down, rows = w_in_ref.shape[0], w_down_ref.shape[0], ff_ref.shape[0]
+    for quarter in range(4):
+        first = quarter * rows
+        last = min(first + rows, n_in + n_down)
+
+        @pl.when(slot // 2 == quarter)
         def _():
-            fetch(w_in_ref, 0).start()
-
-        @pl.when((at >= n_in) & (at < n_in + n_down))
-        def _():
-            fetch(w_down_ref, n_in).start()
-
-        @pl.when(at >= n_in + n_down)
-        def _():
-            there[...] = jnp.zeros(there.shape, BF16)
+            mine = []
+            for ref, base, count in ((w_in_ref, 0, n_in), (w_down_ref, n_in, n_down)):
+                low, high = max(first, base), min(last, base + count)
+                if low < high:
+                    there = ff_ref.at[low - first : high - first, :]
+                    here = ref.at[low - base : high - base, cols]
+                    mine.append(pltpu.make_async_copy(here, there, sems.at[len(mine)]))
+            for copy in mine:
+                copy.start()
+            if last < first + rows:
+                ff_ref[last - first :, :] = jnp.zeros((first + rows - last, D // 2), BF16)
+            for copy in mine:
+                copy.wait()
 
     for copy in copies:
         copy.wait()
-    for i in range(parts):
-        there = ff_ref.at[i * PART : (i + 1) * PART, :]
-
-        @pl.when((slot // 2) * parts + i < n_in + n_down)
-        def _():
-            pltpu.make_async_copy(w_in_ref.at[:PART, : D // 2], there, sems.at[i]).wait()
 
 
 def arrived_kernel(s_ref, f1, f2, f3, out_ref):
@@ -662,7 +654,7 @@
             pack_kernel,
             (scalars, in_hbm(w_in), in_hbm(down_weight), in_hbm(output_weight)),
             (sds((2 * few, D // 2), BF16), sds((many, D // 2), BF16)),
-            [pltpu.SemaphoreType.DMA((many // PART,)), pltpu.SemaphoreType.DMA((2,))],
+            [pltpu.SemaphoreType.DMA((2,)), pltpu.SemaphoreType.DMA((2,))],
             place=pltpu.HBM,
         )
         out_fetched = [along_narrow(slot_out, k) for k in (1, 2, 3)]

time: 130 us -> 130 us (level)
  no operation moved by 1% of the time
where the time goes in v7:
time: 130 us
  Pallas kernels  51.2 us (39%)
  starting transfers between devices  44.9 us (35%)
  waiting for transfers between devices  30.8 us (24%)
  local copies, waits for them, and re-layouts  1.88 us (1%)
    pallas_call x21, Pallas kernels, call(): pl.pallas_call(body, name=name, out_shape=tuple((pltpu.HBM(o.shape, o.dty...  51.2 us
    ppermute x21, starting transfers between devices, along_narrow(): return lax.ppermute(x, 'narrow', [(i, i ^ k) for i in range(NARROW)])  32.5 us
    ppermute x21, waiting for transfers between devices, along_narrow(): return lax.ppermute(x, 'narrow', [(i, i ^ k) for i in range(NARROW)])  30.8 us
    ppermute x10, starting transfers between devices, along_wide(): lax.ppermute(x, 'wide', [(i, i ^ k) for i in range(lax.axis_size('wide'))])  8.81 us
    all_to_all x1, starting transfers between devices, per_device(): lax.all_to_all(qkv_part, 'wide', 0, 0)  3.56 us
  transfers between devices with their start and end apart: 32, of which 8 were waited for; matrix products, arithmetic and copies ran while one was open for 0% of the time, Pallas kernels for 34%

profile of v7, /device:TPU:0, one launch (start us, length us, event | category | flops | bytes accessed | tf_op | source)
XLA Modules:
  0.0 130.0 jit_solution(6930632301212583092)
XLA Ops:
  0.7 1.8 %pack_kernel.1 = (bf16[96,384]{1,0:T(8,128)(2,1)S(1)}, bf16[224,384]{1,0:T(8,128)(2,1)S(1)}) custom-call(s32[2]{0:T(128)S(1)} %pad_add_fusion.s_ref, bf16[576,768]{1,0:T(8,128)(2,1)} %bitcast.10, bf16[288,768]{1,0:T(8,128)(2,1)} %dw_ref.5, bf16[192,768]{1,0:T(8,128)(2,1)} %w_ref.3), custom_call_target="tpu_custom_call" | custom-call | flops 1000000000 | bytes 1867784 | tf_op jit(solution)/shard_map/pack_kernel/pallas_call | solution.py:69
  2.6 5.1 %collective-permute-start.5 = (bf16[96,384]{1,0:T(8,128)(2,1)S(1)}, bf16[96,384]{1,0:T(8,128)(2,1)S(1)}, u32[]{:S(2)}, u32[]{:S(2)}) collective-permute-start(bf16[96,384]{1,0:T(8,128)(2,1)S(1)} %get-tuple-element.96), channel_id=1, source_target_pairs={{0,3},{1,2},{2,1},{3,0},{4,7},{5,6},{6,5},{7,4},{8,11},{9,10},{10,... | collective-permute-start | bytes 221192 | tf_op jit(solution)/shard_map/ppermute | solution.py:602
  8.3 2.3 %collective-permute-start.8 = (bf16[224,384]{1,0:T(8,128)(2,1)S(1)}, bf16[224,384]{1,0:T(8,128)(2,1)S(1)}, u32[]{:S(2)}, u32[]{:S(2)}) collective-permute-start(bf16[224,384]{1,0:T(8,128)(2,1)S(1)} %get-tuple-element.101), channel_id=1, source_target_pairs={{0,2},{1,3},{2,0},{3,1},{4,6},{5,7},{6,4},{7,5},{8,10},{9,11},{10,... | collective-permute-start | bytes 516104 | tf_op jit(solution)/shard_map/ppermute | solution.py:602
  10.7 3.2 %project_kernel.1 = (bf16[1024,256]{1,0:T(8,128)(2,1)S(1)}, bf16[1024,256]{1,0:T(8,128)(2,1)S(1)}, bf16[1024,256]{1,0:T(8,128)(2,1)S(1)}, bf16[1024,768]{1,0:T(8...) custom-call(bf16[1024,768]{1,0:T(8,128)(2,1)S(1)} %copy-done.5, s32[1,1024]{1,0:T(1,128)S(1)} %copy-done.10, ...), custom_call_target="tpu_custom_call" | custom-call | flops 6000000000 | bytes 7445504 | tf_op jit(solution)/shard_map/project_kernel/pallas_call | solution.py:69
  13.9 4.3 %attend_kernel.1 = (bf16[256,384]{1,0:T(8,128)(2,1)S(1)}, bf16[256,384]{1,0:T(8,128)(2,1)S(1)}, bf16[256,384]{1,0:T(8,128)(2,1)S(1)}, bf16[256,384]{1,0:T(8,128)(2,1)S(1)}, f32[1024,128]{1,0:T(8,128)S(1)}) custom-call(s32[2]{0:T(128)S(1)} %pad_add_fusion.s_ref, s32[1,1024]{1,0:T(1,128)S(1)} %copy-done.10, f32[1024,128]{1,0:T(8,128)S(1)} %get-tuple-element.82.segc_ref, ...), custom_call_target="tpu_custom_call" | custom-call | flops 99999997952 | bytes 3411976 | tf_op jit(solution)/shard_map/attend_kernel/pallas_call | solution.py:69
  18.9 1.6 %collective-permute-start.6 = (bf16[288,384]{1,0:T(8,128)(2,1)S(1)}, bf16[288,384]{1,0:T(8,128)(2,1)S(1)}, u32[]{:S(2)}, u32[]{:S(2)}) collective-permute-start(bf16[288,384]{1,0:T(8,128)(2,1)S(1)} %arrived_kernel.1.a0), channel_id=1, source_target_pairs={{0,8},{4,12},{8,0},{12,4},{16,24},{20,28},{24,16},{28,20},{1,9},{5... | collective-permute-start | bytes 663560 | tf_op jit(solution)/shard_map/ppermute | solution.py:606
  21.3 1.5 %collective-permute-start.9 = (bf16[224,384]{1,0:T(8,128)(2,1)S(1)}, bf16[224,384]{1,0:T(8,128)(2,1)S(1)}, u32[]{:S(2)}, u32[]{:S(2)}) collective-permute-start(bf16[224,384]{1,0:T(8,128)(2,1)S(1)} %collective-permute-done.8.a0), channel_id=1, source_target_pairs={{0,16},{4,20},{8,24},{12,28},{16,0},{20,4},{24,8},{28,12},{1,17},{... | collective-permute-start | bytes 516104 | tf_op jit(solution)/shard_map/ppermute | solution.py:606
  24.0 2.1 %collective-permute-start.1 = (bf16[256,384]{1,0:T(8,128)(2,1)S(1)}, bf16[256,384]{1,0:T(8,128)(2,1)S(1)}, u32[]{:S(2)}, u32[]{:S(2)}) collective-permute-start(bf16[256,384]{1,0:T(8,128)(2,1)S(1)} %get-tuple-element.88), channel_id=1, source_target_pairs={{0,2},{1,3},{2,0},{3,1},{4,6},{5,7},{6,4},{7,5},{8,10},{9,11},{10,... | collective-permute-start | bytes 589832 | tf_op jit(solution)/shard_map/ppermute | solution.py:602
  28.5 1.5 %collective-permute-start.10 = (bf16[2,224,384]{2,1,0:T(8,128)(2,1)S(1)}, bf16[2,224,384]{2,1,0:T(8,128)(2,1)S(1)}, u32[]{:S(2)}, u32[]{:S(2)}) collective-permute-start(bf16[2,224,384]{2,1,0:T(8,128)(2,1)S(1)} %pair_kernel.3.f0), channel_id=1, source_target_pairs={{0,8},{4,12},{8,0},{12,4},{16,24},{20,28},{24,16},{28,20},{1,9},{5... | collective-permute-start | bytes 1032200 | tf_op jit(solution)/shard_map/ppermute | solution.py:606
  30.0 1.8 %collective-permute-done.c1 = bf16[256,384]{1,0:T(8,128)(2,1)S(1)} collective-permute-done((bf16[256,384]{1,0:T(8,128)(2,1)S(1)}, bf16[256,384]{1,0:T(8,128)(2,1)S(1)}, u32[]{:S(2)}, u32[]{:S(2)}) %collective-permute-start) | collective-permute-done | bytes 196640 | tf_op jit(solution)/shard_map/ppermute | solution.py:602
  31.8 8.6 %collective-permute-done.1.c2 = bf16[256,384]{1,0:T(8,128)(2,1)S(1)} collective-permute-done((bf16[256,384]{1,0:T(8,128)(2,1)S(1)}, bf16[256,384]{1,0:T(8,128)(2,1)S(1)}, u32[]{:S(2)}, u32[]{:S(2)}) %collective-permute-start.1) | collective-permute-done | bytes 196640 | tf_op jit(solution)/shard_map/ppermute | solution.py:602
  42.4 3.4 %middle_kernel.1 = (f32[256,768]{1,0:T(8,128)S(1)}, bf16[512,768]{1,0:T(8,128)(2,1)S(1)}, bf16[256,288]{1,0:T(8,128)(2,1)S(1)}, bf16[256,576]{1,0:T(8,128)(2,1)S...) custom-call(s32[2]{0:T(128)S(1)} %pad_add_fusion.s_ref, ...), custom_call_target="tpu_custom_call" | custom-call | flops 5000000000 | bytes 10816520 | tf_op jit(solution)/shard_map/middle_kernel/pallas_call | solution.py:69
  45.8 3.0 %partner_kernel.1 = (bf16[256,288]{1,0:T(8,128)(2,1)S(1)}, bf16[256,576]{1,0:T(8,128)(2,1)S(1)}, bf16[256,768]{1,0:T(8,128)(2,1)}, bf16[256,768]{1,0:T(8,128)(2,1)S(1)}, bf16[896,768]{1,0:T(8,128)(2,1)S(1)}) custom-call(s32[2]{0:T(128)S(1)} %pad_add_fusion.s_ref, bf16[512,768]{1,0:T(8,128)(2,1)S(1)} %get-tuple-element.97.normed_ref, ...), custom_call_target="tpu_custom_call" | custom-call | flops 3000000000 | bytes 7127048 | tf_op jit(solution)/shard_map/partner_kernel/pallas_call | solution.py:69
  48.8 2.7 %collective-permute-start.13 = (bf16[256,768]{1,0:T(8,128)(2,1)S(1)}, bf16[256,768]{1,0:T(8,128)(2,1)S(1)}, u32[]{:S(2)}, u32[]{:S(2)}) collective-permute-start(bf16[256,768]{1,0:T(8,128)(2,1)S(1)} %get-tuple-element.109), channel_id=1, source_target_pairs={{0,1},{1,0},{2,3},{3,2},{4,5},{5,4},{6,7},{7,6},{8,9},{9,8},{10,11... | collective-permute-start | bytes 1179656 | tf_op jit(solution)/shard_map/ppermute | solution.py:602
  51.4 5.7 %own_kernel.1 = (f32[256,768]{1,0:T(8,128)S(1)}, f32[256,768]{1,0:T(8,128)S(1)}, bf16[768,1792]{1,0:T(8,128)(2,1)S(1)}) custom-call(s32[2]{0:T(128)S(1)} %pad_add_fusion.s_ref, bf16[512,768]{1,0:T(8,128)(2,1)S(1)} %get-tuple-element.97.normed_ref, bf16[512,768]{1,0:T(8,128)(2,1)S(1)} %get-tuple-element.92.cot_ref, ...), custom_call_target="tpu_custom_call" | custom-call | flops 10000000000 | bytes 10862600 | tf_op jit(solution)/shard_map/own_kernel/pallas_call | solution.py:69
  57.1 3.7 %collective-permute-done.13.recv_ref = bf16[256,768]{1,0:T(8,128)(2,1)S(1)} collective-permute-done((bf16[256,768]{1,0:T(8,128)(2,1)S(1)}, bf16[256,768]{1,0:T(8,128)(2,1)S(1)}, u32[]{:S(2)}, u32[]{:S(2)}) %collective-permute-start.13) | collective-permute-done | bytes 393248 | tf_op jit(solution)/shard_map/ppermute | solution.py:602
  63.6 1.8 %collective-permute-start.15 = (bf16[128,384]{1,0:T(8,128)(2,1)S(1)}, bf16[128,384]{1,0:T(8,128)(2,1)S(1)}, u32[]{:S(2)}, u32[]{:S(2)}) collective-permute-start(bf16[128,384]{1,0:T(8,128)(2,1)S(1)} %get-tuple-element.122), channel_id=1, source_target_pairs={{0,1},{1,0},{2,3},{3,2},{4,5},{5,4},{6,7},{7,6},{8,9},{9,8},{10,11... | collective-permute-start | bytes 294920 | tf_op jit(solution)/shard_map/ppermute | solution.py:602
  68.1 1.8 %fold_kernel.1 = (f32[96,2560]{1,0:T(8,128)}, bf16[96,2560]{1,0:T(8,128)(2,1)}, bf16[96,2560]{1,0:T(8,128)(2,1)}, bf16[96,2560]{1,0:T(8,128)(2,1)}) custom-call(bf16[4,96,2560]{2,1,0:T(8,128)(2,1)S(1)} %get-tuple-element.115.even_ref, bf16[4,96,2560]{2,1,0:T(8,128)(2,1)S(1)} %collective-permute-done.14.recv_ref), custom_call_target="tpu_custom_call" | custom-call | flops 2000000000 | bytes 6389760 | tf_op jit(solution)/shard_map/fold_kernel/pallas_call | solution.py:69
  73.4 2.8 %collective-permute-done.16.b2 = bf16[128,384]{1,0:T(8,128)(2,1)S(1)} collective-permute-done((bf16[128,384]{1,0:T(8,128)(2,1)S(1)}, bf16[128,384]{1,0:T(8,128)(2,1)S(1)}, u32[]{:S(2)}, u32[]{:S(2)}) %collective-permute-start.16) | collective-permute-done | bytes 98336 | tf_op jit(solution)/shard_map/ppermute | solution.py:602
  76.2 7.9 %backward_far_kernel.1 = (f32[256,768]{1,0:T(8,128)S(1)}, bf16[256,768]{1,0:T(8,128)(2,1)S(1)}, bf16[512,576]{1,0:T(8,128)(2,1)S(1)}, bf16[1024,256]{1,0:T(8,128...) custom-call(s32[2]{0:T(128)S(1)} %pad_add_fusion.s_ref, ...), custom_call_target="tpu_custom_call" | custom-call | flops 99999997952 | bytes 10391560 | tf_op jit(solution)/shard_map/backward_far_kernel/pallas_call | solution.py:69
  84.2 2.1 %collective-permute-start.20 = (bf16[256,768]{1,0:T(8,128)(2,1)S(1)}, bf16[256,768]{1,0:T(8,128)(2,1)S(1)}, u32[]{:S(2)}, u32[]{:S(2)}) collective-permute-start(bf16[256,768]{1,0:T(8,128)(2,1)S(1)} %get-tuple-element.140), channel_id=1, source_target_pairs={{0,1},{1,0},{2,3},{3,2},{4,5},{5,4},{6,7},{7,6},{8,9},{9,8},{10,11... | collective-permute-start | bytes 1179656 | tf_op jit(solution)/shard_map/ppermute | solution.py:602
  86.3 3.7 %backward_near_kernel.1 = (f32[256,768]{1,0:T(8,128)S(1)}, bf16[256,768]{1,0:T(8,128)(2,1)S(1)}, bf16[512,576]{1,0:T(8,128)(2,1)S(1)}) custom-call(s32[2]{0:T(128)S(1)} %pad_add_fusion.s_ref, s32[1,1024]{1,0:T(1,128)S(1)} %copy-done.11, f32[1024,128]{1,0:T(8,128)S(1)} %copy-done.20, bf16[1024,256]{1,0:T(8,128)(2,1)S(1)} %copy-done.14, ...), custom_call_target="tpu_custom_call" | custom-call | flops 99999997952 | bytes 9998344 | tf_op jit(solution)/shard_map/backward_near_kernel/pallas_call | solution.py:69
  90.1 4.1 %qkv_grad_kernel.1 = bf16[8,112,576]{2,1,0:T(8,128)(2,1)} custom-call(s32[2]{0:T(128)S(1)} %pad_add_fusion.s_ref, bf16[1024,768]{1,0:T(8,128)(2,1)S(1)} %get-tuple-element.135.normed_ref, bf16[512,576]{1,0:T(8,128)(2,1)S(1)} %get-tuple-element.136.near_ref, bf16[512,576]{1,0:T(8,128)(2,1)S(1)} %get-tuple-element.137.far_ref, ...), custom_call_target="tpu_custom_call" | custom-call | flops 1000000000 | bytes 4675592 | tf_op jit(solution)/shard_map/qkv_grad_kernel/pallas_call | solution.py:69
  94.1 2.2 %collective-permute-done.20.recv_ref = bf16[256,768]{1,0:T(8,128)(2,1)S(1)} collective-permute-done((bf16[256,768]{1,0:T(8,128)(2,1)S(1)}, bf16[256,768]{1,0:T(8,128)(2,1)S(1)}, u32[]{:S(2)}, u32[]{:S(2)}) %collective-permute-start.20) | collective-permute-done | bytes 393248 | tf_op jit(solution)/shard_map/ppermute | solution.py:602
  96.4 2.8 %collective-permute-start.21 = (bf16[256,768]{1,0:T(8,128)(2,1)S(1)}, bf16[256,768]{1,0:T(8,128)(2,1)S(1)}, u32[]{:S(2)}, u32[]{:S(2)}) collective-permute-start(bf16[256,768]{1,0:T(8,128)(2,1)S(1)} %add_kernel.1), channel_id=1, source_target_pairs={{0,2},{1,3},{2,0},{3,1},{4,6},{5,7},{6,4},{7,5},{8,10},{9,11},{10,... | collective-permute-start | bytes 1179656 | tf_op jit(solution)/shard_map/ppermute | solution.py:602
  99.2 3.6 %all-to-all-start = ((bf16[8,112,576]{2,1,0:T(8,128)(2,1)}), bf16[8,112,576]{2,1,0:T(8,128)(2,1)S(1)}, u32[]{:S(2)}, u32[]{:S(2)}) async-start(bf16[8,112,576]{2,1,0:T(8,128)(2,1)} %qkv_grad_kernel.1), calls=%async_computation | async-start | bytes 2293760 | tf_op jit(solution)/shard_map/all_to_all | solution.py:793
  102.7 8.7 %collective-permute-done.18.n1 = bf16[256,768]{1,0:T(8,128)(2,1)S(1)} collective-permute-done((bf16[256,768]{1,0:T(8,128)(2,1)S(1)}, bf16[256,768]{1,0:T(8,128)(2,1)S(1)}, u32[]{:S(2)}, u32[]{:S(2)}) %collective-permute-start.18) | collective-permute-done | bytes 393248 | tf_op jit(solution)/shard_map/ppermute | solution.py:602
  111.4 2.1 %collect_kernel.1 = (f32[96,1088]{1,0:T(8,128)S(1)}, bf16[96,192]{1,0:T(8,128)(2,1)S(1)}, bf16[96,1088]{1,0:T(8,128)(2,1)S(1)}, bf16[96,192]{1,0:T(8,128)(2,1)S(1)}) custom-call(f32[96,2560]{1,0:T(8,128)} %get-tuple-element.147.own_ref, bf16[96,2560]{1,0:T(8,128)(2,1)} %collective-permute-done.25.r1, bf16[96,2560]{1,0:T(8,128)(2,1)} %collective-permute-done.26.r2, ...), custom_call_target="tpu_custom_call" | custom-call | flops 1000000000 | bytes 3158016 | tf_op jit(solution)/shard_map/collect_kernel/pallas_call | solution.py:69
  114.8 2.3 %collective-permute-start.29 = (bf16[96,1088]{1,0:T(8,128)(2,1)S(1)}, bf16[96,1088]{1,0:T(8,128)(2,1)S(1)}, u32[]{:S(2)}, u32[]{:S(2)}) collective-permute-start(bf16[96,1088]{1,0:T(8,128)(2,1)S(1)} %get-tuple-element.151), channel_id=1, source_target_pairs={{0,2},{1,3},{2,0},{3,1},{4,6},{5,7},{6,4},{7,5},{8,10},{9,11},{10,... | collective-permute-start | bytes 626696 | tf_op jit(solution)/shard_map/ppermute | solution.py:602
  118.3 2.6 %final_kernel.1 = (f32[256,768]{1,0:T(8,128)}, bf16[256,768]{1,0:T(8,128)(2,1)}) custom-call(s32[2]{0:T(128)S(1)} %pad_add_fusion.s_ref, bf16[1024,768]{1,0:T(8,128)(2,1)S(1)} %copy-done.6, f32[1,768]{1,0:T(1,128)S(1)} %copy-done.3, f32[256,768]{1,0:T(8,128)S(1)} %copy-done.26, f32[256,768]{1,0:T(8,128)S(1)} %copy-done.24, ...), custom_call_target="tpu_custom_call" | custom-call | flops 99999997952 | bytes 6294536 | tf_op jit(solution)/shard_map/final_kernel/pallas_call | solution.py:69
  124.2 1.9 %collective-permute-start.22 = (f32[2,768]{1,0:T(2,128)S(1)}, f32[2,768]{1,0:T(2,128)S(1)}, u32[]{:S(2)}, u32[]{:S(2)}) collective-permute-start(f32[2,768]{1,0:T(2,128)S(1)} %get-tuple-element.144), channel_id=1, source_target_pairs={{0,1},{1,0},{2,3},{3,2},{4,5},{5,4},{6,7},{7,6},{8,9},{9,8},{10,11... | collective-permute-start | bytes 18440 | tf_op jit(solution)/shard_map/ppermute | solution.py:602
  126.2 2.2 %collective-permute-done.29.r2 = bf16[96,1088]{1,0:T(8,128)(2,1)S(1)} collective-permute-done((bf16[96,1088]{1,0:T(8,128)(2,1)S(1)}, bf16[96,1088]{1,0:T(8,128)(2,1)S(1)}, u32[]{:S(2)}, u32[]{:S(2)}) %collective-permute-start.29) | collective-permute-done | bytes 208928 | tf_op jit(solution)/shard_map/ppermute | solution.py:602
  (116 shorter events, 24.1 us)
Async XLA Ops:
  2.6 15.7 %collective-permute-start.5 = (bf16[96,384]{1,0:T(8,128)(2,1)S(1)}, bf16[96,384]{1,0:T(8,128)(2,1)S(1)}, u32[]{:S(2)}, u32[]{:S(2)}) collective-permute-start(bf16[96,384]{1,0:T(8,128)(2,1)S(1)} %get-tuple-element.96), channel_id=1, source_target_pairs={{0,3},{1,2},{2,1},{3,0},{4,7},{5,6},{6,5},{7,4},{8,11},{9,10},{10,... | collective-permute-start | bytes 221192 | tf_op jit(solution)/shard_map/ppermute | solution.py:602
  7.7 10.6 %collective-permute-start.4 = (bf16[96,384]{1,0:T(8,128)(2,1)S(1)}, bf16[96,384]{1,0:T(8,128)(2,1)S(1)}, u32[]{:S(2)}, u32[]{:S(2)}) collective-permute-start(bf16[96,384]{1,0:T(8,128)(2,1)S(1)} %get-tuple-element.96), channel_id=1, source_target_pairs={{0,2},{1,3},{2,0},{3,1},{4,6},{5,7},{6,4},{7,5},{8,10},{9,11},{10,... | collective-permute-start | bytes 221192 | tf_op jit(solution)/shard_map/ppermute | solution.py:602
  7.7 10.6 %collective-permute-start.3 = (bf16[96,384]{1,0:T(8,128)(2,1)S(1)}, bf16[96,384]{1,0:T(8,128)(2,1)S(1)}, u32[]{:S(2)}, u32[]{:S(2)}) collective-permute-start(bf16[96,384]{1,0:T(8,128)(2,1)S(1)} %get-tuple-element.96), channel_id=1, source_target_pairs={{0,1},{1,0},{2,3},{3,2},{4,5},{5,4},{6,7},{7,6},{8,9},{9,8},{10,11... | collective-permute-start | bytes 221192 | tf_op jit(solution)/shard_map/ppermute | solution.py:602
  8.3 12.9 %collective-permute-start.8 = (bf16[224,384]{1,0:T(8,128)(2,1)S(1)}, bf16[224,384]{1,0:T(8,128)(2,1)S(1)}, u32[]{:S(2)}, u32[]{:S(2)}) collective-permute-start(bf16[224,384]{1,0:T(8,128)(2,1)S(1)} %get-tuple-element.101), channel_id=1, source_target_pairs={{0,2},{1,3},{2,0},{3,1},{4,6},{5,7},{6,4},{7,5},{8,10},{9,11},{10,... | collective-permute-start | bytes 516104 | tf_op jit(solution)/shard_map/ppermute | solution.py:602
  18.9 8.3 %collective-permute-start.6 = (bf16[288,384]{1,0:T(8,128)(2,1)S(1)}, bf16[288,384]{1,0:T(8,128)(2,1)S(1)}, u32[]{:S(2)}, u32[]{:S(2)}) collective-permute-start(bf16[288,384]{1,0:T(8,128)(2,1)S(1)} %arrived_kernel.1.a0), channel_id=1, source_target_pairs={{0,8},{4,12},{8,0},{12,4},{16,24},{20,28},{24,16},{28,20},{1,9},{5... | collective-permute-start | bytes 663560 | tf_op jit(solution)/shard_map/ppermute | solution.py:606
  21.3 6.6 %collective-permute-start.9 = (bf16[224,384]{1,0:T(8,128)(2,1)S(1)}, bf16[224,384]{1,0:T(8,128)(2,1)S(1)}, u32[]{:S(2)}, u32[]{:S(2)}) collective-permute-start(bf16[224,384]{1,0:T(8,128)(2,1)S(1)} %collective-permute-done.8.a0), channel_id=1, source_target_pairs={{0,16},{4,20},{8,24},{12,28},{16,0},{20,4},{24,8},{28,12},{1,17},{... | collective-permute-start | bytes 516104 | tf_op jit(solution)/shard_map/ppermute | solution.py:606
  22.8 9.0 %collective-permute-start = (bf16[256,384]{1,0:T(8,128)(2,1)S(1)}, bf16[256,384]{1,0:T(8,128)(2,1)S(1)}, u32[]{:S(2)}, u32[]{:S(2)}) collective-permute-start(bf16[256,384]{1,0:T(8,128)(2,1)S(1)} %get-tuple-element.87), channel_id=1, source_target_pairs={{0,1},{1,0},{2,3},{3,2},{4,5},{5,4},{6,7},{7,6},{8,9},{9,8},{10,11... | collective-permute-start | bytes 589832 | tf_op jit(solution)/shard_map/ppermute | solution.py:602
  24.0 16.5 %collective-permute-start.1 = (bf16[256,384]{1,0:T(8,128)(2,1)S(1)}, bf16[256,384]{1,0:T(8,128)(2,1)S(1)}, u32[]{:S(2)}, u32[]{:S(2)}) collective-permute-start(bf16[256,384]{1,0:T(8,128)(2,1)S(1)} %get-tuple-element.88), channel_id=1, source_target_pairs={{0,2},{1,3},{2,0},{3,1},{4,6},{5,7},{6,4},{7,5},{8,10},{9,11},{10,... | collective-permute-start | bytes 589832 | tf_op jit(solution)/shard_map/ppermute | solution.py:602
  26.1 14.4 %collective-permute-start.2 = (bf16[256,384]{1,0:T(8,128)(2,1)S(1)}, bf16[256,384]{1,0:T(8,128)(2,1)S(1)}, u32[]{:S(2)}, u32[]{:S(2)}) collective-permute-start(bf16[256,384]{1,0:T(8,128)(2,1)S(1)} %get-tuple-element.89), channel_id=1, source_target_pairs={{0,3},{1,2},{2,1},{3,0},{4,7},{5,6},{6,5},{7,4},{8,11},{9,10},{10,... | collective-permute-start | bytes 589832 | tf_op jit(solution)/shard_map/ppermute | solution.py:602
  27.8 14.6 %collective-permute-start.7 = (bf16[2,288,384]{2,1,0:T(8,128)(2,1)S(1)}, bf16[2,288,384]{2,1,0:T(8,128)(2,1)S(1)}, u32[]{:S(2)}, u32[]{:S(2)}) collective-permute-start(bf16[2,288,384]{2,1,0:T(8,128)(2,1)S(1)} %pair_kernel.2.here_ref), channel_id=1, source_target_pairs={{0,4},{4,0},{8,12},{12,8},{16,20},{20,16},{24,28},{28,24},{1,5},{5... | collective-permute-start | bytes 1327112 | tf_op jit(solution)/shard_map/ppermute | solution.py:606
  28.5 13.4 %collective-permute-start.10 = (bf16[2,224,384]{2,1,0:T(8,128)(2,1)S(1)}, bf16[2,224,384]{2,1,0:T(8,128)(2,1)S(1)}, u32[]{:S(2)}, u32[]{:S(2)}) collective-permute-start(bf16[2,224,384]{2,1,0:T(8,128)(2,1)S(1)} %pair_kernel.3.f0), channel_id=1, source_target_pairs={{0,8},{4,12},{8,0},{12,4},{16,24},{20,28},{24,16},{28,20},{1,9},{5... | collective-permute-start | bytes 1032200 | tf_op jit(solution)/shard_map/ppermute | solution.py:606
  41.8 4.0 %collective-permute-start.11 = (bf16[2,224,384]{2,1,0:T(8,128)(2,1)S(1)}, bf16[2,224,384]{2,1,0:T(8,128)(2,1)S(1)}, u32[]{:S(2)}, u32[]{:S(2)}) collective-permute-start(bf16[2,224,384]{2,1,0:T(8,128)(2,1)S(1)} %pair_kernel.3.f0), channel_id=1, source_target_pairs={{0,4},{4,0},{8,12},{12,8},{16,20},{20,16},{24,28},{28,24},{1,5},{5... | collective-permute-start | bytes 1032200 | tf_op jit(solution)/shard_map/ppermute | solution.py:606
  41.9 3.9 %collective-permute-start.12 = (bf16[2,224,384]{2,1,0:T(8,128)(2,1)S(1)}, bf16[2,224,384]{2,1,0:T(8,128)(2,1)S(1)}, u32[]{:S(2)}, u32[]{:S(2)}) collective-permute-start(bf16[2,224,384]{2,1,0:T(8,128)(2,1)S(1)} %collective-permute-done.10.f1), channel_id=1, source_target_pairs={{0,4},{4,0},{8,12},{12,8},{16,20},{20,16},{24,28},{28,24},{1,5},{5... | collective-permute-start | bytes 1032200 | tf_op jit(solution)/shard_map/ppermute | solution.py:606
  48.8 12.0 %collective-permute-start.13 = (bf16[256,768]{1,0:T(8,128)(2,1)S(1)}, bf16[256,768]{1,0:T(8,128)(2,1)S(1)}, u32[]{:S(2)}, u32[]{:S(2)}) collective-permute-start(bf16[256,768]{1,0:T(8,128)(2,1)S(1)} %get-tuple-element.109), channel_id=1, source_target_pairs={{0,1},{1,0},{2,3},{3,2},{4,5},{5,4},{6,7},{7,6},{8,9},{9,8},{10,11... | collective-permute-start | bytes 1179656 | tf_op jit(solution)/shard_map/ppermute | solution.py:602
  63.5 4.5 %collective-permute-start.14 = (bf16[4,96,2560]{2,1,0:T(8,128)(2,1)S(1)}, bf16[4,96,2560]{2,1,0:T(8,128)(2,1)S(1)}, u32[]{:S(2)}, u32[]{:S(2)}) collective-permute-start(bf16[4,96,2560]{2,1,0:T(8,128)(2,1)S(1)} %get-tuple-element.116), channel_id=1, source_target_pairs={{0,4},{4,0},{8,12},{12,8},{16,20},{20,16},{24,28},{28,24},{1,5},{5... | collective-permute-start | bytes 5898248 | tf_op jit(solution)/shard_map/ppermute | solution.py:606
  63.6 8.3 %collective-permute-start.15 = (bf16[128,384]{1,0:T(8,128)(2,1)S(1)}, bf16[128,384]{1,0:T(8,128)(2,1)S(1)}, u32[]{:S(2)}, u32[]{:S(2)}) collective-permute-start(bf16[128,384]{1,0:T(8,128)(2,1)S(1)} %get-tuple-element.122), channel_id=1, source_target_pairs={{0,1},{1,0},{2,3},{3,2},{4,5},{5,4},{6,7},{7,6},{8,9},{9,8},{10,11... | collective-permute-start | bytes 294920 | tf_op jit(solution)/shard_map/ppermute | solution.py:602
  65.4 10.8 %collective-permute-start.16 = (bf16[128,384]{1,0:T(8,128)(2,1)S(1)}, bf16[128,384]{1,0:T(8,128)(2,1)S(1)}, u32[]{:S(2)}, u32[]{:S(2)}) collective-permute-start(bf16[128,384]{1,0:T(8,128)(2,1)S(1)} %get-tuple-element.123), channel_id=1, source_target_pairs={{0,2},{1,3},{2,0},{3,1},{4,6},{5,7},{6,4},{7,5},{8,10},{9,11},{10,... | collective-permute-start | bytes 294920 | tf_op jit(solution)/shard_map/ppermute | solution.py:602
  66.6 9.6 %collective-permute-start.17 = (bf16[128,384]{1,0:T(8,128)(2,1)S(1)}, bf16[128,384]{1,0:T(8,128)(2,1)S(1)}, u32[]{:S(2)}, u32[]{:S(2)}) collective-permute-start(bf16[128,384]{1,0:T(8,128)(2,1)S(1)} %get-tuple-element.124), channel_id=1, source_target_pairs={{0,3},{1,2},{2,1},{3,0},{4,7},{5,6},{6,5},{7,4},{8,11},{9,10},{10,... | collective-permute-start | bytes 294920 | tf_op jit(solution)/shard_map/ppermute | solution.py:602
  69.9 41.5 %collective-permute-start.25 = (bf16[96,2560]{1,0:T(8,128)(2,1)}, bf16[96,2560]{1,0:T(8,128)(2,1)}, u32[]{:S(2)}, u32[]{:S(2)}) collective-permute-start(bf16[96,2560]{1,0:T(8,128)(2,1)} %get-tuple-element.117), channel_id=1, source_target_pairs={{0,8},{4,12},{8,0},{12,4},{16,24},{20,28},{24,16},{28,20},{1,9},{5... | collective-permute-start | bytes 1474568 | tf_op jit(solution)/shard_map/ppermute | solution.py:606
  71.4 40.0 %collective-permute-start.26 = (bf16[96,2560]{1,0:T(8,128)(2,1)}, bf16[96,2560]{1,0:T(8,128)(2,1)}, u32[]{:S(2)}, u32[]{:S(2)}) collective-permute-start(bf16[96,2560]{1,0:T(8,128)(2,1)} %get-tuple-element.118), channel_id=1, source_target_pairs={{0,16},{4,20},{8,24},{12,28},{16,0},{20,4},{24,8},{28,12},{1,17},{... | collective-permute-start | bytes 1474568 | tf_op jit(solution)/shard_map/ppermute | solution.py:606
  71.9 39.5 %collective-permute-start.27 = (bf16[96,2560]{1,0:T(8,128)(2,1)}, bf16[96,2560]{1,0:T(8,128)(2,1)}, u32[]{:S(2)}, u32[]{:S(2)}) collective-permute-start(bf16[96,2560]{1,0:T(8,128)(2,1)} %get-tuple-element.119), channel_id=1, source_target_pairs={{0,24},{4,28},{8,16},{12,20},{16,8},{20,12},{24,0},{28,4},{1,25},{... | collective-permute-start | bytes 1474568 | tf_op jit(solution)/shard_map/ppermute | solution.py:606
  76.2 13.8 %collective-permute-start.19 = (bf16[256,768]{1,0:T(8,128)(2,1)}, bf16[256,768]{1,0:T(8,128)(2,1)}, u32[]{:S(2)}, u32[]{:S(2)}) collective-permute-start(bf16[256,768]{1,0:T(8,128)(2,1)} %get-tuple-element.133), channel_id=1, source_target_pairs={{0,1},{1,0},{2,3},{3,2},{4,5},{5,4},{6,7},{7,6},{8,9},{9,8},{10,11... | collective-permute-start | bytes 1179656 | tf_op jit(solution)/shard_map/ppermute | solution.py:602
  84.2 12.1 %collective-permute-start.20 = (bf16[256,768]{1,0:T(8,128)(2,1)S(1)}, bf16[256,768]{1,0:T(8,128)(2,1)S(1)}, u32[]{:S(2)}, u32[]{:S(2)}) collective-permute-start(bf16[256,768]{1,0:T(8,128)(2,1)S(1)} %get-tuple-element.140), channel_id=1, source_target_pairs={{0,1},{1,0},{2,3},{3,2},{4,5},{5,4},{6,7},{7,6},{8,9},{9,8},{10,11... | collective-permute-start | bytes 1179656 | tf_op jit(solution)/shard_map/ppermute | solution.py:602
  90.0 21.4 %collective-permute-start.18 = (bf16[256,768]{1,0:T(8,128)(2,1)S(1)}, bf16[256,768]{1,0:T(8,128)(2,1)S(1)}, u32[]{:S(2)}, u32[]{:S(2)}) collective-permute-start(bf16[256,768]{1,0:T(8,128)(2,1)S(1)} %get-tuple-element.130), channel_id=1, source_target_pairs={{0,1},{1,0},{2,3},{3,2},{4,5},{5,4},{6,7},{7,6},{8,9},{9,8},{10,11... | collective-permute-start | bytes 1179656 | tf_op jit(solution)/shard_map/ppermute | solution.py:602
  96.4 20.8 %collective-permute-start.21 = (bf16[256,768]{1,0:T(8,128)(2,1)S(1)}, bf16[256,768]{1,0:T(8,128)(2,1)S(1)}, u32[]{:S(2)}, u32[]{:S(2)}) collective-permute-start(bf16[256,768]{1,0:T(8,128)(2,1)S(1)} %add_kernel.1), channel_id=1, source_target_pairs={{0,2},{1,3},{2,0},{3,1},{4,6},{5,7},{6,4},{7,5},{8,10},{9,11},{10,... | collective-permute-start | bytes 1179656 | tf_op jit(solution)/shard_map/ppermute | solution.py:602
  99.2 21.7 %all-to-all-start = ((bf16[8,112,576]{2,1,0:T(8,128)(2,1)}), bf16[8,112,576]{2,1,0:T(8,128)(2,1)S(1)}, u32[]{:S(2)}, u32[]{:S(2)}) async-start(bf16[8,112,576]{2,1,0:T(8,128)(2,1)} %qkv_grad_kernel.1), calls=%async_computation | async-start | bytes 2293760 | tf_op jit(solution)/shard_map/all_to_all | solution.py:793
  113.6 10.7 %collective-permute-start.28 = (bf16[96,192]{1,0:T(8,128)(2,1)S(1)}, bf16[96,192]{1,0:T(8,128)(2,1)S(1)}, u32[]{:S(2)}, u32[]{:S(2)}) collective-permute-start(bf16[96,192]{1,0:T(8,128)(2,1)S(1)} %get-tuple-element.150), channel_id=1, source_target_pairs={{0,1},{1,0},{2,3},{3,2},{4,5},{5,4},{6,7},{7,6},{8,9},{9,8},{10,11... | collective-permute-start | bytes 110600 | tf_op jit(solution)/shard_map/ppermute | solution.py:602
  113.6 12.6 %collective-permute-start.30 = (bf16[96,192]{1,0:T(8,128)(2,1)S(1)}, bf16[96,192]{1,0:T(8,128)(2,1)S(1)}, u32[]{:S(2)}, u32[]{:S(2)}) collective-permute-start(bf16[96,192]{1,0:T(8,128)(2,1)S(1)} %get-tuple-element.152), channel_id=1, source_target_pairs={{0,3},{1,2},{2,1},{3,0},{4,7},{5,6},{6,5},{7,4},{8,11},{9,10},{10,... | collective-permute-start | bytes 110600 | tf_op jit(solution)/shard_map/ppermute | solution.py:602
  114.8 13.5 %collective-permute-start.29 = (bf16[96,1088]{1,0:T(8,128)(2,1)S(1)}, bf16[96,1088]{1,0:T(8,128)(2,1)S(1)}, u32[]{:S(2)}, u32[]{:S(2)}) collective-permute-start(bf16[96,1088]{1,0:T(8,128)(2,1)S(1)} %get-tuple-element.151), channel_id=1, source_target_pairs={{0,2},{1,3},{2,0},{3,1},{4,6},{5,7},{6,4},{7,5},{8,10},{9,11},{10,... | collective-permute-start | bytes 626696 | tf_op jit(solution)/shard_map/ppermute | solution.py:602
  121.8 7.6 %collective-permute-start.24 = (f32[2,768]{1,0:T(2,128)S(1)}, f32[2,768]{1,0:T(2,128)S(1)}, u32[]{:S(2)}, u32[]{:S(2)}) collective-permute-start(f32[2,768]{1,0:T(2,128)S(1)} %get-tuple-element.144), channel_id=1, source_target_pairs={{0,3},{1,2},{2,1},{3,0},{4,7},{5,6},{6,5},{7,4},{8,11},{9,10},{10,... | collective-permute-start | bytes 18440 | tf_op jit(solution)/shard_map/ppermute | solution.py:602
  122.9 6.4 %collective-permute-start.23 = (f32[2,768]{1,0:T(2,128)S(1)}, f32[2,768]{1,0:T(2,128)S(1)}, u32[]{:S(2)}, u32[]{:S(2)}) collective-permute-start(f32[2,768]{1,0:T(2,128)S(1)} %get-tuple-element.144), channel_id=1, source_target_pairs={{0,2},{1,3},{2,0},{3,1},{4,6},{5,7},{6,4},{7,5},{8,10},{9,11},{10,... | collective-permute-start | bytes 18440 | tf_op jit(solution)/shard_map/ppermute | solution.py:602
  124.2 5.2 %collective-permute-start.22 = (f32[2,768]{1,0:T(2,128)S(1)}, f32[2,768]{1,0:T(2,128)S(1)}, u32[]{:S(2)}, u32[]{:S(2)}) collective-permute-start(f32[2,768]{1,0:T(2,128)S(1)} %get-tuple-element.144), channel_id=1, source_target_pairs={{0,1},{1,0},{2,3},{3,2},{4,5},{5,4},{6,7},{7,6},{8,9},{9,8},{10,11... | collective-permute-start | bytes 18440 | tf_op jit(solution)/shard_map/ppermute | solution.py:602
  (29 other events, 200.5 us)
